TPU v7x, 256 devices: a whole 4x4x8 slice. The times are simulated.
256 devices in a mesh: grp: 8 (over z_lo, core), cut: 8 (over z_hi, x), st: 4 (over y).
Axes of the slice: x: 4, y: 4, z: 8 (z_hi: 2, z_lo: 4; z = z_hi * 4 + z_lo), core: 2. Of those that a mesh axis runs over, the one named last changes fastest.
Arguments:
- coefficients: bfloat16 [8192, 2048], P(('grp', 'cut')), may hold values from -0.125 to 0.125
- intercepts: bfloat16 [8192], P(('grp', 'cut')), may hold values from -6 to 6
- states: bfloat16 [65536, 2048], P(('grp', 'st')), may hold values from -6 to 6
- old_values: float32 [65536], P(('grp', 'st')), may hold values from 3.5 to 6.5
Outputs:
- new_values: float32 [65536], P(('grp', 'st'))
- cut_gaps: float32 [8192], P(('grp', 'cut'))
All inputs are finite; a program needn't handle non-finite values.
Results may differ from a plain program's by a relative error of at most 0.0003.
Values may be sent and summed in bfloat16 or wider, within the bound.
No kernel may reach another device: no remote copies, remote signals or barrier semaphores. Data moves between devices by JAX's collectives and lax.ppermute only.
A program may use at most 64 MiB of HBM per device.

v0:
```python
import jax
import jax.numpy as jnp
from jax import lax
from jax.sharding import PartitionSpec as P


def shifted(block, axis, distance):
    devices = range(lax.axis_size(axis))
    route = [((i - distance) % len(devices), i) for i in devices]
    return lax.ppermute(block, axis, route)


def body(coefficients, intercepts, states, old_values):
    groups = lax.axis_size("grp")
    own_group = lax.axis_index("grp")
    cut_rows = coefficients.shape[0]
    start_value = jnp.full((states.shape[0],), -jnp.inf, dtype=jnp.float32)
    visiting = (coefficients, intercepts)
    top_value = start_value
    lift_table = jnp.zeros((groups, cut_rows), jnp.float32)
    for offset in range(groups):
        scores = lax.dot_general(
            visiting[0], states, (((1,), (1,)), ((), ())), preferred_element_type=jnp.float32
        )
        scores = scores + visiting[1].astype(jnp.float32)[:, None]
        row_best = jnp.max(scores, axis=0)
        lift_row = jnp.max(scores - old_values[None, :], axis=1)
        top_value = jnp.maximum(top_value, row_best)
        source = (own_group - offset) % groups
        lift_table = lax.dynamic_update_slice_in_dim(lift_table, lift_row[None, :], source, 0)
        if offset + 1 < groups:
            visiting = shifted((visiting[0], visiting[1]), "grp", 1)
    returned = lax.all_to_all(lift_table, "grp", split_axis=0, concat_axis=0, tiled=True)
    group_lift = jnp.max(returned, axis=0)
    cut_gaps = lax.pmax(group_lift, "st")
    overall = lax.pmax(top_value, "cut")
    new_values = jnp.maximum(old_values, overall)
    return (new_values, cut_gaps)


def solution(mesh):
    placed = (P(("grp", "cut"), None), P(("grp", "cut")), P(("grp", "st"), None), P(("grp", "st")))
    return jax.shard_map(
        body,
        mesh=mesh,
        in_specs=placed,
        out_specs=(P(("grp", "st")), P(("grp", "cut"))),
        check_vma=False,
    )
```

profile of v0, /device:TPU:32, one launch (start us, length us, event | category | flops | bytes accessed | tf_op | source)
XLA Modules:
  0.0 160.1 jit_solution(3587068488301708246)
XLA Ops:
  0.6 0.1 collective-permute-start
  0.7 2.0 %collective-permute-start.1 = (bf16[128]{0:T(256)(128)(2,1)}, bf16[128]{0:T(256)(128)(2,1)S(1)}, u32[]{:S(2)}, u32[]{:S(2)}) collective-permute-start(bf16[128]{0:T(256)(128)(2,1)} %param.5), channel_id=1, source_target_pairs={{224,0},{0,32},{32,64},{64,96},{96,128},{128,160},{160,192},{192,2... | collective-permute-start | bytes 776 | tf_op jit(solution)/shard_map/ppermute | solution.py:10
  2.7 0.7 convert_element_type.24
  3.4 6.5 %convolution_add_fusion.7 = f32[128,2048]{1,0:T(8,128)S(1)} fusion(bf16[128,2048]{1,0:T(8,128)(2,1)} %param.4, bf16[2048,2048]{1,0:T(8,128)(2,1)} %param.6, f32[128]{0:T(128)S(1)} %convert_element_type.24), kind=kOutput, calls=%fused_computation.7 | convolution fusion | flops 1074003968 | bytes 9961984 | tf_op jit(solution)/shard_map/dot_general | solution.py:22
  9.9 0.0 collective-permute-done.1
  9.9 0.2 collective-permute-start.3
  10.1 2.8 %collective-permute-done.3 = bf16[128]{0:T(256)(128)(2,1)S(1)} collective-permute-done((bf16[128]{0:T(256)(128)(2,1)S(1)}, bf16[128]{0:T(256)(128)(2,1)S(1)}, u32[]{:S(2)}, u32[]{:S(2)}) %collective-permute-start.3) | collective-permute-done | bytes 288 | tf_op jit(solution)/shard_map/ppermute | solution.py:10
  12.9 3.0 %collective-permute-done.5 = bf16[128]{0:T(256)(128)(2,1)S(1)} collective-permute-done((bf16[128]{0:T(256)(128)(2,1)S(1)}, bf16[128]{0:T(256)(128)(2,1)S(1)}, u32[]{:S(2)}, u32[]{:S(2)}) %collective-permute-start.5) | collective-permute-done | bytes 288 | tf_op jit(solution)/shard_map/ppermute | solution.py:10
  15.9 0.0 collective-permute-start.7
  15.9 4.0 %collective-permute-done.7 = bf16[128]{0:T(256)(128)(2,1)S(1)} collective-permute-done((bf16[128]{0:T(256)(128)(2,1)S(1)}, bf16[128]{0:T(256)(128)(2,1)S(1)}, u32[]{:S(2)}, u32[]{:S(2)}) %collective-permute-start.7) | collective-permute-done | bytes 288 | tf_op jit(solution)/shard_map/ppermute | solution.py:10
  19.9 0.0 collective-permute-start.9
  19.9 4.8 %collective-permute-done.9 = bf16[128]{0:T(256)(128)(2,1)S(1)} collective-permute-done((bf16[128]{0:T(256)(128)(2,1)S(1)}, bf16[128]{0:T(256)(128)(2,1)S(1)}, u32[]{:S(2)}, u32[]{:S(2)}) %collective-permute-start.9) | collective-permute-done | bytes 288 | tf_op jit(solution)/shard_map/ppermute | solution.py:10
  24.7 0.0 collective-permute-start.11
  24.7 4.8 %collective-permute-done.11 = bf16[128]{0:T(256)(128)(2,1)S(1)} collective-permute-done((bf16[128]{0:T(256)(128)(2,1)S(1)}, bf16[128]{0:T(256)(128)(2,1)S(1)}, u32[]{:S(2)}, u32[]{:S(2)}) %collective-permute-start.11) | collective-permute-done | bytes 288 | tf_op jit(solution)/shard_map/ppermute | solution.py:10
  29.5 0.0 collective-permute-start.13
  29.5 4.7 %collective-permute-done.13 = bf16[128]{0:T(256)(128)(2,1)S(1)} collective-permute-done((bf16[128]{0:T(256)(128)(2,1)S(1)}, bf16[128]{0:T(256)(128)(2,1)S(1)}, u32[]{:S(2)}, u32[]{:S(2)}) %collective-permute-start.13) | collective-permute-done | bytes 288 | tf_op jit(solution)/shard_map/ppermute | solution.py:10
  34.2 0.1 collective-permute-start.2
  34.3 6.4 %convolution_add_fusion.6 = f32[128,2048]{1,0:T(8,128)S(1)} fusion(bf16[128,2048]{1,0:T(8,128)(2,1)S(1)} %collective-permute-done, bf16[2048,2048]{1,0:T(8,128)(2,1)} %param.6, f32[128]{0:T(128)S(1)} %convert_element_type.25), kind=kOutput, calls=%fused_computation.6 | convolution fusion | flops 1074003968 | bytes 9961984 | tf_op jit(solution)/shard_map/dot_general | solution.py:22
  40.8 0.0 slice-start.1
  40.8 4.0 %collective-permute-done.2 = bf16[128,2048]{1,0:T(8,128)(2,1)S(1)} collective-permute-done((bf16[128,2048]{1,0:T(8,128)(2,1)S(1)}, bf16[128,2048]{1,0:T(8,128)(2,1)S(1)}, u32[]{:S(2)}, u32[]{:S(2)}) %collective-permute-start.2) | collective-permute-done | bytes 524320 | tf_op jit(solution)/shard_map/ppermute | solution.py:10
  44.7 0.0 collective-permute-start.4
  44.7 6.3 %convolution_add_fusion.5 = f32[128,2048]{1,0:T(8,128)S(1)} fusion(bf16[128,2048]{1,0:T(8,128)(2,1)S(1)} %collective-permute-done.2, bf16[2048,2048]{1,0:T(8,128)(2,1)} %param.6, f32[128]{0:T(128)S(1)} %convert_element_type.26), kind=kOutput, calls=%fused_computation.5 | convolution fusion | flops 1074003968 | bytes 9961984 | tf_op jit(solution)/shard_map/dot_general | solution.py:22
  51.0 2.3 %collective-permute-done.4 = bf16[128,2048]{1,0:T(8,128)(2,1)S(1)} collective-permute-done((bf16[128,2048]{1,0:T(8,128)(2,1)S(1)}, bf16[128,2048]{1,0:T(8,128)(2,1)S(1)}, u32[]{:S(2)}, u32[]{:S(2)}) %collective-permute-start.4) | collective-permute-done | bytes 524320 | tf_op jit(solution)/shard_map/ppermute | solution.py:10
  53.3 0.0 collective-permute-start.6
  53.4 2.9 %convolution_add_fusion.4 = f32[128,2048]{1,0:T(8,128)S(1)} fusion(bf16[128,2048]{1,0:T(8,128)(2,1)S(1)} %collective-permute-done.4, bf16[2048,2048]{1,0:T(8,128)(2,1)S(1)} %bitcast.33, f32[128]{0:T(128)S(1)} %convert_element_type.27), kind=kOutput, calls=%fused_computation.4 | convolution fusion | flops 1074003968 | bytes 9961984 | tf_op jit(solution)/shard_map/dot_general | solution.py:22
  56.3 5.7 %collective-permute-done.6 = bf16[128,2048]{1,0:T(8,128)(2,1)S(1)} collective-permute-done((bf16[128,2048]{1,0:T(8,128)(2,1)S(1)}, bf16[128,2048]{1,0:T(8,128)(2,1)S(1)}, u32[]{:S(2)}, u32[]{:S(2)}) %collective-permute-start.6) | collective-permute-done | bytes 524320 | tf_op jit(solution)/shard_map/ppermute | solution.py:10
  62.0 2.9 %convolution_add_fusion.3 = f32[128,2048]{1,0:T(8,128)S(1)} fusion(bf16[128,2048]{1,0:T(8,128)(2,1)S(1)} %collective-permute-done.6, bf16[2048,2048]{1,0:T(8,128)(2,1)S(1)} %bitcast.33, f32[128]{0:T(128)S(1)} %convert_element_type.28), kind=kOutput, calls=%fused_computation.3 | convolution fusion | flops 1074003968 | bytes 9961984 | tf_op jit(solution)/shard_map/dot_general | solution.py:22
  64.9 0.0 copy-start
  64.9 6.2 %collective-permute-done.8 = bf16[128,2048]{1,0:T(8,128)(2,1)S(1)} collective-permute-done((bf16[128,2048]{1,0:T(8,128)(2,1)S(1)}, bf16[128,2048]{1,0:T(8,128)(2,1)S(1)}, u32[]{:S(2)}, u32[]{:S(2)}) %collective-permute-start.8) | collective-permute-done | bytes 524320 | tf_op jit(solution)/shard_map/ppermute | solution.py:10
  71.1 2.9 %convolution_add_fusion.2 = f32[128,2048]{1,0:T(8,128)S(1)} fusion(bf16[128,2048]{1,0:T(8,128)(2,1)S(1)} %collective-permute-done.8, bf16[2048,2048]{1,0:T(8,128)(2,1)S(1)} %bitcast.33, f32[128]{0:T(128)S(1)} %convert_element_type.29), kind=kOutput, calls=%fused_computation.2 | convolution fusion | flops 1074003968 | bytes 9961984 | tf_op jit(solution)/shard_map/dot_general | solution.py:22
  74.0 7.5 %collective-permute-done.10 = bf16[128,2048]{1,0:T(8,128)(2,1)S(1)} collective-permute-done((bf16[128,2048]{1,0:T(8,128)(2,1)S(1)}, bf16[128,2048]{1,0:T(8,128)(2,1)S(1)}, u32[]{:S(2)}, u32[]{:S(2)}) %collective-permute-start.10) | collective-permute-done | bytes 524320 | tf_op jit(solution)/shard_map/ppermute | solution.py:10
  81.5 0.0 collective-permute-start.12
  81.5 2.9 %convolution_add_fusion.1 = f32[128,2048]{1,0:T(8,128)S(1)} fusion(bf16[128,2048]{1,0:T(8,128)(2,1)S(1)} %collective-permute-done.10, bf16[2048,2048]{1,0:T(8,128)(2,1)S(1)} %bitcast.33, f32[128]{0:T(128)S(1)} %convert_element_type.30), kind=kOutput, calls=%fused_computation.1 | convolution fusion | flops 1074003968 | bytes 9961984 | tf_op jit(solution)/shard_map/dot_general | solution.py:22
  84.4 7.5 %collective-permute-done.12 = bf16[128,2048]{1,0:T(8,128)(2,1)S(1)} collective-permute-done((bf16[128,2048]{1,0:T(8,128)(2,1)S(1)}, bf16[128,2048]{1,0:T(8,128)(2,1)S(1)}, u32[]{:S(2)}, u32[]{:S(2)}) %collective-permute-start.12) | collective-permute-done | bytes 524320 | tf_op jit(solution)/shard_map/ppermute | solution.py:10
  91.9 4.0 %subtract_reduce_fusion = (f32[128]{0:T(128)S(1)}, f32[2048]{0:T(1024)S(1)}, f32[2048]{0:T(1024)S(1)}, f32[128]{0:T(128)S(1)}, f32[2048]{0:T(1024)S(1)}, /*index...) fusion(f32[2048]{0:T(1024)S(1)} %copy-done, ...), kind=kOutput, calls=%fused_computation.8 | convolution fusion | flops 1080278016 | bytes 16331264 | tf_op jit(solution)/shard_map/dot_general | solution.py:22
  95.9 0.6 all_to_all.22
  96.5 0.5 constant_dynamic-update-slice_fusion.7
  97.0 0.5 constant_dynamic-update-slice_fusion.6
  97.5 0.6 constant_dynamic-update-slice_fusion.5
  98.1 0.5 constant_dynamic-update-slice_fusion.4
  98.6 0.6 constant_dynamic-update-slice_fusion.3
  99.2 0.6 constant_dynamic-update-slice_fusion.2
  99.7 0.5 constant_dynamic-update-slice_fusion.1
  100.3 0.6 constant_dynamic-update-slice_fusion
  100.9 15.7 %all-to-all-start = ((f32[8,1,128]{2,1,0:T(1,128)}), f32[8,1,128]{2,1,0:T(1,128)S(1)}, u32[]{:S(2)}, u32[]{:S(2)}) async-start(f32[8,1,128]{2,1,0:T(1,128)} %constant_dynamic-update-slice_fusion), calls=%async_computation | async-start | bytes 8192 | tf_op jit(solution)/shard_map/all_to_all | solution.py:33
  116.5 31.7 %pmax.14 = f32[2048]{0:T(1024)S(1)} all-reduce(f32[2048]{0:T(1024)S(1)} %maximum_maximum_fusion), channel_id=1, replica_groups=mesh['grp'=8,'cut'=8,'st'=4] {'cut'}, use_global_device_ids=true, to_apply=%region_8.9 | all-reduce | flops 2048 | bytes 16384 | tf_op jit(solution)/shard_map/pmax | solution.py:36
  148.2 0.6 max.35
  148.8 11.3 %pmax.15 = f32[128]{0:T(128)} all-reduce(f32[128]{0:T(128)S(1)} %reduce_max.169), channel_id=1, replica_groups=mesh['grp'=8,'cut'=8,'st'=4] {'st'}, use_global_device_ids=true, to_apply=%region_18.19 | all-reduce | flops 128 | bytes 1024 | tf_op jit(solution)/shard_map/pmax | solution.py:35
  (19 shorter events, 0.1 us)
Async XLA Ops:
  0.6 33.6 %collective-permute-start = (bf16[128,2048]{1,0:T(8,128)(2,1)}, bf16[128,2048]{1,0:T(8,128)(2,1)S(1)}, u32[]{:S(2)}, u32[]{:S(2)}) collective-permute-start(bf16[128,2048]{1,0:T(8,128)(2,1)} %param.4), channel_id=1, source_target_pairs={{224,0},{0,32},{32,64},{64,96},{96,128},{128,160},{160,192},{192,2... | collective-permute-start | bytes 1572872 | tf_op jit(solution)/shard_map/ppermute | solution.py:10
  0.7 9.2 %collective-permute-start.1 = (bf16[128]{0:T(256)(128)(2,1)}, bf16[128]{0:T(256)(128)(2,1)S(1)}, u32[]{:S(2)}, u32[]{:S(2)}) collective-permute-start(bf16[128]{0:T(256)(128)(2,1)} %param.5), channel_id=1, source_target_pairs={{224,0},{0,32},{32,64},{64,96},{96,128},{128,160},{160,192},{192,2... | collective-permute-start | bytes 776 | tf_op jit(solution)/shard_map/ppermute | solution.py:10
  9.9 3.0 %collective-permute-start.3 = (bf16[128]{0:T(256)(128)(2,1)S(1)}, bf16[128]{0:T(256)(128)(2,1)S(1)}, u32[]{:S(2)}, u32[]{:S(2)}) collective-permute-start(bf16[128]{0:T(256)(128)(2,1)S(1)} %collective-permute-done.1), channel_id=1, source_target_pairs={{224,0},{0,32},{32,64},{64,96},{96,128},{128,160},{160,192},{192,2... | collective-permute-start | bytes 776 | tf_op jit(solution)/shard_map/ppermute | solution.py:10
  12.9 3.0 %collective-permute-start.5 = (bf16[128]{0:T(256)(128)(2,1)S(1)}, bf16[128]{0:T(256)(128)(2,1)S(1)}, u32[]{:S(2)}, u32[]{:S(2)}) collective-permute-start(bf16[128]{0:T(256)(128)(2,1)S(1)} %collective-permute-done.3), channel_id=1, source_target_pairs={{224,0},{0,32},{32,64},{64,96},{96,128},{128,160},{160,192},{192,2... | collective-permute-start | bytes 776 | tf_op jit(solution)/shard_map/ppermute | solution.py:10
  15.9 4.0 %collective-permute-start.7 = (bf16[128]{0:T(256)(128)(2,1)S(1)}, bf16[128]{0:T(256)(128)(2,1)S(1)}, u32[]{:S(2)}, u32[]{:S(2)}) collective-permute-start(bf16[128]{0:T(256)(128)(2,1)S(1)} %collective-permute-done.5), channel_id=1, source_target_pairs={{224,0},{0,32},{32,64},{64,96},{96,128},{128,160},{160,192},{192,2... | collective-permute-start | bytes 776 | tf_op jit(solution)/shard_map/ppermute | solution.py:10
  19.9 4.8 %collective-permute-start.9 = (bf16[128]{0:T(256)(128)(2,1)S(1)}, bf16[128]{0:T(256)(128)(2,1)S(1)}, u32[]{:S(2)}, u32[]{:S(2)}) collective-permute-start(bf16[128]{0:T(256)(128)(2,1)S(1)} %collective-permute-done.7), channel_id=1, source_target_pairs={{224,0},{0,32},{32,64},{64,96},{96,128},{128,160},{160,192},{192,2... | collective-permute-start | bytes 776 | tf_op jit(solution)/shard_map/ppermute | solution.py:10
  24.7 4.8 %collective-permute-start.11 = (bf16[128]{0:T(256)(128)(2,1)S(1)}, bf16[128]{0:T(256)(128)(2,1)S(1)}, u32[]{:S(2)}, u32[]{:S(2)}) collective-permute-start(bf16[128]{0:T(256)(128)(2,1)S(1)} %collective-permute-done.9), channel_id=1, source_target_pairs={{224,0},{0,32},{32,64},{64,96},{96,128},{128,160},{160,192},{192,2... | collective-permute-start | bytes 776 | tf_op jit(solution)/shard_map/ppermute | solution.py:10
  29.5 4.8 %collective-permute-start.13 = (bf16[128]{0:T(256)(128)(2,1)S(1)}, bf16[128]{0:T(256)(128)(2,1)S(1)}, u32[]{:S(2)}, u32[]{:S(2)}) collective-permute-start(bf16[128]{0:T(256)(128)(2,1)S(1)} %collective-permute-done.11), channel_id=1, source_target_pairs={{224,0},{0,32},{32,64},{64,96},{96,128},{128,160},{160,192},{192,2... | collective-permute-start | bytes 776 | tf_op jit(solution)/shard_map/ppermute | solution.py:10
  34.2 19.1 %slice-start = ((s8[8388608]{0:T(1024)(128)(4,1)}), s8[4194304]{0:T(1024)(128)(4,1)S(1)}, s32[]{:S(2)}) async-start(s8[8388608]{0:T(1024)(128)(4,1)} %bitcast.32), calls=%async_computation.1 | async-start | bytes 8388608
  34.2 10.5 %collective-permute-start.2 = (bf16[128,2048]{1,0:T(8,128)(2,1)S(1)}, bf16[128,2048]{1,0:T(8,128)(2,1)S(1)}, u32[]{:S(2)}, u32[]{:S(2)}) collective-permute-start(bf16[128,2048]{1,0:T(8,128)(2,1)S(1)} %collective-permute-done), channel_id=1, source_target_pairs={{224,0},{0,32},{32,64},{64,96},{96,128},{128,160},{160,192},{192,2... | collective-permute-start | bytes 1572872 | tf_op jit(solution)/shard_map/ppermute | solution.py:10
  40.8 12.6 %slice-start.1 = ((s8[8388608]{0:T(1024)(128)(4,1)}), s8[4194304]{0:T(1024)(128)(4,1)S(1)}, s32[]{:S(2)}) async-start(s8[8388608]{0:T(1024)(128)(4,1)} %bitcast.32), calls=%async_computation.2 | async-start | bytes 8388608
  44.7 8.6 %collective-permute-start.4 = (bf16[128,2048]{1,0:T(8,128)(2,1)S(1)}, bf16[128,2048]{1,0:T(8,128)(2,1)S(1)}, u32[]{:S(2)}, u32[]{:S(2)}) collective-permute-start(bf16[128,2048]{1,0:T(8,128)(2,1)S(1)} %collective-permute-done.2), channel_id=1, source_target_pairs={{224,0},{0,32},{32,64},{64,96},{96,128},{128,160},{160,192},{192,2... | collective-permute-start | bytes 1572872 | tf_op jit(solution)/shard_map/ppermute | solution.py:10
  53.3 8.6 %collective-permute-start.6 = (bf16[128,2048]{1,0:T(8,128)(2,1)S(1)}, bf16[128,2048]{1,0:T(8,128)(2,1)S(1)}, u32[]{:S(2)}, u32[]{:S(2)}) collective-permute-start(bf16[128,2048]{1,0:T(8,128)(2,1)S(1)} %collective-permute-done.4), channel_id=1, source_target_pairs={{224,0},{0,32},{32,64},{64,96},{96,128},{128,160},{160,192},{192,2... | collective-permute-start | bytes 1572872 | tf_op jit(solution)/shard_map/ppermute | solution.py:10
  61.9 9.1 %collective-permute-start.8 = (bf16[128,2048]{1,0:T(8,128)(2,1)S(1)}, bf16[128,2048]{1,0:T(8,128)(2,1)S(1)}, u32[]{:S(2)}, u32[]{:S(2)}) collective-permute-start(bf16[128,2048]{1,0:T(8,128)(2,1)S(1)} %collective-permute-done.6), channel_id=1, source_target_pairs={{224,0},{0,32},{32,64},{64,96},{96,128},{128,160},{160,192},{192,2... | collective-permute-start | bytes 1572872 | tf_op jit(solution)/shard_map/ppermute | solution.py:10
  64.9 27.1 %copy-start = (f32[2048]{0:T(1024)S(1)}, f32[2048]{0:T(1024)}, u32[]{:S(2)}) copy-start(f32[2048]{0:T(1024)} %param.7) | copy-start | bytes 24580
  71.1 10.4 %collective-permute-start.10 = (bf16[128,2048]{1,0:T(8,128)(2,1)S(1)}, bf16[128,2048]{1,0:T(8,128)(2,1)S(1)}, u32[]{:S(2)}, u32[]{:S(2)}) collective-permute-start(bf16[128,2048]{1,0:T(8,128)(2,1)S(1)} %collective-permute-done.8), channel_id=1, source_target_pairs={{224,0},{0,32},{32,64},{64,96},{96,128},{128,160},{160,192},{192,2... | collective-permute-start | bytes 1572872 | tf_op jit(solution)/shard_map/ppermute | solution.py:10
  81.5 10.4 %collective-permute-start.12 = (bf16[128,2048]{1,0:T(8,128)(2,1)S(1)}, bf16[128,2048]{1,0:T(8,128)(2,1)S(1)}, u32[]{:S(2)}, u32[]{:S(2)}) collective-permute-start(bf16[128,2048]{1,0:T(8,128)(2,1)S(1)} %collective-permute-done.10), channel_id=1, source_target_pairs={{224,0},{0,32},{32,64},{64,96},{96,128},{128,160},{160,192},{192,2... | collective-permute-start | bytes 1572872 | tf_op jit(solution)/shard_map/ppermute | solution.py:10
  100.9 47.9 %all-to-all-start = ((f32[8,1,128]{2,1,0:T(1,128)}), f32[8,1,128]{2,1,0:T(1,128)S(1)}, u32[]{:S(2)}, u32[]{:S(2)}) async-start(f32[8,1,128]{2,1,0:T(1,128)} %constant_dynamic-update-slice_fusion), calls=%async_computation | async-start | bytes 8192 | tf_op jit(solution)/shard_map/all_to_all | solution.py:33
where the time goes:
time: 160 us
  waiting for transfers between devices  57.3 us (36%)
  blocking collectives  42.9 us (27%)
  matrix products  34.7 us (22%)
  starting transfers between devices  18.1 us (11%)
  local copies, waits for them, and re-layouts  4.98 us (3%)
    ppermute x14, waiting for transfers between devices, shifted(): return lax.ppermute(block, axis, route)  57.3 us
    dot_general x8, matrix products, body(): lax.dot_general(visiting[0], states, (((1,), (1,)), ((), ())), preferred_...  34.7 us
    pmax x1, blocking collectives, body(): overall = lax.pmax(top_value, 'cut')  31.7 us
    all_to_all x1, starting transfers between devices, body(): lax.all_to_all(lift_table, 'grp', split_axis=0, concat_axis=0, tiled=True)  15.7 us
    pmax x1, blocking collectives, body(): cut_gaps = lax.pmax(group_lift, 'st')  11.3 us
    dynamic_update_slice x8, local copies, waits for them, and re-layouts, body(): lax.dynamic_update_slice_in_dim(lift_table, lift_row[None, :], source, 0)  4.37 us
  transfers between devices with their start and end apart: 15, of which 12 were waited for; matrix products, arithmetic and copies ran while one was open for 20% of the time, Pallas kernels for 0%

commit v1 on v0

v1 whole, which is shorter than its diff:
```python
import functools

import jax
import jax.numpy as jnp
from jax import lax
from jax.experimental import pallas as pl
from jax.experimental.pallas import tpu as pltpu
from jax.sharding import PartitionSpec as P

AXES = ("grp", "cut", "st")
NX, NY, NZ, NC = 4, 4, 8, 2


def position(x, y, z, c):
    z_hi, z_lo = divmod(z % NZ, 4)
    return (((z_lo * NC + c % NC) * 8) + z_hi * NX + x % NX) * NY + y % NY


def routes(move):
    pairs = []
    for x in range(NX):
        for y in range(NY):
            for z in range(NZ):
                for c in range(NC):
                    pairs.append((position(x, y, z, c), position(*move(x, y, z, c))))
    return pairs


def send(block, move):
    return lax.ppermute(block, AXES, routes(move))


def over_core(x, y, z, c):
    return x, y, z, 1 - c


def up(x, y, z, c):
    return x, y, z + 1, c


def down(x, y, z, c):
    return x, y, z - 1, c


def two_out(x, y, z, c):
    return x, y, z - 2 if c == 0 else z + 2, c


def two_back(x, y, z, c):
    return x, y, z + 2 if c == 0 else z - 2, c


def far(x, y, z, c):
    return x, y, z + 4, c


def score_body(tile, tiles, mine, other, bias, old, prev, states, top, lift, slopes, best, offset):
    rows = mine.shape[0]
    step = pl.program_id(0)

    @pl.when(step == 0)
    def _():
        slopes[:rows, :] = mine[...]
        slopes[rows:, :] = other[...]
        for part in range(2):
            spread = jnp.broadcast_to(bias[part : part + 1, :], (128, rows))
            offset[part * rows : (part + 1) * rows, :] = spread.T
        best[...] = jnp.full(best.shape, -jnp.inf, jnp.float32)

    scores = lax.dot_general(
        slopes[...], states[...], (((1,), (1,)), ((), ())), preferred_element_type=jnp.float32
    )
    lifted = scores - old[...]
    most = best[...]
    for lane in range(0, tile, 128):
        most = jnp.maximum(most, lifted[:, lane : lane + 128])
    best[...] = most
    wide = offset[...]
    valued = jnp.concatenate(
        [scores[:, lane : lane + 128] + wide for lane in range(0, tile, 128)], axis=1
    )
    top[...] = jnp.maximum(prev[...], jnp.max(valued, axis=0, keepdims=True))

    @pl.when(step == tiles - 1)
    def _():
        turned = jnp.max(best[...].T, axis=0, keepdims=True)
        for part in range(2):
            lift[part : part + 1, :] = turned[:, part * rows : (part + 1) * rows] + bias[part : part + 1, :]


def score(mine, other, bias, old, prev, states, tile=1024):
    rows, depth = mine.shape
    count = states.shape[0]
    tiles = count // tile
    whole = lambda shape: pl.BlockSpec(shape, lambda i: (0, 0))
    along = pl.BlockSpec((1, tile), lambda i: (0, i))
    return pl.pallas_call(
        functools.partial(score_body, tile, tiles),
        grid=(tiles,),
        in_specs=[
            whole((rows, depth)),
            whole((rows, depth)),
            whole((2, rows)),
            along,
            along,
            pl.BlockSpec((tile, depth), lambda i: (i, 0)),
        ],
        out_specs=[along, whole((2, rows))],
        out_shape=[
            jax.ShapeDtypeStruct((1, count), jnp.float32),
            jax.ShapeDtypeStruct((2, rows), jnp.float32),
        ],
        scratch_shapes=[
            pltpu.VMEM((2 * rows, depth), jnp.bfloat16),
            pltpu.VMEM((2 * rows, 128), jnp.float32),
            pltpu.VMEM((2 * rows, 128), jnp.float32),
        ],
        compiler_params=pltpu.CompilerParams(vmem_limit_bytes=24 << 20),
        cost_estimate=pl.CostEstimate(
            flops=4 * rows * depth * count, bytes_accessed=2 * (count + 2 * rows) * depth, transcendentals=0
        ),
    )(mine, other, bias, old, prev, states)


def body(coefficients, intercepts, states, old_values):
    old = old_values[None, :]
    offsets = intercepts.astype(jnp.float32)[None, :]

    two = send(coefficients, two_out)
    lower = send(coefficients, up)
    upper = send(coefficients, down)
    peer = send(coefficients, over_core)
    offsets_two = send(offsets, two_out)
    pair = jnp.concatenate([offsets, send(offsets, over_core)], axis=0)
    pair_lower = send(pair, up)
    pair_upper = send(pair, down)
    pair_two = jnp.concatenate([offsets_two, send(offsets_two, over_core)], axis=0)

    top, lift_own = score(coefficients, peer, pair, old, old, states)
    top, lift_lower = score(lower, send(lower, over_core), pair_lower, old, top, states)
    top, lift_upper = score(upper, send(upper, over_core), pair_upper, old, top, states)
    top, lift_two = score(two, send(two, over_core), pair_two, old, top, states)

    for_x = [send(top, lambda x, y, z, c, d=d: (x ^ d, y, z, c)) for d in (1, 2, 3)]
    top = functools.reduce(jnp.maximum, for_x, top)
    new_values = jnp.maximum(top, send(top, far))

    lifts = jnp.concatenate([lift_own, lift_lower, lift_upper, lift_two], axis=0).reshape(4, 2, -1)
    lifts = jnp.maximum(lifts[:, 0], send(lifts[:, 1], over_core))
    for_y = [send(lifts, lambda x, y, z, c, d=d: (x, y ^ d, z, c)) for d in (1, 2, 3)]
    lifts = functools.reduce(jnp.maximum, for_y, lifts)
    back = [send(lifts[1:2], down), send(lifts[2:3], up), send(lifts[3:4], two_back)]
    cut_gaps = functools.reduce(jnp.maximum, back, lifts[0:1])
    return new_values[0], cut_gaps[0]


def solution(mesh):
    placed = (P(("grp", "cut"), None), P(("grp", "cut")), P(("grp", "st"), None), P(("grp", "st")))
    return jax.shard_map(
        body,
        mesh=mesh,
        in_specs=placed,
        out_specs=(P(("grp", "st")), P(("grp", "cut"))),
        check_vma=False,
    )
```

time: 160 us -> 76.4 us (0.48)
  the two profiles are of different devices: /device:TPU:32 before, /device:TPU:2 now
where the time goes in v1:
time: 76.4 us; the launch traced here: 76 us
  starting transfers between devices  36.9 us (48%)
  waiting for transfers between devices  19.6 us (26%)
  Pallas kernels  11.4 us (15%)
  local copies, waits for them, and re-layouts  5.63 us (7%)
  other arithmetic  1.83 us (2%)
    ppermute x23, starting transfers between devices, send(): return lax.ppermute(block, AXES, routes(move))  36.9 us
    ppermute x23, waiting for transfers between devices, send(): return lax.ppermute(block, AXES, routes(move))  19.6 us
    pallas_call x4, Pallas kernels, score(): pl.pallas_call(functools.partial(score_body, tile, tiles), grid=(tiles,),...  11.4 us
    unnamed x8, local copies, waits for them, and re-layouts  5.62 us
  transfers between devices with their start and end apart: 23, of which 7 were waited for; matrix products, arithmetic and copies ran while one was open for 2% of the time, Pallas kernels for 11%

profile of v1, /device:TPU:2, one launch (start us, length us, event | category | flops | bytes accessed | tf_op | source)
XLA Modules:
  0.0 76.0 jit_solution(1279332481180636169)
XLA Ops:
  0.6 2.0 %collective-permute-start.8 = (bf16[128,2048]{1,0:T(8,128)(2,1)}, bf16[128,2048]{1,0:T(8,128)(2,1)S(1)}, u32[]{:S(2)}, u32[]{:S(2)}) collective-permute-start(bf16[128,2048]{1,0:T(8,128)(2,1)} %mine.1), channel_id=1, source_target_pairs={{0,64},{32,96},{64,128},{96,160},{128,192},{160,224},{192,16},{224... | collective-permute-start | bytes 1572872 | tf_op jit(solution)/shard_map/ppermute | solution.py:30
  2.6 4.0 %collective-permute-start.4 = (bf16[128,2048]{1,0:T(8,128)(2,1)}, bf16[128,2048]{1,0:T(8,128)(2,1)S(1)}, u32[]{:S(2)}, u32[]{:S(2)}) collective-permute-start(bf16[128,2048]{1,0:T(8,128)(2,1)} %mine.1), channel_id=1, source_target_pairs={{0,208},{32,240},{64,0},{96,32},{128,64},{160,96},{192,128},{224,1... | collective-permute-start | bytes 1572872 | tf_op jit(solution)/shard_map/ppermute | solution.py:30
  6.7 2.4 %collective-permute-start = (bf16[128,2048]{1,0:T(8,128)(2,1)}, bf16[128,2048]{1,0:T(8,128)(2,1)S(1)}, u32[]{:S(2)}, u32[]{:S(2)}) collective-permute-start(bf16[128,2048]{1,0:T(8,128)(2,1)} %mine.1), channel_id=1, source_target_pairs={{0,144},{32,160},{64,208},{96,224},{128,0},{160,48},{192,64},{224,... | collective-permute-start | bytes 1572872 | tf_op jit(solution)/shard_map/ppermute | solution.py:30
  9.0 11.0 %collective-permute-done.8.mine = bf16[128,2048]{1,0:T(8,128)(2,1)S(1)} collective-permute-done((bf16[128,2048]{1,0:T(8,128)(2,1)}, bf16[128,2048]{1,0:T(8,128)(2,1)S(1)}, u32[]{:S(2)}, u32[]{:S(2)}) %collective-permute-start.8) | collective-permute-done | bytes 524320 | tf_op jit(solution)/shard_map/ppermute | solution.py:30
  20.0 0.7 bitcast_convert_fusion
  20.7 0.5 collective-permute-start.6
  21.2 0.8 %collective-permute-done.6 = f32[1,128]{1,0:T(1,128)S(1)} collective-permute-done((f32[1,128]{1,0:T(1,128)S(1)}, f32[1,128]{1,0:T(1,128)S(1)}, u32[]{:S(2)}, u32[]{:S(2)}) %collective-permute-start.6) | collective-permute-done | bytes 544 | tf_op jit(solution)/shard_map/ppermute | solution.py:30
  22.0 7.6 %collective-permute-start.2 = (f32[1,128]{1,0:T(1,128)S(1)}, f32[1,128]{1,0:T(1,128)S(1)}, u32[]{:S(2)}, u32[]{:S(2)}) collective-permute-start(f32[1,128]{1,0:T(1,128)S(1)} %bitcast_convert_fusion), channel_id=1, source_target_pairs={{0,144},{32,160},{64,208},{96,224},{128,0},{160,48},{192,64},{224,... | collective-permute-start | bytes 1544 | tf_op jit(solution)/shard_map/ppermute | solution.py:30
  29.6 1.3 %collective-permute-done.2 = f32[1,128]{1,0:T(1,128)S(1)} collective-permute-done((f32[1,128]{1,0:T(1,128)S(1)}, f32[1,128]{1,0:T(1,128)S(1)}, u32[]{:S(2)}, u32[]{:S(2)}) %collective-permute-start.2) | collective-permute-done | bytes 544 | tf_op jit(solution)/shard_map/ppermute | solution.py:30
  30.9 0.0 collective-permute-start.3
  30.9 0.0 collective-permute-done.4.mine
  30.9 0.5 collective-permute-start.5
  31.5 0.6 collective-permute-done.3
  32.1 0.1 collective-permute-start.10
  32.1 0.0 collective-permute-done.11.other
  32.1 3.3 %collective-permute-start.7 = (f32[2,128]{1,0:T(2,128)S(1)}, f32[2,128]{1,0:T(2,128)S(1)}, u32[]{:S(2)}, u32[]{:S(2)}) collective-permute-start(f32[2,128]{1,0:T(2,128)S(1)} %pad_maximum_fusion.2.bias), channel_id=1, source_target_pairs={{0,208},{32,240},{64,0},{96,32},{128,64},{160,96},{192,128},{224,1... | collective-permute-start | bytes 3080 | tf_op jit(solution)/shard_map/ppermute | solution.py:30
  35.4 0.0 collective-permute-done.mine
  35.4 0.0 collective-permute-start.1
  35.4 3.4 %copy-done = bf16[2048,2048]{1,0:T(8,128)(2,1)S(1)} copy-done((bf16[2048,2048]{1,0:T(8,128)(2,1)S(1)}, bf16[2048,2048]{1,0:T(8,128)(2,1)}, u32[]{:S(2)}) %copy-start) | copy-done | bytes 8388632
  38.8 1.0 %copy-done.2 = bf16[128,2048]{1,0:T(8,128)(2,1)S(1)} copy-done((bf16[128,2048]{1,0:T(8,128)(2,1)S(1)}, bf16[128,2048]{1,0:T(8,128)(2,1)}, u32[]{:S(2)}) %copy-start.2) | copy-done | bytes 524312
  39.8 0.7 copy-done.3
  40.5 2.9 %shard_map.59 = (f32[1,2048]{1,0:T(1,128)S(1)}, f32[2,128]{1,0:T(2,128)S(1)}) custom-call(bf16[128,2048]{1,0:T(8,128)(2,1)S(1)} %copy-done.2, bf16[128,2048]{1,0:T(8,128)(2,1)S(1)} %collective-permute-done.11.other, f32[2,128]{1,0:T(2,128)S(1)} %pad_maximum_fusion.2.bias, f32[1,2048]{1,0:T(1,128)S(1)} %bitcast.14, f32[1,2048]{1,0:T(1,128)S(1)} %bitcast.15, ...), custom_call_target="tpu_custom_call" | custom-call | flops 2147483648 | bytes 9437184 | tf_op jit(solution)/shard_map/pallas_call | solution.py:97
  43.4 0.0 collective-permute-done.10.bias
  43.4 0.5 copy-done.1
  43.9 2.8 %shard_map.60 = (f32[1,2048]{1,0:T(1,128)S(1)}, f32[2,128]{1,0:T(2,128)S(1)}) custom-call(bf16[128,2048]{1,0:T(8,128)(2,1)S(1)} %collective-permute-done.8.mine, bf16[128,2048]{1,0:T(8,128)(2,1)S(1)} %collective-permute-done.9.other, f32[2,128]{1,0:T(2,128)S(1)} %collective-permute-done.10.bias, f32[1,2048]{1,0:T(1,128)S(1)} %bitcast.16, ...), custom_call_target="tpu_custom_call" | custom-call | flops 2147483648 | bytes 9437184 | tf_op jit(solution)/shard_map/pallas_call | solution.py:97
  46.7 0.0 collective-permute-done.7.bias
  46.7 2.8 %shard_map.61 = (f32[1,2048]{1,0:T(1,128)S(1)}, f32[2,128]{1,0:T(2,128)S(1)}) custom-call(bf16[128,2048]{1,0:T(8,128)(2,1)S(1)} %collective-permute-done.4.mine, bf16[128,2048]{1,0:T(8,128)(2,1)S(1)} %collective-permute-done.5.other, f32[2,128]{1,0:T(2,128)S(1)} %collective-permute-done.7.bias, f32[1,2048]{1,0:T(1,128)S(1)} %bitcast.17, ...), custom_call_target="tpu_custom_call" | custom-call | flops 2147483648 | bytes 9437184 | tf_op jit(solution)/shard_map/pallas_call | solution.py:97
  49.6 2.9 %shard_map.62 = (f32[1,2048]{1,0:T(1,128)S(1)}, f32[2,128]{1,0:T(2,128)S(1)}) custom-call(bf16[128,2048]{1,0:T(8,128)(2,1)S(1)} %collective-permute-done.mine, bf16[128,2048]{1,0:T(8,128)(2,1)S(1)} %collective-permute-done.1.other, f32[2,128]{1,0:T(2,128)S(1)} %pad_maximum_fusion.1.bias, f32[1,2048]{1,0:T(1,128)S(1)} %bitcast.18, ...), custom_call_target="tpu_custom_call" | custom-call | flops 2147483648 | bytes 9437184 | tf_op jit(solution)/shard_map/pallas_call | solution.py:97
  52.5 0.6 collective-permute-start.16
  53.1 0.8 %collective-permute-done.16 = f32[4,128]{1,0:T(4,128)S(1)} collective-permute-done((f32[4,128]{1,0:T(4,128)S(1)}, f32[4,128]{1,0:T(4,128)S(1)}, u32[]{:S(2)}, u32[]{:S(2)}) %collective-permute-start.16) | collective-permute-done | bytes 2080 | tf_op jit(solution)/shard_map/ppermute | solution.py:30
  53.9 1.6 %collective-permute-start.17 = (f32[4,128]{1,0:T(4,128)S(1)}, f32[4,128]{1,0:T(4,128)S(1)}, u32[]{:S(2)}, u32[]{:S(2)}) collective-permute-start(f32[4,128]{1,0:T(4,128)S(1)} %max.37), channel_id=1, source_target_pairs={{0,1},{32,33},{64,65},{96,97},{128,129},{160,161},{192,193},{224,2... | collective-permute-start | bytes 6152 | tf_op jit(solution)/shard_map/ppermute | solution.py:30
  55.5 2.9 %collective-permute-start.18 = (f32[4,128]{1,0:T(4,128)S(1)}, f32[4,128]{1,0:T(4,128)S(1)}, u32[]{:S(2)}, u32[]{:S(2)}) collective-permute-start(f32[4,128]{1,0:T(4,128)S(1)} %max.37), channel_id=1, source_target_pairs={{0,2},{32,34},{64,66},{96,98},{128,130},{160,162},{192,194},{224,2... | collective-permute-start | bytes 6152 | tf_op jit(solution)/shard_map/ppermute | solution.py:30
  58.4 0.2 collective-permute-start.19
  58.6 0.5 collective-permute-start.12
  59.2 2.4 %collective-permute-start.13 = (f32[1,2048]{1,0:T(1,128)S(1)}, f32[1,2048]{1,0:T(1,128)S(1)}, u32[]{:S(2)}, u32[]{:S(2)}) collective-permute-start(f32[1,2048]{1,0:T(1,128)S(1)} %get-tuple-element.13), channel_id=1, source_target_pairs={{0,8},{32,40},{64,72},{96,104},{128,136},{160,168},{192,200},{224,... | collective-permute-start | bytes 24584 | tf_op jit(solution)/shard_map/ppermute | solution.py:30
  61.6 0.0 collective-permute-done.17
  61.6 0.5 collective-permute-start.14
  62.1 0.0 collective-permute-done.18
  62.1 1.1 %collective-permute-done.19 = f32[4,128]{1,0:T(4,128)S(1)} collective-permute-done((f32[4,128]{1,0:T(4,128)S(1)}, f32[4,128]{1,0:T(4,128)S(1)}, u32[]{:S(2)}, u32[]{:S(2)}) %collective-permute-start.19) | collective-permute-done | bytes 2080 | tf_op jit(solution)/shard_map/ppermute | solution.py:30
  63.2 1.8 %collective-permute-start.20 = (f32[1,128]{1,0:T(1,128)S(1)}, f32[1,128]{1,0:T(1,128)S(1)}, u32[]{:S(2)}, u32[]{:S(2)}) collective-permute-start(f32[1,128]{1,0:T(1,128)S(1)} %get-tuple-element.20), channel_id=1, source_target_pairs={{0,208},{32,240},{64,0},{96,32},{128,64},{160,96},{192,128},{224,1... | collective-permute-start | bytes 1544 | tf_op jit(solution)/shard_map/ppermute | solution.py:30
  65.0 0.3 collective-permute-start.21
  65.3 2.4 %collective-permute-start.22 = (f32[1,128]{1,0:T(1,128)S(1)}, f32[1,128]{1,0:T(1,128)S(1)}, u32[]{:S(2)}, u32[]{:S(2)}) collective-permute-start(f32[1,128]{1,0:T(1,128)S(1)} %get-tuple-element.21), channel_id=1, source_target_pairs={{0,128},{32,176},{64,192},{96,240},{128,16},{160,32},{192,80},{224... | collective-permute-start | bytes 1544 | tf_op jit(solution)/shard_map/ppermute | solution.py:30
  67.7 0.0 collective-permute-done.13
  67.8 3.2 %collective-permute-start.15 = (f32[1,2048]{1,0:T(1,128)S(1)}, f32[1,2048]{1,0:T(1,128)S(1)}, u32[]{:S(2)}, u32[]{:S(2)}) collective-permute-start(f32[1,2048]{1,0:T(1,128)S(1)} %maximum_maximum_fusion), channel_id=1, source_target_pairs={{0,16},{32,48},{64,80},{96,112},{128,144},{160,176},{192,208},{224... | collective-permute-start | bytes 24584 | tf_op jit(solution)/shard_map/ppermute | solution.py:30
  70.9 0.0 collective-permute-done.22
  71.0 0.5 maximum_bitcast_fusion
  71.5 3.9 %collective-permute-done.15 = f32[1,2048]{1,0:T(1,128)S(1)} collective-permute-done((f32[1,2048]{1,0:T(1,128)S(1)}, f32[1,2048]{1,0:T(1,128)S(1)}, u32[]{:S(2)}, u32[]{:S(2)}) %collective-permute-start.15) | collective-permute-done | bytes 8224 | tf_op jit(solution)/shard_map/ppermute | solution.py:30
  75.4 0.6 max.36
  (21 shorter events, 0.1 us)
Async XLA Ops:
  0.6 19.4 %collective-permute-start.8 = (bf16[128,2048]{1,0:T(8,128)(2,1)}, bf16[128,2048]{1,0:T(8,128)(2,1)S(1)}, u32[]{:S(2)}, u32[]{:S(2)}) collective-permute-start(bf16[128,2048]{1,0:T(8,128)(2,1)} %mine.1), channel_id=1, source_target_pairs={{0,64},{32,96},{64,128},{96,160},{128,192},{160,224},{192,16},{224... | collective-permute-start | bytes 1572872 | tf_op jit(solution)/shard_map/ppermute | solution.py:30
  2.6 28.3 %collective-permute-start.4 = (bf16[128,2048]{1,0:T(8,128)(2,1)}, bf16[128,2048]{1,0:T(8,128)(2,1)S(1)}, u32[]{:S(2)}, u32[]{:S(2)}) collective-permute-start(bf16[128,2048]{1,0:T(8,128)(2,1)} %mine.1), channel_id=1, source_target_pairs={{0,208},{32,240},{64,0},{96,32},{128,64},{160,96},{192,128},{224,1... | collective-permute-start | bytes 1572872 | tf_op jit(solution)/shard_map/ppermute | solution.py:30
  6.7 25.5 %collective-permute-start.11 = (bf16[128,2048]{1,0:T(8,128)(2,1)}, bf16[128,2048]{1,0:T(8,128)(2,1)S(1)}, u32[]{:S(2)}, u32[]{:S(2)}) collective-permute-start(bf16[128,2048]{1,0:T(8,128)(2,1)} %mine.1), channel_id=1, source_target_pairs={{0,32},{32,0},{64,96},{96,64},{128,160},{160,128},{192,224},{224,1... | collective-permute-start | bytes 1572872 | tf_op jit(solution)/shard_map/ppermute | solution.py:30
  6.7 28.7 %collective-permute-start = (bf16[128,2048]{1,0:T(8,128)(2,1)}, bf16[128,2048]{1,0:T(8,128)(2,1)S(1)}, u32[]{:S(2)}, u32[]{:S(2)}) collective-permute-start(bf16[128,2048]{1,0:T(8,128)(2,1)} %mine.1), channel_id=1, source_target_pairs={{0,144},{32,160},{64,208},{96,224},{128,0},{160,48},{192,64},{224,... | collective-permute-start | bytes 1572872 | tf_op jit(solution)/shard_map/ppermute | solution.py:30
  20.0 23.4 %collective-permute-start.9 = (bf16[128,2048]{1,0:T(8,128)(2,1)S(1)}, bf16[128,2048]{1,0:T(8,128)(2,1)S(1)}, u32[]{:S(2)}, u32[]{:S(2)}) collective-permute-start(bf16[128,2048]{1,0:T(8,128)(2,1)S(1)} %collective-permute-done.8.mine), channel_id=1, source_target_pairs={{0,32},{32,0},{64,96},{96,64},{128,160},{160,128},{192,224},{224,1... | collective-permute-start | bytes 1572872 | tf_op jit(solution)/shard_map/ppermute | solution.py:30
  20.7 1.3 %collective-permute-start.6 = (f32[1,128]{1,0:T(1,128)S(1)}, f32[1,128]{1,0:T(1,128)S(1)}, u32[]{:S(2)}, u32[]{:S(2)}) collective-permute-start(f32[1,128]{1,0:T(1,128)S(1)} %bitcast_convert_fusion), channel_id=1, source_target_pairs={{0,32},{32,0},{64,96},{96,64},{128,160},{160,128},{192,224},{224,1... | collective-permute-start | bytes 1544 | tf_op jit(solution)/shard_map/ppermute | solution.py:30
  22.0 8.9 %collective-permute-start.2 = (f32[1,128]{1,0:T(1,128)S(1)}, f32[1,128]{1,0:T(1,128)S(1)}, u32[]{:S(2)}, u32[]{:S(2)}) collective-permute-start(f32[1,128]{1,0:T(1,128)S(1)} %bitcast_convert_fusion), channel_id=1, source_target_pairs={{0,144},{32,160},{64,208},{96,224},{128,0},{160,48},{192,64},{224,... | collective-permute-start | bytes 1544 | tf_op jit(solution)/shard_map/ppermute | solution.py:30
  30.9 1.1 %collective-permute-start.3 = (f32[1,128]{1,0:T(1,128)S(1)}, f32[1,128]{1,0:T(1,128)S(1)}, u32[]{:S(2)}, u32[]{:S(2)}) collective-permute-start(f32[1,128]{1,0:T(1,128)S(1)} %collective-permute-done.2), channel_id=1, source_target_pairs={{0,32},{32,0},{64,96},{96,64},{128,160},{160,128},{192,224},{224,1... | collective-permute-start | bytes 1544 | tf_op jit(solution)/shard_map/ppermute | solution.py:30
  30.9 15.8 %collective-permute-start.5 = (bf16[128,2048]{1,0:T(8,128)(2,1)S(1)}, bf16[128,2048]{1,0:T(8,128)(2,1)S(1)}, u32[]{:S(2)}, u32[]{:S(2)}) collective-permute-start(bf16[128,2048]{1,0:T(8,128)(2,1)S(1)} %collective-permute-done.4.mine), channel_id=1, source_target_pairs={{0,32},{32,0},{64,96},{96,64},{128,160},{160,128},{192,224},{224,1... | collective-permute-start | bytes 1572872 | tf_op jit(solution)/shard_map/ppermute | solution.py:30
  32.1 11.3 %collective-permute-start.10 = (f32[2,128]{1,0:T(2,128)S(1)}, f32[2,128]{1,0:T(2,128)S(1)}, u32[]{:S(2)}, u32[]{:S(2)}) collective-permute-start(f32[2,128]{1,0:T(2,128)S(1)} %pad_maximum_fusion.2.bias), channel_id=1, source_target_pairs={{0,64},{32,96},{64,128},{96,160},{128,192},{160,224},{192,16},{224... | collective-permute-start | bytes 3080 | tf_op jit(solution)/shard_map/ppermute | solution.py:30
  32.1 14.6 %collective-permute-start.7 = (f32[2,128]{1,0:T(2,128)S(1)}, f32[2,128]{1,0:T(2,128)S(1)}, u32[]{:S(2)}, u32[]{:S(2)}) collective-permute-start(f32[2,128]{1,0:T(2,128)S(1)} %pad_maximum_fusion.2.bias), channel_id=1, source_target_pairs={{0,208},{32,240},{64,0},{96,32},{128,64},{160,96},{192,128},{224,1... | collective-permute-start | bytes 3080 | tf_op jit(solution)/shard_map/ppermute | solution.py:30
  35.4 14.2 %collective-permute-start.1 = (bf16[128,2048]{1,0:T(8,128)(2,1)S(1)}, bf16[128,2048]{1,0:T(8,128)(2,1)S(1)}, u32[]{:S(2)}, u32[]{:S(2)}) collective-permute-start(bf16[128,2048]{1,0:T(8,128)(2,1)S(1)} %collective-permute-done.mine), channel_id=1, source_target_pairs={{0,32},{32,0},{64,96},{96,64},{128,160},{160,128},{192,224},{224,1... | collective-permute-start | bytes 1572872 | tf_op jit(solution)/shard_map/ppermute | solution.py:30
  35.4 3.4 %copy-start = (bf16[2048,2048]{1,0:T(8,128)(2,1)S(1)}, bf16[2048,2048]{1,0:T(8,128)(2,1)}, u32[]{:S(2)}) copy-start(bf16[2048,2048]{1,0:T(8,128)(2,1)} %states.7) | copy-start | bytes 25165828
  38.8 1.0 %copy-start.2 = (bf16[128,2048]{1,0:T(8,128)(2,1)S(1)}, bf16[128,2048]{1,0:T(8,128)(2,1)}, u32[]{:S(2)}) copy-start(bf16[128,2048]{1,0:T(8,128)(2,1)} %mine.1) | copy-start | bytes 1572868
  39.8 0.7 copy-start.3
  40.5 3.4 %copy-start.1 = (bf16[2048,2048]{1,0:T(8,128)(2,1)S(1)}, bf16[2048,2048]{1,0:T(8,128)(2,1)}, u32[]{:S(2)}) copy-start(bf16[2048,2048]{1,0:T(8,128)(2,1)} %states.7) | copy-start | bytes 25165828
  52.5 1.4 %collective-permute-start.16 = (f32[4,128]{1,0:T(4,128)S(1)}, f32[4,128]{1,0:T(4,128)S(1)}, u32[]{:S(2)}, u32[]{:S(2)}) collective-permute-start(f32[4,128]{1,0:T(4,128)S(1)} %bitcast.22), channel_id=1, source_target_pairs={{0,32},{32,0},{64,96},{96,64},{128,160},{160,128},{192,224},{224,1... | collective-permute-start | bytes 6152 | tf_op jit(solution)/shard_map/ppermute | solution.py:30
  53.9 7.7 %collective-permute-start.17 = (f32[4,128]{1,0:T(4,128)S(1)}, f32[4,128]{1,0:T(4,128)S(1)}, u32[]{:S(2)}, u32[]{:S(2)}) collective-permute-start(f32[4,128]{1,0:T(4,128)S(1)} %max.37), channel_id=1, source_target_pairs={{0,1},{32,33},{64,65},{96,97},{128,129},{160,161},{192,193},{224,2... | collective-permute-start | bytes 6152 | tf_op jit(solution)/shard_map/ppermute | solution.py:30
  55.5 6.6 %collective-permute-start.18 = (f32[4,128]{1,0:T(4,128)S(1)}, f32[4,128]{1,0:T(4,128)S(1)}, u32[]{:S(2)}, u32[]{:S(2)}) collective-permute-start(f32[4,128]{1,0:T(4,128)S(1)} %max.37), channel_id=1, source_target_pairs={{0,2},{32,34},{64,66},{96,98},{128,130},{160,162},{192,194},{224,2... | collective-permute-start | bytes 6152 | tf_op jit(solution)/shard_map/ppermute | solution.py:30
  58.4 4.8 %collective-permute-start.19 = (f32[4,128]{1,0:T(4,128)S(1)}, f32[4,128]{1,0:T(4,128)S(1)}, u32[]{:S(2)}, u32[]{:S(2)}) collective-permute-start(f32[4,128]{1,0:T(4,128)S(1)} %max.37), channel_id=1, source_target_pairs={{0,3},{32,35},{64,67},{96,99},{128,131},{160,163},{192,195},{224,2... | collective-permute-start | bytes 6152 | tf_op jit(solution)/shard_map/ppermute | solution.py:30
  58.6 6.7 %collective-permute-start.12 = (f32[1,2048]{1,0:T(1,128)S(1)}, f32[1,2048]{1,0:T(1,128)S(1)}, u32[]{:S(2)}, u32[]{:S(2)}) collective-permute-start(f32[1,2048]{1,0:T(1,128)S(1)} %get-tuple-element.13), channel_id=1, source_target_pairs={{0,4},{32,36},{64,68},{96,100},{128,132},{160,164},{192,196},{224,... | collective-permute-start | bytes 24584 | tf_op jit(solution)/shard_map/ppermute | solution.py:30
  59.2 8.6 %collective-permute-start.13 = (f32[1,2048]{1,0:T(1,128)S(1)}, f32[1,2048]{1,0:T(1,128)S(1)}, u32[]{:S(2)}, u32[]{:S(2)}) collective-permute-start(f32[1,2048]{1,0:T(1,128)S(1)} %get-tuple-element.13), channel_id=1, source_target_pairs={{0,8},{32,40},{64,72},{96,104},{128,136},{160,168},{192,200},{224,... | collective-permute-start | bytes 24584 | tf_op jit(solution)/shard_map/ppermute | solution.py:30
  61.6 6.2 %collective-permute-start.14 = (f32[1,2048]{1,0:T(1,128)S(1)}, f32[1,2048]{1,0:T(1,128)S(1)}, u32[]{:S(2)}, u32[]{:S(2)}) collective-permute-start(f32[1,2048]{1,0:T(1,128)S(1)} %get-tuple-element.13), channel_id=1, source_target_pairs={{0,12},{32,44},{64,76},{96,108},{128,140},{160,172},{192,204},{224... | collective-permute-start | bytes 24584 | tf_op jit(solution)/shard_map/ppermute | solution.py:30
  63.2 7.7 %collective-permute-start.20 = (f32[1,128]{1,0:T(1,128)S(1)}, f32[1,128]{1,0:T(1,128)S(1)}, u32[]{:S(2)}, u32[]{:S(2)}) collective-permute-start(f32[1,128]{1,0:T(1,128)S(1)} %get-tuple-element.20), channel_id=1, source_target_pairs={{0,208},{32,240},{64,0},{96,32},{128,64},{160,96},{192,128},{224,1... | collective-permute-start | bytes 1544 | tf_op jit(solution)/shard_map/ppermute | solution.py:30
  65.0 6.0 %collective-permute-start.21 = (f32[1,128]{1,0:T(1,128)S(1)}, f32[1,128]{1,0:T(1,128)S(1)}, u32[]{:S(2)}, u32[]{:S(2)}) collective-permute-start(f32[1,128]{1,0:T(1,128)S(1)} %get-tuple-element.22), channel_id=1, source_target_pairs={{0,64},{32,96},{64,128},{96,160},{128,192},{160,224},{192,16},{224... | collective-permute-start | bytes 1544 | tf_op jit(solution)/shard_map/ppermute | solution.py:30
  65.3 5.7 %collective-permute-start.22 = (f32[1,128]{1,0:T(1,128)S(1)}, f32[1,128]{1,0:T(1,128)S(1)}, u32[]{:S(2)}, u32[]{:S(2)}) collective-permute-start(f32[1,128]{1,0:T(1,128)S(1)} %get-tuple-element.21), channel_id=1, source_target_pairs={{0,128},{32,176},{64,192},{96,240},{128,16},{160,32},{192,80},{224... | collective-permute-start | bytes 1544 | tf_op jit(solution)/shard_map/ppermute | solution.py:30
  67.8 7.6 %collective-permute-start.15 = (f32[1,2048]{1,0:T(1,128)S(1)}, f32[1,2048]{1,0:T(1,128)S(1)}, u32[]{:S(2)}, u32[]{:S(2)}) collective-permute-start(f32[1,2048]{1,0:T(1,128)S(1)} %maximum_maximum_fusion), channel_id=1, source_target_pairs={{0,16},{32,48},{64,80},{96,112},{128,144},{160,176},{192,208},{224... | collective-permute-start | bytes 24584 | tf_op jit(solution)/shard_map/ppermute | solution.py:30

commit v2 on v1

v2 whole, which is shorter than its diff:
```python
import functools

import jax
import jax.numpy as jnp
from jax import lax
from jax.experimental import pallas as pl
from jax.experimental.pallas import tpu as pltpu
from jax.sharding import PartitionSpec as P

AXES = ("grp", "cut", "st")
NX, NY, NZ, NC = 4, 4, 8, 2
LANES = 128


def position(x, y, z, c):
    z_hi, z_lo = divmod(z % NZ, 4)
    return (((z_lo * NC + c % NC) * 8) + z_hi * NX + x % NX) * NY + y % NY


def routes(move):
    pairs = []
    for x in range(NX):
        for y in range(NY):
            for z in range(NZ):
                for c in range(NC):
                    pairs.append((position(x, y, z, c), position(*move(x, y, z, c))))
    return pairs


def send(block, move):
    return lax.ppermute(block, AXES, routes(move))


def over_core(x, y, z, c):
    return x, y, z, 1 - c


def up(x, y, z, c):
    return x, y, z + 1, c


def down(x, y, z, c):
    return x, y, z - 1, c


def two_out(x, y, z, c):
    return x, y, z - 2 if c == 0 else z + 2, c


def two_back(x, y, z, c):
    return x, y, z + 2 if c == 0 else z - 2, c


def far(x, y, z, c):
    return x, y, z + 4, c


def over_x(d):
    return lambda x, y, z, c: (x ^ d, y, z, c)


def over_y(d):
    return lambda x, y, z, c: (x, y ^ d, z, c)


def score_body(tile, tiles, count, spots, y, old, prev, states, *refs):
    blocks, (top, mine, other, slopes, best, offset) = refs[:count], refs[count:]
    depth = states.shape[1]
    half = mine.shape[1]
    step = pl.program_id(0)

    @pl.when(step == 0)
    def _():
        for block, start, rows, base, mask in spots:
            place = base if mask is None else pl.multiple_of(base + (y[0] ^ mask) * rows, rows)
            slopes[pl.ds(place, rows), :] = blocks[block][start : start + rows, :depth]
            offset[pl.ds(place, rows), :] = blocks[block][start : start + rows, depth:].astype(jnp.float32)
        best[...] = jnp.full(best.shape, -jnp.inf, jnp.float32)

    scores = lax.dot_general(
        slopes[...], states[...], (((1,), (1,)), ((), ())), preferred_element_type=jnp.float32
    )
    lifted = scores - old[...]
    most = best[...]
    for lane in range(0, tile, LANES):
        most = jnp.maximum(most, lifted[:, lane : lane + LANES])
    best[...] = most
    wide = offset[...]
    valued = jnp.concatenate(
        [scores[:, lane : lane + LANES] + wide for lane in range(0, tile, LANES)], axis=1
    )
    top[...] = jnp.maximum(prev[...], jnp.max(valued, axis=0, keepdims=True))

    @pl.when(step == tiles - 1)
    def _():
        lift = jnp.max((best[...] + offset[...]).T, axis=0, keepdims=True)
        mine[...] = lift[:, :half]
        other[...] = lift[:, half:]


def score(spots, blocks, y, old, prev, states, tile=1024):
    count, depth = states.shape
    cuts = sum(spot[2] for spot in spots)
    tiles = count // tile
    whole = lambda shape: pl.BlockSpec(shape, lambda i, y: (0, 0))
    along = pl.BlockSpec((1, tile), lambda i, y: (0, i))
    lift = jax.ShapeDtypeStruct((1, cuts // 2), jnp.float32)
    return pl.pallas_call(
        functools.partial(score_body, tile, tiles, len(blocks), spots),
        grid_spec=pltpu.PrefetchScalarGridSpec(
            num_scalar_prefetch=1,
            grid=(tiles,),
            in_specs=[along, along, pl.BlockSpec((tile, depth), lambda i, y: (i, 0))]
            + [whole(block.shape) for block in blocks],
            out_specs=[along, whole(lift.shape), whole(lift.shape)],
            scratch_shapes=[
                pltpu.VMEM((cuts, depth), jnp.bfloat16),
                pltpu.VMEM((cuts, LANES), jnp.float32),
                pltpu.VMEM((cuts, LANES), jnp.float32),
            ],
        ),
        out_shape=[jax.ShapeDtypeStruct((1, count), jnp.float32), lift, lift],
        compiler_params=pltpu.CompilerParams(vmem_limit_bytes=24 << 20),
        cost_estimate=pl.CostEstimate(
            flops=2 * cuts * depth * count, bytes_accessed=2 * (count + cuts) * depth, transcendentals=0
        ),
    )(y, old, prev, states, *blocks)


def body(coefficients, intercepts, states, old_values):
    old = old_values[None, :]
    cuts = coefficients.shape[0]
    run = cuts // NY
    spread = jnp.broadcast_to(intercepts[:, None], (cuts, LANES))
    own = jnp.concatenate([coefficients, spread], axis=1)
    pair = ((0, 0, cuts, 0, None), (1, 0, cuts, cuts, None))

    y = lax.axis_index("st")
    quarter = lax.dynamic_slice_in_dim(own, y * run, run, 0)
    y = y[None]
    part = send(quarter, two_out)
    lower = send(own, up)
    upper = send(own, down)
    peer = send(own, over_core)
    parts = [part] + [send(part, over_y(d)) for d in (1, 2, 3)]
    top, own_mine, own_other = score(pair, [own, peer], y, old, old, states)
    lower, upper, top = lax.optimization_barrier((lower, upper, top))
    two = jnp.concatenate(parts, axis=0)
    runs = tuple((b, k * run, run, b * cuts, k) for b in range(2) for k in range(NY))
    top, lower_mine, lower_other = score(pair, [lower, send(lower, over_core)], y, old, top, states)
    top, upper_mine, upper_other = score(pair, [upper, send(upper, over_core)], y, old, top, states)
    top, two_mine, two_other = score(runs, [two, send(two, over_core)], y, old, top, states)

    mine = jnp.concatenate([own_mine, lower_mine, upper_mine, two_mine], axis=0)
    other = jnp.concatenate([own_other, lower_other, upper_other, two_other], axis=0)
    swapped = send(other, over_core)
    for_x = [send(top, over_x(d)) for d in (1, 2, 3)]
    swapped, *for_x = lax.optimization_barrier((swapped, *for_x))
    lifts = jnp.maximum(mine, swapped)
    for_y = [send(lifts, over_y(d)) for d in (1, 2, 3)]
    top = functools.reduce(jnp.maximum, for_x, top)
    new_values = jnp.maximum(top, send(top, far))
    lifts = functools.reduce(jnp.maximum, for_y, lifts)
    back = [send(lifts[1:2], down), send(lifts[2:3], up), send(lifts[3:4], two_back)]
    cut_gaps = functools.reduce(jnp.maximum, back, lifts[0:1])
    return new_values[0], cut_gaps[0]


def solution(mesh):
    placed = (P(("grp", "cut"), None), P(("grp", "cut")), P(("grp", "st"), None), P(("grp", "st")))
    return jax.shard_map(
        body,
        mesh=mesh,
        in_specs=placed,
        out_specs=(P(("grp", "st")), P(("grp", "cut"))),
        check_vma=False,
    )
```

time: 76.4 us -> 67.5 us (0.88)
  the two profiles are of different devices: /device:TPU:2 before, /device:TPU:32 now
where the time goes in v2:
time: 67.5 us; the launch traced here: 67.3 us
  starting transfers between devices  36.3 us (54%)
  waiting for transfers between devices  11.4 us (17%)
  Pallas kernels  11.4 us (17%)
  local copies, waits for them, and re-layouts  4.19 us (6%)
  other arithmetic  3.18 us (5%)
  between operations  0.82 us (1%)
    ppermute x21, starting transfers between devices, send(): return lax.ppermute(block, AXES, routes(move))  36.3 us
    pallas_call x4, Pallas kernels, score(): pl.pallas_call(functools.partial(score_body, tile, tiles, len(blocks), sp...  11.4 us
    ppermute x21, waiting for transfers between devices, send(): return lax.ppermute(block, AXES, routes(move))  11.4 us
    unnamed x7, local copies, waits for them, and re-layouts  3.43 us
    concatenate x2, other arithmetic, body(): own = jnp.concatenate([coefficients, spread], axis=1)  2 us
  transfers between devices with their start and end apart: 21, of which 8 were waited for; matrix products, arithmetic and copies ran while one was open for 3% of the time, Pallas kernels for 13%

profile of v2, /device:TPU:32, one launch (start us, length us, event | category | flops | bytes accessed | tf_op | source)
XLA Modules:
  0.0 67.3 jit_solution(7828029187328862716)
XLA Ops:
  0.6 0.7 %broadcast_in_dim.14 = bf16[128,128]{1,0:T(8,128)(2,1)S(1)} broadcast(bf16[128]{0:T(256)(128)(2,1)} %param.5), dimensions={0} | broadcast | bytes 33024 | tf_op jit(solution)/shard_map/broadcast_in_dim | solution.py:134
  1.4 0.0 copy-start.1
  1.4 0.9 %fusion = bf16[32,2176]{1,0:T(8,128)(2,1)S(1)} fusion(s32[]{:T(128)S(6)} %select_n.3, bf16[128,128]{1,0:T(8,128)(2,1)S(1)} %broadcast_in_dim.14, bf16[128,2048]{1,0:T(8,128)(2,1)} %param.4), kind=kLoop, calls=%fused_computation.3 | loop fusion | flops 278528 | bytes 696324 | tf_op jit(solution)/shard_map/concatenate | solution.py:135
  2.3 5.5 %collective-permute-start.5 = (bf16[32,2176]{1,0:T(8,128)(2,1)S(1)}, bf16[32,2176]{1,0:T(8,128)(2,1)S(1)}, u32[]{:S(2)}, u32[]{:S(2)}) collective-permute-start(bf16[32,2176]{1,0:T(8,128)(2,1)S(1)} %fusion), channel_id=1, source_target_pairs={{0,144},{32,160},{64,208},{96,224},{128,0},{160,48},{192,64},{224,... | collective-permute-start | bytes 417800 | tf_op jit(solution)/shard_map/ppermute | solution.py:31
  7.8 1.1 %pad_maximum_fusion.refs_0_ = bf16[128,2176]{1,0:T(8,128)(2,1)S(1)} fusion(bf16[128,128]{1,0:T(8,128)(2,1)S(1)} %broadcast_in_dim.14, bf16[128,2048]{1,0:T(8,128)(2,1)} %param.4), kind=kLoop, calls=%fused_computation.1 | loop fusion | flops 1114112 | bytes 1114112 | tf_op jit(solution)/shard_map/concatenate | solution.py:135
  8.9 0.1 collective-permute-start.2
  9.0 0.5 collective-permute-start
  9.5 1.6 %collective-permute-start.1 = (bf16[128,2176]{1,0:T(8,128)(2,1)S(1)}, bf16[128,2176]{1,0:T(8,128)(2,1)S(1)}, u32[]{:S(2)}, u32[]{:S(2)}) collective-permute-start(bf16[128,2176]{1,0:T(8,128)(2,1)S(1)} %pad_maximum_fusion.refs_0_), channel_id=1, source_target_pairs={{0,208},{32,240},{64,0},{96,32},{128,64},{160,96},{192,128},{224,1... | collective-permute-start | bytes 1671176 | tf_op jit(solution)/shard_map/ppermute | solution.py:31
  11.1 1.6 %collective-permute-start.6 = (bf16[32,2176]{1,0:T(8,128)(2,1)S(1)}, bf16[32,2176]{1,0:T(8,128)(2,1)S(1)}, u32[]{:S(2)}, u32[]{:S(2)}) collective-permute-start(bf16[32,2176]{1,0:T(8,128)(2,1)S(1)} %collective-permute-done.5), channel_id=1, source_target_pairs={{0,1},{32,33},{64,65},{96,97},{128,129},{160,161},{192,193},{224,2... | collective-permute-start | bytes 417800 | tf_op jit(solution)/shard_map/ppermute | solution.py:31
  12.7 3.0 %collective-permute-start.7 = (bf16[32,2176]{1,0:T(8,128)(2,1)S(1)}, bf16[32,2176]{1,0:T(8,128)(2,1)S(1)}, u32[]{:S(2)}, u32[]{:S(2)}) collective-permute-start(bf16[32,2176]{1,0:T(8,128)(2,1)S(1)} %collective-permute-done.5), channel_id=1, source_target_pairs={{0,2},{32,34},{64,66},{96,98},{128,130},{160,162},{192,194},{224,2... | collective-permute-start | bytes 417800 | tf_op jit(solution)/shard_map/ppermute | solution.py:31
  15.7 1.7 %collective-permute-done.6 = bf16[32,2176]{1,0:T(8,128)(2,1)S(1)} collective-permute-done((bf16[32,2176]{1,0:T(8,128)(2,1)S(1)}, bf16[32,2176]{1,0:T(8,128)(2,1)S(1)}, u32[]{:S(2)}, u32[]{:S(2)}) %collective-permute-start.6) | collective-permute-done | bytes 139296 | tf_op jit(solution)/shard_map/ppermute | solution.py:31
  17.4 3.2 %collective-permute-start.8 = (bf16[32,2176]{1,0:T(8,128)(2,1)S(1)}, bf16[32,2176]{1,0:T(8,128)(2,1)S(1)}, u32[]{:S(2)}, u32[]{:S(2)}) collective-permute-start(bf16[32,2176]{1,0:T(8,128)(2,1)S(1)} %collective-permute-done.5), channel_id=1, source_target_pairs={{0,3},{32,35},{64,67},{96,99},{128,131},{160,163},{192,195},{224,2... | collective-permute-start | bytes 417800 | tf_op jit(solution)/shard_map/ppermute | solution.py:31
  20.6 0.0 collective-permute-done.2.refs_1_
  20.7 0.0 copy-start
  20.7 3.4 %copy-done = bf16[2048,2048]{1,0:T(8,128)(2,1)S(1)} copy-done((bf16[2048,2048]{1,0:T(8,128)(2,1)S(1)}, bf16[2048,2048]{1,0:T(8,128)(2,1)}, u32[]{:S(2)}) %copy-start) | copy-done | bytes 8388632
  24.0 2.8 %shard_map.59 = (f32[1,2048]{1,0:T(1,128)S(1)}, f32[1,128]{1,0:T(1,128)S(1)}, f32[1,128]{1,0:T(1,128)S(1)}) custom-call(s32[1]{0:T(128)} %bitcast.y, f32[1,2048]{1,0:T(1,128)S(1)} %bitcast.5, f32[1,2048]{1,0:T(1,128)S(1)} %bitcast.6, bf16[2048,2048]{1,0:T(8,128)(2,1)S(1)} %copy-done, bf16[128,2176]{1,0:T(8,128)(2,1)S(1)} %pad_maximum_fusion.refs_0_, ...), custom_call_target="tpu_custom_call" | custom-call | flops 2147483648 | bytes 9437184 | tf_op jit(solution)/shard_map/pallas_call | solution.py:108
  26.9 0.0 collective-permute-done.1.refs_0_
  26.9 0.1 collective-permute-start.3
  27.0 0.6 collective-permute-start.4
  27.6 0.1 collective-permute-start.9
  27.7 1.2 %collective-permute-done.3.refs_1_ = bf16[128,2176]{1,0:T(8,128)(2,1)S(1)} collective-permute-done((bf16[128,2176]{1,0:T(8,128)(2,1)S(1)}, bf16[128,2176]{1,0:T(8,128)(2,1)S(1)}, u32[]{:S(2)}, u32[]{:S(2)}) %collective-permute-start.3) | collective-permute-done | bytes 557088 | tf_op jit(solution)/shard_map/ppermute | solution.py:31
  29.0 2.8 %shard_map.60 = (f32[1,2048]{1,0:T(1,128)S(1)}, f32[1,128]{1,0:T(1,128)S(1)}, f32[1,128]{1,0:T(1,128)S(1)}) custom-call(s32[1]{0:T(128)} %bitcast.y, f32[1,2048]{1,0:T(1,128)S(1)} %bitcast.7, f32[1,2048]{1,0:T(1,128)S(1)} %get-tuple-element.22.prev, bf16[2048,2048]{1,0:T(8,128)(2,1)S(1)} %copy-done, bf16[128,2176]{1,0:T(8,128)(2,1)S(1)} %collective-permute-done.refs_0_, ...), custom_call_target="tpu_custom_call" | custom-call | flops 2147483648 | bytes 9437184 | tf_op jit(solution)/shard_map/pallas_call | solution.py:108
  31.8 0.0 collective-permute-done.4.refs_1_
  31.8 2.9 %shard_map.61 = (f32[1,2048]{1,0:T(1,128)S(1)}, f32[1,128]{1,0:T(1,128)S(1)}, f32[1,128]{1,0:T(1,128)S(1)}) custom-call(s32[1]{0:T(128)} %bitcast.y, f32[1,2048]{1,0:T(1,128)S(1)} %bitcast.8, f32[1,2048]{1,0:T(1,128)S(1)} %get-tuple-element.24.prev, bf16[2048,2048]{1,0:T(8,128)(2,1)S(1)} %copy-done, bf16[128,2176]{1,0:T(8,128)(2,1)S(1)} %collective-permute-done.1.refs_0_, ...), custom_call_target="tpu_custom_call" | custom-call | flops 2147483648 | bytes 9437184 | tf_op jit(solution)/shard_map/pallas_call | solution.py:108
  34.7 0.0 collective-permute-done.9.refs_1_
  34.7 2.9 %shard_map.62 = (f32[1,2048]{1,0:T(1,128)S(1)}, f32[1,128]{1,0:T(1,128)S(1)}, f32[1,128]{1,0:T(1,128)S(1)}) custom-call(s32[1]{0:T(128)} %bitcast.y, f32[1,2048]{1,0:T(1,128)S(1)} %bitcast.9, f32[1,2048]{1,0:T(1,128)S(1)} %get-tuple-element.26.prev, bf16[2048,2048]{1,0:T(8,128)(2,1)S(1)} %copy-done, ...), custom_call_target="tpu_custom_call" | custom-call | flops 2147483648 | bytes 9437184 | tf_op jit(solution)/shard_map/pallas_call | solution.py:108
  37.6 1.6 %collective-permute-start.11 = (f32[1,2048]{1,0:T(1,128)S(1)}, f32[1,2048]{1,0:T(1,128)S(1)}, u32[]{:S(2)}, u32[]{:S(2)}) collective-permute-start(f32[1,2048]{1,0:T(1,128)S(1)} %get-tuple-element.27), channel_id=1, source_target_pairs={{0,4},{32,36},{64,68},{96,100},{128,132},{160,164},{192,196},{224,... | collective-permute-start | bytes 24584 | tf_op jit(solution)/shard_map/ppermute | solution.py:31
  39.1 2.7 %collective-permute-start.12 = (f32[1,2048]{1,0:T(1,128)S(1)}, f32[1,2048]{1,0:T(1,128)S(1)}, u32[]{:S(2)}, u32[]{:S(2)}) collective-permute-start(f32[1,2048]{1,0:T(1,128)S(1)} %get-tuple-element.27), channel_id=1, source_target_pairs={{0,8},{32,40},{64,72},{96,104},{128,136},{160,168},{192,200},{224,... | collective-permute-start | bytes 24584 | tf_op jit(solution)/shard_map/ppermute | solution.py:31
  41.9 0.5 collective-permute-start.13
  42.4 0.1 collective-permute-start.10
  42.5 1.1 %collective-permute-done.10 = f32[4,128]{1,0:T(4,128)S(1)} collective-permute-done((f32[4,128]{1,0:T(4,128)S(1)}, f32[4,128]{1,0:T(4,128)S(1)}, u32[]{:S(2)}, u32[]{:S(2)}) %collective-permute-start.10) | collective-permute-done | bytes 2080 | tf_op jit(solution)/shard_map/ppermute | solution.py:31
  43.6 0.7 %collective-permute-done.12 = f32[1,2048]{1,0:T(1,128)S(1)} collective-permute-done((f32[1,2048]{1,0:T(1,128)S(1)}, f32[1,2048]{1,0:T(1,128)S(1)}, u32[]{:S(2)}, u32[]{:S(2)}) %collective-permute-start.12) | collective-permute-done | bytes 8224 | tf_op jit(solution)/shard_map/ppermute | solution.py:31
  44.3 2.4 %collective-permute-done.13 = f32[1,2048]{1,0:T(1,128)S(1)} collective-permute-done((f32[1,2048]{1,0:T(1,128)S(1)}, f32[1,2048]{1,0:T(1,128)S(1)}, u32[]{:S(2)}, u32[]{:S(2)}) %collective-permute-start.13) | collective-permute-done | bytes 8224 | tf_op jit(solution)/shard_map/ppermute | solution.py:31
  46.8 0.2 collective-permute-start.15
  47.0 1.4 %collective-permute-start.16 = (f32[4,128]{1,0:T(4,128)S(1)}, f32[4,128]{1,0:T(4,128)S(1)}, u32[]{:S(2)}, u32[]{:S(2)}) collective-permute-start(f32[4,128]{1,0:T(4,128)S(1)} %maximum_maximum_fusion.1), channel_id=1, source_target_pairs={{0,2},{32,34},{64,66},{96,98},{128,130},{160,162},{192,194},{224,2... | collective-permute-start | bytes 6152 | tf_op jit(solution)/shard_map/ppermute | solution.py:31
  48.4 3.2 %collective-permute-start.17 = (f32[4,128]{1,0:T(4,128)S(1)}, f32[4,128]{1,0:T(4,128)S(1)}, u32[]{:S(2)}, u32[]{:S(2)}) collective-permute-start(f32[4,128]{1,0:T(4,128)S(1)} %maximum_maximum_fusion.1), channel_id=1, source_target_pairs={{0,3},{32,35},{64,67},{96,99},{128,131},{160,163},{192,195},{224,2... | collective-permute-start | bytes 6152 | tf_op jit(solution)/shard_map/ppermute | solution.py:31
  51.5 0.5 collective-permute-done.16
  52.1 1.1 %collective-permute-done.17 = f32[4,128]{1,0:T(4,128)S(1)} collective-permute-done((f32[4,128]{1,0:T(4,128)S(1)}, f32[4,128]{1,0:T(4,128)S(1)}, u32[]{:S(2)}, u32[]{:S(2)}) %collective-permute-start.17) | collective-permute-done | bytes 2080 | tf_op jit(solution)/shard_map/ppermute | solution.py:31
  53.2 2.3 %collective-permute-start.18 = (f32[1,128]{1,0:T(1,128)S(1)}, f32[1,128]{1,0:T(1,128)S(1)}, u32[]{:S(2)}, u32[]{:S(2)}) collective-permute-start(f32[1,128]{1,0:T(1,128)S(1)} %get-tuple-element.40), channel_id=1, source_target_pairs={{0,208},{32,240},{64,0},{96,32},{128,64},{160,96},{192,128},{224,1... | collective-permute-start | bytes 1544 | tf_op jit(solution)/shard_map/ppermute | solution.py:31
  55.5 0.0 collective-permute-start.19
  55.5 3.5 %collective-permute-start.20 = (f32[1,128]{1,0:T(1,128)S(1)}, f32[1,128]{1,0:T(1,128)S(1)}, u32[]{:S(2)}, u32[]{:S(2)}) collective-permute-start(f32[1,128]{1,0:T(1,128)S(1)} %get-tuple-element.41), channel_id=1, source_target_pairs={{0,128},{32,176},{64,192},{96,240},{128,16},{160,32},{192,80},{224... | collective-permute-start | bytes 1544 | tf_op jit(solution)/shard_map/ppermute | solution.py:31
  59.0 4.5 %collective-permute-start.14 = (f32[1,2048]{1,0:T(1,128)S(1)}, f32[1,2048]{1,0:T(1,128)S(1)}, u32[]{:S(2)}, u32[]{:S(2)}) collective-permute-start(f32[1,2048]{1,0:T(1,128)S(1)} %maximum_maximum_fusion), channel_id=1, source_target_pairs={{0,16},{32,48},{64,80},{96,112},{128,144},{160,176},{192,208},{224... | collective-permute-start | bytes 24584 | tf_op jit(solution)/shard_map/ppermute | solution.py:31
  63.6 0.0 collective-permute-done.18
  63.6 0.0 collective-permute-done.19
  63.6 0.0 collective-permute-done.20
  63.6 0.5 maximum_bitcast_fusion
  64.1 2.6 %collective-permute-done.14 = f32[1,2048]{1,0:T(1,128)S(1)} collective-permute-done((f32[1,2048]{1,0:T(1,128)S(1)}, f32[1,2048]{1,0:T(1,128)S(1)}, u32[]{:S(2)}, u32[]{:S(2)}) %collective-permute-start.14) | collective-permute-done | bytes 8224 | tf_op jit(solution)/shard_map/ppermute | solution.py:31
  66.7 0.6 max.36
  (16 shorter events, 0.1 us)
Async XLA Ops:
  1.4 19.3 %copy-start.1 = (f32[2048]{0:T(1024)S(1)}, f32[2048]{0:T(1024)}, u32[]{:S(2)}) copy-start(f32[2048]{0:T(1024)} %param.7) | copy-start | bytes 24580
  2.3 8.8 %collective-permute-start.5 = (bf16[32,2176]{1,0:T(8,128)(2,1)S(1)}, bf16[32,2176]{1,0:T(8,128)(2,1)S(1)}, u32[]{:S(2)}, u32[]{:S(2)}) collective-permute-start(bf16[32,2176]{1,0:T(8,128)(2,1)S(1)} %fusion), channel_id=1, source_target_pairs={{0,144},{32,160},{64,208},{96,224},{128,0},{160,48},{192,64},{224,... | collective-permute-start | bytes 417800 | tf_op jit(solution)/shard_map/ppermute | solution.py:31
  8.9 11.8 %collective-permute-start.2 = (bf16[128,2176]{1,0:T(8,128)(2,1)S(1)}, bf16[128,2176]{1,0:T(8,128)(2,1)S(1)}, u32[]{:S(2)}, u32[]{:S(2)}) collective-permute-start(bf16[128,2176]{1,0:T(8,128)(2,1)S(1)} %pad_maximum_fusion.refs_0_), channel_id=1, source_target_pairs={{0,32},{32,0},{64,96},{96,64},{128,160},{160,128},{192,224},{224,1... | collective-permute-start | bytes 1671176 | tf_op jit(solution)/shard_map/ppermute | solution.py:31
  9.0 17.9 %collective-permute-start = (bf16[128,2176]{1,0:T(8,128)(2,1)S(1)}, bf16[128,2176]{1,0:T(8,128)(2,1)S(1)}, u32[]{:S(2)}, u32[]{:S(2)}) collective-permute-start(bf16[128,2176]{1,0:T(8,128)(2,1)S(1)} %pad_maximum_fusion.refs_0_), channel_id=1, source_target_pairs={{0,64},{32,96},{64,128},{96,160},{128,192},{160,224},{192,16},{224... | collective-permute-start | bytes 1671176 | tf_op jit(solution)/shard_map/ppermute | solution.py:31
  9.5 17.4 %collective-permute-start.1 = (bf16[128,2176]{1,0:T(8,128)(2,1)S(1)}, bf16[128,2176]{1,0:T(8,128)(2,1)S(1)}, u32[]{:S(2)}, u32[]{:S(2)}) collective-permute-start(bf16[128,2176]{1,0:T(8,128)(2,1)S(1)} %pad_maximum_fusion.refs_0_), channel_id=1, source_target_pairs={{0,208},{32,240},{64,0},{96,32},{128,64},{160,96},{192,128},{224,1... | collective-permute-start | bytes 1671176 | tf_op jit(solution)/shard_map/ppermute | solution.py:31
  11.1 6.3 %collective-permute-start.6 = (bf16[32,2176]{1,0:T(8,128)(2,1)S(1)}, bf16[32,2176]{1,0:T(8,128)(2,1)S(1)}, u32[]{:S(2)}, u32[]{:S(2)}) collective-permute-start(bf16[32,2176]{1,0:T(8,128)(2,1)S(1)} %collective-permute-done.5), channel_id=1, source_target_pairs={{0,1},{32,33},{64,65},{96,97},{128,129},{160,161},{192,193},{224,2... | collective-permute-start | bytes 417800 | tf_op jit(solution)/shard_map/ppermute | solution.py:31
  12.7 14.3 %collective-permute-start.7 = (bf16[32,2176]{1,0:T(8,128)(2,1)S(1)}, bf16[32,2176]{1,0:T(8,128)(2,1)S(1)}, u32[]{:S(2)}, u32[]{:S(2)}) collective-permute-start(bf16[32,2176]{1,0:T(8,128)(2,1)S(1)} %collective-permute-done.5), channel_id=1, source_target_pairs={{0,2},{32,34},{64,66},{96,98},{128,130},{160,162},{192,194},{224,2... | collective-permute-start | bytes 417800 | tf_op jit(solution)/shard_map/ppermute | solution.py:31
  17.4 10.2 %collective-permute-start.8 = (bf16[32,2176]{1,0:T(8,128)(2,1)S(1)}, bf16[32,2176]{1,0:T(8,128)(2,1)S(1)}, u32[]{:S(2)}, u32[]{:S(2)}) collective-permute-start(bf16[32,2176]{1,0:T(8,128)(2,1)S(1)} %collective-permute-done.5), channel_id=1, source_target_pairs={{0,3},{32,35},{64,67},{96,99},{128,131},{160,163},{192,195},{224,2... | collective-permute-start | bytes 417800 | tf_op jit(solution)/shard_map/ppermute | solution.py:31
  20.7 3.4 %copy-start = (bf16[2048,2048]{1,0:T(8,128)(2,1)S(1)}, bf16[2048,2048]{1,0:T(8,128)(2,1)}, u32[]{:S(2)}) copy-start(bf16[2048,2048]{1,0:T(8,128)(2,1)} %states.7) | copy-start | bytes 25165828
  26.9 2.0 %collective-permute-start.3 = (bf16[128,2176]{1,0:T(8,128)(2,1)S(1)}, bf16[128,2176]{1,0:T(8,128)(2,1)S(1)}, u32[]{:S(2)}, u32[]{:S(2)}) collective-permute-start(bf16[128,2176]{1,0:T(8,128)(2,1)S(1)} %collective-permute-done.refs_0_), channel_id=1, source_target_pairs={{0,32},{32,0},{64,96},{96,64},{128,160},{160,128},{192,224},{224,1... | collective-permute-start | bytes 1671176 | tf_op jit(solution)/shard_map/ppermute | solution.py:31
  27.0 4.8 %collective-permute-start.4 = (bf16[128,2176]{1,0:T(8,128)(2,1)S(1)}, bf16[128,2176]{1,0:T(8,128)(2,1)S(1)}, u32[]{:S(2)}, u32[]{:S(2)}) collective-permute-start(bf16[128,2176]{1,0:T(8,128)(2,1)S(1)} %collective-permute-done.1.refs_0_), channel_id=1, source_target_pairs={{0,32},{32,0},{64,96},{96,64},{128,160},{160,128},{192,224},{224,1... | collective-permute-start | bytes 1671176 | tf_op jit(solution)/shard_map/ppermute | solution.py:31
  27.6 7.1 %collective-permute-start.9 = (bf16[128,2176]{1,0:T(8,128)(2,1)S(1)}, bf16[128,2176]{1,0:T(8,128)(2,1)S(1)}, u32[]{:S(2)}, u32[]{:S(2)}) collective-permute-start(bf16[128,2176]{1,0:T(8,128)(2,1)S(1)} %constant_dynamic-update-slice_fusion.refs_0_), channel_id=1, source_target_pairs={{0,32},{32,0},{64,96},{96,64},{128,160},{160,128},{192,224},{224,1... | collective-permute-start | bytes 1671176 | tf_op jit(solution)/shard_map/ppermute | solution.py:31
  37.6 6.0 %collective-permute-start.11 = (f32[1,2048]{1,0:T(1,128)S(1)}, f32[1,2048]{1,0:T(1,128)S(1)}, u32[]{:S(2)}, u32[]{:S(2)}) collective-permute-start(f32[1,2048]{1,0:T(1,128)S(1)} %get-tuple-element.27), channel_id=1, source_target_pairs={{0,4},{32,36},{64,68},{96,100},{128,132},{160,164},{192,196},{224,... | collective-permute-start | bytes 24584 | tf_op jit(solution)/shard_map/ppermute | solution.py:31
  39.1 5.2 %collective-permute-start.12 = (f32[1,2048]{1,0:T(1,128)S(1)}, f32[1,2048]{1,0:T(1,128)S(1)}, u32[]{:S(2)}, u32[]{:S(2)}) collective-permute-start(f32[1,2048]{1,0:T(1,128)S(1)} %get-tuple-element.27), channel_id=1, source_target_pairs={{0,8},{32,40},{64,72},{96,104},{128,136},{160,168},{192,200},{224,... | collective-permute-start | bytes 24584 | tf_op jit(solution)/shard_map/ppermute | solution.py:31
  41.9 4.9 %collective-permute-start.13 = (f32[1,2048]{1,0:T(1,128)S(1)}, f32[1,2048]{1,0:T(1,128)S(1)}, u32[]{:S(2)}, u32[]{:S(2)}) collective-permute-start(f32[1,2048]{1,0:T(1,128)S(1)} %get-tuple-element.27), channel_id=1, source_target_pairs={{0,12},{32,44},{64,76},{96,108},{128,140},{160,172},{192,204},{224... | collective-permute-start | bytes 24584 | tf_op jit(solution)/shard_map/ppermute | solution.py:31
  42.4 1.2 %collective-permute-start.10 = (f32[4,128]{1,0:T(4,128)S(1)}, f32[4,128]{1,0:T(4,128)S(1)}, u32[]{:S(2)}, u32[]{:S(2)}) collective-permute-start(f32[4,128]{1,0:T(4,128)S(1)} %pad_maximum_fusion.1), channel_id=1, source_target_pairs={{0,32},{32,0},{64,96},{96,64},{128,160},{160,128},{192,224},{224,1... | collective-permute-start | bytes 6152 | tf_op jit(solution)/shard_map/ppermute | solution.py:31
  46.8 4.8 %collective-permute-start.15 = (f32[4,128]{1,0:T(4,128)S(1)}, f32[4,128]{1,0:T(4,128)S(1)}, u32[]{:S(2)}, u32[]{:S(2)}) collective-permute-start(f32[4,128]{1,0:T(4,128)S(1)} %maximum_maximum_fusion.1), channel_id=1, source_target_pairs={{0,1},{32,33},{64,65},{96,97},{128,129},{160,161},{192,193},{224,2... | collective-permute-start | bytes 6152 | tf_op jit(solution)/shard_map/ppermute | solution.py:31
  47.0 5.1 %collective-permute-start.16 = (f32[4,128]{1,0:T(4,128)S(1)}, f32[4,128]{1,0:T(4,128)S(1)}, u32[]{:S(2)}, u32[]{:S(2)}) collective-permute-start(f32[4,128]{1,0:T(4,128)S(1)} %maximum_maximum_fusion.1), channel_id=1, source_target_pairs={{0,2},{32,34},{64,66},{96,98},{128,130},{160,162},{192,194},{224,2... | collective-permute-start | bytes 6152 | tf_op jit(solution)/shard_map/ppermute | solution.py:31
  48.4 4.8 %collective-permute-start.17 = (f32[4,128]{1,0:T(4,128)S(1)}, f32[4,128]{1,0:T(4,128)S(1)}, u32[]{:S(2)}, u32[]{:S(2)}) collective-permute-start(f32[4,128]{1,0:T(4,128)S(1)} %maximum_maximum_fusion.1), channel_id=1, source_target_pairs={{0,3},{32,35},{64,67},{96,99},{128,131},{160,163},{192,195},{224,2... | collective-permute-start | bytes 6152 | tf_op jit(solution)/shard_map/ppermute | solution.py:31
  53.2 10.4 %collective-permute-start.18 = (f32[1,128]{1,0:T(1,128)S(1)}, f32[1,128]{1,0:T(1,128)S(1)}, u32[]{:S(2)}, u32[]{:S(2)}) collective-permute-start(f32[1,128]{1,0:T(1,128)S(1)} %get-tuple-element.40), channel_id=1, source_target_pairs={{0,208},{32,240},{64,0},{96,32},{128,64},{160,96},{192,128},{224,1... | collective-permute-start | bytes 1544 | tf_op jit(solution)/shard_map/ppermute | solution.py:31
  55.5 8.1 %collective-permute-start.19 = (f32[1,128]{1,0:T(1,128)S(1)}, f32[1,128]{1,0:T(1,128)S(1)}, u32[]{:S(2)}, u32[]{:S(2)}) collective-permute-start(f32[1,128]{1,0:T(1,128)S(1)} %get-tuple-element.42), channel_id=1, source_target_pairs={{0,64},{32,96},{64,128},{96,160},{128,192},{160,224},{192,16},{224... | collective-permute-start | bytes 1544 | tf_op jit(solution)/shard_map/ppermute | solution.py:31
  55.5 8.1 %collective-permute-start.20 = (f32[1,128]{1,0:T(1,128)S(1)}, f32[1,128]{1,0:T(1,128)S(1)}, u32[]{:S(2)}, u32[]{:S(2)}) collective-permute-start(f32[1,128]{1,0:T(1,128)S(1)} %get-tuple-element.41), channel_id=1, source_target_pairs={{0,128},{32,176},{64,192},{96,240},{128,16},{160,32},{192,80},{224... | collective-permute-start | bytes 1544 | tf_op jit(solution)/shard_map/ppermute | solution.py:31
  59.0 7.6 %collective-permute-start.14 = (f32[1,2048]{1,0:T(1,128)S(1)}, f32[1,2048]{1,0:T(1,128)S(1)}, u32[]{:S(2)}, u32[]{:S(2)}) collective-permute-start(f32[1,2048]{1,0:T(1,128)S(1)} %maximum_maximum_fusion), channel_id=1, source_target_pairs={{0,16},{32,48},{64,80},{96,112},{128,144},{160,176},{192,208},{224... | collective-permute-start | bytes 24584 | tf_op jit(solution)/shard_map/ppermute | solution.py:31

commit v3 on v2

--- a/solution.py
+++ b/solution.py
@@ -10,6 +10,7 @@
 AXES = ("grp", "cut", "st")
 NX, NY, NZ, NC = 4, 4, 8, 2
 LANES = 128
+PACK_FLOPS = 10**10
 
 
 def position(x, y, z, c):
@@ -17,18 +18,18 @@
     return (((z_lo * NC + c % NC) * 8) + z_hi * NX + x % NX) * NY + y % NY
 
 
-def routes(move):
+def routes(move, cores):
     pairs = []
     for x in range(NX):
         for y in range(NY):
             for z in range(NZ):
-                for c in range(NC):
+                for c in cores:
                     pairs.append((position(x, y, z, c), position(*move(x, y, z, c))))
     return pairs
 
 
-def send(block, move):
-    return lax.ppermute(block, AXES, routes(move))
+def send(block, move, cores=range(NC)):
+    return lax.ppermute(block, AXES, routes(move, cores))
 
 
 def over_core(x, y, z, c):
@@ -61,6 +62,34 @@
 
 def over_y(d):
     return lambda x, y, z, c: (x, y ^ d, z, c)
+
+
+def pack_body(y, coefficients, intercepts, own, quarter):
+    cuts, depth = coefficients.shape
+    run = quarter.shape[0]
+    rows = pl.ds(pl.multiple_of(y[0] * run, run), run)
+    own[:, :depth] = coefficients[...]
+    wide = jnp.broadcast_to(intercepts[...].astype(jnp.float32), (LANES, cuts)).T
+    own[:, depth:] = wide.astype(jnp.bfloat16)
+    quarter[...] = own[rows, :]
+
+
+def pack(y, coefficients, intercepts):
+    cuts, depth = coefficients.shape
+    whole = lambda shape: pl.BlockSpec(shape, lambda i, y: (0, 0))
+    shapes = [(cuts, depth + LANES), (cuts // NY, depth + LANES)]
+    return pl.pallas_call(
+        pack_body,
+        grid_spec=pltpu.PrefetchScalarGridSpec(
+            num_scalar_prefetch=1,
+            grid=(1,),
+            in_specs=[whole((cuts, depth)), whole((1, cuts))],
+            out_specs=[whole(shape) for shape in shapes],
+        ),
+        out_shape=[jax.ShapeDtypeStruct(shape, jnp.bfloat16) for shape in shapes],
+        compiler_params=pltpu.CompilerParams(vmem_limit_bytes=24 << 20),
+        cost_estimate=pl.CostEstimate(flops=PACK_FLOPS, bytes_accessed=4 * cuts * depth, transcendentals=0),
+    )(y, coefficients, intercepts[None, :])
 
 
 def score_body(tile, tiles, count, spots, y, old, prev, states, *refs):
@@ -131,13 +160,12 @@
     old = old_values[None, :]
     cuts = coefficients.shape[0]
     run = cuts // NY
-    spread = jnp.broadcast_to(intercepts[:, None], (cuts, LANES))
-    own = jnp.concatenate([coefficients, spread], axis=1)
     pair = ((0, 0, cuts, 0, None), (1, 0, cuts, cuts, None))
-
-    y = lax.axis_index("st")
-    quarter = lax.dynamic_slice_in_dim(own, y * run, run, 0)
-    y = y[None]
+    runs = tuple((b, k * run, run, b * cuts, k) for b in range(2) for k in range(NY))
+    y = lax.axis_index("st")[None]
+    core = lax.axis_index("grp") % NC
+
+    own, quarter = pack(y, coefficients, intercepts)
     part = send(quarter, two_out)
     lower = send(own, up)
     upper = send(own, down)
@@ -146,24 +174,40 @@
     top, own_mine, own_other = score(pair, [own, peer], y, old, old, states)
     lower, upper, top = lax.optimization_barrier((lower, upper, top))
     two = jnp.concatenate(parts, axis=0)
-    runs = tuple((b, k * run, run, b * cuts, k) for b in range(2) for k in range(NY))
     top, lower_mine, lower_other = score(pair, [lower, send(lower, over_core)], y, old, top, states)
     top, upper_mine, upper_other = score(pair, [upper, send(upper, over_core)], y, old, top, states)
     top, two_mine, two_other = score(runs, [two, send(two, over_core)], y, old, top, states)
 
-    mine = jnp.concatenate([own_mine, lower_mine, upper_mine, two_mine], axis=0)
-    other = jnp.concatenate([own_other, lower_other, upper_other, two_other], axis=0)
-    swapped = send(other, over_core)
-    for_x = [send(top, over_x(d)) for d in (1, 2, 3)]
-    swapped, *for_x = lax.optimization_barrier((swapped, *for_x))
-    lifts = jnp.maximum(mine, swapped)
-    for_y = [send(lifts, over_y(d)) for d in (1, 2, 3)]
-    top = functools.reduce(jnp.maximum, for_x, top)
-    new_values = jnp.maximum(top, send(top, far))
+    mine = jnp.concatenate([own_mine, lower_mine, upper_mine, two_mine], axis=1)
+    other = jnp.concatenate([own_other, lower_other, upper_other, two_other], axis=1)
+    swapped = send(jnp.concatenate([top, mine, other], axis=1), over_core)
+    count, lanes = top.shape[1], mine.shape[1]
+    tops = jnp.concatenate([top, swapped[:, :count]], axis=1)
+    lifts = jnp.concatenate(
+        [
+            jnp.maximum(mine, swapped[:, count + lanes :]),
+            jnp.maximum(other, swapped[:, count : count + lanes]),
+        ],
+        axis=0,
+    )
+    for_x = [send(tops, over_x(d), (0,)) for d in (1, 2, 3)]
+    for_y = [send(lifts, over_y(d), (1,)) for d in (1, 2, 3)]
+    tops = functools.reduce(jnp.maximum, for_x, tops)
     lifts = functools.reduce(jnp.maximum, for_y, lifts)
-    back = [send(lifts[1:2], down), send(lifts[2:3], up), send(lifts[3:4], two_back)]
-    cut_gaps = functools.reduce(jnp.maximum, back, lifts[0:1])
-    return new_values[0], cut_gaps[0]
+    split = [lifts[:, k * cuts : (k + 1) * cuts] for k in range(4)]
+    back = [
+        send(split[1], down, (1,)),
+        send(split[2], up, (1,)),
+        send(split[3][:1], lambda x, y, z, c: (x, y, z - 2, c), (1,)),
+        send(split[3][1:], lambda x, y, z, c: (x, y, z + 2, c), (1,)),
+    ]
+    tops = jnp.maximum(tops, send(tops, far, (0,)))
+    gaps = jnp.maximum(jnp.maximum(back[0], back[1]), jnp.concatenate(back[2:], axis=0))
+    gaps = jnp.maximum(gaps, split[0])
+    swapped = send(jnp.concatenate([tops[:, count:], gaps[1:]], axis=1), over_core)
+    new_values = jnp.where(core == 0, tops[0, :count], swapped[0, :count])
+    cut_gaps = jnp.where(core == 0, swapped[0, count:], gaps[0])
+    return new_values, cut_gaps
 
 
 def solution(mesh):

time: 67.5 us -> 71.1 us (1.053)
  the two profiles are of different devices: /device:TPU:32 before, /device:TPU:37 now
where the time goes in v3:
time: 71.1 us; the launch traced here: 70.7 us
  starting transfers between devices  42.6 us (60%)
  waiting for transfers between devices  12.6 us (18%)
  Pallas kernels  11.5 us (16%)
  local copies, waits for them, and re-layouts  1.85 us (3%)
  other arithmetic  1.25 us (2%)
  between operations  1.02 us (1%)
    ppermute x23, starting transfers between devices, send(): return lax.ppermute(block, AXES, routes(move, cores))  42.6 us
    ppermute x23, waiting for transfers between devices, send(): return lax.ppermute(block, AXES, routes(move, cores))  12.6 us
    pallas_call x4, Pallas kernels, score(): pl.pallas_call(functools.partial(score_body, tile, tiles, len(blocks), sp...  11.4 us
    unnamed x19, local copies, waits for them, and re-layouts  1.81 us
  transfers between devices with their start and end apart: 23, of which 8 were waited for; matrix products, arithmetic and copies ran while one was open for 0% of the time, Pallas kernels for 12%

profile of v3, /device:TPU:37, one launch (start us, length us, event | category | flops | bytes accessed | tf_op | source)
XLA Modules:
  0.0 70.7 jit_solution(4030176869529919820)
XLA Ops:
  0.6 1.0 %copy-done.2 = bf16[128,2048]{1,0:T(8,128)(2,1)S(1)} copy-done((bf16[128,2048]{1,0:T(8,128)(2,1)S(1)}, bf16[128,2048]{1,0:T(8,128)(2,1)}, u32[]{:S(2)}) %copy-start.2) | copy-done | bytes 524312
  1.7 0.7 copy-done.3
  2.3 0.1 shard_map.59
  2.5 3.1 %collective-permute-start.5 = (bf16[32,2176]{1,0:T(8,128)(2,1)S(1)}, bf16[32,2176]{1,0:T(8,128)(2,1)S(1)}, u32[]{:S(2)}, u32[]{:S(2)}) collective-permute-start(bf16[32,2176]{1,0:T(8,128)(2,1)S(1)} %get-tuple-element.26), channel_id=1, source_target_pairs={{0,144},{32,160},{64,208},{96,224},{128,0},{160,48},{192,64},{224,... | collective-permute-start | bytes 417800 | tf_op jit(solution)/shard_map/ppermute | solution.py:32
  5.5 3.1 %collective-permute-start.2 = (bf16[128,2176]{1,0:T(8,128)(2,1)S(1)}, bf16[128,2176]{1,0:T(8,128)(2,1)S(1)}, u32[]{:S(2)}, u32[]{:S(2)}) collective-permute-start(bf16[128,2176]{1,0:T(8,128)(2,1)S(1)} %get-tuple-element.19.refs_0_), channel_id=1, source_target_pairs={{0,32},{32,0},{64,96},{96,64},{128,160},{160,128},{192,224},{224,1... | collective-permute-start | bytes 1671176 | tf_op jit(solution)/shard_map/ppermute | solution.py:32
  8.6 0.0 collective-permute-start
  8.6 1.5 %collective-permute-start.1 = (bf16[128,2176]{1,0:T(8,128)(2,1)S(1)}, bf16[128,2176]{1,0:T(8,128)(2,1)S(1)}, u32[]{:S(2)}, u32[]{:S(2)}) collective-permute-start(bf16[128,2176]{1,0:T(8,128)(2,1)S(1)} %get-tuple-element.19.refs_0_), channel_id=1, source_target_pairs={{0,208},{32,240},{64,0},{96,32},{128,64},{160,96},{192,128},{224,1... | collective-permute-start | bytes 1671176 | tf_op jit(solution)/shard_map/ppermute | solution.py:32
  10.1 1.6 %collective-permute-done.5 = bf16[32,2176]{1,0:T(8,128)(2,1)S(1)} collective-permute-done((bf16[32,2176]{1,0:T(8,128)(2,1)S(1)}, bf16[32,2176]{1,0:T(8,128)(2,1)S(1)}, u32[]{:S(2)}, u32[]{:S(2)}) %collective-permute-start.5) | collective-permute-done | bytes 139296 | tf_op jit(solution)/shard_map/ppermute | solution.py:32
  11.7 1.3 %collective-permute-start.6 = (bf16[32,2176]{1,0:T(8,128)(2,1)S(1)}, bf16[32,2176]{1,0:T(8,128)(2,1)S(1)}, u32[]{:S(2)}, u32[]{:S(2)}) collective-permute-start(bf16[32,2176]{1,0:T(8,128)(2,1)S(1)} %collective-permute-done.5), channel_id=1, source_target_pairs={{0,1},{32,33},{64,65},{96,97},{128,129},{160,161},{192,193},{224,2... | collective-permute-start | bytes 417800 | tf_op jit(solution)/shard_map/ppermute | solution.py:32
  13.0 2.7 %collective-permute-start.7 = (bf16[32,2176]{1,0:T(8,128)(2,1)S(1)}, bf16[32,2176]{1,0:T(8,128)(2,1)S(1)}, u32[]{:S(2)}, u32[]{:S(2)}) collective-permute-start(bf16[32,2176]{1,0:T(8,128)(2,1)S(1)} %collective-permute-done.5), channel_id=1, source_target_pairs={{0,2},{32,34},{64,66},{96,98},{128,130},{160,162},{192,194},{224,2... | collective-permute-start | bytes 417800 | tf_op jit(solution)/shard_map/ppermute | solution.py:32
  15.7 1.4 %collective-permute-done.6 = bf16[32,2176]{1,0:T(8,128)(2,1)S(1)} collective-permute-done((bf16[32,2176]{1,0:T(8,128)(2,1)S(1)}, bf16[32,2176]{1,0:T(8,128)(2,1)S(1)}, u32[]{:S(2)}, u32[]{:S(2)}) %collective-permute-start.6) | collective-permute-done | bytes 139296 | tf_op jit(solution)/shard_map/ppermute | solution.py:32
  17.1 2.7 %collective-permute-start.8 = (bf16[32,2176]{1,0:T(8,128)(2,1)S(1)}, bf16[32,2176]{1,0:T(8,128)(2,1)S(1)}, u32[]{:S(2)}, u32[]{:S(2)}) collective-permute-start(bf16[32,2176]{1,0:T(8,128)(2,1)S(1)} %collective-permute-done.5), channel_id=1, source_target_pairs={{0,3},{32,35},{64,67},{96,99},{128,131},{160,163},{192,195},{224,2... | collective-permute-start | bytes 417800 | tf_op jit(solution)/shard_map/ppermute | solution.py:32
  19.9 0.0 collective-permute-done.2.refs_1_
  19.9 2.8 %shard_map.60 = (f32[1,2048]{1,0:T(1,128)S(1)}, f32[1,128]{1,0:T(1,128)S(1)}, f32[1,128]{1,0:T(1,128)S(1)}) custom-call(s32[1]{0:T(128)} %bitcast.y, f32[1,2048]{1,0:T(1,128)S(1)} %bitcast.6, f32[1,2048]{1,0:T(1,128)S(1)} %bitcast.7, bf16[2048,2048]{1,0:T(8,128)(2,1)S(1)} %copy-done, bf16[128,2176]{1,0:T(8,128)(2,1)S(1)} %get-tuple-element.19.refs_0_, ...), custom_call_target="tpu_custom_call" | custom-call | flops 2147483648 | bytes 9437184 | tf_op jit(solution)/shard_map/pallas_call | solution.py:137
  22.7 1.0 %collective-permute-done.refs_0_ = bf16[128,2176]{1,0:T(8,128)(2,1)S(1)} collective-permute-done((bf16[128,2176]{1,0:T(8,128)(2,1)S(1)}, bf16[128,2176]{1,0:T(8,128)(2,1)S(1)}, u32[]{:S(2)}, u32[]{:S(2)}) %collective-permute-start) | collective-permute-done | bytes 557088 | tf_op jit(solution)/shard_map/ppermute | solution.py:32
  23.8 0.0 collective-permute-done.1.refs_0_
  23.8 0.4 collective-permute-start.3
  24.2 0.2 collective-permute-start.4
  24.4 1.3 %collective-permute-done.8 = bf16[32,2176]{1,0:T(8,128)(2,1)S(1)} collective-permute-done((bf16[32,2176]{1,0:T(8,128)(2,1)S(1)}, bf16[32,2176]{1,0:T(8,128)(2,1)S(1)}, u32[]{:S(2)}, u32[]{:S(2)}) %collective-permute-start.8) | collective-permute-done | bytes 139296 | tf_op jit(solution)/shard_map/ppermute | solution.py:32
  25.7 0.6 collective-permute-start.9
  26.3 2.8 %shard_map.61 = (f32[1,2048]{1,0:T(1,128)S(1)}, f32[1,128]{1,0:T(1,128)S(1)}, f32[1,128]{1,0:T(1,128)S(1)}) custom-call(s32[1]{0:T(128)} %bitcast.y, f32[1,2048]{1,0:T(1,128)S(1)} %bitcast.8, f32[1,2048]{1,0:T(1,128)S(1)} %get-tuple-element.21.prev, bf16[2048,2048]{1,0:T(8,128)(2,1)S(1)} %copy-done, bf16[128,2176]{1,0:T(8,128)(2,1)S(1)} %collective-permute-done.refs_0_, ...), custom_call_target="tpu_custom_call" | custom-call | flops 2147483648 | bytes 9437184 | tf_op jit(solution)/shard_map/pallas_call | solution.py:137
  29.1 2.9 %shard_map.62 = (f32[1,2048]{1,0:T(1,128)S(1)}, f32[1,128]{1,0:T(1,128)S(1)}, f32[1,128]{1,0:T(1,128)S(1)}) custom-call(s32[1]{0:T(128)} %bitcast.y, f32[1,2048]{1,0:T(1,128)S(1)} %bitcast.9, f32[1,2048]{1,0:T(1,128)S(1)} %get-tuple-element.23.prev, bf16[2048,2048]{1,0:T(8,128)(2,1)S(1)} %copy-done, bf16[128,2176]{1,0:T(8,128)(2,1)S(1)} %collective-permute-done.1.refs_0_, ...), custom_call_target="tpu_custom_call" | custom-call | flops 2147483648 | bytes 9437184 | tf_op jit(solution)/shard_map/pallas_call | solution.py:137
  32.0 2.9 %shard_map.63 = (f32[1,2048]{1,0:T(1,128)S(1)}, f32[1,128]{1,0:T(1,128)S(1)}, f32[1,128]{1,0:T(1,128)S(1)}) custom-call(s32[1]{0:T(128)} %bitcast.y, f32[1,2048]{1,0:T(1,128)S(1)} %bitcast.10, f32[1,2048]{1,0:T(1,128)S(1)} %get-tuple-element.25.prev, bf16[2048,2048]{1,0:T(8,128)(2,1)S(1)} %copy-done, ...), custom_call_target="tpu_custom_call" | custom-call | flops 2147483648 | bytes 9437184 | tf_op jit(solution)/shard_map/pallas_call | solution.py:137
  35.0 0.1 collective-permute-start.10
  35.1 1.1 %collective-permute-done.10 = f32[1,3072]{1,0:T(1,128)S(1)} collective-permute-done((f32[1,3072]{1,0:T(1,128)S(1)}, f32[1,3072]{1,0:T(1,128)S(1)}, u32[]{:S(2)}, u32[]{:S(2)}) %collective-permute-start.10) | collective-permute-done | bytes 12320 | tf_op jit(solution)/shard_map/ppermute | solution.py:32
  36.2 2.8 %collective-permute-start.15 = (f32[2,512]{1,0:T(2,128)S(1)}, f32[2,512]{1,0:T(2,128)S(1)}, u32[]{:S(2)}, u32[]{:S(2)}) collective-permute-start(f32[2,512]{1,0:T(2,128)S(1)} %pad_maximum_fusion.2), channel_id=1, source_target_pairs={{32,33},{96,97},{160,161},{224,225},{48,49},{112,113},{176,177},{2... | collective-permute-start | bytes 12296 | tf_op jit(solution)/shard_map/ppermute | solution.py:32
  39.0 4.5 %collective-permute-start.16 = (f32[2,512]{1,0:T(2,128)S(1)}, f32[2,512]{1,0:T(2,128)S(1)}, u32[]{:S(2)}, u32[]{:S(2)}) collective-permute-start(f32[2,512]{1,0:T(2,128)S(1)} %pad_maximum_fusion.2), channel_id=1, source_target_pairs={{32,34},{96,98},{160,162},{224,226},{48,50},{112,114},{176,178},{2... | collective-permute-start | bytes 12296 | tf_op jit(solution)/shard_map/ppermute | solution.py:32
  43.6 2.3 %collective-permute-start.17 = (f32[2,512]{1,0:T(2,128)S(1)}, f32[2,512]{1,0:T(2,128)S(1)}, u32[]{:S(2)}, u32[]{:S(2)}) collective-permute-start(f32[2,512]{1,0:T(2,128)S(1)} %pad_maximum_fusion.2), channel_id=1, source_target_pairs={{32,35},{96,99},{160,163},{224,227},{48,51},{112,115},{176,179},{2... | collective-permute-start | bytes 12296 | tf_op jit(solution)/shard_map/ppermute | solution.py:32
  45.9 0.7 collective-permute-start.11
  46.6 0.7 collective-permute-start.12
  47.2 0.7 collective-permute-start.13
  47.9 0.0 collective-permute-done.16
  47.9 1.2 %collective-permute-done.17 = f32[2,512]{1,0:T(2,128)S(1)} collective-permute-done((f32[2,512]{1,0:T(2,128)S(1)}, f32[2,512]{1,0:T(2,128)S(1)}, u32[]{:S(2)}, u32[]{:S(2)}) %collective-permute-start.17) | collective-permute-done | bytes 4128 | tf_op jit(solution)/shard_map/ppermute | solution.py:32
  49.2 3.3 %collective-permute-start.18 = (f32[2,128]{1,0:T(2,128)S(1)}, f32[2,128]{1,0:T(2,128)S(1)}, u32[]{:S(2)}, u32[]{:S(2)}) collective-permute-start(f32[2,128]{1,0:T(2,128)S(1)} %get-tuple-element.39), channel_id=1, source_target_pairs={{32,240},{96,32},{160,96},{224,160},{48,224},{112,48},{176,112},{2... | collective-permute-start | bytes 3080 | tf_op jit(solution)/shard_map/ppermute | solution.py:32
  52.4 2.0 %collective-permute-start.19 = (f32[2,128]{1,0:T(2,128)S(1)}, f32[2,128]{1,0:T(2,128)S(1)}, u32[]{:S(2)}, u32[]{:S(2)}) collective-permute-start(f32[2,128]{1,0:T(2,128)S(1)} %get-tuple-element.38), channel_id=1, source_target_pairs={{32,96},{96,160},{160,224},{224,48},{48,112},{112,176},{176,240},{... | collective-permute-start | bytes 3080 | tf_op jit(solution)/shard_map/ppermute | solution.py:32
  54.5 7.4 %collective-permute-start.20 = (f32[1,128]{1,0:T(1,128)S(1)}, f32[1,128]{1,0:T(1,128)S(1)}, u32[]{:S(2)}, u32[]{:S(2)}) collective-permute-start(f32[1,128]{1,0:T(1,128)S(1)} %get-tuple-element.40), channel_id=1, source_target_pairs={{32,176},{96,240},{160,32},{224,96},{48,160},{112,224},{176,48},{2... | collective-permute-start | bytes 1544 | tf_op jit(solution)/shard_map/ppermute | solution.py:32
  61.8 0.0 collective-permute-done.12
  61.9 1.9 %collective-permute-start.21 = (f32[1,128]{1,0:T(1,128)S(1)}, f32[1,128]{1,0:T(1,128)S(1)}, u32[]{:S(2)}, u32[]{:S(2)}) collective-permute-start(f32[1,128]{1,0:T(1,128)S(1)} %get-tuple-element.41), channel_id=1, source_target_pairs={{32,160},{96,224},{160,48},{224,112},{48,176},{112,240},{176,32},{... | collective-permute-start | bytes 1544 | tf_op jit(solution)/shard_map/ppermute | solution.py:32
  63.8 0.0 collective-permute-done.13
  63.8 0.7 collective-permute-start.14
  64.5 0.0 collective-permute-done.20
  64.5 3.7 %collective-permute-done.21 = f32[1,128]{1,0:T(1,128)S(1)} collective-permute-done((f32[1,128]{1,0:T(1,128)S(1)}, f32[1,128]{1,0:T(1,128)S(1)}, u32[]{:S(2)}, u32[]{:S(2)}) %collective-permute-start.21) | collective-permute-done | bytes 544 | tf_op jit(solution)/shard_map/ppermute | solution.py:32
  68.2 0.0 collective-permute-done.18
  68.2 0.0 collective-permute-done.19
  68.3 0.1 collective-permute-start.22
  68.5 1.1 %collective-permute-done.22 = f32[1,2176]{1,0:T(1,128)S(1)} collective-permute-done((f32[1,2176]{1,0:T(1,128)S(1)}, f32[1,2176]{1,0:T(1,128)S(1)}, u32[]{:S(2)}, u32[]{:S(2)}) %collective-permute-start.22) | collective-permute-done | bytes 8736 | tf_op jit(solution)/shard_map/ppermute | solution.py:32
  69.6 0.5 fusion
  70.1 0.6 broadcast_select_fusion
  (39 shorter events, 0.3 us)
Async XLA Ops:
  0.6 1.0 %copy-start.2 = (bf16[128,2048]{1,0:T(8,128)(2,1)S(1)}, bf16[128,2048]{1,0:T(8,128)(2,1)}, u32[]{:S(2)}) copy-start(bf16[128,2048]{1,0:T(8,128)(2,1)} %coefficients.1) | copy-start | bytes 1572868
  1.7 0.7 copy-start.3
  2.3 17.5 %copy-start = (bf16[2048,2048]{1,0:T(8,128)(2,1)S(1)}, bf16[2048,2048]{1,0:T(8,128)(2,1)}, u32[]{:S(2)}) copy-start(bf16[2048,2048]{1,0:T(8,128)(2,1)} %states.7) | copy-start | bytes 25165828
  2.3 17.5 %copy-start.1 = (f32[2048]{0:T(1024)S(1)}, f32[2048]{0:T(1024)}, u32[]{:S(2)}) copy-start(f32[2048]{0:T(1024)} %param.7) | copy-start | bytes 24580
  2.5 9.2 %collective-permute-start.5 = (bf16[32,2176]{1,0:T(8,128)(2,1)S(1)}, bf16[32,2176]{1,0:T(8,128)(2,1)S(1)}, u32[]{:S(2)}, u32[]{:S(2)}) collective-permute-start(bf16[32,2176]{1,0:T(8,128)(2,1)S(1)} %get-tuple-element.26), channel_id=1, source_target_pairs={{0,144},{32,160},{64,208},{96,224},{128,0},{160,48},{192,64},{224,... | collective-permute-start | bytes 417800 | tf_op jit(solution)/shard_map/ppermute | solution.py:32
  5.5 14.3 %collective-permute-start.2 = (bf16[128,2176]{1,0:T(8,128)(2,1)S(1)}, bf16[128,2176]{1,0:T(8,128)(2,1)S(1)}, u32[]{:S(2)}, u32[]{:S(2)}) collective-permute-start(bf16[128,2176]{1,0:T(8,128)(2,1)S(1)} %get-tuple-element.19.refs_0_), channel_id=1, source_target_pairs={{0,32},{32,0},{64,96},{96,64},{128,160},{160,128},{192,224},{224,1... | collective-permute-start | bytes 1671176 | tf_op jit(solution)/shard_map/ppermute | solution.py:32
  8.6 15.2 %collective-permute-start = (bf16[128,2176]{1,0:T(8,128)(2,1)S(1)}, bf16[128,2176]{1,0:T(8,128)(2,1)S(1)}, u32[]{:S(2)}, u32[]{:S(2)}) collective-permute-start(bf16[128,2176]{1,0:T(8,128)(2,1)S(1)} %get-tuple-element.19.refs_0_), channel_id=1, source_target_pairs={{0,64},{32,96},{64,128},{96,160},{128,192},{160,224},{192,16},{224... | collective-permute-start | bytes 1671176 | tf_op jit(solution)/shard_map/ppermute | solution.py:32
  8.6 15.2 %collective-permute-start.1 = (bf16[128,2176]{1,0:T(8,128)(2,1)S(1)}, bf16[128,2176]{1,0:T(8,128)(2,1)S(1)}, u32[]{:S(2)}, u32[]{:S(2)}) collective-permute-start(bf16[128,2176]{1,0:T(8,128)(2,1)S(1)} %get-tuple-element.19.refs_0_), channel_id=1, source_target_pairs={{0,208},{32,240},{64,0},{96,32},{128,64},{160,96},{192,128},{224,1... | collective-permute-start | bytes 1671176 | tf_op jit(solution)/shard_map/ppermute | solution.py:32
  11.7 5.4 %collective-permute-start.6 = (bf16[32,2176]{1,0:T(8,128)(2,1)S(1)}, bf16[32,2176]{1,0:T(8,128)(2,1)S(1)}, u32[]{:S(2)}, u32[]{:S(2)}) collective-permute-start(bf16[32,2176]{1,0:T(8,128)(2,1)S(1)} %collective-permute-done.5), channel_id=1, source_target_pairs={{0,1},{32,33},{64,65},{96,97},{128,129},{160,161},{192,193},{224,2... | collective-permute-start | bytes 417800 | tf_op jit(solution)/shard_map/ppermute | solution.py:32
  13.0 11.3 %collective-permute-start.7 = (bf16[32,2176]{1,0:T(8,128)(2,1)S(1)}, bf16[32,2176]{1,0:T(8,128)(2,1)S(1)}, u32[]{:S(2)}, u32[]{:S(2)}) collective-permute-start(bf16[32,2176]{1,0:T(8,128)(2,1)S(1)} %collective-permute-done.5), channel_id=1, source_target_pairs={{0,2},{32,34},{64,66},{96,98},{128,130},{160,162},{192,194},{224,2... | collective-permute-start | bytes 417800 | tf_op jit(solution)/shard_map/ppermute | solution.py:32
  17.1 8.6 %collective-permute-start.8 = (bf16[32,2176]{1,0:T(8,128)(2,1)S(1)}, bf16[32,2176]{1,0:T(8,128)(2,1)S(1)}, u32[]{:S(2)}, u32[]{:S(2)}) collective-permute-start(bf16[32,2176]{1,0:T(8,128)(2,1)S(1)} %collective-permute-done.5), channel_id=1, source_target_pairs={{0,3},{32,35},{64,67},{96,99},{128,131},{160,163},{192,195},{224,2... | collective-permute-start | bytes 417800 | tf_op jit(solution)/shard_map/ppermute | solution.py:32
  23.8 2.5 %collective-permute-start.3 = (bf16[128,2176]{1,0:T(8,128)(2,1)S(1)}, bf16[128,2176]{1,0:T(8,128)(2,1)S(1)}, u32[]{:S(2)}, u32[]{:S(2)}) collective-permute-start(bf16[128,2176]{1,0:T(8,128)(2,1)S(1)} %collective-permute-done.refs_0_), channel_id=1, source_target_pairs={{0,32},{32,0},{64,96},{96,64},{128,160},{160,128},{192,224},{224,1... | collective-permute-start | bytes 1671176 | tf_op jit(solution)/shard_map/ppermute | solution.py:32
  24.2 4.9 %collective-permute-start.4 = (bf16[128,2176]{1,0:T(8,128)(2,1)S(1)}, bf16[128,2176]{1,0:T(8,128)(2,1)S(1)}, u32[]{:S(2)}, u32[]{:S(2)}) collective-permute-start(bf16[128,2176]{1,0:T(8,128)(2,1)S(1)} %collective-permute-done.1.refs_0_), channel_id=1, source_target_pairs={{0,32},{32,0},{64,96},{96,64},{128,160},{160,128},{192,224},{224,1... | collective-permute-start | bytes 1671176 | tf_op jit(solution)/shard_map/ppermute | solution.py:32
  25.7 6.3 %collective-permute-start.9 = (bf16[128,2176]{1,0:T(8,128)(2,1)S(1)}, bf16[128,2176]{1,0:T(8,128)(2,1)S(1)}, u32[]{:S(2)}, u32[]{:S(2)}) collective-permute-start(bf16[128,2176]{1,0:T(8,128)(2,1)S(1)} %constant_dynamic-update-slice_fusion.refs_0_), channel_id=1, source_target_pairs={{0,32},{32,0},{64,96},{96,64},{128,160},{160,128},{192,224},{224,1... | collective-permute-start | bytes 1671176 | tf_op jit(solution)/shard_map/ppermute | solution.py:32
  35.0 1.3 %collective-permute-start.10 = (f32[1,3072]{1,0:T(1,128)S(1)}, f32[1,3072]{1,0:T(1,128)S(1)}, u32[]{:S(2)}, u32[]{:S(2)}) collective-permute-start(f32[1,3072]{1,0:T(1,128)S(1)} %constant_dynamic-update-slice_fusion.4), channel_id=1, source_target_pairs={{0,32},{32,0},{64,96},{96,64},{128,160},{160,128},{192,224},{224,1... | collective-permute-start | bytes 36872 | tf_op jit(solution)/shard_map/ppermute | solution.py:32
  36.2 11.0 %collective-permute-start.15 = (f32[2,512]{1,0:T(2,128)S(1)}, f32[2,512]{1,0:T(2,128)S(1)}, u32[]{:S(2)}, u32[]{:S(2)}) collective-permute-start(f32[2,512]{1,0:T(2,128)S(1)} %pad_maximum_fusion.2), channel_id=1, source_target_pairs={{32,33},{96,97},{160,161},{224,225},{48,49},{112,113},{176,177},{2... | collective-permute-start | bytes 12296 | tf_op jit(solution)/shard_map/ppermute | solution.py:32
  39.0 8.9 %collective-permute-start.16 = (f32[2,512]{1,0:T(2,128)S(1)}, f32[2,512]{1,0:T(2,128)S(1)}, u32[]{:S(2)}, u32[]{:S(2)}) collective-permute-start(f32[2,512]{1,0:T(2,128)S(1)} %pad_maximum_fusion.2), channel_id=1, source_target_pairs={{32,34},{96,98},{160,162},{224,226},{48,50},{112,114},{176,178},{2... | collective-permute-start | bytes 12296 | tf_op jit(solution)/shard_map/ppermute | solution.py:32
  43.6 5.6 %collective-permute-start.17 = (f32[2,512]{1,0:T(2,128)S(1)}, f32[2,512]{1,0:T(2,128)S(1)}, u32[]{:S(2)}, u32[]{:S(2)}) collective-permute-start(f32[2,512]{1,0:T(2,128)S(1)} %pad_maximum_fusion.2), channel_id=1, source_target_pairs={{32,35},{96,99},{160,163},{224,227},{48,51},{112,115},{176,179},{2... | collective-permute-start | bytes 12296 | tf_op jit(solution)/shard_map/ppermute | solution.py:32
  45.9 8.6 %collective-permute-start.11 = (f32[1,4096]{1,0:T(1,128)S(1)}, f32[1,4096]{1,0:T(1,128)S(1)}, u32[]{:S(2)}, u32[]{:S(2)}) collective-permute-start(f32[1,4096]{1,0:T(1,128)S(1)} %pad_maximum_fusion), channel_id=1, source_target_pairs={{0,4},{64,68},{128,132},{192,196},{16,20},{80,84},{144,148},{208,2... | collective-permute-start | bytes 49160 | tf_op jit(solution)/shard_map/ppermute | solution.py:32
  46.6 15.3 %collective-permute-start.12 = (f32[1,4096]{1,0:T(1,128)S(1)}, f32[1,4096]{1,0:T(1,128)S(1)}, u32[]{:S(2)}, u32[]{:S(2)}) collective-permute-start(f32[1,4096]{1,0:T(1,128)S(1)} %pad_maximum_fusion), channel_id=1, source_target_pairs={{0,8},{64,72},{128,136},{192,200},{16,24},{80,88},{144,152},{208,2... | collective-permute-start | bytes 49160 | tf_op jit(solution)/shard_map/ppermute | solution.py:32
  47.2 16.5 %collective-permute-start.13 = (f32[1,4096]{1,0:T(1,128)S(1)}, f32[1,4096]{1,0:T(1,128)S(1)}, u32[]{:S(2)}, u32[]{:S(2)}) collective-permute-start(f32[1,4096]{1,0:T(1,128)S(1)} %pad_maximum_fusion), channel_id=1, source_target_pairs={{0,12},{64,76},{128,140},{192,204},{16,28},{80,92},{144,156},{208,... | collective-permute-start | bytes 49160 | tf_op jit(solution)/shard_map/ppermute | solution.py:32
  49.2 19.1 %collective-permute-start.18 = (f32[2,128]{1,0:T(2,128)S(1)}, f32[2,128]{1,0:T(2,128)S(1)}, u32[]{:S(2)}, u32[]{:S(2)}) collective-permute-start(f32[2,128]{1,0:T(2,128)S(1)} %get-tuple-element.39), channel_id=1, source_target_pairs={{32,240},{96,32},{160,96},{224,160},{48,224},{112,48},{176,112},{2... | collective-permute-start | bytes 3080 | tf_op jit(solution)/shard_map/ppermute | solution.py:32
  52.4 15.8 %collective-permute-start.19 = (f32[2,128]{1,0:T(2,128)S(1)}, f32[2,128]{1,0:T(2,128)S(1)}, u32[]{:S(2)}, u32[]{:S(2)}) collective-permute-start(f32[2,128]{1,0:T(2,128)S(1)} %get-tuple-element.38), channel_id=1, source_target_pairs={{32,96},{96,160},{160,224},{224,48},{48,112},{112,176},{176,240},{... | collective-permute-start | bytes 3080 | tf_op jit(solution)/shard_map/ppermute | solution.py:32
  54.5 10.0 %collective-permute-start.20 = (f32[1,128]{1,0:T(1,128)S(1)}, f32[1,128]{1,0:T(1,128)S(1)}, u32[]{:S(2)}, u32[]{:S(2)}) collective-permute-start(f32[1,128]{1,0:T(1,128)S(1)} %get-tuple-element.40), channel_id=1, source_target_pairs={{32,176},{96,240},{160,32},{224,96},{48,160},{112,224},{176,48},{2... | collective-permute-start | bytes 1544 | tf_op jit(solution)/shard_map/ppermute | solution.py:32
  61.9 6.4 %collective-permute-start.21 = (f32[1,128]{1,0:T(1,128)S(1)}, f32[1,128]{1,0:T(1,128)S(1)}, u32[]{:S(2)}, u32[]{:S(2)}) collective-permute-start(f32[1,128]{1,0:T(1,128)S(1)} %get-tuple-element.41), channel_id=1, source_target_pairs={{32,160},{96,224},{160,48},{224,112},{48,176},{112,240},{176,32},{... | collective-permute-start | bytes 1544 | tf_op jit(solution)/shard_map/ppermute | solution.py:32
  63.8 4.4 %collective-permute-start.14 = (f32[1,4096]{1,0:T(1,128)S(1)}, f32[1,4096]{1,0:T(1,128)S(1)}, u32[]{:S(2)}, u32[]{:S(2)}) collective-permute-start(f32[1,4096]{1,0:T(1,128)S(1)} %maximum_maximum_fusion), channel_id=1, source_target_pairs={{0,16},{64,80},{128,144},{192,208},{16,0},{80,64},{144,128},{208,1... | collective-permute-start | bytes 49160 | tf_op jit(solution)/shard_map/ppermute | solution.py:32
  68.3 1.3 %collective-permute-start.22 = (f32[1,2176]{1,0:T(1,128)S(1)}, f32[1,2176]{1,0:T(1,128)S(1)}, u32[]{:S(2)}, u32[]{:S(2)}) collective-permute-start(f32[1,2176]{1,0:T(1,128)S(1)} %pad_maximum_fusion.1), channel_id=1, source_target_pairs={{0,32},{32,0},{64,96},{96,64},{128,160},{160,128},{192,224},{224,1... | collective-permute-start | bytes 26120 | tf_op jit(solution)/shard_map/ppermute | solution.py:32

commit v4 on v2

v4 whole, which is shorter than its diff:
```python
import functools

import jax
import jax.numpy as jnp
from jax import lax
from jax.experimental import pallas as pl
from jax.experimental.pallas import tpu as pltpu
from jax.sharding import PartitionSpec as P

AXES = ("grp", "cut", "st")
NX, NY, NZ, NC = 4, 4, 8, 2
LANES = 128
PACK_FLOPS = 10**10
PACK_VMEM = 24 << 20


def position(x, y, z, c):
    z_hi, z_lo = divmod(z % NZ, 4)
    return (((z_lo * NC + c % NC) * 8) + z_hi * NX + x % NX) * NY + y % NY


def routes(move):
    pairs = []
    for x in range(NX):
        for y in range(NY):
            for z in range(NZ):
                for c in range(NC):
                    pairs.append((position(x, y, z, c), position(*move(x, y, z, c))))
    return pairs


def send(block, move):
    return lax.ppermute(block, AXES, routes(move))


def over_core(x, y, z, c):
    return x, y, z, 1 - c


def toward(x, y, z, c):
    return x, y, z - 1 if c == 0 else z + 1, c


def against(x, y, z, c):
    return x, y, z + 1 if c == 0 else z - 1, c


def two_back(x, y, z, c):
    return x, y, z + 2 if c == 0 else z - 2, c


def far(x, y, z, c):
    return x, y, z + 4, c


def over_x(d):
    return lambda x, y, z, c: (x ^ d, y, z, c)


def over_y(d):
    return lambda x, y, z, c: (x, y ^ d, z, c)


def pack_body(coefficients, intercepts, own, slopes, row, arrived):
    depth = coefficients.shape[1]
    copies = [
        pltpu.make_async_copy(coefficients, slopes, arrived.at[0]),
        pltpu.make_async_copy(intercepts, row, arrived.at[1]),
    ]
    for copy in copies:
        copy.start()
    for copy in copies:
        copy.wait()
    own[:, :depth] = slopes[...]
    wide = jnp.broadcast_to(row[...].astype(jnp.float32), (LANES, row.shape[1])).T
    own[:, depth:] = wide.astype(jnp.bfloat16)


def pack(coefficients, intercepts):
    cuts, depth = coefficients.shape
    there = pl.BlockSpec(memory_space=pl.ANY)
    return pl.pallas_call(
        pack_body,
        in_specs=[there, there],
        out_specs=pl.BlockSpec(memory_space=pltpu.VMEM),
        out_shape=jax.ShapeDtypeStruct((cuts, depth + LANES), jnp.bfloat16),
        scratch_shapes=[
            pltpu.VMEM((cuts, depth), jnp.bfloat16),
            pltpu.VMEM((1, cuts), jnp.bfloat16),
            pltpu.SemaphoreType.DMA((2,)),
        ],
        compiler_params=pltpu.CompilerParams(vmem_limit_bytes=PACK_VMEM),
        cost_estimate=pl.CostEstimate(flops=PACK_FLOPS, bytes_accessed=4 * cuts * depth, transcendentals=0),
    )(coefficients, intercepts[None, :])


def score_body(tile, tiles, count, old, prev, states, *refs):
    blocks, (top, mine, other, slopes, best, offset) = refs[:count], refs[count:]
    depth = states.shape[1]
    half = mine.shape[1]
    step = pl.program_id(0)

    @pl.when(step == 0)
    def _():
        row = 0
        for block in blocks:
            rows = block.shape[0]
            slopes[row : row + rows, :] = block[:, :depth]
            offset[row : row + rows, :] = block[:, depth:].astype(jnp.float32)
            row += rows
        best[...] = jnp.full(best.shape, -jnp.inf, jnp.float32)

    scores = lax.dot_general(
        slopes[...], states[...], (((1,), (1,)), ((), ())), preferred_element_type=jnp.float32
    )
    lifted = scores - old[...]
    most = best[...]
    for lane in range(0, tile, LANES):
        most = jnp.maximum(most, lifted[:, lane : lane + LANES])
    best[...] = most
    wide = offset[...]
    valued = jnp.concatenate(
        [scores[:, lane : lane + LANES] + wide for lane in range(0, tile, LANES)], axis=1
    )
    top[...] = jnp.maximum(prev[...], jnp.max(valued, axis=0, keepdims=True))

    @pl.when(step == tiles - 1)
    def _():
        lift = jnp.max((best[...] + offset[...]).T, axis=0, keepdims=True)
        mine[...] = lift[:, :half]
        other[...] = lift[:, half:]


def score(blocks, old, prev, states, tile=1024):
    count, depth = states.shape
    cuts = sum(block.shape[0] for block in blocks)
    tiles = count // tile
    whole = lambda shape: pl.BlockSpec(shape, lambda i: (0, 0))
    along = pl.BlockSpec((1, tile), lambda i: (0, i))
    lift = jax.ShapeDtypeStruct((1, cuts // 2), jnp.float32)
    return pl.pallas_call(
        functools.partial(score_body, tile, tiles, len(blocks)),
        grid=(tiles,),
        in_specs=[along, along, pl.BlockSpec((tile, depth), lambda i: (i, 0))]
        + [whole(block.shape) for block in blocks],
        out_specs=[along, whole(lift.shape), whole(lift.shape)],
        out_shape=[jax.ShapeDtypeStruct((1, count), jnp.float32), lift, lift],
        scratch_shapes=[
            pltpu.VMEM((cuts, depth), jnp.bfloat16),
            pltpu.VMEM((cuts, LANES), jnp.float32),
            pltpu.VMEM((cuts, LANES), jnp.float32),
        ],
        compiler_params=pltpu.CompilerParams(vmem_limit_bytes=24 << 20),
        cost_estimate=pl.CostEstimate(
            flops=2 * cuts * depth * count, bytes_accessed=2 * (count + cuts) * depth, transcendentals=0
        ),
    )(old, prev, states, *blocks)


def body(coefficients, intercepts, states, old_values):
    old = old_values[None, :]
    fence = lax.optimization_barrier

    own = pack(coefficients, intercepts)
    near = send(own, toward)
    next_ = send(own, against)
    peer = send(own, over_core)
    top, own_mine, own_other = score([own, peer], old, old, states)
    near, next_, top = fence((near, next_, top))
    two = send(near, toward)
    top, near_mine, near_other = score([near, send(near, over_core)], old, top, states)
    top, next_mine, next_other = score([next_, send(next_, over_core)], old, top, states)

    mine = jnp.concatenate([own_mine, near_mine, next_mine], axis=0)
    other = jnp.concatenate([own_other, near_other, next_other], axis=0)
    lifts = jnp.maximum(mine, send(other, over_core))
    two, top, lifts = fence((two, top, lifts))
    back = [send(lifts[1:2], against), send(lifts[2:3], toward)]
    top, two_mine, two_other = score([two, send(two, over_core)], old, top, states)

    swapped = send(two_other, over_core)
    for_x = [send(top, over_x(d)) for d in (1, 2, 3)]
    held = functools.reduce(jnp.maximum, back, lifts[0:1])
    last = jnp.maximum(two_mine, swapped)
    lifts = jnp.concatenate([held, last], axis=0)
    for_y = [send(lifts, over_y(d)) for d in (1, 2, 3)]
    top = functools.reduce(jnp.maximum, for_x, top)
    lifts = functools.reduce(jnp.maximum, for_y, lifts)
    for_z = send(lifts[1:2], two_back)
    new_values = jnp.maximum(top, send(top, far))
    cut_gaps = jnp.maximum(lifts[0:1], for_z)
    return new_values[0], cut_gaps[0]


def solution(mesh):
    placed = (P(("grp", "cut"), None), P(("grp", "cut")), P(("grp", "st"), None), P(("grp", "st")))
    return jax.shard_map(
        body,
        mesh=mesh,
        in_specs=placed,
        out_specs=(P(("grp", "st")), P(("grp", "cut"))),
        check_vma=False,
    )
```

time: 67.5 us -> 62 us (0.919)
  the two profiles are of different devices: /device:TPU:32 before, /device:TPU:2 now
where the time goes in v4:
time: 62 us; the launch traced here: 61.9 us
  starting transfers between devices  25.6 us (41%)
  waiting for transfers between devices  21.1 us (34%)
  Pallas kernels  11.5 us (19%)
  local copies, waits for them, and re-layouts  1.71 us (3%)
  other arithmetic  1.19 us (2%)
  between operations  0.77 us (1%)
    ppermute x19, starting transfers between devices, send(): return lax.ppermute(block, AXES, routes(move))  25.6 us
    ppermute x19, waiting for transfers between devices, send(): return lax.ppermute(block, AXES, routes(move))  21.1 us
    pallas_call x4, Pallas kernels, score(): pl.pallas_call(functools.partial(score_body, tile, tiles, len(blocks)), g...  11.3 us
    unnamed x8, local copies, waits for them, and re-layouts  1.7 us
  transfers between devices with their start and end apart: 19, of which 9 were waited for; matrix products, arithmetic and copies ran while one was open for 1% of the time, Pallas kernels for 18%

profile of v4, /device:TPU:2, one launch (start us, length us, event | category | flops | bytes accessed | tf_op | source)
XLA Modules:
  0.0 61.9 jit_solution(10214076407351841633)
XLA Ops:
  0.6 0.0 copy-start.2
  0.6 1.0 %copy-done.2 = bf16[128,2048]{1,0:T(8,128)(2,1)S(1)} copy-done((bf16[128,2048]{1,0:T(8,128)(2,1)S(1)}, bf16[128,2048]{1,0:T(8,128)(2,1)}, u32[]{:S(2)}) %copy-start.2) | copy-done | bytes 524312
  1.7 0.7 %copy-done.3 = bf16[128]{0:T(256)(128)(2,1)S(1)} copy-done((bf16[128]{0:T(256)(128)(2,1)S(1)}, bf16[128]{0:T(256)(128)(2,1)}, u32[]{:S(2)}) %copy-start.3) | copy-done | bytes 280
  2.3 0.2 shard_map.59.refs_0_
  2.5 0.1 collective-permute-start.2
  2.6 5.9 %collective-permute-start = (bf16[128,2176]{1,0:T(8,128)(2,1)S(1)}, bf16[128,2176]{1,0:T(8,128)(2,1)S(1)}, u32[]{:S(2)}, u32[]{:S(2)}) collective-permute-start(bf16[128,2176]{1,0:T(8,128)(2,1)S(1)} %shard_map.59.refs_0_), channel_id=1, source_target_pairs={{0,208},{32,96},{64,0},{96,160},{128,64},{160,224},{192,128},{224,... | collective-permute-start | bytes 1671176 | tf_op jit(solution)/shard_map/ppermute | solution.py:33
  8.6 0.0 collective-permute-start.1
  8.6 0.0 collective-permute-done.2.refs_1_
  8.6 2.8 %shard_map.60 = (f32[1,2048]{1,0:T(1,128)S(1)}, f32[1,128]{1,0:T(1,128)S(1)}, f32[1,128]{1,0:T(1,128)S(1)}) custom-call(f32[1,2048]{1,0:T(1,128)S(1)} %bitcast.5, f32[1,2048]{1,0:T(1,128)S(1)} %bitcast.6, bf16[2048,2048]{1,0:T(8,128)(2,1)S(1)} %copy-done, bf16[128,2176]{1,0:T(8,128)(2,1)S(1)} %shard_map.59.refs_0_, ...), custom_call_target="tpu_custom_call" | custom-call | flops 2147483648 | bytes 9437184 | tf_op jit(solution)/shard_map/pallas_call | solution.py:141
  11.4 9.6 %collective-permute-done.refs_0_ = bf16[128,2176]{1,0:T(8,128)(2,1)S(1)} collective-permute-done((bf16[128,2176]{1,0:T(8,128)(2,1)S(1)}, bf16[128,2176]{1,0:T(8,128)(2,1)S(1)}, u32[]{:S(2)}, u32[]{:S(2)}) %collective-permute-start) | collective-permute-done | bytes 557088 | tf_op jit(solution)/shard_map/ppermute | solution.py:33
  21.1 0.7 %collective-permute-done.1.refs_0_ = bf16[128,2176]{1,0:T(8,128)(2,1)S(1)} collective-permute-done((bf16[128,2176]{1,0:T(8,128)(2,1)S(1)}, bf16[128,2176]{1,0:T(8,128)(2,1)S(1)}, u32[]{:S(2)}, u32[]{:S(2)}) %collective-permute-start.1) | collective-permute-done | bytes 557088 | tf_op jit(solution)/shard_map/ppermute | solution.py:33
  21.8 0.0 collective-permute-start.4
  21.8 0.5 collective-permute-start.5
  22.3 3.0 %collective-permute-start.3 = (bf16[128,2176]{1,0:T(8,128)(2,1)S(1)}, bf16[128,2176]{1,0:T(8,128)(2,1)S(1)}, u32[]{:S(2)}, u32[]{:S(2)}) collective-permute-start(bf16[128,2176]{1,0:T(8,128)(2,1)S(1)} %collective-permute-done.refs_0_), channel_id=1, source_target_pairs={{0,208},{32,96},{64,0},{96,160},{128,64},{160,224},{192,128},{224,... | collective-permute-start | bytes 1671176 | tf_op jit(solution)/shard_map/ppermute | solution.py:33
  25.3 0.0 collective-permute-done.4.refs_1_
  25.3 2.8 %shard_map.61 = (f32[1,2048]{1,0:T(1,128)S(1)}, f32[1,128]{1,0:T(1,128)S(1)}, f32[1,128]{1,0:T(1,128)S(1)}) custom-call(f32[1,2048]{1,0:T(1,128)S(1)} %bitcast.7, f32[1,2048]{1,0:T(1,128)S(1)} %get-tuple-element.22.prev, bf16[2048,2048]{1,0:T(8,128)(2,1)S(1)} %copy-done, bf16[128,2176]{1,0:T(8,128)(2,1)S(1)} %collective-permute-done.refs_0_, ...), custom_call_target="tpu_custom_call" | custom-call | flops 2147483648 | bytes 9437184 | tf_op jit(solution)/shard_map/pallas_call | solution.py:141
  28.1 0.0 collective-permute-done.5.refs_1_
  28.1 2.8 %shard_map.62 = (f32[1,2048]{1,0:T(1,128)S(1)}, f32[1,128]{1,0:T(1,128)S(1)}, f32[1,128]{1,0:T(1,128)S(1)}) custom-call(f32[1,2048]{1,0:T(1,128)S(1)} %bitcast.8, f32[1,2048]{1,0:T(1,128)S(1)} %get-tuple-element.23.prev, bf16[2048,2048]{1,0:T(8,128)(2,1)S(1)} %copy-done, bf16[128,2176]{1,0:T(8,128)(2,1)S(1)} %collective-permute-done.1.refs_0_, ...), custom_call_target="tpu_custom_call" | custom-call | flops 2147483648 | bytes 9437184 | tf_op jit(solution)/shard_map/pallas_call | solution.py:141
  31.0 0.1 collective-permute-start.6
  31.1 1.1 %collective-permute-done.6 = f32[3,128]{1,0:T(4,128)S(1)} collective-permute-done((f32[3,128]{1,0:T(4,128)S(1)}, f32[3,128]{1,0:T(4,128)S(1)}, u32[]{:S(2)}, u32[]{:S(2)}) %collective-permute-start.6) | collective-permute-done | bytes 1568 | tf_op jit(solution)/shard_map/ppermute | solution.py:33
  32.2 0.1 collective-permute-done.3.refs_0_
  32.3 0.2 collective-permute-start.7
  32.5 0.0 collective-permute-start.12
  32.5 3.6 %collective-permute-start.13 = (f32[1,128]{1,0:T(1,128)S(1)}, f32[1,128]{1,0:T(1,128)S(1)}, u32[]{:S(2)}, u32[]{:S(2)}) collective-permute-start(f32[1,128]{1,0:T(1,128)S(1)} %get-tuple-element.39), channel_id=1, source_target_pairs={{0,208},{32,96},{64,0},{96,160},{128,64},{160,224},{192,128},{224,... | collective-permute-start | bytes 1544 | tf_op jit(solution)/shard_map/ppermute | solution.py:33
  36.1 0.0 collective-permute-done.7.refs_1_
  36.1 2.8 %shard_map.63 = (f32[1,2048]{1,0:T(1,128)S(1)}, f32[1,128]{1,0:T(1,128)S(1)}, f32[1,128]{1,0:T(1,128)S(1)}) custom-call(f32[1,2048]{1,0:T(1,128)S(1)} %bitcast.9, f32[1,2048]{1,0:T(1,128)S(1)} %get-tuple-element.32.prev, bf16[2048,2048]{1,0:T(8,128)(2,1)S(1)} %copy-done, bf16[128,2176]{1,0:T(8,128)(2,1)S(1)} %collective-permute-done.3.refs_0_, ...), custom_call_target="tpu_custom_call" | custom-call | flops 2147483648 | bytes 9437184 | tf_op jit(solution)/shard_map/pallas_call | solution.py:141
  38.9 0.4 collective-permute-start.14
  39.4 0.0 collective-permute-done.12
  39.4 0.0 collective-permute-done.13
  39.4 0.9 %collective-permute-done.14 = f32[1,128]{1,0:T(1,128)S(1)} collective-permute-done((f32[1,128]{1,0:T(1,128)S(1)}, f32[1,128]{1,0:T(1,128)S(1)}, u32[]{:S(2)}, u32[]{:S(2)}) %collective-permute-start.14) | collective-permute-done | bytes 544 | tf_op jit(solution)/shard_map/ppermute | solution.py:33
  40.3 1.7 %collective-permute-start.15 = (f32[2,128]{1,0:T(2,128)S(1)}, f32[2,128]{1,0:T(2,128)S(1)}, u32[]{:S(2)}, u32[]{:S(2)}) collective-permute-start(f32[2,128]{1,0:T(2,128)S(1)} %pad_maximum_fusion.1), channel_id=1, source_target_pairs={{0,1},{32,33},{64,65},{96,97},{128,129},{160,161},{192,193},{224,2... | collective-permute-start | bytes 3080 | tf_op jit(solution)/shard_map/ppermute | solution.py:33
  42.0 2.9 %collective-permute-start.16 = (f32[2,128]{1,0:T(2,128)S(1)}, f32[2,128]{1,0:T(2,128)S(1)}, u32[]{:S(2)}, u32[]{:S(2)}) collective-permute-start(f32[2,128]{1,0:T(2,128)S(1)} %pad_maximum_fusion.1), channel_id=1, source_target_pairs={{0,2},{32,34},{64,66},{96,98},{128,130},{160,162},{192,194},{224,2... | collective-permute-start | bytes 3080 | tf_op jit(solution)/shard_map/ppermute | solution.py:33
  44.9 0.2 collective-permute-start.17
  45.1 1.5 %collective-permute-start.10 = (f32[1,2048]{1,0:T(1,128)S(1)}, f32[1,2048]{1,0:T(1,128)S(1)}, u32[]{:S(2)}, u32[]{:S(2)}) collective-permute-start(f32[1,2048]{1,0:T(1,128)S(1)} %get-tuple-element.34), channel_id=1, source_target_pairs={{0,12},{32,44},{64,76},{96,108},{128,140},{160,172},{192,204},{224... | collective-permute-start | bytes 24584 | tf_op jit(solution)/shard_map/ppermute | solution.py:33
  46.6 1.8 %collective-permute-start.8 = (f32[1,2048]{1,0:T(1,128)S(1)}, f32[1,2048]{1,0:T(1,128)S(1)}, u32[]{:S(2)}, u32[]{:S(2)}) collective-permute-start(f32[1,2048]{1,0:T(1,128)S(1)} %get-tuple-element.34), channel_id=1, source_target_pairs={{0,4},{32,36},{64,68},{96,100},{128,132},{160,164},{192,196},{224,... | collective-permute-start | bytes 24584 | tf_op jit(solution)/shard_map/ppermute | solution.py:33
  48.4 0.0 collective-permute-done.15
  48.4 0.2 collective-permute-start.9
  48.6 0.0 collective-permute-done.16
  48.6 1.1 %collective-permute-done.17 = f32[2,128]{1,0:T(2,128)S(1)} collective-permute-done((f32[2,128]{1,0:T(2,128)S(1)}, f32[2,128]{1,0:T(2,128)S(1)}, u32[]{:S(2)}, u32[]{:S(2)}) %collective-permute-start.17) | collective-permute-done | bytes 1056 | tf_op jit(solution)/shard_map/ppermute | solution.py:33
  49.7 0.1 collective-permute-start.18
  49.8 0.0 collective-permute-done.10
  49.8 0.5 collective-permute-done.8
  50.3 3.3 %collective-permute-done.9 = f32[1,2048]{1,0:T(1,128)S(1)} collective-permute-done((f32[1,2048]{1,0:T(1,128)S(1)}, f32[1,2048]{1,0:T(1,128)S(1)}, u32[]{:S(2)}, u32[]{:S(2)}) %collective-permute-start.9) | collective-permute-done | bytes 8224 | tf_op jit(solution)/shard_map/ppermute | solution.py:33
  53.6 3.4 %collective-permute-start.11 = (f32[1,2048]{1,0:T(1,128)S(1)}, f32[1,2048]{1,0:T(1,128)S(1)}, u32[]{:S(2)}, u32[]{:S(2)}) collective-permute-start(f32[1,2048]{1,0:T(1,128)S(1)} %maximum_maximum_fusion), channel_id=1, source_target_pairs={{0,16},{32,48},{64,80},{96,112},{128,144},{160,176},{192,208},{224... | collective-permute-start | bytes 24584 | tf_op jit(solution)/shard_map/ppermute | solution.py:33
  57.0 0.0 collective-permute-done.18
  57.0 0.5 maximum_bitcast_fusion
  57.5 3.7 %collective-permute-done.11 = f32[1,2048]{1,0:T(1,128)S(1)} collective-permute-done((f32[1,2048]{1,0:T(1,128)S(1)}, f32[1,2048]{1,0:T(1,128)S(1)}, u32[]{:S(2)}, u32[]{:S(2)}) %collective-permute-start.11) | collective-permute-done | bytes 8224 | tf_op jit(solution)/shard_map/ppermute | solution.py:33
  61.2 0.6 max.40
  (14 shorter events, 0.1 us)
Async XLA Ops:
  0.6 1.0 %copy-start.2 = (bf16[128,2048]{1,0:T(8,128)(2,1)S(1)}, bf16[128,2048]{1,0:T(8,128)(2,1)}, u32[]{:S(2)}) copy-start(bf16[128,2048]{1,0:T(8,128)(2,1)} %coefficients.1) | copy-start | bytes 1572868
  1.7 0.7 %copy-start.3 = (bf16[128]{0:T(256)(128)(2,1)S(1)}, bf16[128]{0:T(256)(128)(2,1)}, u32[]{:S(2)}) copy-start(bf16[128]{0:T(256)(128)(2,1)} %param.5) | copy-start | bytes 772
  2.3 6.2 %copy-start = (bf16[2048,2048]{1,0:T(8,128)(2,1)S(1)}, bf16[2048,2048]{1,0:T(8,128)(2,1)}, u32[]{:S(2)}) copy-start(bf16[2048,2048]{1,0:T(8,128)(2,1)} %states.7) | copy-start | bytes 25165828
  2.3 6.2 %copy-start.1 = (f32[2048]{0:T(1024)S(1)}, f32[2048]{0:T(1024)}, u32[]{:S(2)}) copy-start(f32[2048]{0:T(1024)} %param.7) | copy-start | bytes 24580
  2.5 6.0 %collective-permute-start.2 = (bf16[128,2176]{1,0:T(8,128)(2,1)S(1)}, bf16[128,2176]{1,0:T(8,128)(2,1)S(1)}, u32[]{:S(2)}, u32[]{:S(2)}) collective-permute-start(bf16[128,2176]{1,0:T(8,128)(2,1)S(1)} %shard_map.59.refs_0_), channel_id=1, source_target_pairs={{0,32},{32,0},{64,96},{96,64},{128,160},{160,128},{192,224},{224,1... | collective-permute-start | bytes 1671176 | tf_op jit(solution)/shard_map/ppermute | solution.py:33
  2.6 18.4 %collective-permute-start = (bf16[128,2176]{1,0:T(8,128)(2,1)S(1)}, bf16[128,2176]{1,0:T(8,128)(2,1)S(1)}, u32[]{:S(2)}, u32[]{:S(2)}) collective-permute-start(bf16[128,2176]{1,0:T(8,128)(2,1)S(1)} %shard_map.59.refs_0_), channel_id=1, source_target_pairs={{0,208},{32,96},{64,0},{96,160},{128,64},{160,224},{192,128},{224,... | collective-permute-start | bytes 1671176 | tf_op jit(solution)/shard_map/ppermute | solution.py:33
  8.6 13.2 %collective-permute-start.1 = (bf16[128,2176]{1,0:T(8,128)(2,1)S(1)}, bf16[128,2176]{1,0:T(8,128)(2,1)S(1)}, u32[]{:S(2)}, u32[]{:S(2)}) collective-permute-start(bf16[128,2176]{1,0:T(8,128)(2,1)S(1)} %shard_map.59.refs_0_), channel_id=1, source_target_pairs={{0,64},{32,240},{64,128},{96,32},{128,192},{160,96},{192,16},{224,... | collective-permute-start | bytes 1671176 | tf_op jit(solution)/shard_map/ppermute | solution.py:33
  21.8 3.5 %collective-permute-start.4 = (bf16[128,2176]{1,0:T(8,128)(2,1)S(1)}, bf16[128,2176]{1,0:T(8,128)(2,1)S(1)}, u32[]{:S(2)}, u32[]{:S(2)}) collective-permute-start(bf16[128,2176]{1,0:T(8,128)(2,1)S(1)} %collective-permute-done.refs_0_), channel_id=1, source_target_pairs={{0,32},{32,0},{64,96},{96,64},{128,160},{160,128},{192,224},{224,1... | collective-permute-start | bytes 1671176 | tf_op jit(solution)/shard_map/ppermute | solution.py:33
  21.8 6.3 %collective-permute-start.5 = (bf16[128,2176]{1,0:T(8,128)(2,1)S(1)}, bf16[128,2176]{1,0:T(8,128)(2,1)S(1)}, u32[]{:S(2)}, u32[]{:S(2)}) collective-permute-start(bf16[128,2176]{1,0:T(8,128)(2,1)S(1)} %collective-permute-done.1.refs_0_), channel_id=1, source_target_pairs={{0,32},{32,0},{64,96},{96,64},{128,160},{160,128},{192,224},{224,1... | collective-permute-start | bytes 1671176 | tf_op jit(solution)/shard_map/ppermute | solution.py:33
  22.3 10.0 %collective-permute-start.3 = (bf16[128,2176]{1,0:T(8,128)(2,1)S(1)}, bf16[128,2176]{1,0:T(8,128)(2,1)S(1)}, u32[]{:S(2)}, u32[]{:S(2)}) collective-permute-start(bf16[128,2176]{1,0:T(8,128)(2,1)S(1)} %collective-permute-done.refs_0_), channel_id=1, source_target_pairs={{0,208},{32,96},{64,0},{96,160},{128,64},{160,224},{192,128},{224,... | collective-permute-start | bytes 1671176 | tf_op jit(solution)/shard_map/ppermute | solution.py:33
  31.0 1.2 %collective-permute-start.6 = (f32[3,128]{1,0:T(4,128)S(1)}, f32[3,128]{1,0:T(4,128)S(1)}, u32[]{:S(2)}, u32[]{:S(2)}) collective-permute-start(f32[3,128]{1,0:T(4,128)S(1)} %pad_maximum_fusion), channel_id=1, source_target_pairs={{0,32},{32,0},{64,96},{96,64},{128,160},{160,128},{192,224},{224,1... | collective-permute-start | bytes 4616 | tf_op jit(solution)/shard_map/ppermute | solution.py:33
  32.3 3.8 %collective-permute-start.7 = (bf16[128,2176]{1,0:T(8,128)(2,1)S(1)}, bf16[128,2176]{1,0:T(8,128)(2,1)S(1)}, u32[]{:S(2)}, u32[]{:S(2)}) collective-permute-start(bf16[128,2176]{1,0:T(8,128)(2,1)S(1)} %collective-permute-done.3.refs_0_), channel_id=1, source_target_pairs={{0,32},{32,0},{64,96},{96,64},{128,160},{160,128},{192,224},{224,1... | collective-permute-start | bytes 1671176 | tf_op jit(solution)/shard_map/ppermute | solution.py:33
  32.5 6.9 %collective-permute-start.12 = (f32[1,128]{1,0:T(1,128)S(1)}, f32[1,128]{1,0:T(1,128)S(1)}, u32[]{:S(2)}, u32[]{:S(2)}) collective-permute-start(f32[1,128]{1,0:T(1,128)S(1)} %get-tuple-element.38), channel_id=1, source_target_pairs={{0,64},{32,240},{64,128},{96,32},{128,192},{160,96},{192,16},{224,... | collective-permute-start | bytes 1544 | tf_op jit(solution)/shard_map/ppermute | solution.py:33
  32.5 6.9 %collective-permute-start.13 = (f32[1,128]{1,0:T(1,128)S(1)}, f32[1,128]{1,0:T(1,128)S(1)}, u32[]{:S(2)}, u32[]{:S(2)}) collective-permute-start(f32[1,128]{1,0:T(1,128)S(1)} %get-tuple-element.39), channel_id=1, source_target_pairs={{0,208},{32,96},{64,0},{96,160},{128,64},{160,224},{192,128},{224,... | collective-permute-start | bytes 1544 | tf_op jit(solution)/shard_map/ppermute | solution.py:33
  38.9 1.4 %collective-permute-start.14 = (f32[1,128]{1,0:T(1,128)S(1)}, f32[1,128]{1,0:T(1,128)S(1)}, u32[]{:S(2)}, u32[]{:S(2)}) collective-permute-start(f32[1,128]{1,0:T(1,128)S(1)} %get-tuple-element.37), channel_id=1, source_target_pairs={{0,32},{32,0},{64,96},{96,64},{128,160},{160,128},{192,224},{224,1... | collective-permute-start | bytes 1544 | tf_op jit(solution)/shard_map/ppermute | solution.py:33
  40.3 8.1 %collective-permute-start.15 = (f32[2,128]{1,0:T(2,128)S(1)}, f32[2,128]{1,0:T(2,128)S(1)}, u32[]{:S(2)}, u32[]{:S(2)}) collective-permute-start(f32[2,128]{1,0:T(2,128)S(1)} %pad_maximum_fusion.1), channel_id=1, source_target_pairs={{0,1},{32,33},{64,65},{96,97},{128,129},{160,161},{192,193},{224,2... | collective-permute-start | bytes 3080 | tf_op jit(solution)/shard_map/ppermute | solution.py:33
  42.0 6.6 %collective-permute-start.16 = (f32[2,128]{1,0:T(2,128)S(1)}, f32[2,128]{1,0:T(2,128)S(1)}, u32[]{:S(2)}, u32[]{:S(2)}) collective-permute-start(f32[2,128]{1,0:T(2,128)S(1)} %pad_maximum_fusion.1), channel_id=1, source_target_pairs={{0,2},{32,34},{64,66},{96,98},{128,130},{160,162},{192,194},{224,2... | collective-permute-start | bytes 3080 | tf_op jit(solution)/shard_map/ppermute | solution.py:33
  44.9 4.8 %collective-permute-start.17 = (f32[2,128]{1,0:T(2,128)S(1)}, f32[2,128]{1,0:T(2,128)S(1)}, u32[]{:S(2)}, u32[]{:S(2)}) collective-permute-start(f32[2,128]{1,0:T(2,128)S(1)} %pad_maximum_fusion.1), channel_id=1, source_target_pairs={{0,3},{32,35},{64,67},{96,99},{128,131},{160,163},{192,195},{224,2... | collective-permute-start | bytes 3080 | tf_op jit(solution)/shard_map/ppermute | solution.py:33
  45.1 4.7 %collective-permute-start.10 = (f32[1,2048]{1,0:T(1,128)S(1)}, f32[1,2048]{1,0:T(1,128)S(1)}, u32[]{:S(2)}, u32[]{:S(2)}) collective-permute-start(f32[1,2048]{1,0:T(1,128)S(1)} %get-tuple-element.34), channel_id=1, source_target_pairs={{0,12},{32,44},{64,76},{96,108},{128,140},{160,172},{192,204},{224... | collective-permute-start | bytes 24584 | tf_op jit(solution)/shard_map/ppermute | solution.py:33
  46.6 3.7 %collective-permute-start.8 = (f32[1,2048]{1,0:T(1,128)S(1)}, f32[1,2048]{1,0:T(1,128)S(1)}, u32[]{:S(2)}, u32[]{:S(2)}) collective-permute-start(f32[1,2048]{1,0:T(1,128)S(1)} %get-tuple-element.34), channel_id=1, source_target_pairs={{0,4},{32,36},{64,68},{96,100},{128,132},{160,164},{192,196},{224,... | collective-permute-start | bytes 24584 | tf_op jit(solution)/shard_map/ppermute | solution.py:33
  48.4 5.2 %collective-permute-start.9 = (f32[1,2048]{1,0:T(1,128)S(1)}, f32[1,2048]{1,0:T(1,128)S(1)}, u32[]{:S(2)}, u32[]{:S(2)}) collective-permute-start(f32[1,2048]{1,0:T(1,128)S(1)} %get-tuple-element.34), channel_id=1, source_target_pairs={{0,8},{32,40},{64,72},{96,104},{128,136},{160,168},{192,200},{224,... | collective-permute-start | bytes 24584 | tf_op jit(solution)/shard_map/ppermute | solution.py:33
  49.7 7.3 %collective-permute-start.18 = (f32[1,128]{1,0:T(1,128)S(1)}, f32[1,128]{1,0:T(1,128)S(1)}, u32[]{:S(2)}, u32[]{:S(2)}) collective-permute-start(f32[1,128]{1,0:T(1,128)S(1)} %slice.19), channel_id=1, source_target_pairs={{0,128},{32,176},{64,192},{96,240},{128,16},{160,32},{192,80},{224... | collective-permute-start | bytes 1544 | tf_op jit(solution)/shard_map/ppermute | solution.py:33
  53.6 7.6 %collective-permute-start.11 = (f32[1,2048]{1,0:T(1,128)S(1)}, f32[1,2048]{1,0:T(1,128)S(1)}, u32[]{:S(2)}, u32[]{:S(2)}) collective-permute-start(f32[1,2048]{1,0:T(1,128)S(1)} %maximum_maximum_fusion), channel_id=1, source_target_pairs={{0,16},{32,48},{64,80},{96,112},{128,144},{160,176},{192,208},{224... | collective-permute-start | bytes 24584 | tf_op jit(solution)/shard_map/ppermute | solution.py:33

commit v5 on v4

--- a/solution.py
+++ b/solution.py
@@ -159,36 +159,39 @@
 
 def body(coefficients, intercepts, states, old_values):
     old = old_values[None, :]
+    cuts = coefficients.shape[0]
     fence = lax.optimization_barrier
 
     own = pack(coefficients, intercepts)
     near = send(own, toward)
-    next_ = send(own, against)
     peer = send(own, over_core)
     top, own_mine, own_other = score([own, peer], old, old, states)
-    near, next_, top = fence((near, next_, top))
+    near, own, top = fence((near, own, top))
     two = send(near, toward)
+    next_ = send(own, against)
     top, near_mine, near_other = score([near, send(near, over_core)], old, top, states)
-    top, next_mine, next_other = score([next_, send(next_, over_core)], old, top, states)
-
-    mine = jnp.concatenate([own_mine, near_mine, next_mine], axis=0)
-    other = jnp.concatenate([own_other, near_other, next_other], axis=0)
+
+    mine = jnp.concatenate([own_mine, near_mine], axis=0)
+    other = jnp.concatenate([own_other, near_other], axis=0)
     lifts = jnp.maximum(mine, send(other, over_core))
-    two, top, lifts = fence((two, top, lifts))
-    back = [send(lifts[1:2], against), send(lifts[2:3], toward)]
-    top, two_mine, two_other = score([two, send(two, over_core)], old, top, states)
-
-    swapped = send(two_other, over_core)
+    held = jnp.maximum(lifts[0:1], send(lifts[1:2], against))
+    next_, two, top, held = fence((next_, two, top, held))
+    blocks = [next_, two, send(next_, over_core), send(two, over_core)]
+    top, mine, other = score(blocks, old, top, states)
+
+    swapped = send(other, over_core)
     for_x = [send(top, over_x(d)) for d in (1, 2, 3)]
-    held = functools.reduce(jnp.maximum, back, lifts[0:1])
-    last = jnp.maximum(two_mine, swapped)
-    lifts = jnp.concatenate([held, last], axis=0)
+    swapped, for_x[0] = fence((swapped, for_x[0]))
+    lifts = jnp.concatenate([held, jnp.maximum(mine, swapped)], axis=1)
     for_y = [send(lifts, over_y(d)) for d in (1, 2, 3)]
     top = functools.reduce(jnp.maximum, for_x, top)
+    for_y[0], top = fence((for_y[0], top))
     lifts = functools.reduce(jnp.maximum, for_y, lifts)
-    for_z = send(lifts[1:2], two_back)
-    new_values = jnp.maximum(top, send(top, far))
-    cut_gaps = jnp.maximum(lifts[0:1], for_z)
+    across = send(top, far)
+    for_z = [send(lifts[:, cuts : 2 * cuts], toward), send(lifts[:, 2 * cuts :], two_back)]
+    across, *for_z = fence((across, *for_z))
+    new_values = jnp.maximum(top, across)
+    cut_gaps = functools.reduce(jnp.maximum, for_z, lifts[:, :cuts])
     return new_values[0], cut_gaps[0]
 
 

time: 62 us -> 62.9 us (1.015)
  waiting for transfers between devices: 21.1 us -> 23.3 us
  starting transfers between devices: 25.6 us -> 24.9 us
    ppermute x19, waiting for transfers between devices: 21.1 us -> 23.3 us  [send(): return lax.ppermute(block, AXES, routes(move))]
    ppermute x19, starting transfers between devices: 25.6 us -> 24.9 us  [send(): return lax.ppermute(block, AXES, routes(move))]
    pallas_call x4 -> x3, Pallas kernels: 11.3 us -> 10.8 us  [score(): pl.pallas_call(functools.partial(score_body, tile, tiles, len(blocks)), g...]
  transfers between devices with their start and end apart: 19 -> 19, of which waited for: 9 -> 7; matrix products, arithmetic and copies ran while one was open for 1% -> 0% of each run, Pallas kernels for 18% -> 9%
where the time goes in v5:
time: 62.9 us; the launch traced here: 62.7 us
  starting transfers between devices  24.9 us (40%)
  waiting for transfers between devices  23.3 us (37%)
  Pallas kernels  10.9 us (17%)
  local copies, waits for them, and re-layouts  1.71 us (3%)
  other arithmetic  1.18 us (2%)
  between operations  0.77 us (1%)
    ppermute x19, starting transfers between devices, send(): return lax.ppermute(block, AXES, routes(move))  24.9 us
    ppermute x19, waiting for transfers between devices, send(): return lax.ppermute(block, AXES, routes(move))  23.3 us
    pallas_call x3, Pallas kernels, score(): pl.pallas_call(functools.partial(score_body, tile, tiles, len(blocks)), g...  10.8 us
    unnamed x8, local copies, waits for them, and re-layouts  1.7 us
  transfers between devices with their start and end apart: 19, of which 7 were waited for; matrix products, arithmetic and copies ran while one was open for 0% of the time, Pallas kernels for 9%

profile of v5, /device:TPU:2, one launch (start us, length us, event | category | flops | bytes accessed | tf_op | source)
XLA Modules:
  0.0 62.7 jit_solution(4718104715949091750)
XLA Ops:
  0.6 0.0 copy-start.2
  0.6 1.0 %copy-done.2 = bf16[128,2048]{1,0:T(8,128)(2,1)S(1)} copy-done((bf16[128,2048]{1,0:T(8,128)(2,1)S(1)}, bf16[128,2048]{1,0:T(8,128)(2,1)}, u32[]{:S(2)}) %copy-start.2) | copy-done | bytes 524312
  1.7 0.7 %copy-done.3 = bf16[128]{0:T(256)(128)(2,1)S(1)} copy-done((bf16[128]{0:T(256)(128)(2,1)S(1)}, bf16[128]{0:T(256)(128)(2,1)}, u32[]{:S(2)}) %copy-start.3) | copy-done | bytes 280
  2.3 0.2 shard_map.59.refs_0_
  2.5 0.1 collective-permute-start.1
  2.6 5.9 %collective-permute-start = (bf16[128,2176]{1,0:T(8,128)(2,1)S(1)}, bf16[128,2176]{1,0:T(8,128)(2,1)S(1)}, u32[]{:S(2)}, u32[]{:S(2)}) collective-permute-start(bf16[128,2176]{1,0:T(8,128)(2,1)S(1)} %shard_map.59.refs_0_), channel_id=1, source_target_pairs={{0,208},{32,96},{64,0},{96,160},{128,64},{160,224},{192,128},{224,... | collective-permute-start | bytes 1671176 | tf_op jit(solution)/shard_map/ppermute | solution.py:33
  8.6 0.0 collective-permute-done.1.refs_1_
  8.6 0.0 copy-done
  8.6 2.8 %shard_map.60 = (f32[1,2048]{1,0:T(1,128)S(1)}, f32[1,128]{1,0:T(1,128)S(1)}, f32[1,128]{1,0:T(1,128)S(1)}) custom-call(f32[1,2048]{1,0:T(1,128)S(1)} %bitcast.5, f32[1,2048]{1,0:T(1,128)S(1)} %bitcast.6, bf16[2048,2048]{1,0:T(8,128)(2,1)S(1)} %copy-done, bf16[128,2176]{1,0:T(8,128)(2,1)S(1)} %shard_map.59.refs_0_, ...), custom_call_target="tpu_custom_call" | custom-call | flops 2147483648 | bytes 9437184 | tf_op jit(solution)/shard_map/pallas_call | solution.py:141
  11.4 4.2 %collective-permute-done.refs_0_ = bf16[128,2176]{1,0:T(8,128)(2,1)S(1)} collective-permute-done((bf16[128,2176]{1,0:T(8,128)(2,1)S(1)}, bf16[128,2176]{1,0:T(8,128)(2,1)S(1)}, u32[]{:S(2)}, u32[]{:S(2)}) %collective-permute-start) | collective-permute-done | bytes 557088 | tf_op jit(solution)/shard_map/ppermute | solution.py:33
  15.6 0.0 collective-permute-start.4
  15.6 3.7 %collective-permute-start.3 = (bf16[128,2176]{1,0:T(8,128)(2,1)S(1)}, bf16[128,2176]{1,0:T(8,128)(2,1)S(1)}, u32[]{:S(2)}, u32[]{:S(2)}) collective-permute-start(bf16[128,2176]{1,0:T(8,128)(2,1)S(1)} %collective-permute-done.refs_0_), channel_id=1, source_target_pairs={{0,208},{32,96},{64,0},{96,160},{128,64},{160,224},{192,128},{224,... | collective-permute-start | bytes 1671176 | tf_op jit(solution)/shard_map/ppermute | solution.py:33
  19.3 0.0 collective-permute-start.2
  19.3 0.0 collective-permute-done.4.refs_1_
  19.3 2.8 %shard_map.61 = (f32[1,2048]{1,0:T(1,128)S(1)}, f32[1,128]{1,0:T(1,128)S(1)}, f32[1,128]{1,0:T(1,128)S(1)}) custom-call(f32[1,2048]{1,0:T(1,128)S(1)} %bitcast.7, f32[1,2048]{1,0:T(1,128)S(1)} %get-tuple-element.28.prev, bf16[2048,2048]{1,0:T(8,128)(2,1)S(1)} %copy-done, bf16[128,2176]{1,0:T(8,128)(2,1)S(1)} %collective-permute-done.refs_0_, ...), custom_call_target="tpu_custom_call" | custom-call | flops 2147483648 | bytes 9437184 | tf_op jit(solution)/shard_map/pallas_call | solution.py:141
  22.2 0.3 collective-permute-start.5
  22.5 0.9 %collective-permute-done.5 = f32[2,128]{1,0:T(2,128)S(1)} collective-permute-done((f32[2,128]{1,0:T(2,128)S(1)}, f32[2,128]{1,0:T(2,128)S(1)}, u32[]{:S(2)}, u32[]{:S(2)}) %collective-permute-start.5) | collective-permute-done | bytes 1056 | tf_op jit(solution)/shard_map/ppermute | solution.py:33
  23.4 0.1 collective-permute-start.6
  23.5 9.2 %collective-permute-done.6 = f32[1,128]{1,0:T(1,128)S(1)} collective-permute-done((f32[1,128]{1,0:T(1,128)S(1)}, f32[1,128]{1,0:T(1,128)S(1)}, u32[]{:S(2)}, u32[]{:S(2)}) %collective-permute-start.6) | collective-permute-done | bytes 544 | tf_op jit(solution)/shard_map/ppermute | solution.py:33
  32.7 0.0 collective-permute-done.2.refs_0_
  32.7 0.0 collective-permute-done.3.refs_1_
  32.7 0.1 collective-permute-start.7
  32.8 0.5 collective-permute-start.8
  33.3 1.4 %collective-permute-done.7.refs_2_ = bf16[128,2176]{1,0:T(8,128)(2,1)S(1)} collective-permute-done((bf16[128,2176]{1,0:T(8,128)(2,1)S(1)}, bf16[128,2176]{1,0:T(8,128)(2,1)S(1)}, u32[]{:S(2)}, u32[]{:S(2)}) %collective-permute-start.7) | collective-permute-done | bytes 557088 | tf_op jit(solution)/shard_map/ppermute | solution.py:33
  34.7 0.8 %collective-permute-done.8.refs_3_ = bf16[128,2176]{1,0:T(8,128)(2,1)S(1)} collective-permute-done((bf16[128,2176]{1,0:T(8,128)(2,1)S(1)}, bf16[128,2176]{1,0:T(8,128)(2,1)S(1)}, u32[]{:S(2)}, u32[]{:S(2)}) %collective-permute-start.8) | collective-permute-done | bytes 557088 | tf_op jit(solution)/shard_map/ppermute | solution.py:33
  35.5 5.1 %shard_map.62 = (f32[1,2048]{1,0:T(1,128)S(1)}, f32[1,256]{1,0:T(1,128)S(1)}, f32[1,256]{1,0:T(1,128)S(1)}) custom-call(f32[1,2048]{1,0:T(1,128)S(1)} %bitcast.8, f32[1,2048]{1,0:T(1,128)S(1)} %get-tuple-element.35.prev, bf16[2048,2048]{1,0:T(8,128)(2,1)S(1)} %copy-done, bf16[128,2176]{1,0:T(8,128)(2,1)S(1)} %collective-permute-done.2.refs_0_, ...), custom_call_target="tpu_custom_call" | custom-call | flops 4294967296 | bytes 10485760 | tf_op jit(solution)/shard_map/pallas_call | solution.py:141
  40.6 0.6 collective-permute-start.10
  41.2 0.0 collective-permute-start.9
  41.3 2.2 %collective-permute-start.13 = (f32[1,2048]{1,0:T(1,128)S(1)}, f32[1,2048]{1,0:T(1,128)S(1)}, u32[]{:S(2)}, u32[]{:S(2)}) collective-permute-start(f32[1,2048]{1,0:T(1,128)S(1)} %get-tuple-element.40), channel_id=1, source_target_pairs={{0,12},{32,44},{64,76},{96,108},{128,140},{160,172},{192,204},{224... | collective-permute-start | bytes 24584 | tf_op jit(solution)/shard_map/ppermute | solution.py:33
  43.4 1.4 %collective-permute-start.12 = (f32[1,2048]{1,0:T(1,128)S(1)}, f32[1,2048]{1,0:T(1,128)S(1)}, u32[]{:S(2)}, u32[]{:S(2)}) collective-permute-start(f32[1,2048]{1,0:T(1,128)S(1)} %get-tuple-element.40), channel_id=1, source_target_pairs={{0,8},{32,40},{64,72},{96,104},{128,136},{160,168},{192,200},{224,... | collective-permute-start | bytes 24584 | tf_op jit(solution)/shard_map/ppermute | solution.py:33
  44.8 0.0 collective-permute-done.9
  44.8 0.0 collective-permute-done.10
  44.8 3.3 %collective-permute-start.15 = (f32[1,384]{1,0:T(1,128)S(1)}, f32[1,384]{1,0:T(1,128)S(1)}, u32[]{:S(2)}, u32[]{:S(2)}) collective-permute-start(f32[1,384]{1,0:T(1,128)S(1)} %pad_maximum_fusion), channel_id=1, source_target_pairs={{0,2},{32,34},{64,66},{96,98},{128,130},{160,162},{192,194},{224,2... | collective-permute-start | bytes 4616 | tf_op jit(solution)/shard_map/ppermute | solution.py:33
  48.1 1.1 %collective-permute-start.16 = (f32[1,384]{1,0:T(1,128)S(1)}, f32[1,384]{1,0:T(1,128)S(1)}, u32[]{:S(2)}, u32[]{:S(2)}) collective-permute-start(f32[1,384]{1,0:T(1,128)S(1)} %pad_maximum_fusion), channel_id=1, source_target_pairs={{0,3},{32,35},{64,67},{96,99},{128,131},{160,163},{192,195},{224,2... | collective-permute-start | bytes 4616 | tf_op jit(solution)/shard_map/ppermute | solution.py:33
  49.2 0.0 collective-permute-start.11
  49.2 0.0 collective-permute-done.13
  49.2 0.0 collective-permute-done.12
  49.2 3.5 %collective-permute-done.11 = f32[1,384]{1,0:T(1,128)S(1)} collective-permute-done((f32[1,384]{1,0:T(1,128)S(1)}, f32[1,384]{1,0:T(1,128)S(1)}, u32[]{:S(2)}, u32[]{:S(2)}) %collective-permute-start.11) | collective-permute-done | bytes 1568 | tf_op jit(solution)/shard_map/ppermute | solution.py:33
  52.8 3.1 %collective-permute-start.14 = (f32[1,2048]{1,0:T(1,128)S(1)}, f32[1,2048]{1,0:T(1,128)S(1)}, u32[]{:S(2)}, u32[]{:S(2)}) collective-permute-start(f32[1,2048]{1,0:T(1,128)S(1)} %maximum_maximum_fusion), channel_id=1, source_target_pairs={{0,16},{32,48},{64,80},{96,112},{128,144},{160,176},{192,208},{224... | collective-permute-start | bytes 24584 | tf_op jit(solution)/shard_map/ppermute | solution.py:33
  55.8 0.0 collective-permute-done.15
  55.8 0.0 collective-permute-done.16
  55.9 0.5 collective-permute-start.18
  56.4 2.0 %collective-permute-start.17 = (f32[1,128]{1,0:T(1,128)S(1)}, f32[1,128]{1,0:T(1,128)S(1)}, u32[]{:S(2)}, u32[]{:S(2)}) collective-permute-start(f32[1,128]{1,0:T(1,128)S(1)} %get-tuple-element.49), channel_id=1, source_target_pairs={{0,208},{32,96},{64,0},{96,160},{128,64},{160,224},{192,128},{224,... | collective-permute-start | bytes 1544 | tf_op jit(solution)/shard_map/ppermute | solution.py:33
  58.4 3.2 %collective-permute-done.18 = f32[1,128]{1,0:T(1,128)S(1)} collective-permute-done((f32[1,128]{1,0:T(1,128)S(1)}, f32[1,128]{1,0:T(1,128)S(1)}, u32[]{:S(2)}, u32[]{:S(2)}) %collective-permute-start.18) | collective-permute-done | bytes 544 | tf_op jit(solution)/shard_map/ppermute | solution.py:33
  61.6 0.0 collective-permute-done.17
  61.6 0.0 collective-permute-done.14
  61.6 0.6 max.45
  62.2 0.5 fusion.1
  (13 shorter events, 0.1 us)
Async XLA Ops:
  0.6 1.0 %copy-start.2 = (bf16[128,2048]{1,0:T(8,128)(2,1)S(1)}, bf16[128,2048]{1,0:T(8,128)(2,1)}, u32[]{:S(2)}) copy-start(bf16[128,2048]{1,0:T(8,128)(2,1)} %coefficients.1) | copy-start | bytes 1572868
  1.7 0.7 %copy-start.3 = (bf16[128]{0:T(256)(128)(2,1)S(1)}, bf16[128]{0:T(256)(128)(2,1)}, u32[]{:S(2)}) copy-start(bf16[128]{0:T(256)(128)(2,1)} %param.5) | copy-start | bytes 772
  2.3 6.2 %copy-start = (bf16[2048,2048]{1,0:T(8,128)(2,1)S(1)}, bf16[2048,2048]{1,0:T(8,128)(2,1)}, u32[]{:S(2)}) copy-start(bf16[2048,2048]{1,0:T(8,128)(2,1)} %states.5) | copy-start | bytes 25165828
  2.3 6.2 %copy-start.1 = (f32[2048]{0:T(1024)S(1)}, f32[2048]{0:T(1024)}, u32[]{:S(2)}) copy-start(f32[2048]{0:T(1024)} %param.7) | copy-start | bytes 24580
  2.5 6.0 %collective-permute-start.1 = (bf16[128,2176]{1,0:T(8,128)(2,1)S(1)}, bf16[128,2176]{1,0:T(8,128)(2,1)S(1)}, u32[]{:S(2)}, u32[]{:S(2)}) collective-permute-start(bf16[128,2176]{1,0:T(8,128)(2,1)S(1)} %shard_map.59.refs_0_), channel_id=1, source_target_pairs={{0,32},{32,0},{64,96},{96,64},{128,160},{160,128},{192,224},{224,1... | collective-permute-start | bytes 1671176 | tf_op jit(solution)/shard_map/ppermute | solution.py:33
  2.6 13.0 %collective-permute-start = (bf16[128,2176]{1,0:T(8,128)(2,1)S(1)}, bf16[128,2176]{1,0:T(8,128)(2,1)S(1)}, u32[]{:S(2)}, u32[]{:S(2)}) collective-permute-start(bf16[128,2176]{1,0:T(8,128)(2,1)S(1)} %shard_map.59.refs_0_), channel_id=1, source_target_pairs={{0,208},{32,96},{64,0},{96,160},{128,64},{160,224},{192,128},{224,... | collective-permute-start | bytes 1671176 | tf_op jit(solution)/shard_map/ppermute | solution.py:33
  15.6 3.7 %collective-permute-start.4 = (bf16[128,2176]{1,0:T(8,128)(2,1)S(1)}, bf16[128,2176]{1,0:T(8,128)(2,1)S(1)}, u32[]{:S(2)}, u32[]{:S(2)}) collective-permute-start(bf16[128,2176]{1,0:T(8,128)(2,1)S(1)} %collective-permute-done.refs_0_), channel_id=1, source_target_pairs={{0,32},{32,0},{64,96},{96,64},{128,160},{160,128},{192,224},{224,1... | collective-permute-start | bytes 1671176 | tf_op jit(solution)/shard_map/ppermute | solution.py:33
  15.6 17.1 %collective-permute-start.3 = (bf16[128,2176]{1,0:T(8,128)(2,1)S(1)}, bf16[128,2176]{1,0:T(8,128)(2,1)S(1)}, u32[]{:S(2)}, u32[]{:S(2)}) collective-permute-start(bf16[128,2176]{1,0:T(8,128)(2,1)S(1)} %collective-permute-done.refs_0_), channel_id=1, source_target_pairs={{0,208},{32,96},{64,0},{96,160},{128,64},{160,224},{192,128},{224,... | collective-permute-start | bytes 1671176 | tf_op jit(solution)/shard_map/ppermute | solution.py:33
  19.3 13.4 %collective-permute-start.2 = (bf16[128,2176]{1,0:T(8,128)(2,1)S(1)}, bf16[128,2176]{1,0:T(8,128)(2,1)S(1)}, u32[]{:S(2)}, u32[]{:S(2)}) collective-permute-start(bf16[128,2176]{1,0:T(8,128)(2,1)S(1)} %shard_map.59.refs_0_), channel_id=1, source_target_pairs={{0,64},{32,240},{64,128},{96,32},{128,192},{160,96},{192,16},{224,... | collective-permute-start | bytes 1671176 | tf_op jit(solution)/shard_map/ppermute | solution.py:33
  22.2 1.2 %collective-permute-start.5 = (f32[2,128]{1,0:T(2,128)S(1)}, f32[2,128]{1,0:T(2,128)S(1)}, u32[]{:S(2)}, u32[]{:S(2)}) collective-permute-start(f32[2,128]{1,0:T(2,128)S(1)} %pad_maximum_fusion.1), channel_id=1, source_target_pairs={{0,32},{32,0},{64,96},{96,64},{128,160},{160,128},{192,224},{224,1... | collective-permute-start | bytes 3080 | tf_op jit(solution)/shard_map/ppermute | solution.py:33
  23.4 9.3 %collective-permute-start.6 = (f32[1,128]{1,0:T(1,128)S(1)}, f32[1,128]{1,0:T(1,128)S(1)}, u32[]{:S(2)}, u32[]{:S(2)}) collective-permute-start(f32[1,128]{1,0:T(1,128)S(1)} %slice.16), channel_id=1, source_target_pairs={{0,64},{32,240},{64,128},{96,32},{128,192},{160,96},{192,16},{224,... | collective-permute-start | bytes 1544 | tf_op jit(solution)/shard_map/ppermute | solution.py:33
  32.7 2.0 %collective-permute-start.7 = (bf16[128,2176]{1,0:T(8,128)(2,1)S(1)}, bf16[128,2176]{1,0:T(8,128)(2,1)S(1)}, u32[]{:S(2)}, u32[]{:S(2)}) collective-permute-start(bf16[128,2176]{1,0:T(8,128)(2,1)S(1)} %collective-permute-done.2.refs_0_), channel_id=1, source_target_pairs={{0,32},{32,0},{64,96},{96,64},{128,160},{160,128},{192,224},{224,1... | collective-permute-start | bytes 1671176 | tf_op jit(solution)/shard_map/ppermute | solution.py:33
  32.8 2.7 %collective-permute-start.8 = (bf16[128,2176]{1,0:T(8,128)(2,1)S(1)}, bf16[128,2176]{1,0:T(8,128)(2,1)S(1)}, u32[]{:S(2)}, u32[]{:S(2)}) collective-permute-start(bf16[128,2176]{1,0:T(8,128)(2,1)S(1)} %collective-permute-done.3.refs_1_), channel_id=1, source_target_pairs={{0,32},{32,0},{64,96},{96,64},{128,160},{160,128},{192,224},{224,1... | collective-permute-start | bytes 1671176 | tf_op jit(solution)/shard_map/ppermute | solution.py:33
  40.6 4.2 %collective-permute-start.10 = (f32[1,2048]{1,0:T(1,128)S(1)}, f32[1,2048]{1,0:T(1,128)S(1)}, u32[]{:S(2)}, u32[]{:S(2)}) collective-permute-start(f32[1,2048]{1,0:T(1,128)S(1)} %get-tuple-element.40), channel_id=1, source_target_pairs={{0,4},{32,36},{64,68},{96,100},{128,132},{160,164},{192,196},{224,... | collective-permute-start | bytes 24584 | tf_op jit(solution)/shard_map/ppermute | solution.py:33
  41.2 3.6 %collective-permute-start.9 = (f32[1,256]{1,0:T(1,128)S(1)}, f32[1,256]{1,0:T(1,128)S(1)}, u32[]{:S(2)}, u32[]{:S(2)}) collective-permute-start(f32[1,256]{1,0:T(1,128)S(1)} %get-tuple-element.39), channel_id=1, source_target_pairs={{0,32},{32,0},{64,96},{96,64},{128,160},{160,128},{192,224},{224,1... | collective-permute-start | bytes 3080 | tf_op jit(solution)/shard_map/ppermute | solution.py:33
  41.3 7.9 %collective-permute-start.13 = (f32[1,2048]{1,0:T(1,128)S(1)}, f32[1,2048]{1,0:T(1,128)S(1)}, u32[]{:S(2)}, u32[]{:S(2)}) collective-permute-start(f32[1,2048]{1,0:T(1,128)S(1)} %get-tuple-element.40), channel_id=1, source_target_pairs={{0,12},{32,44},{64,76},{96,108},{128,140},{160,172},{192,204},{224... | collective-permute-start | bytes 24584 | tf_op jit(solution)/shard_map/ppermute | solution.py:33
  43.4 5.8 %collective-permute-start.12 = (f32[1,2048]{1,0:T(1,128)S(1)}, f32[1,2048]{1,0:T(1,128)S(1)}, u32[]{:S(2)}, u32[]{:S(2)}) collective-permute-start(f32[1,2048]{1,0:T(1,128)S(1)} %get-tuple-element.40), channel_id=1, source_target_pairs={{0,8},{32,40},{64,72},{96,104},{128,136},{160,168},{192,200},{224,... | collective-permute-start | bytes 24584 | tf_op jit(solution)/shard_map/ppermute | solution.py:33
  44.8 11.0 %collective-permute-start.15 = (f32[1,384]{1,0:T(1,128)S(1)}, f32[1,384]{1,0:T(1,128)S(1)}, u32[]{:S(2)}, u32[]{:S(2)}) collective-permute-start(f32[1,384]{1,0:T(1,128)S(1)} %pad_maximum_fusion), channel_id=1, source_target_pairs={{0,2},{32,34},{64,66},{96,98},{128,130},{160,162},{192,194},{224,2... | collective-permute-start | bytes 4616 | tf_op jit(solution)/shard_map/ppermute | solution.py:33
  48.1 7.7 %collective-permute-start.16 = (f32[1,384]{1,0:T(1,128)S(1)}, f32[1,384]{1,0:T(1,128)S(1)}, u32[]{:S(2)}, u32[]{:S(2)}) collective-permute-start(f32[1,384]{1,0:T(1,128)S(1)} %pad_maximum_fusion), channel_id=1, source_target_pairs={{0,3},{32,35},{64,67},{96,99},{128,131},{160,163},{192,195},{224,2... | collective-permute-start | bytes 4616 | tf_op jit(solution)/shard_map/ppermute | solution.py:33
  49.2 3.6 %collective-permute-start.11 = (f32[1,384]{1,0:T(1,128)S(1)}, f32[1,384]{1,0:T(1,128)S(1)}, u32[]{:S(2)}, u32[]{:S(2)}) collective-permute-start(f32[1,384]{1,0:T(1,128)S(1)} %pad_maximum_fusion), channel_id=1, source_target_pairs={{0,1},{32,33},{64,65},{96,97},{128,129},{160,161},{192,193},{224,2... | collective-permute-start | bytes 4616 | tf_op jit(solution)/shard_map/ppermute | solution.py:33
  52.8 8.8 %collective-permute-start.14 = (f32[1,2048]{1,0:T(1,128)S(1)}, f32[1,2048]{1,0:T(1,128)S(1)}, u32[]{:S(2)}, u32[]{:S(2)}) collective-permute-start(f32[1,2048]{1,0:T(1,128)S(1)} %maximum_maximum_fusion), channel_id=1, source_target_pairs={{0,16},{32,48},{64,80},{96,112},{128,144},{160,176},{192,208},{224... | collective-permute-start | bytes 24584 | tf_op jit(solution)/shard_map/ppermute | solution.py:33
  55.9 5.7 %collective-permute-start.18 = (f32[1,128]{1,0:T(1,128)S(1)}, f32[1,128]{1,0:T(1,128)S(1)}, u32[]{:S(2)}, u32[]{:S(2)}) collective-permute-start(f32[1,128]{1,0:T(1,128)S(1)} %get-tuple-element.48), channel_id=1, source_target_pairs={{0,128},{32,176},{64,192},{96,240},{128,16},{160,32},{192,80},{224... | collective-permute-start | bytes 1544 | tf_op jit(solution)/shard_map/ppermute | solution.py:33
  56.4 5.2 %collective-permute-start.17 = (f32[1,128]{1,0:T(1,128)S(1)}, f32[1,128]{1,0:T(1,128)S(1)}, u32[]{:S(2)}, u32[]{:S(2)}) collective-permute-start(f32[1,128]{1,0:T(1,128)S(1)} %get-tuple-element.49), channel_id=1, source_target_pairs={{0,208},{32,96},{64,0},{96,160},{128,64},{160,224},{192,128},{224,... | collective-permute-start | bytes 1544 | tf_op jit(solution)/shard_map/ppermute | solution.py:33

commit v6 on v5

--- a/solution.py
+++ b/solution.py
@@ -164,34 +164,31 @@
 
     own = pack(coefficients, intercepts)
     near = send(own, toward)
+    next_ = send(own, against)
     peer = send(own, over_core)
     top, own_mine, own_other = score([own, peer], old, old, states)
-    near, own, top = fence((near, own, top))
+    near, next_, top = fence((near, next_, top))
     two = send(near, toward)
-    next_ = send(own, against)
-    top, near_mine, near_other = score([near, send(near, over_core)], old, top, states)
-
-    mine = jnp.concatenate([own_mine, near_mine], axis=0)
-    other = jnp.concatenate([own_other, near_other], axis=0)
-    lifts = jnp.maximum(mine, send(other, over_core))
-    held = jnp.maximum(lifts[0:1], send(lifts[1:2], against))
-    next_, two, top, held = fence((next_, two, top, held))
-    blocks = [next_, two, send(next_, over_core), send(two, over_core)]
-    top, mine, other = score(blocks, old, top, states)
-
-    swapped = send(other, over_core)
+    blocks = [near, next_, send(near, over_core), send(next_, over_core)]
+    top, side_mine, side_other = score(blocks, old, top, states)
+    two, top = fence((two, top))
+    top, two_mine, two_other = score([two, send(two, over_core)], old, top, states)
+
+    mine = jnp.concatenate([own_mine, side_mine, two_mine], axis=1)
+    swapped = send(jnp.concatenate([own_other, side_other, two_other], axis=1), over_core)
     for_x = [send(top, over_x(d)) for d in (1, 2, 3)]
     swapped, for_x[0] = fence((swapped, for_x[0]))
-    lifts = jnp.concatenate([held, jnp.maximum(mine, swapped)], axis=1)
+    lifts = jnp.maximum(mine, swapped)
     for_y = [send(lifts, over_y(d)) for d in (1, 2, 3)]
     top = functools.reduce(jnp.maximum, for_x, top)
     for_y[0], top = fence((for_y[0], top))
     lifts = functools.reduce(jnp.maximum, for_y, lifts)
     across = send(top, far)
-    for_z = [send(lifts[:, cuts : 2 * cuts], toward), send(lifts[:, 2 * cuts :], two_back)]
+    split = [lifts[:, k * cuts : (k + 1) * cuts] for k in range(4)]
+    for_z = [send(split[1], against), send(split[2], toward), send(split[3], two_back)]
     across, *for_z = fence((across, *for_z))
     new_values = jnp.maximum(top, across)
-    cut_gaps = functools.reduce(jnp.maximum, for_z, lifts[:, :cuts])
+    cut_gaps = functools.reduce(jnp.maximum, for_z, split[0])
     return new_values[0], cut_gaps[0]
 
 

time: 62.9 us -> 62.2 us (0.989)
  the two profiles are of different devices: /device:TPU:2 before, /device:TPU:6 now
where the time goes in v6:
time: 62.2 us; the launch traced here: 62 us
  starting transfers between devices  26.9 us (43%)
  waiting for transfers between devices  20.6 us (33%)
  Pallas kernels  10.9 us (18%)
  local copies, waits for them, and re-layouts  1.7 us (3%)
  other arithmetic  1.16 us (2%)
  between operations  0.74 us (1%)
    ppermute x18, starting transfers between devices, send(): return lax.ppermute(block, AXES, routes(move))  26.9 us
    ppermute x18, waiting for transfers between devices, send(): return lax.ppermute(block, AXES, routes(move))  20.6 us
    pallas_call x3, Pallas kernels, score(): pl.pallas_call(functools.partial(score_body, tile, tiles, len(blocks)), g...  10.8 us
    unnamed x8, local copies, waits for them, and re-layouts  1.7 us
  transfers between devices with their start and end apart: 18, of which 7 were waited for; matrix products, arithmetic and copies ran while one was open for 0% of the time, Pallas kernels for 13%

profile of v6, /device:TPU:6, one launch (start us, length us, event | category | flops | bytes accessed | tf_op | source)
XLA Modules:
  0.0 62.0 jit_solution(12230842080967999607)
XLA Ops:
  0.6 0.0 copy-start.2
  0.6 1.0 %copy-done.2 = bf16[128,2048]{1,0:T(8,128)(2,1)S(1)} copy-done((bf16[128,2048]{1,0:T(8,128)(2,1)S(1)}, bf16[128,2048]{1,0:T(8,128)(2,1)}, u32[]{:S(2)}) %copy-start.2) | copy-done | bytes 524312
  1.7 0.0 copy-start.3
  1.7 0.7 %copy-done.3 = bf16[128]{0:T(256)(128)(2,1)S(1)} copy-done((bf16[128]{0:T(256)(128)(2,1)S(1)}, bf16[128]{0:T(256)(128)(2,1)}, u32[]{:S(2)}) %copy-start.3) | copy-done | bytes 280
  2.3 0.2 shard_map.59.refs_0_
  2.5 0.1 collective-permute-start
  2.6 5.9 %collective-permute-start.1 = (bf16[128,2176]{1,0:T(8,128)(2,1)S(1)}, bf16[128,2176]{1,0:T(8,128)(2,1)S(1)}, u32[]{:S(2)}, u32[]{:S(2)}) collective-permute-start(bf16[128,2176]{1,0:T(8,128)(2,1)S(1)} %shard_map.59.refs_0_), channel_id=1, source_target_pairs={{0,208},{32,96},{64,0},{96,160},{128,64},{160,224},{192,128},{224,... | collective-permute-start | bytes 1671176 | tf_op jit(solution)/shard_map/ppermute | solution.py:33
  8.6 0.0 collective-permute-start.2
  8.6 0.0 collective-permute-done.refs_1_
  8.6 0.0 copy-done
  8.6 0.0 copy-done.1
  8.6 2.8 %shard_map.60 = (f32[1,2048]{1,0:T(1,128)S(1)}, f32[1,128]{1,0:T(1,128)S(1)}, f32[1,128]{1,0:T(1,128)S(1)}) custom-call(f32[1,2048]{1,0:T(1,128)S(1)} %bitcast.5, f32[1,2048]{1,0:T(1,128)S(1)} %bitcast.6, bf16[2048,2048]{1,0:T(8,128)(2,1)S(1)} %copy-done, bf16[128,2176]{1,0:T(8,128)(2,1)S(1)} %shard_map.59.refs_0_, ...), custom_call_target="tpu_custom_call" | custom-call | flops 2147483648 | bytes 9437184 | tf_op jit(solution)/shard_map/pallas_call | solution.py:141
  11.4 9.6 %collective-permute-done.1.refs_0_ = bf16[128,2176]{1,0:T(8,128)(2,1)S(1)} collective-permute-done((bf16[128,2176]{1,0:T(8,128)(2,1)S(1)}, bf16[128,2176]{1,0:T(8,128)(2,1)S(1)}, u32[]{:S(2)}, u32[]{:S(2)}) %collective-permute-start.1) | collective-permute-done | bytes 557088 | tf_op jit(solution)/shard_map/ppermute | solution.py:33
  21.1 0.7 %collective-permute-done.2.refs_1_ = bf16[128,2176]{1,0:T(8,128)(2,1)S(1)} collective-permute-done((bf16[128,2176]{1,0:T(8,128)(2,1)S(1)}, bf16[128,2176]{1,0:T(8,128)(2,1)S(1)}, u32[]{:S(2)}, u32[]{:S(2)}) %collective-permute-start.2) | collective-permute-done | bytes 557088 | tf_op jit(solution)/shard_map/ppermute | solution.py:33
  21.8 0.0 collective-permute-start.3
  21.8 0.5 collective-permute-start.4
  22.3 3.0 %collective-permute-start.5 = (bf16[128,2176]{1,0:T(8,128)(2,1)S(1)}, bf16[128,2176]{1,0:T(8,128)(2,1)S(1)}, u32[]{:S(2)}, u32[]{:S(2)}) collective-permute-start(bf16[128,2176]{1,0:T(8,128)(2,1)S(1)} %collective-permute-done.1.refs_0_), channel_id=1, source_target_pairs={{0,208},{32,96},{64,0},{96,160},{128,64},{160,224},{192,128},{224,... | collective-permute-start | bytes 1671176 | tf_op jit(solution)/shard_map/ppermute | solution.py:33
  25.3 0.0 collective-permute-done.3.refs_2_
  25.3 0.0 collective-permute-done.4.refs_3_
  25.3 5.1 %shard_map.61 = (f32[1,2048]{1,0:T(1,128)S(1)}, f32[1,256]{1,0:T(1,128)S(1)}, f32[1,256]{1,0:T(1,128)S(1)}) custom-call(f32[1,2048]{1,0:T(1,128)S(1)} %bitcast.7, f32[1,2048]{1,0:T(1,128)S(1)} %get-tuple-element.26.prev, bf16[2048,2048]{1,0:T(8,128)(2,1)S(1)} %copy-done, bf16[128,2176]{1,0:T(8,128)(2,1)S(1)} %collective-permute-done.1.refs_0_, ...), custom_call_target="tpu_custom_call" | custom-call | flops 4294967296 | bytes 10485760 | tf_op jit(solution)/shard_map/pallas_call | solution.py:141
  30.4 1.9 %collective-permute-done.5.refs_0_ = bf16[128,2176]{1,0:T(8,128)(2,1)S(1)} collective-permute-done((bf16[128,2176]{1,0:T(8,128)(2,1)S(1)}, bf16[128,2176]{1,0:T(8,128)(2,1)S(1)}, u32[]{:S(2)}, u32[]{:S(2)}) %collective-permute-start.5) | collective-permute-done | bytes 557088 | tf_op jit(solution)/shard_map/ppermute | solution.py:33
  32.3 0.0 collective-permute-start.6
  32.3 2.0 %collective-permute-done.6.refs_1_ = bf16[128,2176]{1,0:T(8,128)(2,1)S(1)} collective-permute-done((bf16[128,2176]{1,0:T(8,128)(2,1)S(1)}, bf16[128,2176]{1,0:T(8,128)(2,1)S(1)}, u32[]{:S(2)}, u32[]{:S(2)}) %collective-permute-start.6) | collective-permute-done | bytes 557088 | tf_op jit(solution)/shard_map/ppermute | solution.py:33
  34.3 2.8 %shard_map.62 = (f32[1,2048]{1,0:T(1,128)S(1)}, f32[1,128]{1,0:T(1,128)S(1)}, f32[1,128]{1,0:T(1,128)S(1)}) custom-call(f32[1,2048]{1,0:T(1,128)S(1)} %bitcast.8, f32[1,2048]{1,0:T(1,128)S(1)} %get-tuple-element.31.prev, bf16[2048,2048]{1,0:T(8,128)(2,1)S(1)} %copy-done, bf16[128,2176]{1,0:T(8,128)(2,1)S(1)} %collective-permute-done.5.refs_0_, ...), custom_call_target="tpu_custom_call" | custom-call | flops 2147483648 | bytes 9437184 | tf_op jit(solution)/shard_map/pallas_call | solution.py:141
  37.1 0.9 %collective-permute-start.8 = (f32[1,2048]{1,0:T(1,128)S(1)}, f32[1,2048]{1,0:T(1,128)S(1)}, u32[]{:S(2)}, u32[]{:S(2)}) collective-permute-start(f32[1,2048]{1,0:T(1,128)S(1)} %get-tuple-element.37), channel_id=1, source_target_pairs={{0,4},{32,36},{64,68},{96,100},{128,132},{160,164},{192,196},{224,... | collective-permute-start | bytes 24584 | tf_op jit(solution)/shard_map/ppermute | solution.py:33
  38.0 0.0 collective-permute-start.7
  38.0 1.2 %collective-permute-start.10 = (f32[1,2048]{1,0:T(1,128)S(1)}, f32[1,2048]{1,0:T(1,128)S(1)}, u32[]{:S(2)}, u32[]{:S(2)}) collective-permute-start(f32[1,2048]{1,0:T(1,128)S(1)} %get-tuple-element.37), channel_id=1, source_target_pairs={{0,8},{32,40},{64,72},{96,104},{128,136},{160,168},{192,200},{224,... | collective-permute-start | bytes 24584 | tf_op jit(solution)/shard_map/ppermute | solution.py:33
  39.2 2.8 %collective-permute-start.11 = (f32[1,2048]{1,0:T(1,128)S(1)}, f32[1,2048]{1,0:T(1,128)S(1)}, u32[]{:S(2)}, u32[]{:S(2)}) collective-permute-start(f32[1,2048]{1,0:T(1,128)S(1)} %get-tuple-element.37), channel_id=1, source_target_pairs={{0,12},{32,44},{64,76},{96,108},{128,140},{160,172},{192,204},{224... | collective-permute-start | bytes 24584 | tf_op jit(solution)/shard_map/ppermute | solution.py:33
  42.0 0.0 collective-permute-done.7
  42.0 0.0 collective-permute-done.8
  42.0 1.7 %collective-permute-start.9 = (f32[1,512]{1,0:T(1,128)S(1)}, f32[1,512]{1,0:T(1,128)S(1)}, u32[]{:S(2)}, u32[]{:S(2)}) collective-permute-start(f32[1,512]{1,0:T(1,128)S(1)} %maximum_maximum_fusion.1), channel_id=1, source_target_pairs={{0,1},{32,33},{64,65},{96,97},{128,129},{160,161},{192,193},{224,2... | collective-permute-start | bytes 6152 | tf_op jit(solution)/shard_map/ppermute | solution.py:33
  43.7 2.9 %collective-permute-start.13 = (f32[1,512]{1,0:T(1,128)S(1)}, f32[1,512]{1,0:T(1,128)S(1)}, u32[]{:S(2)}, u32[]{:S(2)}) collective-permute-start(f32[1,512]{1,0:T(1,128)S(1)} %maximum_maximum_fusion.1), channel_id=1, source_target_pairs={{0,2},{32,34},{64,66},{96,98},{128,130},{160,162},{192,194},{224,2... | collective-permute-start | bytes 6152 | tf_op jit(solution)/shard_map/ppermute | solution.py:33
  46.6 0.2 collective-permute-start.14
  46.8 0.0 collective-permute-done.10
  46.8 0.0 collective-permute-done.11
  46.8 0.0 collective-permute-done.9
  46.8 3.9 %collective-permute-start.12 = (f32[1,2048]{1,0:T(1,128)S(1)}, f32[1,2048]{1,0:T(1,128)S(1)}, u32[]{:S(2)}, u32[]{:S(2)}) collective-permute-start(f32[1,2048]{1,0:T(1,128)S(1)} %maximum_maximum_fusion), channel_id=1, source_target_pairs={{0,16},{32,48},{64,80},{96,112},{128,144},{160,176},{192,208},{224... | collective-permute-start | bytes 24584 | tf_op jit(solution)/shard_map/ppermute | solution.py:33
  50.7 0.0 collective-permute-done.13
  50.7 0.6 %collective-permute-done.14 = f32[1,512]{1,0:T(1,128)S(1)} collective-permute-done((f32[1,512]{1,0:T(1,128)S(1)}, f32[1,512]{1,0:T(1,128)S(1)}, u32[]{:S(2)}, u32[]{:S(2)}) %collective-permute-start.14) | collective-permute-done | bytes 2080 | tf_op jit(solution)/shard_map/ppermute | solution.py:33
  51.4 0.1 collective-permute-start.15
  51.5 3.8 %collective-permute-start.16 = (f32[1,128]{1,0:T(1,128)S(1)}, f32[1,128]{1,0:T(1,128)S(1)}, u32[]{:S(2)}, u32[]{:S(2)}) collective-permute-start(f32[1,128]{1,0:T(1,128)S(1)} %get-tuple-element.47), channel_id=1, source_target_pairs={{0,208},{32,96},{64,0},{96,160},{128,64},{160,224},{192,128},{224,... | collective-permute-start | bytes 1544 | tf_op jit(solution)/shard_map/ppermute | solution.py:33
  55.2 0.0 collective-permute-start.17
  55.2 1.4 %collective-permute-done.15 = f32[1,128]{1,0:T(1,128)S(1)} collective-permute-done((f32[1,128]{1,0:T(1,128)S(1)}, f32[1,128]{1,0:T(1,128)S(1)}, u32[]{:S(2)}, u32[]{:S(2)}) %collective-permute-start.15) | collective-permute-done | bytes 544 | tf_op jit(solution)/shard_map/ppermute | solution.py:33
  56.7 0.0 collective-permute-done.16
  56.7 4.2 %collective-permute-done.17 = f32[1,128]{1,0:T(1,128)S(1)} collective-permute-done((f32[1,128]{1,0:T(1,128)S(1)}, f32[1,128]{1,0:T(1,128)S(1)}, u32[]{:S(2)}, u32[]{:S(2)}) %collective-permute-start.17) | collective-permute-done | bytes 544 | tf_op jit(solution)/shard_map/ppermute | solution.py:33
  60.9 0.0 collective-permute-done.12
  60.9 0.6 max.40
  61.5 0.5 fusion.2
  (7 shorter events, 0.0 us)
Async XLA Ops:
  0.6 1.0 %copy-start.2 = (bf16[128,2048]{1,0:T(8,128)(2,1)S(1)}, bf16[128,2048]{1,0:T(8,128)(2,1)}, u32[]{:S(2)}) copy-start(bf16[128,2048]{1,0:T(8,128)(2,1)} %coefficients.1) | copy-start | bytes 1572868
  1.7 0.7 %copy-start.3 = (bf16[128]{0:T(256)(128)(2,1)S(1)}, bf16[128]{0:T(256)(128)(2,1)}, u32[]{:S(2)}) copy-start(bf16[128]{0:T(256)(128)(2,1)} %param.5) | copy-start | bytes 772
  2.3 6.2 %copy-start = (bf16[2048,2048]{1,0:T(8,128)(2,1)S(1)}, bf16[2048,2048]{1,0:T(8,128)(2,1)}, u32[]{:S(2)}) copy-start(bf16[2048,2048]{1,0:T(8,128)(2,1)} %states.5) | copy-start | bytes 25165828
  2.3 6.2 %copy-start.1 = (f32[2048]{0:T(1024)S(1)}, f32[2048]{0:T(1024)}, u32[]{:S(2)}) copy-start(f32[2048]{0:T(1024)} %param.7) | copy-start | bytes 24580
  2.5 6.0 %collective-permute-start = (bf16[128,2176]{1,0:T(8,128)(2,1)S(1)}, bf16[128,2176]{1,0:T(8,128)(2,1)S(1)}, u32[]{:S(2)}, u32[]{:S(2)}) collective-permute-start(bf16[128,2176]{1,0:T(8,128)(2,1)S(1)} %shard_map.59.refs_0_), channel_id=1, source_target_pairs={{0,32},{32,0},{64,96},{96,64},{128,160},{160,128},{192,224},{224,1... | collective-permute-start | bytes 1671176 | tf_op jit(solution)/shard_map/ppermute | solution.py:33
  2.6 18.4 %collective-permute-start.1 = (bf16[128,2176]{1,0:T(8,128)(2,1)S(1)}, bf16[128,2176]{1,0:T(8,128)(2,1)S(1)}, u32[]{:S(2)}, u32[]{:S(2)}) collective-permute-start(bf16[128,2176]{1,0:T(8,128)(2,1)S(1)} %shard_map.59.refs_0_), channel_id=1, source_target_pairs={{0,208},{32,96},{64,0},{96,160},{128,64},{160,224},{192,128},{224,... | collective-permute-start | bytes 1671176 | tf_op jit(solution)/shard_map/ppermute | solution.py:33
  8.6 13.2 %collective-permute-start.2 = (bf16[128,2176]{1,0:T(8,128)(2,1)S(1)}, bf16[128,2176]{1,0:T(8,128)(2,1)S(1)}, u32[]{:S(2)}, u32[]{:S(2)}) collective-permute-start(bf16[128,2176]{1,0:T(8,128)(2,1)S(1)} %shard_map.59.refs_0_), channel_id=1, source_target_pairs={{0,64},{32,240},{64,128},{96,32},{128,192},{160,96},{192,16},{224,... | collective-permute-start | bytes 1671176 | tf_op jit(solution)/shard_map/ppermute | solution.py:33
  21.8 3.5 %collective-permute-start.3 = (bf16[128,2176]{1,0:T(8,128)(2,1)S(1)}, bf16[128,2176]{1,0:T(8,128)(2,1)S(1)}, u32[]{:S(2)}, u32[]{:S(2)}) collective-permute-start(bf16[128,2176]{1,0:T(8,128)(2,1)S(1)} %collective-permute-done.1.refs_0_), channel_id=1, source_target_pairs={{0,32},{32,0},{64,96},{96,64},{128,160},{160,128},{192,224},{224,1... | collective-permute-start | bytes 1671176 | tf_op jit(solution)/shard_map/ppermute | solution.py:33
  21.8 3.5 %collective-permute-start.4 = (bf16[128,2176]{1,0:T(8,128)(2,1)S(1)}, bf16[128,2176]{1,0:T(8,128)(2,1)S(1)}, u32[]{:S(2)}, u32[]{:S(2)}) collective-permute-start(bf16[128,2176]{1,0:T(8,128)(2,1)S(1)} %collective-permute-done.2.refs_1_), channel_id=1, source_target_pairs={{0,32},{32,0},{64,96},{96,64},{128,160},{160,128},{192,224},{224,1... | collective-permute-start | bytes 1671176 | tf_op jit(solution)/shard_map/ppermute | solution.py:33
  22.3 10.0 %collective-permute-start.5 = (bf16[128,2176]{1,0:T(8,128)(2,1)S(1)}, bf16[128,2176]{1,0:T(8,128)(2,1)S(1)}, u32[]{:S(2)}, u32[]{:S(2)}) collective-permute-start(bf16[128,2176]{1,0:T(8,128)(2,1)S(1)} %collective-permute-done.1.refs_0_), channel_id=1, source_target_pairs={{0,208},{32,96},{64,0},{96,160},{128,64},{160,224},{192,128},{224,... | collective-permute-start | bytes 1671176 | tf_op jit(solution)/shard_map/ppermute | solution.py:33
  32.3 2.0 %collective-permute-start.6 = (bf16[128,2176]{1,0:T(8,128)(2,1)S(1)}, bf16[128,2176]{1,0:T(8,128)(2,1)S(1)}, u32[]{:S(2)}, u32[]{:S(2)}) collective-permute-start(bf16[128,2176]{1,0:T(8,128)(2,1)S(1)} %collective-permute-done.5.refs_0_), channel_id=1, source_target_pairs={{0,32},{32,0},{64,96},{96,64},{128,160},{160,128},{192,224},{224,1... | collective-permute-start | bytes 1671176 | tf_op jit(solution)/shard_map/ppermute | solution.py:33
  37.1 4.9 %collective-permute-start.8 = (f32[1,2048]{1,0:T(1,128)S(1)}, f32[1,2048]{1,0:T(1,128)S(1)}, u32[]{:S(2)}, u32[]{:S(2)}) collective-permute-start(f32[1,2048]{1,0:T(1,128)S(1)} %get-tuple-element.37), channel_id=1, source_target_pairs={{0,4},{32,36},{64,68},{96,100},{128,132},{160,164},{192,196},{224,... | collective-permute-start | bytes 24584 | tf_op jit(solution)/shard_map/ppermute | solution.py:33
  38.0 4.0 %collective-permute-start.7 = (f32[1,512]{1,0:T(1,128)S(1)}, f32[1,512]{1,0:T(1,128)S(1)}, u32[]{:S(2)}, u32[]{:S(2)}) collective-permute-start(f32[1,512]{1,0:T(1,128)S(1)} %pad_maximum_fusion), channel_id=1, source_target_pairs={{0,32},{32,0},{64,96},{96,64},{128,160},{160,128},{192,224},{224,1... | collective-permute-start | bytes 6152 | tf_op jit(solution)/shard_map/ppermute | solution.py:33
  38.0 8.8 %collective-permute-start.10 = (f32[1,2048]{1,0:T(1,128)S(1)}, f32[1,2048]{1,0:T(1,128)S(1)}, u32[]{:S(2)}, u32[]{:S(2)}) collective-permute-start(f32[1,2048]{1,0:T(1,128)S(1)} %get-tuple-element.37), channel_id=1, source_target_pairs={{0,8},{32,40},{64,72},{96,104},{128,136},{160,168},{192,200},{224,... | collective-permute-start | bytes 24584 | tf_op jit(solution)/shard_map/ppermute | solution.py:33
  39.2 7.6 %collective-permute-start.11 = (f32[1,2048]{1,0:T(1,128)S(1)}, f32[1,2048]{1,0:T(1,128)S(1)}, u32[]{:S(2)}, u32[]{:S(2)}) collective-permute-start(f32[1,2048]{1,0:T(1,128)S(1)} %get-tuple-element.37), channel_id=1, source_target_pairs={{0,12},{32,44},{64,76},{96,108},{128,140},{160,172},{192,204},{224... | collective-permute-start | bytes 24584 | tf_op jit(solution)/shard_map/ppermute | solution.py:33
  42.0 4.8 %collective-permute-start.9 = (f32[1,512]{1,0:T(1,128)S(1)}, f32[1,512]{1,0:T(1,128)S(1)}, u32[]{:S(2)}, u32[]{:S(2)}) collective-permute-start(f32[1,512]{1,0:T(1,128)S(1)} %maximum_maximum_fusion.1), channel_id=1, source_target_pairs={{0,1},{32,33},{64,65},{96,97},{128,129},{160,161},{192,193},{224,2... | collective-permute-start | bytes 6152 | tf_op jit(solution)/shard_map/ppermute | solution.py:33
  43.7 7.0 %collective-permute-start.13 = (f32[1,512]{1,0:T(1,128)S(1)}, f32[1,512]{1,0:T(1,128)S(1)}, u32[]{:S(2)}, u32[]{:S(2)}) collective-permute-start(f32[1,512]{1,0:T(1,128)S(1)} %maximum_maximum_fusion.1), channel_id=1, source_target_pairs={{0,2},{32,34},{64,66},{96,98},{128,130},{160,162},{192,194},{224,2... | collective-permute-start | bytes 6152 | tf_op jit(solution)/shard_map/ppermute | solution.py:33
  46.6 4.8 %collective-permute-start.14 = (f32[1,512]{1,0:T(1,128)S(1)}, f32[1,512]{1,0:T(1,128)S(1)}, u32[]{:S(2)}, u32[]{:S(2)}) collective-permute-start(f32[1,512]{1,0:T(1,128)S(1)} %maximum_maximum_fusion.1), channel_id=1, source_target_pairs={{0,3},{32,35},{64,67},{96,99},{128,131},{160,163},{192,195},{224,2... | collective-permute-start | bytes 6152 | tf_op jit(solution)/shard_map/ppermute | solution.py:33
  46.8 14.1 %collective-permute-start.12 = (f32[1,2048]{1,0:T(1,128)S(1)}, f32[1,2048]{1,0:T(1,128)S(1)}, u32[]{:S(2)}, u32[]{:S(2)}) collective-permute-start(f32[1,2048]{1,0:T(1,128)S(1)} %maximum_maximum_fusion), channel_id=1, source_target_pairs={{0,16},{32,48},{64,80},{96,112},{128,144},{160,176},{192,208},{224... | collective-permute-start | bytes 24584 | tf_op jit(solution)/shard_map/ppermute | solution.py:33
  51.4 5.3 %collective-permute-start.15 = (f32[1,128]{1,0:T(1,128)S(1)}, f32[1,128]{1,0:T(1,128)S(1)}, u32[]{:S(2)}, u32[]{:S(2)}) collective-permute-start(f32[1,128]{1,0:T(1,128)S(1)} %get-tuple-element.48), channel_id=1, source_target_pairs={{0,64},{32,240},{64,128},{96,32},{128,192},{160,96},{192,16},{224,... | collective-permute-start | bytes 1544 | tf_op jit(solution)/shard_map/ppermute | solution.py:33
  51.5 5.2 %collective-permute-start.16 = (f32[1,128]{1,0:T(1,128)S(1)}, f32[1,128]{1,0:T(1,128)S(1)}, u32[]{:S(2)}, u32[]{:S(2)}) collective-permute-start(f32[1,128]{1,0:T(1,128)S(1)} %get-tuple-element.47), channel_id=1, source_target_pairs={{0,208},{32,96},{64,0},{96,160},{128,64},{160,224},{192,128},{224,... | collective-permute-start | bytes 1544 | tf_op jit(solution)/shard_map/ppermute | solution.py:33
  55.2 5.7 %collective-permute-start.17 = (f32[1,128]{1,0:T(1,128)S(1)}, f32[1,128]{1,0:T(1,128)S(1)}, u32[]{:S(2)}, u32[]{:S(2)}) collective-permute-start(f32[1,128]{1,0:T(1,128)S(1)} %get-tuple-element.46), channel_id=1, source_target_pairs={{0,128},{32,176},{64,192},{96,240},{128,16},{160,32},{192,80},{224... | collective-permute-start | bytes 1544 | tf_op jit(solution)/shard_map/ppermute | solution.py:33

commit v7 on v6

--- a/solution.py
+++ b/solution.py
@@ -171,24 +171,28 @@
     two = send(near, toward)
     blocks = [near, next_, send(near, over_core), send(next_, over_core)]
     top, side_mine, side_other = score(blocks, old, top, states)
-    two, top = fence((two, top))
+
+    mine = jnp.concatenate([own_mine, side_mine], axis=1)
+    lifts = jnp.maximum(mine, send(jnp.concatenate([own_other, side_other], axis=1), over_core))
+    two, top, lifts = fence((two, top, lifts))
+    split = [lifts[:, k * cuts : (k + 1) * cuts] for k in range(3)]
+    back = [send(split[1], against), send(split[2], toward)]
     top, two_mine, two_other = score([two, send(two, over_core)], old, top, states)
 
-    mine = jnp.concatenate([own_mine, side_mine, two_mine], axis=1)
-    swapped = send(jnp.concatenate([own_other, side_other, two_other], axis=1), over_core)
+    swapped = send(two_other, over_core)
     for_x = [send(top, over_x(d)) for d in (1, 2, 3)]
     swapped, for_x[0] = fence((swapped, for_x[0]))
-    lifts = jnp.maximum(mine, swapped)
+    held = functools.reduce(jnp.maximum, back, split[0])
+    lifts = jnp.concatenate([held, jnp.maximum(two_mine, swapped)], axis=1)
     for_y = [send(lifts, over_y(d)) for d in (1, 2, 3)]
     top = functools.reduce(jnp.maximum, for_x, top)
     for_y[0], top = fence((for_y[0], top))
     lifts = functools.reduce(jnp.maximum, for_y, lifts)
     across = send(top, far)
-    split = [lifts[:, k * cuts : (k + 1) * cuts] for k in range(4)]
-    for_z = [send(split[1], against), send(split[2], toward), send(split[3], two_back)]
-    across, *for_z = fence((across, *for_z))
+    returned = send(lifts[:, cuts:], two_back)
+    across, returned = fence((across, returned))
     new_values = jnp.maximum(top, across)
-    cut_gaps = functools.reduce(jnp.maximum, for_z, split[0])
+    cut_gaps = jnp.maximum(returned, lifts[:, :cuts])
     return new_values[0], cut_gaps[0]
 
 

time: 62.2 us -> 61.8 us (level)
  the two profiles are of different devices: /device:TPU:6 before, /device:TPU:2 now
where the time goes in v7:
time: 61.8 us; the launch traced here: 61.6 us
  starting transfers between devices  26.9 us (44%)
  waiting for transfers between devices  20.2 us (33%)
  Pallas kernels  11 us (18%)
  local copies, waits for them, and re-layouts  1.7 us (3%)
  other arithmetic  1.17 us (2%)
  between operations  0.75 us (1%)
    ppermute x19, starting transfers between devices, send(): return lax.ppermute(block, AXES, routes(move))  26.9 us
    ppermute x19, waiting for transfers between devices, send(): return lax.ppermute(block, AXES, routes(move))  20.2 us
    pallas_call x3, Pallas kernels, score(): pl.pallas_call(functools.partial(score_body, tile, tiles, len(blocks)), g...  10.8 us
    unnamed x8, local copies, waits for them, and re-layouts  1.7 us
  transfers between devices with their start and end apart: 19, of which 6 were waited for; matrix products, arithmetic and copies ran while one was open for 0% of the time, Pallas kernels for 17%

profile of v7, /device:TPU:2, one launch (start us, length us, event | category | flops | bytes accessed | tf_op | source)
XLA Modules:
  0.0 61.6 jit_solution(11662381812297391099)
XLA Ops:
  0.6 0.0 copy-start.2
  0.6 1.0 %copy-done.2 = bf16[128,2048]{1,0:T(8,128)(2,1)S(1)} copy-done((bf16[128,2048]{1,0:T(8,128)(2,1)S(1)}, bf16[128,2048]{1,0:T(8,128)(2,1)}, u32[]{:S(2)}) %copy-start.2) | copy-done | bytes 524312
  1.7 0.7 %copy-done.3 = bf16[128]{0:T(256)(128)(2,1)S(1)} copy-done((bf16[128]{0:T(256)(128)(2,1)S(1)}, bf16[128]{0:T(256)(128)(2,1)}, u32[]{:S(2)}) %copy-start.3) | copy-done | bytes 280
  2.3 0.2 shard_map.59.refs_0_
  2.5 0.1 collective-permute-start.2
  2.6 2.0 %collective-permute-start.1 = (bf16[128,2176]{1,0:T(8,128)(2,1)S(1)}, bf16[128,2176]{1,0:T(8,128)(2,1)S(1)}, u32[]{:S(2)}, u32[]{:S(2)}) collective-permute-start(bf16[128,2176]{1,0:T(8,128)(2,1)S(1)} %shard_map.59.refs_0_), channel_id=1, source_target_pairs={{0,64},{32,240},{64,128},{96,32},{128,192},{160,96},{192,16},{224,... | collective-permute-start | bytes 1671176 | tf_op jit(solution)/shard_map/ppermute | solution.py:33
  4.6 4.0 %collective-permute-start = (bf16[128,2176]{1,0:T(8,128)(2,1)S(1)}, bf16[128,2176]{1,0:T(8,128)(2,1)S(1)}, u32[]{:S(2)}, u32[]{:S(2)}) collective-permute-start(bf16[128,2176]{1,0:T(8,128)(2,1)S(1)} %shard_map.59.refs_0_), channel_id=1, source_target_pairs={{0,208},{32,96},{64,0},{96,160},{128,64},{160,224},{192,128},{224,... | collective-permute-start | bytes 1671176 | tf_op jit(solution)/shard_map/ppermute | solution.py:33
  8.7 0.0 collective-permute-done.2.refs_1_
  8.7 0.0 copy-done
  8.7 2.8 %shard_map.60 = (f32[1,2048]{1,0:T(1,128)S(1)}, f32[1,128]{1,0:T(1,128)S(1)}, f32[1,128]{1,0:T(1,128)S(1)}) custom-call(f32[1,2048]{1,0:T(1,128)S(1)} %bitcast.5, f32[1,2048]{1,0:T(1,128)S(1)} %bitcast.6, bf16[2048,2048]{1,0:T(8,128)(2,1)S(1)} %copy-done, bf16[128,2176]{1,0:T(8,128)(2,1)S(1)} %shard_map.59.refs_0_, ...), custom_call_target="tpu_custom_call" | custom-call | flops 2147483648 | bytes 9437184 | tf_op jit(solution)/shard_map/pallas_call | solution.py:141
  11.5 8.1 %collective-permute-done.1.refs_1_ = bf16[128,2176]{1,0:T(8,128)(2,1)S(1)} collective-permute-done((bf16[128,2176]{1,0:T(8,128)(2,1)S(1)}, bf16[128,2176]{1,0:T(8,128)(2,1)S(1)}, u32[]{:S(2)}, u32[]{:S(2)}) %collective-permute-start.1) | collective-permute-done | bytes 557088 | tf_op jit(solution)/shard_map/ppermute | solution.py:33
  19.6 1.5 %collective-permute-done.refs_0_ = bf16[128,2176]{1,0:T(8,128)(2,1)S(1)} collective-permute-done((bf16[128,2176]{1,0:T(8,128)(2,1)S(1)}, bf16[128,2176]{1,0:T(8,128)(2,1)S(1)}, u32[]{:S(2)}, u32[]{:S(2)}) %collective-permute-start) | collective-permute-done | bytes 557088 | tf_op jit(solution)/shard_map/ppermute | solution.py:33
  21.0 0.8 %collective-permute-start.5 = (bf16[128,2176]{1,0:T(8,128)(2,1)S(1)}, bf16[128,2176]{1,0:T(8,128)(2,1)S(1)}, u32[]{:S(2)}, u32[]{:S(2)}) collective-permute-start(bf16[128,2176]{1,0:T(8,128)(2,1)S(1)} %collective-permute-done.1.refs_1_), channel_id=1, source_target_pairs={{0,32},{32,0},{64,96},{96,64},{128,160},{160,128},{192,224},{224,1... | collective-permute-start | bytes 1671176 | tf_op jit(solution)/shard_map/ppermute | solution.py:33
  21.9 0.0 collective-permute-start.4
  21.9 3.4 %collective-permute-start.3 = (bf16[128,2176]{1,0:T(8,128)(2,1)S(1)}, bf16[128,2176]{1,0:T(8,128)(2,1)S(1)}, u32[]{:S(2)}, u32[]{:S(2)}) collective-permute-start(bf16[128,2176]{1,0:T(8,128)(2,1)S(1)} %collective-permute-done.refs_0_), channel_id=1, source_target_pairs={{0,208},{32,96},{64,0},{96,160},{128,64},{160,224},{192,128},{224,... | collective-permute-start | bytes 1671176 | tf_op jit(solution)/shard_map/ppermute | solution.py:33
  25.2 0.0 collective-permute-done.5.refs_3_
  25.2 0.0 collective-permute-done.4.refs_2_
  25.2 5.1 %shard_map.61 = (f32[1,2048]{1,0:T(1,128)S(1)}, f32[1,256]{1,0:T(1,128)S(1)}, f32[1,256]{1,0:T(1,128)S(1)}) custom-call(f32[1,2048]{1,0:T(1,128)S(1)} %bitcast.7, f32[1,2048]{1,0:T(1,128)S(1)} %get-tuple-element.25.prev, bf16[2048,2048]{1,0:T(8,128)(2,1)S(1)} %copy-done, bf16[128,2176]{1,0:T(8,128)(2,1)S(1)} %collective-permute-done.refs_0_, ...), custom_call_target="tpu_custom_call" | custom-call | flops 4294967296 | bytes 10485760 | tf_op jit(solution)/shard_map/pallas_call | solution.py:141
  30.4 0.1 collective-permute-start.6
  30.5 1.1 %collective-permute-done.6 = f32[1,384]{1,0:T(1,128)S(1)} collective-permute-done((f32[1,384]{1,0:T(1,128)S(1)}, f32[1,384]{1,0:T(1,128)S(1)}, u32[]{:S(2)}, u32[]{:S(2)}) %collective-permute-start.6) | collective-permute-done | bytes 1568 | tf_op jit(solution)/shard_map/ppermute | solution.py:33
  31.6 0.7 %collective-permute-done.3.refs_0_ = bf16[128,2176]{1,0:T(8,128)(2,1)S(1)} collective-permute-done((bf16[128,2176]{1,0:T(8,128)(2,1)S(1)}, bf16[128,2176]{1,0:T(8,128)(2,1)S(1)}, u32[]{:S(2)}, u32[]{:S(2)}) %collective-permute-start.3) | collective-permute-done | bytes 557088 | tf_op jit(solution)/shard_map/ppermute | solution.py:33
  32.3 0.0 collective-permute-start.9
  32.3 0.0 collective-permute-start.7
  32.3 3.8 %collective-permute-start.8 = (f32[1,128]{1,0:T(1,128)S(1)}, f32[1,128]{1,0:T(1,128)S(1)}, u32[]{:S(2)}, u32[]{:S(2)}) collective-permute-start(f32[1,128]{1,0:T(1,128)S(1)} %get-tuple-element.45), channel_id=1, source_target_pairs={{0,208},{32,96},{64,0},{96,160},{128,64},{160,224},{192,128},{224,... | collective-permute-start | bytes 1544 | tf_op jit(solution)/shard_map/ppermute | solution.py:33
  36.1 0.0 collective-permute-done.9.refs_1_
  36.1 2.8 %shard_map.62 = (f32[1,2048]{1,0:T(1,128)S(1)}, f32[1,128]{1,0:T(1,128)S(1)}, f32[1,128]{1,0:T(1,128)S(1)}) custom-call(f32[1,2048]{1,0:T(1,128)S(1)} %bitcast.8, f32[1,2048]{1,0:T(1,128)S(1)} %get-tuple-element.33.prev, bf16[2048,2048]{1,0:T(8,128)(2,1)S(1)} %copy-done, bf16[128,2176]{1,0:T(8,128)(2,1)S(1)} %collective-permute-done.3.refs_0_, ...), custom_call_target="tpu_custom_call" | custom-call | flops 2147483648 | bytes 9437184 | tf_op jit(solution)/shard_map/pallas_call | solution.py:141
  38.9 0.2 collective-permute-start.10
  39.2 0.7 %collective-permute-start.11 = (f32[1,2048]{1,0:T(1,128)S(1)}, f32[1,2048]{1,0:T(1,128)S(1)}, u32[]{:S(2)}, u32[]{:S(2)}) collective-permute-start(f32[1,2048]{1,0:T(1,128)S(1)} %get-tuple-element.37), channel_id=1, source_target_pairs={{0,4},{32,36},{64,68},{96,100},{128,132},{160,164},{192,196},{224,... | collective-permute-start | bytes 24584 | tf_op jit(solution)/shard_map/ppermute | solution.py:33
  39.8 0.0 collective-permute-done.7
  39.8 0.0 collective-permute-done.8
  39.8 2.2 %collective-permute-start.14 = (f32[1,2048]{1,0:T(1,128)S(1)}, f32[1,2048]{1,0:T(1,128)S(1)}, u32[]{:S(2)}, u32[]{:S(2)}) collective-permute-start(f32[1,2048]{1,0:T(1,128)S(1)} %get-tuple-element.37), channel_id=1, source_target_pairs={{0,12},{32,44},{64,76},{96,108},{128,140},{160,172},{192,204},{224... | collective-permute-start | bytes 24584 | tf_op jit(solution)/shard_map/ppermute | solution.py:33
  42.1 1.4 %collective-permute-start.13 = (f32[1,2048]{1,0:T(1,128)S(1)}, f32[1,2048]{1,0:T(1,128)S(1)}, u32[]{:S(2)}, u32[]{:S(2)}) collective-permute-start(f32[1,2048]{1,0:T(1,128)S(1)} %get-tuple-element.37), channel_id=1, source_target_pairs={{0,8},{32,40},{64,72},{96,104},{128,136},{160,168},{192,200},{224,... | collective-permute-start | bytes 24584 | tf_op jit(solution)/shard_map/ppermute | solution.py:33
  43.5 0.0 collective-permute-done.10
  43.5 0.0 collective-permute-done.11
  43.5 3.3 %collective-permute-start.16 = (f32[1,256]{1,0:T(1,128)S(1)}, f32[1,256]{1,0:T(1,128)S(1)}, u32[]{:S(2)}, u32[]{:S(2)}) collective-permute-start(f32[1,256]{1,0:T(1,128)S(1)} %pad_maximum_fusion.1), channel_id=1, source_target_pairs={{0,2},{32,34},{64,66},{96,98},{128,130},{160,162},{192,194},{224,2... | collective-permute-start | bytes 3080 | tf_op jit(solution)/shard_map/ppermute | solution.py:33
  46.8 1.1 %collective-permute-start.17 = (f32[1,256]{1,0:T(1,128)S(1)}, f32[1,256]{1,0:T(1,128)S(1)}, u32[]{:S(2)}, u32[]{:S(2)}) collective-permute-start(f32[1,256]{1,0:T(1,128)S(1)} %pad_maximum_fusion.1), channel_id=1, source_target_pairs={{0,3},{32,35},{64,67},{96,99},{128,131},{160,163},{192,195},{224,2... | collective-permute-start | bytes 3080 | tf_op jit(solution)/shard_map/ppermute | solution.py:33
  47.8 0.0 collective-permute-start.12
  47.8 0.0 collective-permute-done.14
  47.8 0.0 collective-permute-done.13
  47.9 3.5 %collective-permute-done.12 = f32[1,256]{1,0:T(1,128)S(1)} collective-permute-done((f32[1,256]{1,0:T(1,128)S(1)}, f32[1,256]{1,0:T(1,128)S(1)}, u32[]{:S(2)}, u32[]{:S(2)}) %collective-permute-start.12) | collective-permute-done | bytes 1056 | tf_op jit(solution)/shard_map/ppermute | solution.py:33
  51.4 3.4 %collective-permute-start.15 = (f32[1,2048]{1,0:T(1,128)S(1)}, f32[1,2048]{1,0:T(1,128)S(1)}, u32[]{:S(2)}, u32[]{:S(2)}) collective-permute-start(f32[1,2048]{1,0:T(1,128)S(1)} %maximum_maximum_fusion), channel_id=1, source_target_pairs={{0,16},{32,48},{64,80},{96,112},{128,144},{160,176},{192,208},{224... | collective-permute-start | bytes 24584 | tf_op jit(solution)/shard_map/ppermute | solution.py:33
  54.8 0.0 collective-permute-done.16
  54.8 0.0 collective-permute-done.17
  54.8 0.5 collective-permute-start.18
  55.2 5.3 %collective-permute-done.18 = f32[1,128]{1,0:T(1,128)S(1)} collective-permute-done((f32[1,128]{1,0:T(1,128)S(1)}, f32[1,128]{1,0:T(1,128)S(1)}, u32[]{:S(2)}, u32[]{:S(2)}) %collective-permute-start.18) | collective-permute-done | bytes 544 | tf_op jit(solution)/shard_map/ppermute | solution.py:33
  60.5 0.0 collective-permute-done.15
  60.5 0.5 fusion
  61.0 0.6 max.46
  (13 shorter events, 0.1 us)
Async XLA Ops:
  0.6 1.0 %copy-start.2 = (bf16[128,2048]{1,0:T(8,128)(2,1)S(1)}, bf16[128,2048]{1,0:T(8,128)(2,1)}, u32[]{:S(2)}) copy-start(bf16[128,2048]{1,0:T(8,128)(2,1)} %coefficients.1) | copy-start | bytes 1572868
  1.7 0.7 %copy-start.3 = (bf16[128]{0:T(256)(128)(2,1)S(1)}, bf16[128]{0:T(256)(128)(2,1)}, u32[]{:S(2)}) copy-start(bf16[128]{0:T(256)(128)(2,1)} %param.5) | copy-start | bytes 772
  2.3 6.3 %copy-start = (bf16[2048,2048]{1,0:T(8,128)(2,1)S(1)}, bf16[2048,2048]{1,0:T(8,128)(2,1)}, u32[]{:S(2)}) copy-start(bf16[2048,2048]{1,0:T(8,128)(2,1)} %states.5) | copy-start | bytes 25165828
  2.3 6.3 %copy-start.1 = (f32[2048]{0:T(1024)S(1)}, f32[2048]{0:T(1024)}, u32[]{:S(2)}) copy-start(f32[2048]{0:T(1024)} %param.7) | copy-start | bytes 24580
  2.5 6.1 %collective-permute-start.2 = (bf16[128,2176]{1,0:T(8,128)(2,1)S(1)}, bf16[128,2176]{1,0:T(8,128)(2,1)S(1)}, u32[]{:S(2)}, u32[]{:S(2)}) collective-permute-start(bf16[128,2176]{1,0:T(8,128)(2,1)S(1)} %shard_map.59.refs_0_), channel_id=1, source_target_pairs={{0,32},{32,0},{64,96},{96,64},{128,160},{160,128},{192,224},{224,1... | collective-permute-start | bytes 1671176 | tf_op jit(solution)/shard_map/ppermute | solution.py:33
  2.6 16.9 %collective-permute-start.1 = (bf16[128,2176]{1,0:T(8,128)(2,1)S(1)}, bf16[128,2176]{1,0:T(8,128)(2,1)S(1)}, u32[]{:S(2)}, u32[]{:S(2)}) collective-permute-start(bf16[128,2176]{1,0:T(8,128)(2,1)S(1)} %shard_map.59.refs_0_), channel_id=1, source_target_pairs={{0,64},{32,240},{64,128},{96,32},{128,192},{160,96},{192,16},{224,... | collective-permute-start | bytes 1671176 | tf_op jit(solution)/shard_map/ppermute | solution.py:33
  4.6 16.4 %collective-permute-start = (bf16[128,2176]{1,0:T(8,128)(2,1)S(1)}, bf16[128,2176]{1,0:T(8,128)(2,1)S(1)}, u32[]{:S(2)}, u32[]{:S(2)}) collective-permute-start(bf16[128,2176]{1,0:T(8,128)(2,1)S(1)} %shard_map.59.refs_0_), channel_id=1, source_target_pairs={{0,208},{32,96},{64,0},{96,160},{128,64},{160,224},{192,128},{224,... | collective-permute-start | bytes 1671176 | tf_op jit(solution)/shard_map/ppermute | solution.py:33
  21.0 4.2 %collective-permute-start.5 = (bf16[128,2176]{1,0:T(8,128)(2,1)S(1)}, bf16[128,2176]{1,0:T(8,128)(2,1)S(1)}, u32[]{:S(2)}, u32[]{:S(2)}) collective-permute-start(bf16[128,2176]{1,0:T(8,128)(2,1)S(1)} %collective-permute-done.1.refs_1_), channel_id=1, source_target_pairs={{0,32},{32,0},{64,96},{96,64},{128,160},{160,128},{192,224},{224,1... | collective-permute-start | bytes 1671176 | tf_op jit(solution)/shard_map/ppermute | solution.py:33
  21.9 3.4 %collective-permute-start.4 = (bf16[128,2176]{1,0:T(8,128)(2,1)S(1)}, bf16[128,2176]{1,0:T(8,128)(2,1)S(1)}, u32[]{:S(2)}, u32[]{:S(2)}) collective-permute-start(bf16[128,2176]{1,0:T(8,128)(2,1)S(1)} %collective-permute-done.refs_0_), channel_id=1, source_target_pairs={{0,32},{32,0},{64,96},{96,64},{128,160},{160,128},{192,224},{224,1... | collective-permute-start | bytes 1671176 | tf_op jit(solution)/shard_map/ppermute | solution.py:33
  21.9 10.4 %collective-permute-start.3 = (bf16[128,2176]{1,0:T(8,128)(2,1)S(1)}, bf16[128,2176]{1,0:T(8,128)(2,1)S(1)}, u32[]{:S(2)}, u32[]{:S(2)}) collective-permute-start(bf16[128,2176]{1,0:T(8,128)(2,1)S(1)} %collective-permute-done.refs_0_), channel_id=1, source_target_pairs={{0,208},{32,96},{64,0},{96,160},{128,64},{160,224},{192,128},{224,... | collective-permute-start | bytes 1671176 | tf_op jit(solution)/shard_map/ppermute | solution.py:33
  30.4 1.2 %collective-permute-start.6 = (f32[1,384]{1,0:T(1,128)S(1)}, f32[1,384]{1,0:T(1,128)S(1)}, u32[]{:S(2)}, u32[]{:S(2)}) collective-permute-start(f32[1,384]{1,0:T(1,128)S(1)} %pad_maximum_fusion), channel_id=1, source_target_pairs={{0,32},{32,0},{64,96},{96,64},{128,160},{160,128},{192,224},{224,1... | collective-permute-start | bytes 4616 | tf_op jit(solution)/shard_map/ppermute | solution.py:33
  32.3 3.8 %collective-permute-start.9 = (bf16[128,2176]{1,0:T(8,128)(2,1)S(1)}, bf16[128,2176]{1,0:T(8,128)(2,1)S(1)}, u32[]{:S(2)}, u32[]{:S(2)}) collective-permute-start(bf16[128,2176]{1,0:T(8,128)(2,1)S(1)} %collective-permute-done.3.refs_0_), channel_id=1, source_target_pairs={{0,32},{32,0},{64,96},{96,64},{128,160},{160,128},{192,224},{224,1... | collective-permute-start | bytes 1671176 | tf_op jit(solution)/shard_map/ppermute | solution.py:33
  32.3 7.5 %collective-permute-start.7 = (f32[1,128]{1,0:T(1,128)S(1)}, f32[1,128]{1,0:T(1,128)S(1)}, u32[]{:S(2)}, u32[]{:S(2)}) collective-permute-start(f32[1,128]{1,0:T(1,128)S(1)} %get-tuple-element.44), channel_id=1, source_target_pairs={{0,64},{32,240},{64,128},{96,32},{128,192},{160,96},{192,16},{224,... | collective-permute-start | bytes 1544 | tf_op jit(solution)/shard_map/ppermute | solution.py:33
  32.3 7.5 %collective-permute-start.8 = (f32[1,128]{1,0:T(1,128)S(1)}, f32[1,128]{1,0:T(1,128)S(1)}, u32[]{:S(2)}, u32[]{:S(2)}) collective-permute-start(f32[1,128]{1,0:T(1,128)S(1)} %get-tuple-element.45), channel_id=1, source_target_pairs={{0,208},{32,96},{64,0},{96,160},{128,64},{160,224},{192,128},{224,... | collective-permute-start | bytes 1544 | tf_op jit(solution)/shard_map/ppermute | solution.py:33
  38.9 4.6 %collective-permute-start.10 = (f32[1,128]{1,0:T(1,128)S(1)}, f32[1,128]{1,0:T(1,128)S(1)}, u32[]{:S(2)}, u32[]{:S(2)}) collective-permute-start(f32[1,128]{1,0:T(1,128)S(1)} %get-tuple-element.36), channel_id=1, source_target_pairs={{0,32},{32,0},{64,96},{96,64},{128,160},{160,128},{192,224},{224,1... | collective-permute-start | bytes 1544 | tf_op jit(solution)/shard_map/ppermute | solution.py:33
  39.2 4.3 %collective-permute-start.11 = (f32[1,2048]{1,0:T(1,128)S(1)}, f32[1,2048]{1,0:T(1,128)S(1)}, u32[]{:S(2)}, u32[]{:S(2)}) collective-permute-start(f32[1,2048]{1,0:T(1,128)S(1)} %get-tuple-element.37), channel_id=1, source_target_pairs={{0,4},{32,36},{64,68},{96,100},{128,132},{160,164},{192,196},{224,... | collective-permute-start | bytes 24584 | tf_op jit(solution)/shard_map/ppermute | solution.py:33
  39.8 8.0 %collective-permute-start.14 = (f32[1,2048]{1,0:T(1,128)S(1)}, f32[1,2048]{1,0:T(1,128)S(1)}, u32[]{:S(2)}, u32[]{:S(2)}) collective-permute-start(f32[1,2048]{1,0:T(1,128)S(1)} %get-tuple-element.37), channel_id=1, source_target_pairs={{0,12},{32,44},{64,76},{96,108},{128,140},{160,172},{192,204},{224... | collective-permute-start | bytes 24584 | tf_op jit(solution)/shard_map/ppermute | solution.py:33
  42.1 5.8 %collective-permute-start.13 = (f32[1,2048]{1,0:T(1,128)S(1)}, f32[1,2048]{1,0:T(1,128)S(1)}, u32[]{:S(2)}, u32[]{:S(2)}) collective-permute-start(f32[1,2048]{1,0:T(1,128)S(1)} %get-tuple-element.37), channel_id=1, source_target_pairs={{0,8},{32,40},{64,72},{96,104},{128,136},{160,168},{192,200},{224,... | collective-permute-start | bytes 24584 | tf_op jit(solution)/shard_map/ppermute | solution.py:33
  43.5 11.3 %collective-permute-start.16 = (f32[1,256]{1,0:T(1,128)S(1)}, f32[1,256]{1,0:T(1,128)S(1)}, u32[]{:S(2)}, u32[]{:S(2)}) collective-permute-start(f32[1,256]{1,0:T(1,128)S(1)} %pad_maximum_fusion.1), channel_id=1, source_target_pairs={{0,2},{32,34},{64,66},{96,98},{128,130},{160,162},{192,194},{224,2... | collective-permute-start | bytes 3080 | tf_op jit(solution)/shard_map/ppermute | solution.py:33
  46.8 8.0 %collective-permute-start.17 = (f32[1,256]{1,0:T(1,128)S(1)}, f32[1,256]{1,0:T(1,128)S(1)}, u32[]{:S(2)}, u32[]{:S(2)}) collective-permute-start(f32[1,256]{1,0:T(1,128)S(1)} %pad_maximum_fusion.1), channel_id=1, source_target_pairs={{0,3},{32,35},{64,67},{96,99},{128,131},{160,163},{192,195},{224,2... | collective-permute-start | bytes 3080 | tf_op jit(solution)/shard_map/ppermute | solution.py:33
  47.8 3.6 %collective-permute-start.12 = (f32[1,256]{1,0:T(1,128)S(1)}, f32[1,256]{1,0:T(1,128)S(1)}, u32[]{:S(2)}, u32[]{:S(2)}) collective-permute-start(f32[1,256]{1,0:T(1,128)S(1)} %pad_maximum_fusion.1), channel_id=1, source_target_pairs={{0,1},{32,33},{64,65},{96,97},{128,129},{160,161},{192,193},{224,2... | collective-permute-start | bytes 3080 | tf_op jit(solution)/shard_map/ppermute | solution.py:33
  51.4 9.1 %collective-permute-start.15 = (f32[1,2048]{1,0:T(1,128)S(1)}, f32[1,2048]{1,0:T(1,128)S(1)}, u32[]{:S(2)}, u32[]{:S(2)}) collective-permute-start(f32[1,2048]{1,0:T(1,128)S(1)} %maximum_maximum_fusion), channel_id=1, source_target_pairs={{0,16},{32,48},{64,80},{96,112},{128,144},{160,176},{192,208},{224... | collective-permute-start | bytes 24584 | tf_op jit(solution)/shard_map/ppermute | solution.py:33
  54.8 5.7 %collective-permute-start.18 = (f32[1,128]{1,0:T(1,128)S(1)}, f32[1,128]{1,0:T(1,128)S(1)}, u32[]{:S(2)}, u32[]{:S(2)}) collective-permute-start(f32[1,128]{1,0:T(1,128)S(1)} %slice.20), channel_id=1, source_target_pairs={{0,128},{32,176},{64,192},{96,240},{128,16},{160,32},{192,80},{224... | collective-permute-start | bytes 1544 | tf_op jit(solution)/shard_map/ppermute | solution.py:33

commit v8 on v7

--- a/solution.py
+++ b/solution.py
@@ -186,7 +186,6 @@
     lifts = jnp.concatenate([held, jnp.maximum(two_mine, swapped)], axis=1)
     for_y = [send(lifts, over_y(d)) for d in (1, 2, 3)]
     top = functools.reduce(jnp.maximum, for_x, top)
-    for_y[0], top = fence((for_y[0], top))
     lifts = functools.reduce(jnp.maximum, for_y, lifts)
     across = send(top, far)
     returned = send(lifts[:, cuts:], two_back)

time: 61.8 us -> 59 us (0.955)
  waiting for transfers between devices: 20.2 us -> 17.1 us
    ppermute x19, waiting for transfers between devices: 20.2 us -> 17.1 us  [send(): return lax.ppermute(block, AXES, routes(move))]
  transfers between devices with their start and end apart: 19 -> 19, of which waited for: 6 -> 6; matrix products, arithmetic and copies ran while one was open for 0% -> 0% of each run, Pallas kernels for 17% -> 18%
where the time goes in v8:
time: 59 us; the launch traced here: 58.4 us
  starting transfers between devices  26.8 us (45%)
  waiting for transfers between devices  17.1 us (29%)
  Pallas kernels  11 us (19%)
  local copies, waits for them, and re-layouts  1.7 us (3%)
  other arithmetic  1.17 us (2%)
  between operations  0.75 us (1%)
    ppermute x19, starting transfers between devices, send(): return lax.ppermute(block, AXES, routes(move))  26.8 us
    ppermute x19, waiting for transfers between devices, send(): return lax.ppermute(block, AXES, routes(move))  17.1 us
    pallas_call x3, Pallas kernels, score(): pl.pallas_call(functools.partial(score_body, tile, tiles, len(blocks)), g...  10.8 us
    unnamed x8, local copies, waits for them, and re-layouts  1.7 us
  transfers between devices with their start and end apart: 19, of which 6 were waited for; matrix products, arithmetic and copies ran while one was open for 0% of the time, Pallas kernels for 18%

profile of v8, /device:TPU:2, one launch (start us, length us, event | category | flops | bytes accessed | tf_op | source)
XLA Modules:
  0.0 58.4 jit_solution(14175505508550216377)
XLA Ops:
  0.6 0.0 copy-start.2
  0.6 1.0 %copy-done.2 = bf16[128,2048]{1,0:T(8,128)(2,1)S(1)} copy-done((bf16[128,2048]{1,0:T(8,128)(2,1)S(1)}, bf16[128,2048]{1,0:T(8,128)(2,1)}, u32[]{:S(2)}) %copy-start.2) | copy-done | bytes 524312
  1.7 0.7 %copy-done.3 = bf16[128]{0:T(256)(128)(2,1)S(1)} copy-done((bf16[128]{0:T(256)(128)(2,1)S(1)}, bf16[128]{0:T(256)(128)(2,1)}, u32[]{:S(2)}) %copy-start.3) | copy-done | bytes 280
  2.3 0.2 shard_map.59.refs_0_
  2.5 0.1 collective-permute-start.2
  2.6 2.0 %collective-permute-start.1 = (bf16[128,2176]{1,0:T(8,128)(2,1)S(1)}, bf16[128,2176]{1,0:T(8,128)(2,1)S(1)}, u32[]{:S(2)}, u32[]{:S(2)}) collective-permute-start(bf16[128,2176]{1,0:T(8,128)(2,1)S(1)} %shard_map.59.refs_0_), channel_id=1, source_target_pairs={{0,64},{32,240},{64,128},{96,32},{128,192},{160,96},{192,16},{224,... | collective-permute-start | bytes 1671176 | tf_op jit(solution)/shard_map/ppermute | solution.py:33
  4.6 4.0 %collective-permute-start = (bf16[128,2176]{1,0:T(8,128)(2,1)S(1)}, bf16[128,2176]{1,0:T(8,128)(2,1)S(1)}, u32[]{:S(2)}, u32[]{:S(2)}) collective-permute-start(bf16[128,2176]{1,0:T(8,128)(2,1)S(1)} %shard_map.59.refs_0_), channel_id=1, source_target_pairs={{0,208},{32,96},{64,0},{96,160},{128,64},{160,224},{192,128},{224,... | collective-permute-start | bytes 1671176 | tf_op jit(solution)/shard_map/ppermute | solution.py:33
  8.7 0.0 collective-permute-done.2.refs_1_
  8.7 0.0 copy-done
  8.7 2.8 %shard_map.60 = (f32[1,2048]{1,0:T(1,128)S(1)}, f32[1,128]{1,0:T(1,128)S(1)}, f32[1,128]{1,0:T(1,128)S(1)}) custom-call(f32[1,2048]{1,0:T(1,128)S(1)} %bitcast.5, f32[1,2048]{1,0:T(1,128)S(1)} %bitcast.6, bf16[2048,2048]{1,0:T(8,128)(2,1)S(1)} %copy-done, bf16[128,2176]{1,0:T(8,128)(2,1)S(1)} %shard_map.59.refs_0_, ...), custom_call_target="tpu_custom_call" | custom-call | flops 2147483648 | bytes 9437184 | tf_op jit(solution)/shard_map/pallas_call | solution.py:141
  11.5 8.1 %collective-permute-done.1.refs_1_ = bf16[128,2176]{1,0:T(8,128)(2,1)S(1)} collective-permute-done((bf16[128,2176]{1,0:T(8,128)(2,1)S(1)}, bf16[128,2176]{1,0:T(8,128)(2,1)S(1)}, u32[]{:S(2)}, u32[]{:S(2)}) %collective-permute-start.1) | collective-permute-done | bytes 557088 | tf_op jit(solution)/shard_map/ppermute | solution.py:33
  19.6 1.5 %collective-permute-done.refs_0_ = bf16[128,2176]{1,0:T(8,128)(2,1)S(1)} collective-permute-done((bf16[128,2176]{1,0:T(8,128)(2,1)S(1)}, bf16[128,2176]{1,0:T(8,128)(2,1)S(1)}, u32[]{:S(2)}, u32[]{:S(2)}) %collective-permute-start) | collective-permute-done | bytes 557088 | tf_op jit(solution)/shard_map/ppermute | solution.py:33
  21.0 0.8 %collective-permute-start.5 = (bf16[128,2176]{1,0:T(8,128)(2,1)S(1)}, bf16[128,2176]{1,0:T(8,128)(2,1)S(1)}, u32[]{:S(2)}, u32[]{:S(2)}) collective-permute-start(bf16[128,2176]{1,0:T(8,128)(2,1)S(1)} %collective-permute-done.1.refs_1_), channel_id=1, source_target_pairs={{0,32},{32,0},{64,96},{96,64},{128,160},{160,128},{192,224},{224,1... | collective-permute-start | bytes 1671176 | tf_op jit(solution)/shard_map/ppermute | solution.py:33
  21.9 0.0 collective-permute-start.4
  21.9 3.4 %collective-permute-start.3 = (bf16[128,2176]{1,0:T(8,128)(2,1)S(1)}, bf16[128,2176]{1,0:T(8,128)(2,1)S(1)}, u32[]{:S(2)}, u32[]{:S(2)}) collective-permute-start(bf16[128,2176]{1,0:T(8,128)(2,1)S(1)} %collective-permute-done.refs_0_), channel_id=1, source_target_pairs={{0,208},{32,96},{64,0},{96,160},{128,64},{160,224},{192,128},{224,... | collective-permute-start | bytes 1671176 | tf_op jit(solution)/shard_map/ppermute | solution.py:33
  25.2 0.0 collective-permute-done.5.refs_3_
  25.2 0.0 collective-permute-done.4.refs_2_
  25.2 5.1 %shard_map.61 = (f32[1,2048]{1,0:T(1,128)S(1)}, f32[1,256]{1,0:T(1,128)S(1)}, f32[1,256]{1,0:T(1,128)S(1)}) custom-call(f32[1,2048]{1,0:T(1,128)S(1)} %bitcast.7, f32[1,2048]{1,0:T(1,128)S(1)} %get-tuple-element.23.prev, bf16[2048,2048]{1,0:T(8,128)(2,1)S(1)} %copy-done, bf16[128,2176]{1,0:T(8,128)(2,1)S(1)} %collective-permute-done.refs_0_, ...), custom_call_target="tpu_custom_call" | custom-call | flops 4294967296 | bytes 10485760 | tf_op jit(solution)/shard_map/pallas_call | solution.py:141
  30.4 0.1 collective-permute-start.6
  30.5 1.1 %collective-permute-done.6 = f32[1,384]{1,0:T(1,128)S(1)} collective-permute-done((f32[1,384]{1,0:T(1,128)S(1)}, f32[1,384]{1,0:T(1,128)S(1)}, u32[]{:S(2)}, u32[]{:S(2)}) %collective-permute-start.6) | collective-permute-done | bytes 1568 | tf_op jit(solution)/shard_map/ppermute | solution.py:33
  31.6 0.7 %collective-permute-done.3.refs_0_ = bf16[128,2176]{1,0:T(8,128)(2,1)S(1)} collective-permute-done((bf16[128,2176]{1,0:T(8,128)(2,1)S(1)}, bf16[128,2176]{1,0:T(8,128)(2,1)S(1)}, u32[]{:S(2)}, u32[]{:S(2)}) %collective-permute-start.3) | collective-permute-done | bytes 557088 | tf_op jit(solution)/shard_map/ppermute | solution.py:33
  32.3 0.0 collective-permute-start.7
  32.3 0.0 collective-permute-start.13
  32.3 3.8 %collective-permute-start.14 = (f32[1,128]{1,0:T(1,128)S(1)}, f32[1,128]{1,0:T(1,128)S(1)}, u32[]{:S(2)}, u32[]{:S(2)}) collective-permute-start(f32[1,128]{1,0:T(1,128)S(1)} %get-tuple-element.41), channel_id=1, source_target_pairs={{0,208},{32,96},{64,0},{96,160},{128,64},{160,224},{192,128},{224,... | collective-permute-start | bytes 1544 | tf_op jit(solution)/shard_map/ppermute | solution.py:33
  36.1 0.0 collective-permute-done.7.refs_1_
  36.1 2.8 %shard_map.62 = (f32[1,2048]{1,0:T(1,128)S(1)}, f32[1,128]{1,0:T(1,128)S(1)}, f32[1,128]{1,0:T(1,128)S(1)}) custom-call(f32[1,2048]{1,0:T(1,128)S(1)} %bitcast.8, f32[1,2048]{1,0:T(1,128)S(1)} %get-tuple-element.30.prev, bf16[2048,2048]{1,0:T(8,128)(2,1)S(1)} %copy-done, bf16[128,2176]{1,0:T(8,128)(2,1)S(1)} %collective-permute-done.3.refs_0_, ...), custom_call_target="tpu_custom_call" | custom-call | flops 2147483648 | bytes 9437184 | tf_op jit(solution)/shard_map/pallas_call | solution.py:141
  38.9 0.2 collective-permute-start.8
  39.2 0.7 %collective-permute-start.9 = (f32[1,2048]{1,0:T(1,128)S(1)}, f32[1,2048]{1,0:T(1,128)S(1)}, u32[]{:S(2)}, u32[]{:S(2)}) collective-permute-start(f32[1,2048]{1,0:T(1,128)S(1)} %get-tuple-element.32), channel_id=1, source_target_pairs={{0,4},{32,36},{64,68},{96,100},{128,132},{160,164},{192,196},{224,... | collective-permute-start | bytes 24584 | tf_op jit(solution)/shard_map/ppermute | solution.py:33
  39.8 0.0 collective-permute-done.13
  39.8 0.0 collective-permute-done.14
  39.8 2.2 %collective-permute-start.11 = (f32[1,2048]{1,0:T(1,128)S(1)}, f32[1,2048]{1,0:T(1,128)S(1)}, u32[]{:S(2)}, u32[]{:S(2)}) collective-permute-start(f32[1,2048]{1,0:T(1,128)S(1)} %get-tuple-element.32), channel_id=1, source_target_pairs={{0,12},{32,44},{64,76},{96,108},{128,140},{160,172},{192,204},{224... | collective-permute-start | bytes 24584 | tf_op jit(solution)/shard_map/ppermute | solution.py:33
  42.1 1.4 %collective-permute-start.10 = (f32[1,2048]{1,0:T(1,128)S(1)}, f32[1,2048]{1,0:T(1,128)S(1)}, u32[]{:S(2)}, u32[]{:S(2)}) collective-permute-start(f32[1,2048]{1,0:T(1,128)S(1)} %get-tuple-element.32), channel_id=1, source_target_pairs={{0,8},{32,40},{64,72},{96,104},{128,136},{160,168},{192,200},{224,... | collective-permute-start | bytes 24584 | tf_op jit(solution)/shard_map/ppermute | solution.py:33
  43.5 0.0 collective-permute-done.8
  43.5 0.0 collective-permute-done.9
  43.5 3.3 %collective-permute-start.16 = (f32[1,256]{1,0:T(1,128)S(1)}, f32[1,256]{1,0:T(1,128)S(1)}, u32[]{:S(2)}, u32[]{:S(2)}) collective-permute-start(f32[1,256]{1,0:T(1,128)S(1)} %pad_maximum_fusion.1), channel_id=1, source_target_pairs={{0,2},{32,34},{64,66},{96,98},{128,130},{160,162},{192,194},{224,2... | collective-permute-start | bytes 3080 | tf_op jit(solution)/shard_map/ppermute | solution.py:33
  46.8 1.1 %collective-permute-start.17 = (f32[1,256]{1,0:T(1,128)S(1)}, f32[1,256]{1,0:T(1,128)S(1)}, u32[]{:S(2)}, u32[]{:S(2)}) collective-permute-start(f32[1,256]{1,0:T(1,128)S(1)} %pad_maximum_fusion.1), channel_id=1, source_target_pairs={{0,3},{32,35},{64,67},{96,99},{128,131},{160,163},{192,195},{224,2... | collective-permute-start | bytes 3080 | tf_op jit(solution)/shard_map/ppermute | solution.py:33
  47.8 0.0 collective-permute-start.15
  47.8 0.0 collective-permute-done.11
  47.8 0.0 collective-permute-done.10
  47.9 3.5 %collective-permute-start.12 = (f32[1,2048]{1,0:T(1,128)S(1)}, f32[1,2048]{1,0:T(1,128)S(1)}, u32[]{:S(2)}, u32[]{:S(2)}) collective-permute-start(f32[1,2048]{1,0:T(1,128)S(1)} %maximum_maximum_fusion), channel_id=1, source_target_pairs={{0,16},{32,48},{64,80},{96,112},{128,144},{160,176},{192,208},{224... | collective-permute-start | bytes 24584 | tf_op jit(solution)/shard_map/ppermute | solution.py:33
  51.3 0.0 collective-permute-done.16
  51.3 0.2 collective-permute-done.17
  51.6 0.0 collective-permute-done.15
  51.6 0.2 collective-permute-start.18
  51.8 5.5 %collective-permute-done.18 = f32[1,128]{1,0:T(1,128)S(1)} collective-permute-done((f32[1,128]{1,0:T(1,128)S(1)}, f32[1,128]{1,0:T(1,128)S(1)}, u32[]{:S(2)}, u32[]{:S(2)}) %collective-permute-start.18) | collective-permute-done | bytes 544 | tf_op jit(solution)/shard_map/ppermute | solution.py:33
  57.3 0.0 collective-permute-done.12
  57.3 0.5 fusion
  57.8 0.6 %max.46 = f32[1,2048]{1,0:T(1,128)} maximum(f32[1,2048]{1,0:T(1,128)S(1)} %maximum_maximum_fusion, f32[1,2048]{1,0:T(1,128)S(1)} %collective-permute-done.12) | non-fusion elementwise | flops 2048 | bytes 24576 | tf_op jit(solution)/shard_map/max | solution.py:193
  (13 shorter events, 0.1 us)
Async XLA Ops:
  0.6 1.0 %copy-start.2 = (bf16[128,2048]{1,0:T(8,128)(2,1)S(1)}, bf16[128,2048]{1,0:T(8,128)(2,1)}, u32[]{:S(2)}) copy-start(bf16[128,2048]{1,0:T(8,128)(2,1)} %coefficients.1) | copy-start | bytes 1572868
  1.7 0.7 %copy-start.3 = (bf16[128]{0:T(256)(128)(2,1)S(1)}, bf16[128]{0:T(256)(128)(2,1)}, u32[]{:S(2)}) copy-start(bf16[128]{0:T(256)(128)(2,1)} %param.5) | copy-start | bytes 772
  2.3 6.3 %copy-start = (bf16[2048,2048]{1,0:T(8,128)(2,1)S(1)}, bf16[2048,2048]{1,0:T(8,128)(2,1)}, u32[]{:S(2)}) copy-start(bf16[2048,2048]{1,0:T(8,128)(2,1)} %states.5) | copy-start | bytes 25165828
  2.3 6.3 %copy-start.1 = (f32[2048]{0:T(1024)S(1)}, f32[2048]{0:T(1024)}, u32[]{:S(2)}) copy-start(f32[2048]{0:T(1024)} %param.7) | copy-start | bytes 24580
  2.5 6.1 %collective-permute-start.2 = (bf16[128,2176]{1,0:T(8,128)(2,1)S(1)}, bf16[128,2176]{1,0:T(8,128)(2,1)S(1)}, u32[]{:S(2)}, u32[]{:S(2)}) collective-permute-start(bf16[128,2176]{1,0:T(8,128)(2,1)S(1)} %shard_map.59.refs_0_), channel_id=1, source_target_pairs={{0,32},{32,0},{64,96},{96,64},{128,160},{160,128},{192,224},{224,1... | collective-permute-start | bytes 1671176 | tf_op jit(solution)/shard_map/ppermute | solution.py:33
  2.6 16.9 %collective-permute-start.1 = (bf16[128,2176]{1,0:T(8,128)(2,1)S(1)}, bf16[128,2176]{1,0:T(8,128)(2,1)S(1)}, u32[]{:S(2)}, u32[]{:S(2)}) collective-permute-start(bf16[128,2176]{1,0:T(8,128)(2,1)S(1)} %shard_map.59.refs_0_), channel_id=1, source_target_pairs={{0,64},{32,240},{64,128},{96,32},{128,192},{160,96},{192,16},{224,... | collective-permute-start | bytes 1671176 | tf_op jit(solution)/shard_map/ppermute | solution.py:33
  4.6 16.4 %collective-permute-start = (bf16[128,2176]{1,0:T(8,128)(2,1)S(1)}, bf16[128,2176]{1,0:T(8,128)(2,1)S(1)}, u32[]{:S(2)}, u32[]{:S(2)}) collective-permute-start(bf16[128,2176]{1,0:T(8,128)(2,1)S(1)} %shard_map.59.refs_0_), channel_id=1, source_target_pairs={{0,208},{32,96},{64,0},{96,160},{128,64},{160,224},{192,128},{224,... | collective-permute-start | bytes 1671176 | tf_op jit(solution)/shard_map/ppermute | solution.py:33
  21.0 4.2 %collective-permute-start.5 = (bf16[128,2176]{1,0:T(8,128)(2,1)S(1)}, bf16[128,2176]{1,0:T(8,128)(2,1)S(1)}, u32[]{:S(2)}, u32[]{:S(2)}) collective-permute-start(bf16[128,2176]{1,0:T(8,128)(2,1)S(1)} %collective-permute-done.1.refs_1_), channel_id=1, source_target_pairs={{0,32},{32,0},{64,96},{96,64},{128,160},{160,128},{192,224},{224,1... | collective-permute-start | bytes 1671176 | tf_op jit(solution)/shard_map/ppermute | solution.py:33
  21.9 3.4 %collective-permute-start.4 = (bf16[128,2176]{1,0:T(8,128)(2,1)S(1)}, bf16[128,2176]{1,0:T(8,128)(2,1)S(1)}, u32[]{:S(2)}, u32[]{:S(2)}) collective-permute-start(bf16[128,2176]{1,0:T(8,128)(2,1)S(1)} %collective-permute-done.refs_0_), channel_id=1, source_target_pairs={{0,32},{32,0},{64,96},{96,64},{128,160},{160,128},{192,224},{224,1... | collective-permute-start | bytes 1671176 | tf_op jit(solution)/shard_map/ppermute | solution.py:33
  21.9 10.4 %collective-permute-start.3 = (bf16[128,2176]{1,0:T(8,128)(2,1)S(1)}, bf16[128,2176]{1,0:T(8,128)(2,1)S(1)}, u32[]{:S(2)}, u32[]{:S(2)}) collective-permute-start(bf16[128,2176]{1,0:T(8,128)(2,1)S(1)} %collective-permute-done.refs_0_), channel_id=1, source_target_pairs={{0,208},{32,96},{64,0},{96,160},{128,64},{160,224},{192,128},{224,... | collective-permute-start | bytes 1671176 | tf_op jit(solution)/shard_map/ppermute | solution.py:33
  30.4 1.2 %collective-permute-start.6 = (f32[1,384]{1,0:T(1,128)S(1)}, f32[1,384]{1,0:T(1,128)S(1)}, u32[]{:S(2)}, u32[]{:S(2)}) collective-permute-start(f32[1,384]{1,0:T(1,128)S(1)} %pad_maximum_fusion), channel_id=1, source_target_pairs={{0,32},{32,0},{64,96},{96,64},{128,160},{160,128},{192,224},{224,1... | collective-permute-start | bytes 4616 | tf_op jit(solution)/shard_map/ppermute | solution.py:33
  32.3 3.8 %collective-permute-start.7 = (bf16[128,2176]{1,0:T(8,128)(2,1)S(1)}, bf16[128,2176]{1,0:T(8,128)(2,1)S(1)}, u32[]{:S(2)}, u32[]{:S(2)}) collective-permute-start(bf16[128,2176]{1,0:T(8,128)(2,1)S(1)} %collective-permute-done.3.refs_0_), channel_id=1, source_target_pairs={{0,32},{32,0},{64,96},{96,64},{128,160},{160,128},{192,224},{224,1... | collective-permute-start | bytes 1671176 | tf_op jit(solution)/shard_map/ppermute | solution.py:33
  32.3 7.5 %collective-permute-start.13 = (f32[1,128]{1,0:T(1,128)S(1)}, f32[1,128]{1,0:T(1,128)S(1)}, u32[]{:S(2)}, u32[]{:S(2)}) collective-permute-start(f32[1,128]{1,0:T(1,128)S(1)} %get-tuple-element.40), channel_id=1, source_target_pairs={{0,64},{32,240},{64,128},{96,32},{128,192},{160,96},{192,16},{224,... | collective-permute-start | bytes 1544 | tf_op jit(solution)/shard_map/ppermute | solution.py:33
  32.3 7.5 %collective-permute-start.14 = (f32[1,128]{1,0:T(1,128)S(1)}, f32[1,128]{1,0:T(1,128)S(1)}, u32[]{:S(2)}, u32[]{:S(2)}) collective-permute-start(f32[1,128]{1,0:T(1,128)S(1)} %get-tuple-element.41), channel_id=1, source_target_pairs={{0,208},{32,96},{64,0},{96,160},{128,64},{160,224},{192,128},{224,... | collective-permute-start | bytes 1544 | tf_op jit(solution)/shard_map/ppermute | solution.py:33
  38.9 4.6 %collective-permute-start.8 = (f32[1,128]{1,0:T(1,128)S(1)}, f32[1,128]{1,0:T(1,128)S(1)}, u32[]{:S(2)}, u32[]{:S(2)}) collective-permute-start(f32[1,128]{1,0:T(1,128)S(1)} %get-tuple-element.33), channel_id=1, source_target_pairs={{0,32},{32,0},{64,96},{96,64},{128,160},{160,128},{192,224},{224,1... | collective-permute-start | bytes 1544 | tf_op jit(solution)/shard_map/ppermute | solution.py:33
  39.2 4.3 %collective-permute-start.9 = (f32[1,2048]{1,0:T(1,128)S(1)}, f32[1,2048]{1,0:T(1,128)S(1)}, u32[]{:S(2)}, u32[]{:S(2)}) collective-permute-start(f32[1,2048]{1,0:T(1,128)S(1)} %get-tuple-element.32), channel_id=1, source_target_pairs={{0,4},{32,36},{64,68},{96,100},{128,132},{160,164},{192,196},{224,... | collective-permute-start | bytes 24584 | tf_op jit(solution)/shard_map/ppermute | solution.py:33
  39.8 8.0 %collective-permute-start.11 = (f32[1,2048]{1,0:T(1,128)S(1)}, f32[1,2048]{1,0:T(1,128)S(1)}, u32[]{:S(2)}, u32[]{:S(2)}) collective-permute-start(f32[1,2048]{1,0:T(1,128)S(1)} %get-tuple-element.32), channel_id=1, source_target_pairs={{0,12},{32,44},{64,76},{96,108},{128,140},{160,172},{192,204},{224... | collective-permute-start | bytes 24584 | tf_op jit(solution)/shard_map/ppermute | solution.py:33
  42.1 5.8 %collective-permute-start.10 = (f32[1,2048]{1,0:T(1,128)S(1)}, f32[1,2048]{1,0:T(1,128)S(1)}, u32[]{:S(2)}, u32[]{:S(2)}) collective-permute-start(f32[1,2048]{1,0:T(1,128)S(1)} %get-tuple-element.32), channel_id=1, source_target_pairs={{0,8},{32,40},{64,72},{96,104},{128,136},{160,168},{192,200},{224,... | collective-permute-start | bytes 24584 | tf_op jit(solution)/shard_map/ppermute | solution.py:33
  43.5 7.8 %collective-permute-start.16 = (f32[1,256]{1,0:T(1,128)S(1)}, f32[1,256]{1,0:T(1,128)S(1)}, u32[]{:S(2)}, u32[]{:S(2)}) collective-permute-start(f32[1,256]{1,0:T(1,128)S(1)} %pad_maximum_fusion.1), channel_id=1, source_target_pairs={{0,2},{32,34},{64,66},{96,98},{128,130},{160,162},{192,194},{224,2... | collective-permute-start | bytes 3080 | tf_op jit(solution)/shard_map/ppermute | solution.py:33
  46.8 4.8 %collective-permute-start.17 = (f32[1,256]{1,0:T(1,128)S(1)}, f32[1,256]{1,0:T(1,128)S(1)}, u32[]{:S(2)}, u32[]{:S(2)}) collective-permute-start(f32[1,256]{1,0:T(1,128)S(1)} %pad_maximum_fusion.1), channel_id=1, source_target_pairs={{0,3},{32,35},{64,67},{96,99},{128,131},{160,163},{192,195},{224,2... | collective-permute-start | bytes 3080 | tf_op jit(solution)/shard_map/ppermute | solution.py:33
  47.8 3.7 %collective-permute-start.15 = (f32[1,256]{1,0:T(1,128)S(1)}, f32[1,256]{1,0:T(1,128)S(1)}, u32[]{:S(2)}, u32[]{:S(2)}) collective-permute-start(f32[1,256]{1,0:T(1,128)S(1)} %pad_maximum_fusion.1), channel_id=1, source_target_pairs={{0,1},{32,33},{64,65},{96,97},{128,129},{160,161},{192,193},{224,2... | collective-permute-start | bytes 3080 | tf_op jit(solution)/shard_map/ppermute | solution.py:33
  47.9 9.4 %collective-permute-start.12 = (f32[1,2048]{1,0:T(1,128)S(1)}, f32[1,2048]{1,0:T(1,128)S(1)}, u32[]{:S(2)}, u32[]{:S(2)}) collective-permute-start(f32[1,2048]{1,0:T(1,128)S(1)} %maximum_maximum_fusion), channel_id=1, source_target_pairs={{0,16},{32,48},{64,80},{96,112},{128,144},{160,176},{192,208},{224... | collective-permute-start | bytes 24584 | tf_op jit(solution)/shard_map/ppermute | solution.py:33
  51.6 5.7 %collective-permute-start.18 = (f32[1,128]{1,0:T(1,128)S(1)}, f32[1,128]{1,0:T(1,128)S(1)}, u32[]{:S(2)}, u32[]{:S(2)}) collective-permute-start(f32[1,128]{1,0:T(1,128)S(1)} %slice.20), channel_id=1, source_target_pairs={{0,128},{32,176},{64,192},{96,240},{128,16},{160,32},{192,80},{224... | collective-permute-start | bytes 1544 | tf_op jit(solution)/shard_map/ppermute | solution.py:33

commit v9 on v8

--- a/solution.py
+++ b/solution.py
@@ -182,16 +182,15 @@
     swapped = send(two_other, over_core)
     for_x = [send(top, over_x(d)) for d in (1, 2, 3)]
     swapped, for_x[0] = fence((swapped, for_x[0]))
+    returned = send(jnp.maximum(two_mine, swapped), two_back)
     held = functools.reduce(jnp.maximum, back, split[0])
-    lifts = jnp.concatenate([held, jnp.maximum(two_mine, swapped)], axis=1)
+    top = functools.reduce(jnp.maximum, for_x, top)
+    across = send(top, far)
+    lifts = jnp.maximum(held, returned)
     for_y = [send(lifts, over_y(d)) for d in (1, 2, 3)]
-    top = functools.reduce(jnp.maximum, for_x, top)
-    lifts = functools.reduce(jnp.maximum, for_y, lifts)
-    across = send(top, far)
-    returned = send(lifts[:, cuts:], two_back)
-    across, returned = fence((across, returned))
+    across, *for_y = fence((across, *for_y))
     new_values = jnp.maximum(top, across)
-    cut_gaps = jnp.maximum(returned, lifts[:, :cuts])
+    cut_gaps = functools.reduce(jnp.maximum, for_y, lifts)
     return new_values[0], cut_gaps[0]
 
 

time: 59 us -> 61.1 us (1.036)
  waiting for transfers between devices: 17.1 us -> 21.1 us
  starting transfers between devices: 26.8 us -> 25.2 us
    ppermute x19, waiting for transfers between devices: 17.1 us -> 21.1 us  [send(): return lax.ppermute(block, AXES, routes(move))]
    ppermute x19, starting transfers between devices: 26.8 us -> 25.2 us  [send(): return lax.ppermute(block, AXES, routes(move))]
  transfers between devices with their start and end apart: 19 -> 19, of which waited for: 6 -> 9; matrix products, arithmetic and copies ran while one was open for 0% -> 0% of each run, Pallas kernels for 18% -> 13%
where the time goes in v9:
time: 61.1 us; the launch traced here: 60.9 us
  starting transfers between devices  25.2 us (41%)
  waiting for transfers between devices  21.1 us (35%)
  Pallas kernels  11 us (18%)
  local copies, waits for them, and re-layouts  1.7 us (3%)
  other arithmetic  1.16 us (2%)
  between operations  0.75 us (1%)
    ppermute x19, starting transfers between devices, send(): return lax.ppermute(block, AXES, routes(move))  25.2 us
    ppermute x19, waiting for transfers between devices, send(): return lax.ppermute(block, AXES, routes(move))  21.1 us
    pallas_call x3, Pallas kernels, score(): pl.pallas_call(functools.partial(score_body, tile, tiles, len(blocks)), g...  10.8 us
    unnamed x8, local copies, waits for them, and re-layouts  1.7 us
  transfers between devices with their start and end apart: 19, of which 9 were waited for; matrix products, arithmetic and copies ran while one was open for 0% of the time, Pallas kernels for 13%

profile of v9, /device:TPU:2, one launch (start us, length us, event | category | flops | bytes accessed | tf_op | source)
XLA Modules:
  0.0 60.9 jit_solution(16561778597005276146)
XLA Ops:
  0.6 0.0 copy-start.2
  0.6 1.0 %copy-done.2 = bf16[128,2048]{1,0:T(8,128)(2,1)S(1)} copy-done((bf16[128,2048]{1,0:T(8,128)(2,1)S(1)}, bf16[128,2048]{1,0:T(8,128)(2,1)}, u32[]{:S(2)}) %copy-start.2) | copy-done | bytes 524312
  1.7 0.7 %copy-done.3 = bf16[128]{0:T(256)(128)(2,1)S(1)} copy-done((bf16[128]{0:T(256)(128)(2,1)S(1)}, bf16[128]{0:T(256)(128)(2,1)}, u32[]{:S(2)}) %copy-start.3) | copy-done | bytes 280
  2.3 0.2 shard_map.59.refs_0_
  2.5 0.1 collective-permute-start.2
  2.6 2.0 %collective-permute-start.1 = (bf16[128,2176]{1,0:T(8,128)(2,1)S(1)}, bf16[128,2176]{1,0:T(8,128)(2,1)S(1)}, u32[]{:S(2)}, u32[]{:S(2)}) collective-permute-start(bf16[128,2176]{1,0:T(8,128)(2,1)S(1)} %shard_map.59.refs_0_), channel_id=1, source_target_pairs={{0,64},{32,240},{64,128},{96,32},{128,192},{160,96},{192,16},{224,... | collective-permute-start | bytes 1671176 | tf_op jit(solution)/shard_map/ppermute | solution.py:33
  4.6 4.0 %collective-permute-start = (bf16[128,2176]{1,0:T(8,128)(2,1)S(1)}, bf16[128,2176]{1,0:T(8,128)(2,1)S(1)}, u32[]{:S(2)}, u32[]{:S(2)}) collective-permute-start(bf16[128,2176]{1,0:T(8,128)(2,1)S(1)} %shard_map.59.refs_0_), channel_id=1, source_target_pairs={{0,208},{32,96},{64,0},{96,160},{128,64},{160,224},{192,128},{224,... | collective-permute-start | bytes 1671176 | tf_op jit(solution)/shard_map/ppermute | solution.py:33
  8.7 0.0 collective-permute-done.2.refs_1_
  8.7 0.0 copy-done
  8.7 2.8 %shard_map.60 = (f32[1,2048]{1,0:T(1,128)S(1)}, f32[1,128]{1,0:T(1,128)S(1)}, f32[1,128]{1,0:T(1,128)S(1)}) custom-call(f32[1,2048]{1,0:T(1,128)S(1)} %bitcast.5, f32[1,2048]{1,0:T(1,128)S(1)} %bitcast.6, bf16[2048,2048]{1,0:T(8,128)(2,1)S(1)} %copy-done, bf16[128,2176]{1,0:T(8,128)(2,1)S(1)} %shard_map.59.refs_0_, ...), custom_call_target="tpu_custom_call" | custom-call | flops 2147483648 | bytes 9437184 | tf_op jit(solution)/shard_map/pallas_call | solution.py:141
  11.5 8.1 %collective-permute-done.1.refs_1_ = bf16[128,2176]{1,0:T(8,128)(2,1)S(1)} collective-permute-done((bf16[128,2176]{1,0:T(8,128)(2,1)S(1)}, bf16[128,2176]{1,0:T(8,128)(2,1)S(1)}, u32[]{:S(2)}, u32[]{:S(2)}) %collective-permute-start.1) | collective-permute-done | bytes 557088 | tf_op jit(solution)/shard_map/ppermute | solution.py:33
  19.6 1.5 %collective-permute-done.refs_0_ = bf16[128,2176]{1,0:T(8,128)(2,1)S(1)} collective-permute-done((bf16[128,2176]{1,0:T(8,128)(2,1)S(1)}, bf16[128,2176]{1,0:T(8,128)(2,1)S(1)}, u32[]{:S(2)}, u32[]{:S(2)}) %collective-permute-start) | collective-permute-done | bytes 557088 | tf_op jit(solution)/shard_map/ppermute | solution.py:33
  21.0 0.8 %collective-permute-start.5 = (bf16[128,2176]{1,0:T(8,128)(2,1)S(1)}, bf16[128,2176]{1,0:T(8,128)(2,1)S(1)}, u32[]{:S(2)}, u32[]{:S(2)}) collective-permute-start(bf16[128,2176]{1,0:T(8,128)(2,1)S(1)} %collective-permute-done.1.refs_1_), channel_id=1, source_target_pairs={{0,32},{32,0},{64,96},{96,64},{128,160},{160,128},{192,224},{224,1... | collective-permute-start | bytes 1671176 | tf_op jit(solution)/shard_map/ppermute | solution.py:33
  21.9 0.0 collective-permute-start.4
  21.9 3.4 %collective-permute-start.3 = (bf16[128,2176]{1,0:T(8,128)(2,1)S(1)}, bf16[128,2176]{1,0:T(8,128)(2,1)S(1)}, u32[]{:S(2)}, u32[]{:S(2)}) collective-permute-start(bf16[128,2176]{1,0:T(8,128)(2,1)S(1)} %collective-permute-done.refs_0_), channel_id=1, source_target_pairs={{0,208},{32,96},{64,0},{96,160},{128,64},{160,224},{192,128},{224,... | collective-permute-start | bytes 1671176 | tf_op jit(solution)/shard_map/ppermute | solution.py:33
  25.2 0.0 collective-permute-done.5.refs_3_
  25.2 0.0 collective-permute-done.4.refs_2_
  25.2 5.1 %shard_map.61 = (f32[1,2048]{1,0:T(1,128)S(1)}, f32[1,256]{1,0:T(1,128)S(1)}, f32[1,256]{1,0:T(1,128)S(1)}) custom-call(f32[1,2048]{1,0:T(1,128)S(1)} %bitcast.7, f32[1,2048]{1,0:T(1,128)S(1)} %get-tuple-element.25.prev, bf16[2048,2048]{1,0:T(8,128)(2,1)S(1)} %copy-done, bf16[128,2176]{1,0:T(8,128)(2,1)S(1)} %collective-permute-done.refs_0_, ...), custom_call_target="tpu_custom_call" | custom-call | flops 4294967296 | bytes 10485760 | tf_op jit(solution)/shard_map/pallas_call | solution.py:141
  30.4 0.1 collective-permute-start.6
  30.5 1.1 %collective-permute-done.6 = f32[1,384]{1,0:T(1,128)S(1)} collective-permute-done((f32[1,384]{1,0:T(1,128)S(1)}, f32[1,384]{1,0:T(1,128)S(1)}, u32[]{:S(2)}, u32[]{:S(2)}) %collective-permute-start.6) | collective-permute-done | bytes 1568 | tf_op jit(solution)/shard_map/ppermute | solution.py:33
  31.6 0.7 %collective-permute-done.3.refs_0_ = bf16[128,2176]{1,0:T(8,128)(2,1)S(1)} collective-permute-done((bf16[128,2176]{1,0:T(8,128)(2,1)S(1)}, bf16[128,2176]{1,0:T(8,128)(2,1)S(1)}, u32[]{:S(2)}, u32[]{:S(2)}) %collective-permute-start.3) | collective-permute-done | bytes 557088 | tf_op jit(solution)/shard_map/ppermute | solution.py:33
  32.3 0.0 collective-permute-start.7
  32.3 2.0 %collective-permute-done.7.refs_1_ = bf16[128,2176]{1,0:T(8,128)(2,1)S(1)} collective-permute-done((bf16[128,2176]{1,0:T(8,128)(2,1)S(1)}, bf16[128,2176]{1,0:T(8,128)(2,1)S(1)}, u32[]{:S(2)}, u32[]{:S(2)}) %collective-permute-start.7) | collective-permute-done | bytes 557088 | tf_op jit(solution)/shard_map/ppermute | solution.py:33
  34.2 2.8 %shard_map.62 = (f32[1,2048]{1,0:T(1,128)S(1)}, f32[1,128]{1,0:T(1,128)S(1)}, f32[1,128]{1,0:T(1,128)S(1)}) custom-call(f32[1,2048]{1,0:T(1,128)S(1)} %bitcast.8, f32[1,2048]{1,0:T(1,128)S(1)} %get-tuple-element.32.prev, bf16[2048,2048]{1,0:T(8,128)(2,1)S(1)} %copy-done, bf16[128,2176]{1,0:T(8,128)(2,1)S(1)} %collective-permute-done.3.refs_0_, ...), custom_call_target="tpu_custom_call" | custom-call | flops 2147483648 | bytes 9437184 | tf_op jit(solution)/shard_map/pallas_call | solution.py:141
  37.1 1.6 %collective-permute-start.11 = (f32[1,2048]{1,0:T(1,128)S(1)}, f32[1,2048]{1,0:T(1,128)S(1)}, u32[]{:S(2)}, u32[]{:S(2)}) collective-permute-start(f32[1,2048]{1,0:T(1,128)S(1)} %get-tuple-element.34), channel_id=1, source_target_pairs={{0,12},{32,44},{64,76},{96,108},{128,140},{160,172},{192,204},{224... | collective-permute-start | bytes 24584 | tf_op jit(solution)/shard_map/ppermute | solution.py:33
  38.7 1.1 %collective-permute-start.10 = (f32[1,2048]{1,0:T(1,128)S(1)}, f32[1,2048]{1,0:T(1,128)S(1)}, u32[]{:S(2)}, u32[]{:S(2)}) collective-permute-start(f32[1,2048]{1,0:T(1,128)S(1)} %get-tuple-element.34), channel_id=1, source_target_pairs={{0,8},{32,40},{64,72},{96,104},{128,136},{160,168},{192,200},{224,... | collective-permute-start | bytes 24584 | tf_op jit(solution)/shard_map/ppermute | solution.py:33
  39.8 1.5 %collective-permute-start.9 = (f32[1,2048]{1,0:T(1,128)S(1)}, f32[1,2048]{1,0:T(1,128)S(1)}, u32[]{:S(2)}, u32[]{:S(2)}) collective-permute-start(f32[1,2048]{1,0:T(1,128)S(1)} %get-tuple-element.34), channel_id=1, source_target_pairs={{0,4},{32,36},{64,68},{96,100},{128,132},{160,164},{192,196},{224,... | collective-permute-start | bytes 24584 | tf_op jit(solution)/shard_map/ppermute | solution.py:33
  41.3 0.0 collective-permute-start.8
  41.3 0.0 collective-permute-start.13
  41.3 1.1 %collective-permute-done.8 = f32[1,128]{1,0:T(1,128)S(1)} collective-permute-done((f32[1,128]{1,0:T(1,128)S(1)}, f32[1,128]{1,0:T(1,128)S(1)}, u32[]{:S(2)}, u32[]{:S(2)}) %collective-permute-start.8) | collective-permute-done | bytes 544 | tf_op jit(solution)/shard_map/ppermute | solution.py:33
  42.4 3.7 %collective-permute-start.14 = (f32[1,128]{1,0:T(1,128)S(1)}, f32[1,128]{1,0:T(1,128)S(1)}, u32[]{:S(2)}, u32[]{:S(2)}) collective-permute-start(f32[1,128]{1,0:T(1,128)S(1)} %get-tuple-element.45), channel_id=1, source_target_pairs={{0,208},{32,96},{64,0},{96,160},{128,64},{160,224},{192,128},{224,... | collective-permute-start | bytes 1544 | tf_op jit(solution)/shard_map/ppermute | solution.py:33
  46.1 0.0 collective-permute-done.9
  46.1 0.0 collective-permute-start.15
  46.1 0.0 collective-permute-done.11
  46.1 0.0 collective-permute-done.10
  46.1 2.9 %collective-permute-start.12 = (f32[1,2048]{1,0:T(1,128)S(1)}, f32[1,2048]{1,0:T(1,128)S(1)}, u32[]{:S(2)}, u32[]{:S(2)}) collective-permute-start(f32[1,2048]{1,0:T(1,128)S(1)} %maximum_maximum_fusion), channel_id=1, source_target_pairs={{0,16},{32,48},{64,80},{96,112},{128,144},{160,176},{192,208},{224... | collective-permute-start | bytes 24584 | tf_op jit(solution)/shard_map/ppermute | solution.py:33
  49.0 0.0 collective-permute-done.13
  49.0 0.0 collective-permute-done.14
  49.0 2.7 %collective-permute-done.15 = f32[1,128]{1,0:T(1,128)S(1)} collective-permute-done((f32[1,128]{1,0:T(1,128)S(1)}, f32[1,128]{1,0:T(1,128)S(1)}, u32[]{:S(2)}, u32[]{:S(2)}) %collective-permute-start.15) | collective-permute-done | bytes 544 | tf_op jit(solution)/shard_map/ppermute | solution.py:33
  51.7 3.0 %collective-permute-start.18 = (f32[1,128]{1,0:T(1,128)S(1)}, f32[1,128]{1,0:T(1,128)S(1)}, u32[]{:S(2)}, u32[]{:S(2)}) collective-permute-start(f32[1,128]{1,0:T(1,128)S(1)} %maximum_maximum_fusion.2), channel_id=1, source_target_pairs={{0,3},{32,35},{64,67},{96,99},{128,131},{160,163},{192,195},{224,2... | collective-permute-start | bytes 1544 | tf_op jit(solution)/shard_map/ppermute | solution.py:33
  54.8 0.6 %collective-permute-start.17 = (f32[1,128]{1,0:T(1,128)S(1)}, f32[1,128]{1,0:T(1,128)S(1)}, u32[]{:S(2)}, u32[]{:S(2)}) collective-permute-start(f32[1,128]{1,0:T(1,128)S(1)} %maximum_maximum_fusion.2), channel_id=1, source_target_pairs={{0,2},{32,34},{64,66},{96,98},{128,130},{160,162},{192,194},{224,2... | collective-permute-start | bytes 1544 | tf_op jit(solution)/shard_map/ppermute | solution.py:33
  55.4 0.4 collective-permute-start.16
  55.8 0.7 %collective-permute-done.18 = f32[1,128]{1,0:T(1,128)S(1)} collective-permute-done((f32[1,128]{1,0:T(1,128)S(1)}, f32[1,128]{1,0:T(1,128)S(1)}, u32[]{:S(2)}, u32[]{:S(2)}) %collective-permute-start.18) | collective-permute-done | bytes 544 | tf_op jit(solution)/shard_map/ppermute | solution.py:33
  56.5 3.3 %collective-permute-done.17 = f32[1,128]{1,0:T(1,128)S(1)} collective-permute-done((f32[1,128]{1,0:T(1,128)S(1)}, f32[1,128]{1,0:T(1,128)S(1)}, u32[]{:S(2)}, u32[]{:S(2)}) %collective-permute-start.17) | collective-permute-done | bytes 544 | tf_op jit(solution)/shard_map/ppermute | solution.py:33
  59.8 0.0 collective-permute-done.16
  59.8 0.0 collective-permute-done.12
  59.8 0.6 %max.44 = f32[1,2048]{1,0:T(1,128)} maximum(f32[1,2048]{1,0:T(1,128)S(1)} %maximum_maximum_fusion, f32[1,2048]{1,0:T(1,128)S(1)} %collective-permute-done.12) | non-fusion elementwise | flops 2048 | bytes 24576 | tf_op jit(solution)/shard_map/max | solution.py:192
  60.4 0.5 maximum_bitcast_fusion
  (10 shorter events, 0.0 us)
Async XLA Ops:
  0.6 1.0 %copy-start.2 = (bf16[128,2048]{1,0:T(8,128)(2,1)S(1)}, bf16[128,2048]{1,0:T(8,128)(2,1)}, u32[]{:S(2)}) copy-start(bf16[128,2048]{1,0:T(8,128)(2,1)} %coefficients.1) | copy-start | bytes 1572868
  1.7 0.7 %copy-start.3 = (bf16[128]{0:T(256)(128)(2,1)S(1)}, bf16[128]{0:T(256)(128)(2,1)}, u32[]{:S(2)}) copy-start(bf16[128]{0:T(256)(128)(2,1)} %param.5) | copy-start | bytes 772
  2.3 6.3 %copy-start = (bf16[2048,2048]{1,0:T(8,128)(2,1)S(1)}, bf16[2048,2048]{1,0:T(8,128)(2,1)}, u32[]{:S(2)}) copy-start(bf16[2048,2048]{1,0:T(8,128)(2,1)} %states.5) | copy-start | bytes 25165828
  2.3 6.3 %copy-start.1 = (f32[2048]{0:T(1024)S(1)}, f32[2048]{0:T(1024)}, u32[]{:S(2)}) copy-start(f32[2048]{0:T(1024)} %param.7) | copy-start | bytes 24580
  2.5 6.1 %collective-permute-start.2 = (bf16[128,2176]{1,0:T(8,128)(2,1)S(1)}, bf16[128,2176]{1,0:T(8,128)(2,1)S(1)}, u32[]{:S(2)}, u32[]{:S(2)}) collective-permute-start(bf16[128,2176]{1,0:T(8,128)(2,1)S(1)} %shard_map.59.refs_0_), channel_id=1, source_target_pairs={{0,32},{32,0},{64,96},{96,64},{128,160},{160,128},{192,224},{224,1... | collective-permute-start | bytes 1671176 | tf_op jit(solution)/shard_map/ppermute | solution.py:33
  2.6 16.9 %collective-permute-start.1 = (bf16[128,2176]{1,0:T(8,128)(2,1)S(1)}, bf16[128,2176]{1,0:T(8,128)(2,1)S(1)}, u32[]{:S(2)}, u32[]{:S(2)}) collective-permute-start(bf16[128,2176]{1,0:T(8,128)(2,1)S(1)} %shard_map.59.refs_0_), channel_id=1, source_target_pairs={{0,64},{32,240},{64,128},{96,32},{128,192},{160,96},{192,16},{224,... | collective-permute-start | bytes 1671176 | tf_op jit(solution)/shard_map/ppermute | solution.py:33
  4.6 16.4 %collective-permute-start = (bf16[128,2176]{1,0:T(8,128)(2,1)S(1)}, bf16[128,2176]{1,0:T(8,128)(2,1)S(1)}, u32[]{:S(2)}, u32[]{:S(2)}) collective-permute-start(bf16[128,2176]{1,0:T(8,128)(2,1)S(1)} %shard_map.59.refs_0_), channel_id=1, source_target_pairs={{0,208},{32,96},{64,0},{96,160},{128,64},{160,224},{192,128},{224,... | collective-permute-start | bytes 1671176 | tf_op jit(solution)/shard_map/ppermute | solution.py:33
  21.0 4.2 %collective-permute-start.5 = (bf16[128,2176]{1,0:T(8,128)(2,1)S(1)}, bf16[128,2176]{1,0:T(8,128)(2,1)S(1)}, u32[]{:S(2)}, u32[]{:S(2)}) collective-permute-start(bf16[128,2176]{1,0:T(8,128)(2,1)S(1)} %collective-permute-done.1.refs_1_), channel_id=1, source_target_pairs={{0,32},{32,0},{64,96},{96,64},{128,160},{160,128},{192,224},{224,1... | collective-permute-start | bytes 1671176 | tf_op jit(solution)/shard_map/ppermute | solution.py:33
  21.9 3.4 %collective-permute-start.4 = (bf16[128,2176]{1,0:T(8,128)(2,1)S(1)}, bf16[128,2176]{1,0:T(8,128)(2,1)S(1)}, u32[]{:S(2)}, u32[]{:S(2)}) collective-permute-start(bf16[128,2176]{1,0:T(8,128)(2,1)S(1)} %collective-permute-done.refs_0_), channel_id=1, source_target_pairs={{0,32},{32,0},{64,96},{96,64},{128,160},{160,128},{192,224},{224,1... | collective-permute-start | bytes 1671176 | tf_op jit(solution)/shard_map/ppermute | solution.py:33
  21.9 10.4 %collective-permute-start.3 = (bf16[128,2176]{1,0:T(8,128)(2,1)S(1)}, bf16[128,2176]{1,0:T(8,128)(2,1)S(1)}, u32[]{:S(2)}, u32[]{:S(2)}) collective-permute-start(bf16[128,2176]{1,0:T(8,128)(2,1)S(1)} %collective-permute-done.refs_0_), channel_id=1, source_target_pairs={{0,208},{32,96},{64,0},{96,160},{128,64},{160,224},{192,128},{224,... | collective-permute-start | bytes 1671176 | tf_op jit(solution)/shard_map/ppermute | solution.py:33
  30.4 1.2 %collective-permute-start.6 = (f32[1,384]{1,0:T(1,128)S(1)}, f32[1,384]{1,0:T(1,128)S(1)}, u32[]{:S(2)}, u32[]{:S(2)}) collective-permute-start(f32[1,384]{1,0:T(1,128)S(1)} %pad_maximum_fusion), channel_id=1, source_target_pairs={{0,32},{32,0},{64,96},{96,64},{128,160},{160,128},{192,224},{224,1... | collective-permute-start | bytes 4616 | tf_op jit(solution)/shard_map/ppermute | solution.py:33
  32.3 2.0 %collective-permute-start.7 = (bf16[128,2176]{1,0:T(8,128)(2,1)S(1)}, bf16[128,2176]{1,0:T(8,128)(2,1)S(1)}, u32[]{:S(2)}, u32[]{:S(2)}) collective-permute-start(bf16[128,2176]{1,0:T(8,128)(2,1)S(1)} %collective-permute-done.3.refs_0_), channel_id=1, source_target_pairs={{0,32},{32,0},{64,96},{96,64},{128,160},{160,128},{192,224},{224,1... | collective-permute-start | bytes 1671176 | tf_op jit(solution)/shard_map/ppermute | solution.py:33
  37.1 9.0 %collective-permute-start.11 = (f32[1,2048]{1,0:T(1,128)S(1)}, f32[1,2048]{1,0:T(1,128)S(1)}, u32[]{:S(2)}, u32[]{:S(2)}) collective-permute-start(f32[1,2048]{1,0:T(1,128)S(1)} %get-tuple-element.34), channel_id=1, source_target_pairs={{0,12},{32,44},{64,76},{96,108},{128,140},{160,172},{192,204},{224... | collective-permute-start | bytes 24584 | tf_op jit(solution)/shard_map/ppermute | solution.py:33
  38.7 7.4 %collective-permute-start.10 = (f32[1,2048]{1,0:T(1,128)S(1)}, f32[1,2048]{1,0:T(1,128)S(1)}, u32[]{:S(2)}, u32[]{:S(2)}) collective-permute-start(f32[1,2048]{1,0:T(1,128)S(1)} %get-tuple-element.34), channel_id=1, source_target_pairs={{0,8},{32,40},{64,72},{96,104},{128,136},{160,168},{192,200},{224,... | collective-permute-start | bytes 24584 | tf_op jit(solution)/shard_map/ppermute | solution.py:33
  39.8 6.3 %collective-permute-start.9 = (f32[1,2048]{1,0:T(1,128)S(1)}, f32[1,2048]{1,0:T(1,128)S(1)}, u32[]{:S(2)}, u32[]{:S(2)}) collective-permute-start(f32[1,2048]{1,0:T(1,128)S(1)} %get-tuple-element.34), channel_id=1, source_target_pairs={{0,4},{32,36},{64,68},{96,100},{128,132},{160,164},{192,196},{224,... | collective-permute-start | bytes 24584 | tf_op jit(solution)/shard_map/ppermute | solution.py:33
  41.3 1.1 %collective-permute-start.8 = (f32[1,128]{1,0:T(1,128)S(1)}, f32[1,128]{1,0:T(1,128)S(1)}, u32[]{:S(2)}, u32[]{:S(2)}) collective-permute-start(f32[1,128]{1,0:T(1,128)S(1)} %get-tuple-element.35), channel_id=1, source_target_pairs={{0,32},{32,0},{64,96},{96,64},{128,160},{160,128},{192,224},{224,1... | collective-permute-start | bytes 1544 | tf_op jit(solution)/shard_map/ppermute | solution.py:33
  41.3 7.7 %collective-permute-start.13 = (f32[1,128]{1,0:T(1,128)S(1)}, f32[1,128]{1,0:T(1,128)S(1)}, u32[]{:S(2)}, u32[]{:S(2)}) collective-permute-start(f32[1,128]{1,0:T(1,128)S(1)} %get-tuple-element.44), channel_id=1, source_target_pairs={{0,64},{32,240},{64,128},{96,32},{128,192},{160,96},{192,16},{224,... | collective-permute-start | bytes 1544 | tf_op jit(solution)/shard_map/ppermute | solution.py:33
  42.4 6.6 %collective-permute-start.14 = (f32[1,128]{1,0:T(1,128)S(1)}, f32[1,128]{1,0:T(1,128)S(1)}, u32[]{:S(2)}, u32[]{:S(2)}) collective-permute-start(f32[1,128]{1,0:T(1,128)S(1)} %get-tuple-element.45), channel_id=1, source_target_pairs={{0,208},{32,96},{64,0},{96,160},{128,64},{160,224},{192,128},{224,... | collective-permute-start | bytes 1544 | tf_op jit(solution)/shard_map/ppermute | solution.py:33
  46.1 5.7 %collective-permute-start.15 = (f32[1,128]{1,0:T(1,128)S(1)}, f32[1,128]{1,0:T(1,128)S(1)}, u32[]{:S(2)}, u32[]{:S(2)}) collective-permute-start(f32[1,128]{1,0:T(1,128)S(1)} %max.42), channel_id=1, source_target_pairs={{0,128},{32,176},{64,192},{96,240},{128,16},{160,32},{192,80},{224... | collective-permute-start | bytes 1544 | tf_op jit(solution)/shard_map/ppermute | solution.py:33
  46.1 13.7 %collective-permute-start.12 = (f32[1,2048]{1,0:T(1,128)S(1)}, f32[1,2048]{1,0:T(1,128)S(1)}, u32[]{:S(2)}, u32[]{:S(2)}) collective-permute-start(f32[1,2048]{1,0:T(1,128)S(1)} %maximum_maximum_fusion), channel_id=1, source_target_pairs={{0,16},{32,48},{64,80},{96,112},{128,144},{160,176},{192,208},{224... | collective-permute-start | bytes 24584 | tf_op jit(solution)/shard_map/ppermute | solution.py:33
  51.7 4.8 %collective-permute-start.18 = (f32[1,128]{1,0:T(1,128)S(1)}, f32[1,128]{1,0:T(1,128)S(1)}, u32[]{:S(2)}, u32[]{:S(2)}) collective-permute-start(f32[1,128]{1,0:T(1,128)S(1)} %maximum_maximum_fusion.2), channel_id=1, source_target_pairs={{0,3},{32,35},{64,67},{96,99},{128,131},{160,163},{192,195},{224,2... | collective-permute-start | bytes 1544 | tf_op jit(solution)/shard_map/ppermute | solution.py:33
  54.8 5.0 %collective-permute-start.17 = (f32[1,128]{1,0:T(1,128)S(1)}, f32[1,128]{1,0:T(1,128)S(1)}, u32[]{:S(2)}, u32[]{:S(2)}) collective-permute-start(f32[1,128]{1,0:T(1,128)S(1)} %maximum_maximum_fusion.2), channel_id=1, source_target_pairs={{0,2},{32,34},{64,66},{96,98},{128,130},{160,162},{192,194},{224,2... | collective-permute-start | bytes 1544 | tf_op jit(solution)/shard_map/ppermute | solution.py:33
  55.4 4.4 %collective-permute-start.16 = (f32[1,128]{1,0:T(1,128)S(1)}, f32[1,128]{1,0:T(1,128)S(1)}, u32[]{:S(2)}, u32[]{:S(2)}) collective-permute-start(f32[1,128]{1,0:T(1,128)S(1)} %maximum_maximum_fusion.2), channel_id=1, source_target_pairs={{0,1},{32,33},{64,65},{96,97},{128,129},{160,161},{192,193},{224,2... | collective-permute-start | bytes 1544 | tf_op jit(solution)/shard_map/ppermute | solution.py:33

commit v10 on v8

--- a/solution.py
+++ b/solution.py
@@ -11,7 +11,7 @@
 NX, NY, NZ, NC = 4, 4, 8, 2
 LANES = 128
 PACK_FLOPS = 10**10
-PACK_VMEM = 24 << 20
+PACK_VMEM = 55 << 20
 
 
 def position(x, y, z, c):
@@ -189,8 +189,8 @@
     lifts = functools.reduce(jnp.maximum, for_y, lifts)
     across = send(top, far)
     returned = send(lifts[:, cuts:], two_back)
-    across, returned = fence((across, returned))
     new_values = jnp.maximum(top, across)
+    new_values, returned = fence((new_values, returned))
     cut_gaps = jnp.maximum(returned, lifts[:, :cuts])
     return new_values[0], cut_gaps[0]
 

time: 59 us -> 58.9 us (level)
  Pallas kernels: 11 us -> 12.9 us
  waiting for transfers between devices: 17.1 us -> 15.7 us
  local copies, waits for them, and re-layouts: 1.7 us -> 1.08 us
    pallas_call x1, Pallas kernels: 0.19 us -> 2.13 us  [pack(): pl.pallas_call(pack_body, in_specs=[there, there], out_specs=pl.BlockSpec...]
    ppermute x19, waiting for transfers between devices: 17.1 us -> 15.7 us  [send(): return lax.ppermute(block, AXES, routes(move))]
    unnamed x8 -> x6, local copies, waits for them, and re-layouts: 1.7 us -> 1.08 us
  transfers between devices with their start and end apart: 19 -> 19, of which waited for: 6 -> 7; matrix products, arithmetic and copies ran while one was open for 0% -> 1% of each run, Pallas kernels for 18% -> 18%
where the time goes in v10:
time: 58.9 us; the launch traced here: 58.3 us
  starting transfers between devices  26.7 us (45%)
  waiting for transfers between devices  15.7 us (27%)
  Pallas kernels  12.9 us (22%)
  other arithmetic  1.17 us (2%)
  local copies, waits for them, and re-layouts  1.08 us (2%)
  between operations  0.76 us (1%)
    ppermute x19, starting transfers between devices, send(): return lax.ppermute(block, AXES, routes(move))  26.7 us
    ppermute x19, waiting for transfers between devices, send(): return lax.ppermute(block, AXES, routes(move))  15.7 us
    pallas_call x3, Pallas kernels, score(): pl.pallas_call(functools.partial(score_body, tile, tiles, len(blocks)), g...  10.7 us
    pallas_call x1, Pallas kernels, pack(): pl.pallas_call(pack_body, in_specs=[there, there], out_specs=pl.BlockSpec...  2.13 us
  transfers between devices with their start and end apart: 19, of which 7 were waited for; matrix products, arithmetic and copies ran while one was open for 1% of the time, Pallas kernels for 18%

profile of v10, /device:TPU:2, one launch (start us, length us, event | category | flops | bytes accessed | tf_op | source)
XLA Modules:
  0.0 58.3 jit_solution(12636808319446559627)
XLA Ops:
  0.6 0.0 copy-start
  0.6 0.0 copy-start.2
  0.7 2.1 %shard_map.59.refs_0_ = bf16[128,2176]{1,0:T(8,128)(2,1)} custom-call(bf16[128,2048]{1,0:T(8,128)(2,1)} %coefficients.1, bf16[1,128]{1,0:T(2,128)(2,1)} %bitcast.10), custom_call_target="tpu_custom_call" | custom-call | flops 10000000000 | bytes 1048576 | tf_op jit(solution)/shard_map/pallas_call | solution.py:82
  2.8 0.1 collective-permute-start.2
  2.9 2.0 %collective-permute-start.1 = (bf16[128,2176]{1,0:T(8,128)(2,1)}, bf16[128,2176]{1,0:T(8,128)(2,1)S(1)}, u32[]{:S(2)}, u32[]{:S(2)}) collective-permute-start(bf16[128,2176]{1,0:T(8,128)(2,1)} %shard_map.59.refs_0_), channel_id=1, source_target_pairs={{0,64},{32,240},{64,128},{96,32},{128,192},{160,96},{192,16},{224,... | collective-permute-start | bytes 1671176 | tf_op jit(solution)/shard_map/ppermute | solution.py:33
  4.9 4.0 %collective-permute-start = (bf16[128,2176]{1,0:T(8,128)(2,1)}, bf16[128,2176]{1,0:T(8,128)(2,1)S(1)}, u32[]{:S(2)}, u32[]{:S(2)}) collective-permute-start(bf16[128,2176]{1,0:T(8,128)(2,1)} %shard_map.59.refs_0_), channel_id=1, source_target_pairs={{0,208},{32,96},{64,0},{96,160},{128,64},{160,224},{192,128},{224,... | collective-permute-start | bytes 1671176 | tf_op jit(solution)/shard_map/ppermute | solution.py:33
  8.9 0.0 collective-permute-done.2.refs_1_
  8.9 0.0 copy-done.2
  8.9 1.1 %copy-done.1 = bf16[128,2176]{1,0:T(8,128)(2,1)S(1)} copy-done((bf16[128,2176]{1,0:T(8,128)(2,1)S(1)}, bf16[128,2176]{1,0:T(8,128)(2,1)}, u32[]{:S(2)}) %copy-start.1) | copy-done | bytes 557080
  10.0 2.8 %shard_map.60 = (f32[1,2048]{1,0:T(1,128)S(1)}, f32[1,128]{1,0:T(1,128)S(1)}, f32[1,128]{1,0:T(1,128)S(1)}) custom-call(f32[1,2048]{1,0:T(1,128)S(1)} %bitcast.5, f32[1,2048]{1,0:T(1,128)S(1)} %bitcast.6, bf16[2048,2048]{1,0:T(8,128)(2,1)S(1)} %copy-done, bf16[128,2176]{1,0:T(8,128)(2,1)S(1)} %copy-done.1, bf16[128,2176]{1,0:T(8,128)(2,1)S(1)} %collective-permute-done.2.refs_1_), custom_call_target="tpu_custom_call" | custom-call | flops 2147483648 | bytes 9437184 | tf_op jit(solution)/shard_map/pallas_call | solution.py:141
  12.8 7.2 %collective-permute-done.1.refs_1_ = bf16[128,2176]{1,0:T(8,128)(2,1)S(1)} collective-permute-done((bf16[128,2176]{1,0:T(8,128)(2,1)}, bf16[128,2176]{1,0:T(8,128)(2,1)S(1)}, u32[]{:S(2)}, u32[]{:S(2)}) %collective-permute-start.1) | collective-permute-done | bytes 557088 | tf_op jit(solution)/shard_map/ppermute | solution.py:33
  20.0 1.6 %collective-permute-done.refs_0_ = bf16[128,2176]{1,0:T(8,128)(2,1)S(1)} collective-permute-done((bf16[128,2176]{1,0:T(8,128)(2,1)}, bf16[128,2176]{1,0:T(8,128)(2,1)S(1)}, u32[]{:S(2)}, u32[]{:S(2)}) %collective-permute-start) | collective-permute-done | bytes 557088 | tf_op jit(solution)/shard_map/ppermute | solution.py:33
  21.6 0.7 %collective-permute-start.5 = (bf16[128,2176]{1,0:T(8,128)(2,1)S(1)}, bf16[128,2176]{1,0:T(8,128)(2,1)S(1)}, u32[]{:S(2)}, u32[]{:S(2)}) collective-permute-start(bf16[128,2176]{1,0:T(8,128)(2,1)S(1)} %collective-permute-done.1.refs_1_), channel_id=1, source_target_pairs={{0,32},{32,0},{64,96},{96,64},{128,160},{160,128},{192,224},{224,1... | collective-permute-start | bytes 1671176 | tf_op jit(solution)/shard_map/ppermute | solution.py:33
  22.3 0.0 collective-permute-start.4
  22.3 3.4 %collective-permute-start.3 = (bf16[128,2176]{1,0:T(8,128)(2,1)S(1)}, bf16[128,2176]{1,0:T(8,128)(2,1)S(1)}, u32[]{:S(2)}, u32[]{:S(2)}) collective-permute-start(bf16[128,2176]{1,0:T(8,128)(2,1)S(1)} %collective-permute-done.refs_0_), channel_id=1, source_target_pairs={{0,208},{32,96},{64,0},{96,160},{128,64},{160,224},{192,128},{224,... | collective-permute-start | bytes 1671176 | tf_op jit(solution)/shard_map/ppermute | solution.py:33
  25.7 0.0 collective-permute-done.5.refs_3_
  25.7 0.0 collective-permute-done.4.refs_2_
  25.7 5.1 %shard_map.61 = (f32[1,2048]{1,0:T(1,128)S(1)}, f32[1,256]{1,0:T(1,128)S(1)}, f32[1,256]{1,0:T(1,128)S(1)}) custom-call(f32[1,2048]{1,0:T(1,128)S(1)} %bitcast.7, f32[1,2048]{1,0:T(1,128)S(1)} %get-tuple-element.23.prev, bf16[2048,2048]{1,0:T(8,128)(2,1)S(1)} %copy-done, bf16[128,2176]{1,0:T(8,128)(2,1)S(1)} %collective-permute-done.refs_0_, ...), custom_call_target="tpu_custom_call" | custom-call | flops 4294967296 | bytes 10485760 | tf_op jit(solution)/shard_map/pallas_call | solution.py:141
  30.8 0.1 collective-permute-start.6
  30.9 1.1 %collective-permute-done.6 = f32[1,384]{1,0:T(1,128)S(1)} collective-permute-done((f32[1,384]{1,0:T(1,128)S(1)}, f32[1,384]{1,0:T(1,128)S(1)}, u32[]{:S(2)}, u32[]{:S(2)}) %collective-permute-start.6) | collective-permute-done | bytes 1568 | tf_op jit(solution)/shard_map/ppermute | solution.py:33
  32.1 0.7 %collective-permute-done.3.refs_0_ = bf16[128,2176]{1,0:T(8,128)(2,1)S(1)} collective-permute-done((bf16[128,2176]{1,0:T(8,128)(2,1)S(1)}, bf16[128,2176]{1,0:T(8,128)(2,1)S(1)}, u32[]{:S(2)}, u32[]{:S(2)}) %collective-permute-start.3) | collective-permute-done | bytes 557088 | tf_op jit(solution)/shard_map/ppermute | solution.py:33
  32.8 0.0 collective-permute-start.7
  32.8 0.0 collective-permute-start.13
  32.8 3.8 %collective-permute-start.14 = (f32[1,128]{1,0:T(1,128)S(1)}, f32[1,128]{1,0:T(1,128)S(1)}, u32[]{:S(2)}, u32[]{:S(2)}) collective-permute-start(f32[1,128]{1,0:T(1,128)S(1)} %get-tuple-element.41), channel_id=1, source_target_pairs={{0,208},{32,96},{64,0},{96,160},{128,64},{160,224},{192,128},{224,... | collective-permute-start | bytes 1544 | tf_op jit(solution)/shard_map/ppermute | solution.py:33
  36.5 0.0 collective-permute-done.7.refs_1_
  36.5 2.8 %shard_map.62 = (f32[1,2048]{1,0:T(1,128)S(1)}, f32[1,128]{1,0:T(1,128)S(1)}, f32[1,128]{1,0:T(1,128)S(1)}) custom-call(f32[1,2048]{1,0:T(1,128)S(1)} %bitcast.8, f32[1,2048]{1,0:T(1,128)S(1)} %get-tuple-element.30.prev, bf16[2048,2048]{1,0:T(8,128)(2,1)S(1)} %copy-done, bf16[128,2176]{1,0:T(8,128)(2,1)S(1)} %collective-permute-done.3.refs_0_, ...), custom_call_target="tpu_custom_call" | custom-call | flops 2147483648 | bytes 9437184 | tf_op jit(solution)/shard_map/pallas_call | solution.py:141
  39.4 0.2 collective-permute-start.8
  39.6 0.7 %collective-permute-start.9 = (f32[1,2048]{1,0:T(1,128)S(1)}, f32[1,2048]{1,0:T(1,128)S(1)}, u32[]{:S(2)}, u32[]{:S(2)}) collective-permute-start(f32[1,2048]{1,0:T(1,128)S(1)} %get-tuple-element.32), channel_id=1, source_target_pairs={{0,4},{32,36},{64,68},{96,100},{128,132},{160,164},{192,196},{224,... | collective-permute-start | bytes 24584 | tf_op jit(solution)/shard_map/ppermute | solution.py:33
  40.3 0.0 collective-permute-done.13
  40.3 0.0 collective-permute-done.14
  40.3 2.2 %collective-permute-start.11 = (f32[1,2048]{1,0:T(1,128)S(1)}, f32[1,2048]{1,0:T(1,128)S(1)}, u32[]{:S(2)}, u32[]{:S(2)}) collective-permute-start(f32[1,2048]{1,0:T(1,128)S(1)} %get-tuple-element.32), channel_id=1, source_target_pairs={{0,12},{32,44},{64,76},{96,108},{128,140},{160,172},{192,204},{224... | collective-permute-start | bytes 24584 | tf_op jit(solution)/shard_map/ppermute | solution.py:33
  42.5 1.4 %collective-permute-start.10 = (f32[1,2048]{1,0:T(1,128)S(1)}, f32[1,2048]{1,0:T(1,128)S(1)}, u32[]{:S(2)}, u32[]{:S(2)}) collective-permute-start(f32[1,2048]{1,0:T(1,128)S(1)} %get-tuple-element.32), channel_id=1, source_target_pairs={{0,8},{32,40},{64,72},{96,104},{128,136},{160,168},{192,200},{224,... | collective-permute-start | bytes 24584 | tf_op jit(solution)/shard_map/ppermute | solution.py:33
  43.9 0.0 collective-permute-done.8
  43.9 0.0 collective-permute-done.9
  44.0 3.3 %collective-permute-start.16 = (f32[1,256]{1,0:T(1,128)S(1)}, f32[1,256]{1,0:T(1,128)S(1)}, u32[]{:S(2)}, u32[]{:S(2)}) collective-permute-start(f32[1,256]{1,0:T(1,128)S(1)} %pad_maximum_fusion.1), channel_id=1, source_target_pairs={{0,2},{32,34},{64,66},{96,98},{128,130},{160,162},{192,194},{224,2... | collective-permute-start | bytes 3080 | tf_op jit(solution)/shard_map/ppermute | solution.py:33
  47.2 1.1 %collective-permute-start.17 = (f32[1,256]{1,0:T(1,128)S(1)}, f32[1,256]{1,0:T(1,128)S(1)}, u32[]{:S(2)}, u32[]{:S(2)}) collective-permute-start(f32[1,256]{1,0:T(1,128)S(1)} %pad_maximum_fusion.1), channel_id=1, source_target_pairs={{0,3},{32,35},{64,67},{96,99},{128,131},{160,163},{192,195},{224,2... | collective-permute-start | bytes 3080 | tf_op jit(solution)/shard_map/ppermute | solution.py:33
  48.3 0.0 collective-permute-start.15
  48.3 0.0 collective-permute-done.11
  48.3 0.0 collective-permute-done.10
  48.3 3.5 %collective-permute-start.12 = (f32[1,2048]{1,0:T(1,128)S(1)}, f32[1,2048]{1,0:T(1,128)S(1)}, u32[]{:S(2)}, u32[]{:S(2)}) collective-permute-start(f32[1,2048]{1,0:T(1,128)S(1)} %maximum_maximum_fusion), channel_id=1, source_target_pairs={{0,16},{32,48},{64,80},{96,112},{128,144},{160,176},{192,208},{224... | collective-permute-start | bytes 24584 | tf_op jit(solution)/shard_map/ppermute | solution.py:33
  51.8 0.0 collective-permute-done.16
  51.8 0.2 collective-permute-done.17
  52.0 0.0 collective-permute-done.15
  52.0 0.2 collective-permute-start.18
  52.3 3.7 %collective-permute-done.12 = f32[1,2048]{1,0:T(1,128)S(1)} collective-permute-done((f32[1,2048]{1,0:T(1,128)S(1)}, f32[1,2048]{1,0:T(1,128)S(1)}, u32[]{:S(2)}, u32[]{:S(2)}) %collective-permute-start.12) | collective-permute-done | bytes 8224 | tf_op jit(solution)/shard_map/ppermute | solution.py:33
  56.0 0.6 %max.40 = f32[1,2048]{1,0:T(1,128)} maximum(f32[1,2048]{1,0:T(1,128)S(1)} %maximum_maximum_fusion, f32[1,2048]{1,0:T(1,128)S(1)} %collective-permute-done.12) | non-fusion elementwise | flops 2048 | bytes 24576 | tf_op jit(solution)/shard_map/max | solution.py:192
  56.6 1.2 %collective-permute-done.18 = f32[1,128]{1,0:T(1,128)S(1)} collective-permute-done((f32[1,128]{1,0:T(1,128)S(1)}, f32[1,128]{1,0:T(1,128)S(1)}, u32[]{:S(2)}, u32[]{:S(2)}) %collective-permute-start.18) | collective-permute-done | bytes 544 | tf_op jit(solution)/shard_map/ppermute | solution.py:33
  57.8 0.5 fusion
  (11 shorter events, 0.1 us)
Async XLA Ops:
  0.6 8.3 %copy-start = (bf16[2048,2048]{1,0:T(8,128)(2,1)S(1)}, bf16[2048,2048]{1,0:T(8,128)(2,1)}, u32[]{:S(2)}) copy-start(bf16[2048,2048]{1,0:T(8,128)(2,1)} %states.5) | copy-start | bytes 25165828
  0.6 8.3 %copy-start.2 = (f32[2048]{0:T(1024)S(1)}, f32[2048]{0:T(1024)}, u32[]{:S(2)}) copy-start(f32[2048]{0:T(1024)} %param.7) | copy-start | bytes 24580
  2.8 6.1 %collective-permute-start.2 = (bf16[128,2176]{1,0:T(8,128)(2,1)}, bf16[128,2176]{1,0:T(8,128)(2,1)S(1)}, u32[]{:S(2)}, u32[]{:S(2)}) collective-permute-start(bf16[128,2176]{1,0:T(8,128)(2,1)} %shard_map.59.refs_0_), channel_id=1, source_target_pairs={{0,32},{32,0},{64,96},{96,64},{128,160},{160,128},{192,224},{224,1... | collective-permute-start | bytes 1671176 | tf_op jit(solution)/shard_map/ppermute | solution.py:33
  2.9 17.2 %collective-permute-start.1 = (bf16[128,2176]{1,0:T(8,128)(2,1)}, bf16[128,2176]{1,0:T(8,128)(2,1)S(1)}, u32[]{:S(2)}, u32[]{:S(2)}) collective-permute-start(bf16[128,2176]{1,0:T(8,128)(2,1)} %shard_map.59.refs_0_), channel_id=1, source_target_pairs={{0,64},{32,240},{64,128},{96,32},{128,192},{160,96},{192,16},{224,... | collective-permute-start | bytes 1671176 | tf_op jit(solution)/shard_map/ppermute | solution.py:33
  4.9 16.7 %collective-permute-start = (bf16[128,2176]{1,0:T(8,128)(2,1)}, bf16[128,2176]{1,0:T(8,128)(2,1)S(1)}, u32[]{:S(2)}, u32[]{:S(2)}) collective-permute-start(bf16[128,2176]{1,0:T(8,128)(2,1)} %shard_map.59.refs_0_), channel_id=1, source_target_pairs={{0,208},{32,96},{64,0},{96,160},{128,64},{160,224},{192,128},{224,... | collective-permute-start | bytes 1671176 | tf_op jit(solution)/shard_map/ppermute | solution.py:33
  8.9 1.1 %copy-start.1 = (bf16[128,2176]{1,0:T(8,128)(2,1)S(1)}, bf16[128,2176]{1,0:T(8,128)(2,1)}, u32[]{:S(2)}) copy-start(bf16[128,2176]{1,0:T(8,128)(2,1)} %shard_map.59.refs_0_) | copy-start | bytes 1671172
  21.6 4.1 %collective-permute-start.5 = (bf16[128,2176]{1,0:T(8,128)(2,1)S(1)}, bf16[128,2176]{1,0:T(8,128)(2,1)S(1)}, u32[]{:S(2)}, u32[]{:S(2)}) collective-permute-start(bf16[128,2176]{1,0:T(8,128)(2,1)S(1)} %collective-permute-done.1.refs_1_), channel_id=1, source_target_pairs={{0,32},{32,0},{64,96},{96,64},{128,160},{160,128},{192,224},{224,1... | collective-permute-start | bytes 1671176 | tf_op jit(solution)/shard_map/ppermute | solution.py:33
  22.3 3.4 %collective-permute-start.4 = (bf16[128,2176]{1,0:T(8,128)(2,1)S(1)}, bf16[128,2176]{1,0:T(8,128)(2,1)S(1)}, u32[]{:S(2)}, u32[]{:S(2)}) collective-permute-start(bf16[128,2176]{1,0:T(8,128)(2,1)S(1)} %collective-permute-done.refs_0_), channel_id=1, source_target_pairs={{0,32},{32,0},{64,96},{96,64},{128,160},{160,128},{192,224},{224,1... | collective-permute-start | bytes 1671176 | tf_op jit(solution)/shard_map/ppermute | solution.py:33
  22.3 10.4 %collective-permute-start.3 = (bf16[128,2176]{1,0:T(8,128)(2,1)S(1)}, bf16[128,2176]{1,0:T(8,128)(2,1)S(1)}, u32[]{:S(2)}, u32[]{:S(2)}) collective-permute-start(bf16[128,2176]{1,0:T(8,128)(2,1)S(1)} %collective-permute-done.refs_0_), channel_id=1, source_target_pairs={{0,208},{32,96},{64,0},{96,160},{128,64},{160,224},{192,128},{224,... | collective-permute-start | bytes 1671176 | tf_op jit(solution)/shard_map/ppermute | solution.py:33
  30.8 1.2 %collective-permute-start.6 = (f32[1,384]{1,0:T(1,128)S(1)}, f32[1,384]{1,0:T(1,128)S(1)}, u32[]{:S(2)}, u32[]{:S(2)}) collective-permute-start(f32[1,384]{1,0:T(1,128)S(1)} %pad_maximum_fusion), channel_id=1, source_target_pairs={{0,32},{32,0},{64,96},{96,64},{128,160},{160,128},{192,224},{224,1... | collective-permute-start | bytes 4616 | tf_op jit(solution)/shard_map/ppermute | solution.py:33
  32.8 3.8 %collective-permute-start.7 = (bf16[128,2176]{1,0:T(8,128)(2,1)S(1)}, bf16[128,2176]{1,0:T(8,128)(2,1)S(1)}, u32[]{:S(2)}, u32[]{:S(2)}) collective-permute-start(bf16[128,2176]{1,0:T(8,128)(2,1)S(1)} %collective-permute-done.3.refs_0_), channel_id=1, source_target_pairs={{0,32},{32,0},{64,96},{96,64},{128,160},{160,128},{192,224},{224,1... | collective-permute-start | bytes 1671176 | tf_op jit(solution)/shard_map/ppermute | solution.py:33
  32.8 7.5 %collective-permute-start.13 = (f32[1,128]{1,0:T(1,128)S(1)}, f32[1,128]{1,0:T(1,128)S(1)}, u32[]{:S(2)}, u32[]{:S(2)}) collective-permute-start(f32[1,128]{1,0:T(1,128)S(1)} %get-tuple-element.40), channel_id=1, source_target_pairs={{0,64},{32,240},{64,128},{96,32},{128,192},{160,96},{192,16},{224,... | collective-permute-start | bytes 1544 | tf_op jit(solution)/shard_map/ppermute | solution.py:33
  32.8 7.5 %collective-permute-start.14 = (f32[1,128]{1,0:T(1,128)S(1)}, f32[1,128]{1,0:T(1,128)S(1)}, u32[]{:S(2)}, u32[]{:S(2)}) collective-permute-start(f32[1,128]{1,0:T(1,128)S(1)} %get-tuple-element.41), channel_id=1, source_target_pairs={{0,208},{32,96},{64,0},{96,160},{128,64},{160,224},{192,128},{224,... | collective-permute-start | bytes 1544 | tf_op jit(solution)/shard_map/ppermute | solution.py:33
  39.4 4.6 %collective-permute-start.8 = (f32[1,128]{1,0:T(1,128)S(1)}, f32[1,128]{1,0:T(1,128)S(1)}, u32[]{:S(2)}, u32[]{:S(2)}) collective-permute-start(f32[1,128]{1,0:T(1,128)S(1)} %get-tuple-element.33), channel_id=1, source_target_pairs={{0,32},{32,0},{64,96},{96,64},{128,160},{160,128},{192,224},{224,1... | collective-permute-start | bytes 1544 | tf_op jit(solution)/shard_map/ppermute | solution.py:33
  39.6 4.3 %collective-permute-start.9 = (f32[1,2048]{1,0:T(1,128)S(1)}, f32[1,2048]{1,0:T(1,128)S(1)}, u32[]{:S(2)}, u32[]{:S(2)}) collective-permute-start(f32[1,2048]{1,0:T(1,128)S(1)} %get-tuple-element.32), channel_id=1, source_target_pairs={{0,4},{32,36},{64,68},{96,100},{128,132},{160,164},{192,196},{224,... | collective-permute-start | bytes 24584 | tf_op jit(solution)/shard_map/ppermute | solution.py:33
  40.3 8.0 %collective-permute-start.11 = (f32[1,2048]{1,0:T(1,128)S(1)}, f32[1,2048]{1,0:T(1,128)S(1)}, u32[]{:S(2)}, u32[]{:S(2)}) collective-permute-start(f32[1,2048]{1,0:T(1,128)S(1)} %get-tuple-element.32), channel_id=1, source_target_pairs={{0,12},{32,44},{64,76},{96,108},{128,140},{160,172},{192,204},{224... | collective-permute-start | bytes 24584 | tf_op jit(solution)/shard_map/ppermute | solution.py:33
  42.5 5.8 %collective-permute-start.10 = (f32[1,2048]{1,0:T(1,128)S(1)}, f32[1,2048]{1,0:T(1,128)S(1)}, u32[]{:S(2)}, u32[]{:S(2)}) collective-permute-start(f32[1,2048]{1,0:T(1,128)S(1)} %get-tuple-element.32), channel_id=1, source_target_pairs={{0,8},{32,40},{64,72},{96,104},{128,136},{160,168},{192,200},{224,... | collective-permute-start | bytes 24584 | tf_op jit(solution)/shard_map/ppermute | solution.py:33
  44.0 7.8 %collective-permute-start.16 = (f32[1,256]{1,0:T(1,128)S(1)}, f32[1,256]{1,0:T(1,128)S(1)}, u32[]{:S(2)}, u32[]{:S(2)}) collective-permute-start(f32[1,256]{1,0:T(1,128)S(1)} %pad_maximum_fusion.1), channel_id=1, source_target_pairs={{0,2},{32,34},{64,66},{96,98},{128,130},{160,162},{192,194},{224,2... | collective-permute-start | bytes 3080 | tf_op jit(solution)/shard_map/ppermute | solution.py:33
  47.2 4.8 %collective-permute-start.17 = (f32[1,256]{1,0:T(1,128)S(1)}, f32[1,256]{1,0:T(1,128)S(1)}, u32[]{:S(2)}, u32[]{:S(2)}) collective-permute-start(f32[1,256]{1,0:T(1,128)S(1)} %pad_maximum_fusion.1), channel_id=1, source_target_pairs={{0,3},{32,35},{64,67},{96,99},{128,131},{160,163},{192,195},{224,2... | collective-permute-start | bytes 3080 | tf_op jit(solution)/shard_map/ppermute | solution.py:33
  48.3 3.7 %collective-permute-start.15 = (f32[1,256]{1,0:T(1,128)S(1)}, f32[1,256]{1,0:T(1,128)S(1)}, u32[]{:S(2)}, u32[]{:S(2)}) collective-permute-start(f32[1,256]{1,0:T(1,128)S(1)} %pad_maximum_fusion.1), channel_id=1, source_target_pairs={{0,1},{32,33},{64,65},{96,97},{128,129},{160,161},{192,193},{224,2... | collective-permute-start | bytes 3080 | tf_op jit(solution)/shard_map/ppermute | solution.py:33
  48.3 7.6 %collective-permute-start.12 = (f32[1,2048]{1,0:T(1,128)S(1)}, f32[1,2048]{1,0:T(1,128)S(1)}, u32[]{:S(2)}, u32[]{:S(2)}) collective-permute-start(f32[1,2048]{1,0:T(1,128)S(1)} %maximum_maximum_fusion), channel_id=1, source_target_pairs={{0,16},{32,48},{64,80},{96,112},{128,144},{160,176},{192,208},{224... | collective-permute-start | bytes 24584 | tf_op jit(solution)/shard_map/ppermute | solution.py:33
  52.0 5.7 %collective-permute-start.18 = (f32[1,128]{1,0:T(1,128)S(1)}, f32[1,128]{1,0:T(1,128)S(1)}, u32[]{:S(2)}, u32[]{:S(2)}) collective-permute-start(f32[1,128]{1,0:T(1,128)S(1)} %slice.20), channel_id=1, source_target_pairs={{0,128},{32,176},{64,192},{96,240},{128,16},{160,32},{192,80},{224... | collective-permute-start | bytes 1544 | tf_op jit(solution)/shard_map/ppermute | solution.py:33

commit v11 on v10

--- a/solution.py
+++ b/solution.py
@@ -10,8 +10,8 @@
 AXES = ("grp", "cut", "st")
 NX, NY, NZ, NC = 4, 4, 8, 2
 LANES = 128
-PACK_FLOPS = 10**10
-PACK_VMEM = 55 << 20
+PACK_FLOPS = 10**7
+PACK_VMEM = 56 << 20
 
 
 def position(x, y, z, c):

time: 58.9 us -> 58.8 us (level)
  local copies, waits for them, and re-layouts: 1.08 us -> 5.14 us
  waiting for transfers between devices: 15.7 us -> 11.7 us
    ppermute x19, waiting for transfers between devices: 15.7 us -> 11.7 us  [send(): return lax.ppermute(block, AXES, routes(move))]
    unnamed x6 -> x8, local copies, waits for them, and re-layouts: 1.08 us -> 5.13 us
  transfers between devices with their start and end apart: 19 -> 19, of which waited for: 7 -> 7; matrix products, arithmetic and copies ran while one was open for 1% -> 1% of each run, Pallas kernels for 18% -> 19%
where the time goes in v11:
time: 58.8 us; the launch traced here: 58.1 us
  starting transfers between devices  26.7 us (45%)
  Pallas kernels  12.7 us (22%)
  waiting for transfers between devices  11.7 us (20%)
  local copies, waits for them, and re-layouts  5.14 us (9%)
  other arithmetic  1.17 us (2%)
  between operations  0.74 us (1%)
    ppermute x19, starting transfers between devices, send(): return lax.ppermute(block, AXES, routes(move))  26.7 us
    ppermute x19, waiting for transfers between devices, send(): return lax.ppermute(block, AXES, routes(move))  11.7 us
    pallas_call x3, Pallas kernels, score(): pl.pallas_call(functools.partial(score_body, tile, tiles, len(blocks)), g...  10.8 us
    unnamed x8, local copies, waits for them, and re-layouts  5.13 us
    pallas_call x1, Pallas kernels, pack(): pl.pallas_call(pack_body, in_specs=[there, there], out_specs=pl.BlockSpec...  1.98 us
  transfers between devices with their start and end apart: 19, of which 7 were waited for; matrix products, arithmetic and copies ran while one was open for 1% of the time, Pallas kernels for 19%

profile of v11, /device:TPU:2, one launch (start us, length us, event | category | flops | bytes accessed | tf_op | source)
XLA Modules:
  0.0 58.1 jit_solution(174031511645131329)
XLA Ops:
  0.6 2.0 %shard_map.59.refs_0_ = bf16[128,2176]{1,0:T(8,128)(2,1)} custom-call(bf16[128,2048]{1,0:T(8,128)(2,1)} %coefficients.1, bf16[1,128]{1,0:T(2,128)(2,1)} %bitcast.10), custom_call_target="tpu_custom_call" | custom-call | flops 10000000 | bytes 1048576 | tf_op jit(solution)/shard_map/pallas_call | solution.py:82
  2.6 0.1 collective-permute-start.2
  2.7 2.0 %collective-permute-start.1 = (bf16[128,2176]{1,0:T(8,128)(2,1)}, bf16[128,2176]{1,0:T(8,128)(2,1)S(1)}, u32[]{:S(2)}, u32[]{:S(2)}) collective-permute-start(bf16[128,2176]{1,0:T(8,128)(2,1)} %shard_map.59.refs_0_), channel_id=1, source_target_pairs={{0,64},{32,240},{64,128},{96,32},{128,192},{160,96},{192,16},{224,... | collective-permute-start | bytes 1671176 | tf_op jit(solution)/shard_map/ppermute | solution.py:33
  4.7 4.0 %collective-permute-start = (bf16[128,2176]{1,0:T(8,128)(2,1)}, bf16[128,2176]{1,0:T(8,128)(2,1)S(1)}, u32[]{:S(2)}, u32[]{:S(2)}) collective-permute-start(bf16[128,2176]{1,0:T(8,128)(2,1)} %shard_map.59.refs_0_), channel_id=1, source_target_pairs={{0,208},{32,96},{64,0},{96,160},{128,64},{160,224},{192,128},{224,... | collective-permute-start | bytes 1671176 | tf_op jit(solution)/shard_map/ppermute | solution.py:33
  8.7 0.0 collective-permute-done.2.refs_1_
  8.7 3.4 %copy-done = bf16[2048,2048]{1,0:T(8,128)(2,1)S(1)} copy-done((bf16[2048,2048]{1,0:T(8,128)(2,1)S(1)}, bf16[2048,2048]{1,0:T(8,128)(2,1)}, u32[]{:S(2)}) %copy-start) | copy-done | bytes 8388632
  12.1 1.1 %copy-done.2 = bf16[128,2176]{1,0:T(8,128)(2,1)S(1)} copy-done((bf16[128,2176]{1,0:T(8,128)(2,1)S(1)}, bf16[128,2176]{1,0:T(8,128)(2,1)}, u32[]{:S(2)}) %copy-start.2) | copy-done | bytes 557080
  13.2 0.7 %copy-done.3 = f32[2048]{0:T(1024)S(1)} copy-done((f32[2048]{0:T(1024)S(1)}, f32[2048]{0:T(1024)}, u32[]{:S(2)}) %copy-start.3) | copy-done | bytes 8216
  13.9 2.8 %shard_map.60 = (f32[1,2048]{1,0:T(1,128)S(1)}, f32[1,128]{1,0:T(1,128)S(1)}, f32[1,128]{1,0:T(1,128)S(1)}) custom-call(f32[1,2048]{1,0:T(1,128)S(1)} %bitcast.5, f32[1,2048]{1,0:T(1,128)S(1)} %bitcast.6, bf16[2048,2048]{1,0:T(8,128)(2,1)S(1)} %copy-done, bf16[128,2176]{1,0:T(8,128)(2,1)S(1)} %copy-done.2, bf16[128,2176]{1,0:T(8,128)(2,1)S(1)} %collective-permute-done.2.refs_1_), custom_call_target="tpu_custom_call" | custom-call | flops 2147483648 | bytes 9437184 | tf_op jit(solution)/shard_map/pallas_call | solution.py:141
  16.7 3.2 %collective-permute-done.1.refs_1_ = bf16[128,2176]{1,0:T(8,128)(2,1)S(1)} collective-permute-done((bf16[128,2176]{1,0:T(8,128)(2,1)}, bf16[128,2176]{1,0:T(8,128)(2,1)S(1)}, u32[]{:S(2)}, u32[]{:S(2)}) %collective-permute-start.1) | collective-permute-done | bytes 557088 | tf_op jit(solution)/shard_map/ppermute | solution.py:33
  19.9 1.6 %collective-permute-done.refs_0_ = bf16[128,2176]{1,0:T(8,128)(2,1)S(1)} collective-permute-done((bf16[128,2176]{1,0:T(8,128)(2,1)}, bf16[128,2176]{1,0:T(8,128)(2,1)S(1)}, u32[]{:S(2)}, u32[]{:S(2)}) %collective-permute-start) | collective-permute-done | bytes 557088 | tf_op jit(solution)/shard_map/ppermute | solution.py:33
  21.4 0.7 %collective-permute-start.5 = (bf16[128,2176]{1,0:T(8,128)(2,1)S(1)}, bf16[128,2176]{1,0:T(8,128)(2,1)S(1)}, u32[]{:S(2)}, u32[]{:S(2)}) collective-permute-start(bf16[128,2176]{1,0:T(8,128)(2,1)S(1)} %collective-permute-done.1.refs_1_), channel_id=1, source_target_pairs={{0,32},{32,0},{64,96},{96,64},{128,160},{160,128},{192,224},{224,1... | collective-permute-start | bytes 1671176 | tf_op jit(solution)/shard_map/ppermute | solution.py:33
  22.2 0.0 collective-permute-start.4
  22.2 3.4 %collective-permute-start.3 = (bf16[128,2176]{1,0:T(8,128)(2,1)S(1)}, bf16[128,2176]{1,0:T(8,128)(2,1)S(1)}, u32[]{:S(2)}, u32[]{:S(2)}) collective-permute-start(bf16[128,2176]{1,0:T(8,128)(2,1)S(1)} %collective-permute-done.refs_0_), channel_id=1, source_target_pairs={{0,208},{32,96},{64,0},{96,160},{128,64},{160,224},{192,128},{224,... | collective-permute-start | bytes 1671176 | tf_op jit(solution)/shard_map/ppermute | solution.py:33
  25.5 0.0 collective-permute-done.5.refs_3_
  25.5 0.0 collective-permute-done.4.refs_2_
  25.5 0.0 copy-done.1
  25.5 5.1 %shard_map.61 = (f32[1,2048]{1,0:T(1,128)S(1)}, f32[1,256]{1,0:T(1,128)S(1)}, f32[1,256]{1,0:T(1,128)S(1)}) custom-call(f32[1,2048]{1,0:T(1,128)S(1)} %bitcast.7, f32[1,2048]{1,0:T(1,128)S(1)} %get-tuple-element.23.prev, bf16[2048,2048]{1,0:T(8,128)(2,1)S(1)} %copy-done.1, bf16[128,2176]{1,0:T(8,128)(2,1)S(1)} %collective-permute-done.refs_0_, ...), custom_call_target="tpu_custom_call" | custom-call | flops 4294967296 | bytes 10485760 | tf_op jit(solution)/shard_map/pallas_call | solution.py:141
  30.7 0.1 collective-permute-start.6
  30.8 1.1 %collective-permute-done.6 = f32[1,384]{1,0:T(1,128)S(1)} collective-permute-done((f32[1,384]{1,0:T(1,128)S(1)}, f32[1,384]{1,0:T(1,128)S(1)}, u32[]{:S(2)}, u32[]{:S(2)}) %collective-permute-start.6) | collective-permute-done | bytes 1568 | tf_op jit(solution)/shard_map/ppermute | solution.py:33
  31.9 0.7 %collective-permute-done.3.refs_0_ = bf16[128,2176]{1,0:T(8,128)(2,1)S(1)} collective-permute-done((bf16[128,2176]{1,0:T(8,128)(2,1)S(1)}, bf16[128,2176]{1,0:T(8,128)(2,1)S(1)}, u32[]{:S(2)}, u32[]{:S(2)}) %collective-permute-start.3) | collective-permute-done | bytes 557088 | tf_op jit(solution)/shard_map/ppermute | solution.py:33
  32.6 0.0 collective-permute-start.7
  32.6 0.0 collective-permute-start.13
  32.6 3.8 %collective-permute-start.14 = (f32[1,128]{1,0:T(1,128)S(1)}, f32[1,128]{1,0:T(1,128)S(1)}, u32[]{:S(2)}, u32[]{:S(2)}) collective-permute-start(f32[1,128]{1,0:T(1,128)S(1)} %get-tuple-element.41), channel_id=1, source_target_pairs={{0,208},{32,96},{64,0},{96,160},{128,64},{160,224},{192,128},{224,... | collective-permute-start | bytes 1544 | tf_op jit(solution)/shard_map/ppermute | solution.py:33
  36.4 0.0 collective-permute-done.7.refs_1_
  36.4 2.8 %shard_map.62 = (f32[1,2048]{1,0:T(1,128)S(1)}, f32[1,128]{1,0:T(1,128)S(1)}, f32[1,128]{1,0:T(1,128)S(1)}) custom-call(f32[1,2048]{1,0:T(1,128)S(1)} %bitcast.8, f32[1,2048]{1,0:T(1,128)S(1)} %get-tuple-element.30.prev, bf16[2048,2048]{1,0:T(8,128)(2,1)S(1)} %copy-done.1, bf16[128,2176]{1,0:T(8,128)(2,1)S(1)} %collective-permute-done.3.refs_0_, ...), custom_call_target="tpu_custom_call" | custom-call | flops 2147483648 | bytes 9437184 | tf_op jit(solution)/shard_map/pallas_call | solution.py:141
  39.2 0.2 collective-permute-start.8
  39.4 0.7 %collective-permute-start.9 = (f32[1,2048]{1,0:T(1,128)S(1)}, f32[1,2048]{1,0:T(1,128)S(1)}, u32[]{:S(2)}, u32[]{:S(2)}) collective-permute-start(f32[1,2048]{1,0:T(1,128)S(1)} %get-tuple-element.32), channel_id=1, source_target_pairs={{0,4},{32,36},{64,68},{96,100},{128,132},{160,164},{192,196},{224,... | collective-permute-start | bytes 24584 | tf_op jit(solution)/shard_map/ppermute | solution.py:33
  40.1 0.0 collective-permute-done.13
  40.1 0.0 collective-permute-done.14
  40.1 2.2 %collective-permute-start.11 = (f32[1,2048]{1,0:T(1,128)S(1)}, f32[1,2048]{1,0:T(1,128)S(1)}, u32[]{:S(2)}, u32[]{:S(2)}) collective-permute-start(f32[1,2048]{1,0:T(1,128)S(1)} %get-tuple-element.32), channel_id=1, source_target_pairs={{0,12},{32,44},{64,76},{96,108},{128,140},{160,172},{192,204},{224... | collective-permute-start | bytes 24584 | tf_op jit(solution)/shard_map/ppermute | solution.py:33
  42.4 1.4 %collective-permute-start.10 = (f32[1,2048]{1,0:T(1,128)S(1)}, f32[1,2048]{1,0:T(1,128)S(1)}, u32[]{:S(2)}, u32[]{:S(2)}) collective-permute-start(f32[1,2048]{1,0:T(1,128)S(1)} %get-tuple-element.32), channel_id=1, source_target_pairs={{0,8},{32,40},{64,72},{96,104},{128,136},{160,168},{192,200},{224,... | collective-permute-start | bytes 24584 | tf_op jit(solution)/shard_map/ppermute | solution.py:33
  43.8 0.0 collective-permute-done.8
  43.8 0.0 collective-permute-done.9
  43.8 3.3 %collective-permute-start.16 = (f32[1,256]{1,0:T(1,128)S(1)}, f32[1,256]{1,0:T(1,128)S(1)}, u32[]{:S(2)}, u32[]{:S(2)}) collective-permute-start(f32[1,256]{1,0:T(1,128)S(1)} %pad_maximum_fusion.1), channel_id=1, source_target_pairs={{0,2},{32,34},{64,66},{96,98},{128,130},{160,162},{192,194},{224,2... | collective-permute-start | bytes 3080 | tf_op jit(solution)/shard_map/ppermute | solution.py:33
  47.1 1.1 %collective-permute-start.17 = (f32[1,256]{1,0:T(1,128)S(1)}, f32[1,256]{1,0:T(1,128)S(1)}, u32[]{:S(2)}, u32[]{:S(2)}) collective-permute-start(f32[1,256]{1,0:T(1,128)S(1)} %pad_maximum_fusion.1), channel_id=1, source_target_pairs={{0,3},{32,35},{64,67},{96,99},{128,131},{160,163},{192,195},{224,2... | collective-permute-start | bytes 3080 | tf_op jit(solution)/shard_map/ppermute | solution.py:33
  48.1 0.0 collective-permute-start.15
  48.1 0.0 collective-permute-done.11
  48.1 0.0 collective-permute-done.10
  48.2 3.4 %collective-permute-start.12 = (f32[1,2048]{1,0:T(1,128)S(1)}, f32[1,2048]{1,0:T(1,128)S(1)}, u32[]{:S(2)}, u32[]{:S(2)}) collective-permute-start(f32[1,2048]{1,0:T(1,128)S(1)} %maximum_maximum_fusion), channel_id=1, source_target_pairs={{0,16},{32,48},{64,80},{96,112},{128,144},{160,176},{192,208},{224... | collective-permute-start | bytes 24584 | tf_op jit(solution)/shard_map/ppermute | solution.py:33
  51.6 0.0 collective-permute-done.16
  51.6 0.2 collective-permute-done.17
  51.8 0.0 collective-permute-done.15
  51.9 0.2 collective-permute-start.18
  52.1 3.7 %collective-permute-done.12 = f32[1,2048]{1,0:T(1,128)S(1)} collective-permute-done((f32[1,2048]{1,0:T(1,128)S(1)}, f32[1,2048]{1,0:T(1,128)S(1)}, u32[]{:S(2)}, u32[]{:S(2)}) %collective-permute-start.12) | collective-permute-done | bytes 8224 | tf_op jit(solution)/shard_map/ppermute | solution.py:33
  55.8 0.6 %max.40 = f32[1,2048]{1,0:T(1,128)} maximum(f32[1,2048]{1,0:T(1,128)S(1)} %maximum_maximum_fusion, f32[1,2048]{1,0:T(1,128)S(1)} %collective-permute-done.12) | non-fusion elementwise | flops 2048 | bytes 24576 | tf_op jit(solution)/shard_map/max | solution.py:192
  56.4 1.2 %collective-permute-done.18 = f32[1,128]{1,0:T(1,128)S(1)} collective-permute-done((f32[1,128]{1,0:T(1,128)S(1)}, f32[1,128]{1,0:T(1,128)S(1)}, u32[]{:S(2)}, u32[]{:S(2)}) %collective-permute-start.18) | collective-permute-done | bytes 544 | tf_op jit(solution)/shard_map/ppermute | solution.py:33
  57.6 0.5 fusion
  (13 shorter events, 0.1 us)
Async XLA Ops:
  2.6 6.1 %collective-permute-start.2 = (bf16[128,2176]{1,0:T(8,128)(2,1)}, bf16[128,2176]{1,0:T(8,128)(2,1)S(1)}, u32[]{:S(2)}, u32[]{:S(2)}) collective-permute-start(bf16[128,2176]{1,0:T(8,128)(2,1)} %shard_map.59.refs_0_), channel_id=1, source_target_pairs={{0,32},{32,0},{64,96},{96,64},{128,160},{160,128},{192,224},{224,1... | collective-permute-start | bytes 1671176 | tf_op jit(solution)/shard_map/ppermute | solution.py:33
  2.7 17.2 %collective-permute-start.1 = (bf16[128,2176]{1,0:T(8,128)(2,1)}, bf16[128,2176]{1,0:T(8,128)(2,1)S(1)}, u32[]{:S(2)}, u32[]{:S(2)}) collective-permute-start(bf16[128,2176]{1,0:T(8,128)(2,1)} %shard_map.59.refs_0_), channel_id=1, source_target_pairs={{0,64},{32,240},{64,128},{96,32},{128,192},{160,96},{192,16},{224,... | collective-permute-start | bytes 1671176 | tf_op jit(solution)/shard_map/ppermute | solution.py:33
  4.7 16.7 %collective-permute-start = (bf16[128,2176]{1,0:T(8,128)(2,1)}, bf16[128,2176]{1,0:T(8,128)(2,1)S(1)}, u32[]{:S(2)}, u32[]{:S(2)}) collective-permute-start(bf16[128,2176]{1,0:T(8,128)(2,1)} %shard_map.59.refs_0_), channel_id=1, source_target_pairs={{0,208},{32,96},{64,0},{96,160},{128,64},{160,224},{192,128},{224,... | collective-permute-start | bytes 1671176 | tf_op jit(solution)/shard_map/ppermute | solution.py:33
  8.7 3.4 %copy-start = (bf16[2048,2048]{1,0:T(8,128)(2,1)S(1)}, bf16[2048,2048]{1,0:T(8,128)(2,1)}, u32[]{:S(2)}) copy-start(bf16[2048,2048]{1,0:T(8,128)(2,1)} %states.5) | copy-start | bytes 25165828
  12.1 1.1 %copy-start.2 = (bf16[128,2176]{1,0:T(8,128)(2,1)S(1)}, bf16[128,2176]{1,0:T(8,128)(2,1)}, u32[]{:S(2)}) copy-start(bf16[128,2176]{1,0:T(8,128)(2,1)} %shard_map.59.refs_0_) | copy-start | bytes 1671172
  13.2 0.7 %copy-start.3 = (f32[2048]{0:T(1024)S(1)}, f32[2048]{0:T(1024)}, u32[]{:S(2)}) copy-start(f32[2048]{0:T(1024)} %param.7) | copy-start | bytes 24580
  13.9 11.7 %copy-start.1 = (bf16[2048,2048]{1,0:T(8,128)(2,1)S(1)}, bf16[2048,2048]{1,0:T(8,128)(2,1)}, u32[]{:S(2)}) copy-start(bf16[2048,2048]{1,0:T(8,128)(2,1)} %states.5) | copy-start | bytes 25165828
  21.4 4.1 %collective-permute-start.5 = (bf16[128,2176]{1,0:T(8,128)(2,1)S(1)}, bf16[128,2176]{1,0:T(8,128)(2,1)S(1)}, u32[]{:S(2)}, u32[]{:S(2)}) collective-permute-start(bf16[128,2176]{1,0:T(8,128)(2,1)S(1)} %collective-permute-done.1.refs_1_), channel_id=1, source_target_pairs={{0,32},{32,0},{64,96},{96,64},{128,160},{160,128},{192,224},{224,1... | collective-permute-start | bytes 1671176 | tf_op jit(solution)/shard_map/ppermute | solution.py:33
  22.2 3.4 %collective-permute-start.4 = (bf16[128,2176]{1,0:T(8,128)(2,1)S(1)}, bf16[128,2176]{1,0:T(8,128)(2,1)S(1)}, u32[]{:S(2)}, u32[]{:S(2)}) collective-permute-start(bf16[128,2176]{1,0:T(8,128)(2,1)S(1)} %collective-permute-done.refs_0_), channel_id=1, source_target_pairs={{0,32},{32,0},{64,96},{96,64},{128,160},{160,128},{192,224},{224,1... | collective-permute-start | bytes 1671176 | tf_op jit(solution)/shard_map/ppermute | solution.py:33
  22.2 10.4 %collective-permute-start.3 = (bf16[128,2176]{1,0:T(8,128)(2,1)S(1)}, bf16[128,2176]{1,0:T(8,128)(2,1)S(1)}, u32[]{:S(2)}, u32[]{:S(2)}) collective-permute-start(bf16[128,2176]{1,0:T(8,128)(2,1)S(1)} %collective-permute-done.refs_0_), channel_id=1, source_target_pairs={{0,208},{32,96},{64,0},{96,160},{128,64},{160,224},{192,128},{224,... | collective-permute-start | bytes 1671176 | tf_op jit(solution)/shard_map/ppermute | solution.py:33
  30.7 1.2 %collective-permute-start.6 = (f32[1,384]{1,0:T(1,128)S(1)}, f32[1,384]{1,0:T(1,128)S(1)}, u32[]{:S(2)}, u32[]{:S(2)}) collective-permute-start(f32[1,384]{1,0:T(1,128)S(1)} %pad_maximum_fusion), channel_id=1, source_target_pairs={{0,32},{32,0},{64,96},{96,64},{128,160},{160,128},{192,224},{224,1... | collective-permute-start | bytes 4616 | tf_op jit(solution)/shard_map/ppermute | solution.py:33
  32.6 3.8 %collective-permute-start.7 = (bf16[128,2176]{1,0:T(8,128)(2,1)S(1)}, bf16[128,2176]{1,0:T(8,128)(2,1)S(1)}, u32[]{:S(2)}, u32[]{:S(2)}) collective-permute-start(bf16[128,2176]{1,0:T(8,128)(2,1)S(1)} %collective-permute-done.3.refs_0_), channel_id=1, source_target_pairs={{0,32},{32,0},{64,96},{96,64},{128,160},{160,128},{192,224},{224,1... | collective-permute-start | bytes 1671176 | tf_op jit(solution)/shard_map/ppermute | solution.py:33
  32.6 7.5 %collective-permute-start.13 = (f32[1,128]{1,0:T(1,128)S(1)}, f32[1,128]{1,0:T(1,128)S(1)}, u32[]{:S(2)}, u32[]{:S(2)}) collective-permute-start(f32[1,128]{1,0:T(1,128)S(1)} %get-tuple-element.40), channel_id=1, source_target_pairs={{0,64},{32,240},{64,128},{96,32},{128,192},{160,96},{192,16},{224,... | collective-permute-start | bytes 1544 | tf_op jit(solution)/shard_map/ppermute | solution.py:33
  32.6 7.5 %collective-permute-start.14 = (f32[1,128]{1,0:T(1,128)S(1)}, f32[1,128]{1,0:T(1,128)S(1)}, u32[]{:S(2)}, u32[]{:S(2)}) collective-permute-start(f32[1,128]{1,0:T(1,128)S(1)} %get-tuple-element.41), channel_id=1, source_target_pairs={{0,208},{32,96},{64,0},{96,160},{128,64},{160,224},{192,128},{224,... | collective-permute-start | bytes 1544 | tf_op jit(solution)/shard_map/ppermute | solution.py:33
  39.2 4.6 %collective-permute-start.8 = (f32[1,128]{1,0:T(1,128)S(1)}, f32[1,128]{1,0:T(1,128)S(1)}, u32[]{:S(2)}, u32[]{:S(2)}) collective-permute-start(f32[1,128]{1,0:T(1,128)S(1)} %get-tuple-element.33), channel_id=1, source_target_pairs={{0,32},{32,0},{64,96},{96,64},{128,160},{160,128},{192,224},{224,1... | collective-permute-start | bytes 1544 | tf_op jit(solution)/shard_map/ppermute | solution.py:33
  39.4 4.3 %collective-permute-start.9 = (f32[1,2048]{1,0:T(1,128)S(1)}, f32[1,2048]{1,0:T(1,128)S(1)}, u32[]{:S(2)}, u32[]{:S(2)}) collective-permute-start(f32[1,2048]{1,0:T(1,128)S(1)} %get-tuple-element.32), channel_id=1, source_target_pairs={{0,4},{32,36},{64,68},{96,100},{128,132},{160,164},{192,196},{224,... | collective-permute-start | bytes 24584 | tf_op jit(solution)/shard_map/ppermute | solution.py:33
  40.1 8.0 %collective-permute-start.11 = (f32[1,2048]{1,0:T(1,128)S(1)}, f32[1,2048]{1,0:T(1,128)S(1)}, u32[]{:S(2)}, u32[]{:S(2)}) collective-permute-start(f32[1,2048]{1,0:T(1,128)S(1)} %get-tuple-element.32), channel_id=1, source_target_pairs={{0,12},{32,44},{64,76},{96,108},{128,140},{160,172},{192,204},{224... | collective-permute-start | bytes 24584 | tf_op jit(solution)/shard_map/ppermute | solution.py:33
  42.4 5.8 %collective-permute-start.10 = (f32[1,2048]{1,0:T(1,128)S(1)}, f32[1,2048]{1,0:T(1,128)S(1)}, u32[]{:S(2)}, u32[]{:S(2)}) collective-permute-start(f32[1,2048]{1,0:T(1,128)S(1)} %get-tuple-element.32), channel_id=1, source_target_pairs={{0,8},{32,40},{64,72},{96,104},{128,136},{160,168},{192,200},{224,... | collective-permute-start | bytes 24584 | tf_op jit(solution)/shard_map/ppermute | solution.py:33
  43.8 7.8 %collective-permute-start.16 = (f32[1,256]{1,0:T(1,128)S(1)}, f32[1,256]{1,0:T(1,128)S(1)}, u32[]{:S(2)}, u32[]{:S(2)}) collective-permute-start(f32[1,256]{1,0:T(1,128)S(1)} %pad_maximum_fusion.1), channel_id=1, source_target_pairs={{0,2},{32,34},{64,66},{96,98},{128,130},{160,162},{192,194},{224,2... | collective-permute-start | bytes 3080 | tf_op jit(solution)/shard_map/ppermute | solution.py:33
  47.1 4.8 %collective-permute-start.17 = (f32[1,256]{1,0:T(1,128)S(1)}, f32[1,256]{1,0:T(1,128)S(1)}, u32[]{:S(2)}, u32[]{:S(2)}) collective-permute-start(f32[1,256]{1,0:T(1,128)S(1)} %pad_maximum_fusion.1), channel_id=1, source_target_pairs={{0,3},{32,35},{64,67},{96,99},{128,131},{160,163},{192,195},{224,2... | collective-permute-start | bytes 3080 | tf_op jit(solution)/shard_map/ppermute | solution.py:33
  48.1 3.7 %collective-permute-start.15 = (f32[1,256]{1,0:T(1,128)S(1)}, f32[1,256]{1,0:T(1,128)S(1)}, u32[]{:S(2)}, u32[]{:S(2)}) collective-permute-start(f32[1,256]{1,0:T(1,128)S(1)} %pad_maximum_fusion.1), channel_id=1, source_target_pairs={{0,1},{32,33},{64,65},{96,97},{128,129},{160,161},{192,193},{224,2... | collective-permute-start | bytes 3080 | tf_op jit(solution)/shard_map/ppermute | solution.py:33
  48.2 7.6 %collective-permute-start.12 = (f32[1,2048]{1,0:T(1,128)S(1)}, f32[1,2048]{1,0:T(1,128)S(1)}, u32[]{:S(2)}, u32[]{:S(2)}) collective-permute-start(f32[1,2048]{1,0:T(1,128)S(1)} %maximum_maximum_fusion), channel_id=1, source_target_pairs={{0,16},{32,48},{64,80},{96,112},{128,144},{160,176},{192,208},{224... | collective-permute-start | bytes 24584 | tf_op jit(solution)/shard_map/ppermute | solution.py:33
  51.9 5.7 %collective-permute-start.18 = (f32[1,128]{1,0:T(1,128)S(1)}, f32[1,128]{1,0:T(1,128)S(1)}, u32[]{:S(2)}, u32[]{:S(2)}) collective-permute-start(f32[1,128]{1,0:T(1,128)S(1)} %slice.20), channel_id=1, source_target_pairs={{0,128},{32,176},{64,192},{96,240},{128,16},{160,32},{192,80},{224... | collective-permute-start | bytes 1544 | tf_op jit(solution)/shard_map/ppermute | solution.py:33

commit v12 on v8

--- a/solution.py
+++ b/solution.py
@@ -180,16 +180,17 @@
     top, two_mine, two_other = score([two, send(two, over_core)], old, top, states)
 
     swapped = send(two_other, over_core)
-    for_x = [send(top, over_x(d)) for d in (1, 2, 3)]
-    swapped, for_x[0] = fence((swapped, for_x[0]))
     held = functools.reduce(jnp.maximum, back, split[0])
+    top = jnp.maximum(top, send(top, over_x(1)))
+    swapped, top = fence((swapped, top))
     lifts = jnp.concatenate([held, jnp.maximum(two_mine, swapped)], axis=1)
-    for_y = [send(lifts, over_y(d)) for d in (1, 2, 3)]
-    top = functools.reduce(jnp.maximum, for_x, top)
-    lifts = functools.reduce(jnp.maximum, for_y, lifts)
+    lifts = jnp.maximum(lifts, send(lifts, over_y(1)))
+    top_two = send(top, over_x(2))
+    lifts, top_two = fence((lifts, top_two))
+    top = jnp.maximum(top, top_two)
+    lifts = jnp.maximum(lifts, send(lifts, over_y(2)))
     across = send(top, far)
     returned = send(lifts[:, cuts:], two_back)
-    across, returned = fence((across, returned))
     new_values = jnp.maximum(top, across)
     cut_gaps = jnp.maximum(returned, lifts[:, :cuts])
     return new_values[0], cut_gaps[0]

time: 59 us -> 63.9 us (1.083)
  waiting for transfers between devices: 17.1 us -> 23 us
  starting transfers between devices: 26.8 us -> 25.6 us
    ppermute x19 -> x17, waiting for transfers between devices: 17.1 us -> 23 us  [send(): return lax.ppermute(block, AXES, routes(move))]
    ppermute x19 -> x17, starting transfers between devices: 26.8 us -> 25.6 us  [send(): return lax.ppermute(block, AXES, routes(move))]
  transfers between devices with their start and end apart: 19 -> 17, of which waited for: 6 -> 9; matrix products, arithmetic and copies ran while one was open for 0% -> 1% of each run, Pallas kernels for 18% -> 17%
where the time goes in v12:
time: 63.9 us; the launch traced here: 63.2 us
  starting transfers between devices  25.6 us (40%)
  waiting for transfers between devices  23 us (36%)
  Pallas kernels  11 us (17%)
  local copies, waits for them, and re-layouts  1.7 us (3%)
  other arithmetic  1.18 us (2%)
  between operations  0.76 us (1%)
    ppermute x17, starting transfers between devices, send(): return lax.ppermute(block, AXES, routes(move))  25.6 us
    ppermute x17, waiting for transfers between devices, send(): return lax.ppermute(block, AXES, routes(move))  23 us
    pallas_call x3, Pallas kernels, score(): pl.pallas_call(functools.partial(score_body, tile, tiles, len(blocks)), g...  10.8 us
    unnamed x8, local copies, waits for them, and re-layouts  1.7 us
  transfers between devices with their start and end apart: 17, of which 9 were waited for; matrix products, arithmetic and copies ran while one was open for 1% of the time, Pallas kernels for 17%

profile of v12, /device:TPU:2, one launch (start us, length us, event | category | flops | bytes accessed | tf_op | source)
XLA Modules:
  0.0 63.2 jit_solution(10360400233734352852)
XLA Ops:
  0.6 0.0 copy-start.2
  0.6 1.0 %copy-done.2 = bf16[128,2048]{1,0:T(8,128)(2,1)S(1)} copy-done((bf16[128,2048]{1,0:T(8,128)(2,1)S(1)}, bf16[128,2048]{1,0:T(8,128)(2,1)}, u32[]{:S(2)}) %copy-start.2) | copy-done | bytes 524312
  1.7 0.0 copy-start.3
  1.7 0.7 %copy-done.3 = bf16[128]{0:T(256)(128)(2,1)S(1)} copy-done((bf16[128]{0:T(256)(128)(2,1)S(1)}, bf16[128]{0:T(256)(128)(2,1)}, u32[]{:S(2)}) %copy-start.3) | copy-done | bytes 280
  2.3 0.0 copy-start
  2.3 0.0 copy-start.1
  2.3 0.2 shard_map.59.refs_0_
  2.5 0.1 collective-permute-start.2
  2.6 2.0 %collective-permute-start.1 = (bf16[128,2176]{1,0:T(8,128)(2,1)S(1)}, bf16[128,2176]{1,0:T(8,128)(2,1)S(1)}, u32[]{:S(2)}, u32[]{:S(2)}) collective-permute-start(bf16[128,2176]{1,0:T(8,128)(2,1)S(1)} %shard_map.59.refs_0_), channel_id=1, source_target_pairs={{0,64},{32,240},{64,128},{96,32},{128,192},{160,96},{192,16},{224,... | collective-permute-start | bytes 1671176 | tf_op jit(solution)/shard_map/ppermute | solution.py:33
  4.6 4.0 %collective-permute-start = (bf16[128,2176]{1,0:T(8,128)(2,1)S(1)}, bf16[128,2176]{1,0:T(8,128)(2,1)S(1)}, u32[]{:S(2)}, u32[]{:S(2)}) collective-permute-start(bf16[128,2176]{1,0:T(8,128)(2,1)S(1)} %shard_map.59.refs_0_), channel_id=1, source_target_pairs={{0,208},{32,96},{64,0},{96,160},{128,64},{160,224},{192,128},{224,... | collective-permute-start | bytes 1671176 | tf_op jit(solution)/shard_map/ppermute | solution.py:33
  8.7 0.0 collective-permute-done.2.refs_1_
  8.7 0.0 copy-done
  8.7 0.0 copy-done.1
  8.7 2.8 %shard_map.60 = (f32[1,2048]{1,0:T(1,128)S(1)}, f32[1,128]{1,0:T(1,128)S(1)}, f32[1,128]{1,0:T(1,128)S(1)}) custom-call(f32[1,2048]{1,0:T(1,128)S(1)} %bitcast.5, f32[1,2048]{1,0:T(1,128)S(1)} %bitcast.6, bf16[2048,2048]{1,0:T(8,128)(2,1)S(1)} %copy-done, bf16[128,2176]{1,0:T(8,128)(2,1)S(1)} %shard_map.59.refs_0_, ...), custom_call_target="tpu_custom_call" | custom-call | flops 2147483648 | bytes 9437184 | tf_op jit(solution)/shard_map/pallas_call | solution.py:141
  11.5 8.1 %collective-permute-done.1.refs_1_ = bf16[128,2176]{1,0:T(8,128)(2,1)S(1)} collective-permute-done((bf16[128,2176]{1,0:T(8,128)(2,1)S(1)}, bf16[128,2176]{1,0:T(8,128)(2,1)S(1)}, u32[]{:S(2)}, u32[]{:S(2)}) %collective-permute-start.1) | collective-permute-done | bytes 557088 | tf_op jit(solution)/shard_map/ppermute | solution.py:33
  19.6 1.5 %collective-permute-done.refs_0_ = bf16[128,2176]{1,0:T(8,128)(2,1)S(1)} collective-permute-done((bf16[128,2176]{1,0:T(8,128)(2,1)S(1)}, bf16[128,2176]{1,0:T(8,128)(2,1)S(1)}, u32[]{:S(2)}, u32[]{:S(2)}) %collective-permute-start) | collective-permute-done | bytes 557088 | tf_op jit(solution)/shard_map/ppermute | solution.py:33
  21.0 0.8 %collective-permute-start.5 = (bf16[128,2176]{1,0:T(8,128)(2,1)S(1)}, bf16[128,2176]{1,0:T(8,128)(2,1)S(1)}, u32[]{:S(2)}, u32[]{:S(2)}) collective-permute-start(bf16[128,2176]{1,0:T(8,128)(2,1)S(1)} %collective-permute-done.1.refs_1_), channel_id=1, source_target_pairs={{0,32},{32,0},{64,96},{96,64},{128,160},{160,128},{192,224},{224,1... | collective-permute-start | bytes 1671176 | tf_op jit(solution)/shard_map/ppermute | solution.py:33
  21.9 0.0 collective-permute-start.4
  21.9 3.4 %collective-permute-start.3 = (bf16[128,2176]{1,0:T(8,128)(2,1)S(1)}, bf16[128,2176]{1,0:T(8,128)(2,1)S(1)}, u32[]{:S(2)}, u32[]{:S(2)}) collective-permute-start(bf16[128,2176]{1,0:T(8,128)(2,1)S(1)} %collective-permute-done.refs_0_), channel_id=1, source_target_pairs={{0,208},{32,96},{64,0},{96,160},{128,64},{160,224},{192,128},{224,... | collective-permute-start | bytes 1671176 | tf_op jit(solution)/shard_map/ppermute | solution.py:33
  25.2 0.0 collective-permute-done.5.refs_3_
  25.2 0.0 collective-permute-done.4.refs_2_
  25.2 5.1 %shard_map.61 = (f32[1,2048]{1,0:T(1,128)S(1)}, f32[1,256]{1,0:T(1,128)S(1)}, f32[1,256]{1,0:T(1,128)S(1)}) custom-call(f32[1,2048]{1,0:T(1,128)S(1)} %bitcast.7, f32[1,2048]{1,0:T(1,128)S(1)} %get-tuple-element.23.prev, bf16[2048,2048]{1,0:T(8,128)(2,1)S(1)} %copy-done, bf16[128,2176]{1,0:T(8,128)(2,1)S(1)} %collective-permute-done.refs_0_, ...), custom_call_target="tpu_custom_call" | custom-call | flops 4294967296 | bytes 10485760 | tf_op jit(solution)/shard_map/pallas_call | solution.py:141
  30.4 0.1 collective-permute-start.6
  30.5 1.1 %collective-permute-done.6 = f32[1,384]{1,0:T(1,128)S(1)} collective-permute-done((f32[1,384]{1,0:T(1,128)S(1)}, f32[1,384]{1,0:T(1,128)S(1)}, u32[]{:S(2)}, u32[]{:S(2)}) %collective-permute-start.6) | collective-permute-done | bytes 1568 | tf_op jit(solution)/shard_map/ppermute | solution.py:33
  31.6 0.7 %collective-permute-done.3.refs_0_ = bf16[128,2176]{1,0:T(8,128)(2,1)S(1)} collective-permute-done((bf16[128,2176]{1,0:T(8,128)(2,1)S(1)}, bf16[128,2176]{1,0:T(8,128)(2,1)S(1)}, u32[]{:S(2)}, u32[]{:S(2)}) %collective-permute-start.3) | collective-permute-done | bytes 557088 | tf_op jit(solution)/shard_map/ppermute | solution.py:33
  32.3 0.0 collective-permute-start.7
  32.3 0.0 collective-permute-start.10
  32.3 3.8 %collective-permute-start.11 = (f32[1,128]{1,0:T(1,128)S(1)}, f32[1,128]{1,0:T(1,128)S(1)}, u32[]{:S(2)}, u32[]{:S(2)}) collective-permute-start(f32[1,128]{1,0:T(1,128)S(1)} %get-tuple-element.41), channel_id=1, source_target_pairs={{0,208},{32,96},{64,0},{96,160},{128,64},{160,224},{192,128},{224,... | collective-permute-start | bytes 1544 | tf_op jit(solution)/shard_map/ppermute | solution.py:33
  36.1 0.0 collective-permute-done.7.refs_1_
  36.1 2.8 %shard_map.62 = (f32[1,2048]{1,0:T(1,128)S(1)}, f32[1,128]{1,0:T(1,128)S(1)}, f32[1,128]{1,0:T(1,128)S(1)}) custom-call(f32[1,2048]{1,0:T(1,128)S(1)} %bitcast.8, f32[1,2048]{1,0:T(1,128)S(1)} %get-tuple-element.30.prev, bf16[2048,2048]{1,0:T(8,128)(2,1)S(1)} %copy-done, bf16[128,2176]{1,0:T(8,128)(2,1)S(1)} %collective-permute-done.3.refs_0_, ...), custom_call_target="tpu_custom_call" | custom-call | flops 2147483648 | bytes 9437184 | tf_op jit(solution)/shard_map/pallas_call | solution.py:141
  38.9 0.2 collective-permute-start.8
  39.2 0.7 %collective-permute-start.9 = (f32[1,2048]{1,0:T(1,128)S(1)}, f32[1,2048]{1,0:T(1,128)S(1)}, u32[]{:S(2)}, u32[]{:S(2)}) collective-permute-start(f32[1,2048]{1,0:T(1,128)S(1)} %get-tuple-element.33), channel_id=1, source_target_pairs={{0,4},{32,36},{64,68},{96,100},{128,132},{160,164},{192,196},{224,... | collective-permute-start | bytes 24584 | tf_op jit(solution)/shard_map/ppermute | solution.py:33
  39.8 0.0 collective-permute-done.10
  39.8 0.0 collective-permute-done.11
  39.8 3.1 %collective-permute-done.9 = f32[1,2048]{1,0:T(1,128)S(1)} collective-permute-done((f32[1,2048]{1,0:T(1,128)S(1)}, f32[1,2048]{1,0:T(1,128)S(1)}, u32[]{:S(2)}, u32[]{:S(2)}) %collective-permute-start.9) | collective-permute-done | bytes 8224 | tf_op jit(solution)/shard_map/ppermute | solution.py:33
  42.9 0.0 collective-permute-done.8
  43.0 1.7 %collective-permute-start.12 = (f32[1,256]{1,0:T(1,128)S(1)}, f32[1,256]{1,0:T(1,128)S(1)}, u32[]{:S(2)}, u32[]{:S(2)}) collective-permute-start(f32[1,256]{1,0:T(1,128)S(1)} %pad_maximum_fusion.1), channel_id=1, source_target_pairs={{0,1},{32,33},{64,65},{96,97},{128,129},{160,161},{192,193},{224,2... | collective-permute-start | bytes 3080 | tf_op jit(solution)/shard_map/ppermute | solution.py:33
  44.6 2.1 %collective-permute-start.13 = (f32[1,2048]{1,0:T(1,128)S(1)}, f32[1,2048]{1,0:T(1,128)S(1)}, u32[]{:S(2)}, u32[]{:S(2)}) collective-permute-start(f32[1,2048]{1,0:T(1,128)S(1)} %max.31), channel_id=1, source_target_pairs={{0,8},{32,40},{64,72},{96,104},{128,136},{160,168},{192,200},{224,... | collective-permute-start | bytes 24584 | tf_op jit(solution)/shard_map/ppermute | solution.py:33
  46.8 0.0 collective-permute-done.12
  46.8 3.0 %collective-permute-done.13 = f32[1,2048]{1,0:T(1,128)S(1)} collective-permute-done((f32[1,2048]{1,0:T(1,128)S(1)}, f32[1,2048]{1,0:T(1,128)S(1)}, u32[]{:S(2)}, u32[]{:S(2)}) %collective-permute-start.13) | collective-permute-done | bytes 8224 | tf_op jit(solution)/shard_map/ppermute | solution.py:33
  49.8 2.9 %collective-permute-start.15 = (f32[1,256]{1,0:T(1,128)S(1)}, f32[1,256]{1,0:T(1,128)S(1)}, u32[]{:S(2)}, u32[]{:S(2)}) collective-permute-start(f32[1,256]{1,0:T(1,128)S(1)} %fusion.1), channel_id=1, source_target_pairs={{0,2},{32,34},{64,66},{96,98},{128,130},{160,162},{192,194},{224,2... | collective-permute-start | bytes 3080 | tf_op jit(solution)/shard_map/ppermute | solution.py:33
  52.7 2.2 %collective-permute-done.15 = f32[1,256]{1,0:T(1,128)S(1)} collective-permute-done((f32[1,256]{1,0:T(1,128)S(1)}, f32[1,256]{1,0:T(1,128)S(1)}, u32[]{:S(2)}, u32[]{:S(2)}) %collective-permute-start.15) | collective-permute-done | bytes 1056 | tf_op jit(solution)/shard_map/ppermute | solution.py:33
  54.9 0.0 collective-permute-start.16
  54.9 3.8 %collective-permute-start.14 = (f32[1,2048]{1,0:T(1,128)S(1)}, f32[1,2048]{1,0:T(1,128)S(1)}, u32[]{:S(2)}, u32[]{:S(2)}) collective-permute-start(f32[1,2048]{1,0:T(1,128)S(1)} %max.36), channel_id=1, source_target_pairs={{0,16},{32,48},{64,80},{96,112},{128,144},{160,176},{192,208},{224... | collective-permute-start | bytes 24584 | tf_op jit(solution)/shard_map/ppermute | solution.py:33
  58.7 1.8 %collective-permute-done.16 = f32[1,128]{1,0:T(1,128)S(1)} collective-permute-done((f32[1,128]{1,0:T(1,128)S(1)}, f32[1,128]{1,0:T(1,128)S(1)}, u32[]{:S(2)}, u32[]{:S(2)}) %collective-permute-start.16) | collective-permute-done | bytes 544 | tf_op jit(solution)/shard_map/ppermute | solution.py:33
  60.5 0.5 fusion
  61.0 1.5 %collective-permute-done.14 = f32[1,2048]{1,0:T(1,128)S(1)} collective-permute-done((f32[1,2048]{1,0:T(1,128)S(1)}, f32[1,2048]{1,0:T(1,128)S(1)}, u32[]{:S(2)}, u32[]{:S(2)}) %collective-permute-start.14) | collective-permute-done | bytes 8224 | tf_op jit(solution)/shard_map/ppermute | solution.py:33
  62.5 0.6 max.37
  (11 shorter events, 0.1 us)
Async XLA Ops:
  0.6 1.0 %copy-start.2 = (bf16[128,2048]{1,0:T(8,128)(2,1)S(1)}, bf16[128,2048]{1,0:T(8,128)(2,1)}, u32[]{:S(2)}) copy-start(bf16[128,2048]{1,0:T(8,128)(2,1)} %coefficients.1) | copy-start | bytes 1572868
  1.7 0.7 %copy-start.3 = (bf16[128]{0:T(256)(128)(2,1)S(1)}, bf16[128]{0:T(256)(128)(2,1)}, u32[]{:S(2)}) copy-start(bf16[128]{0:T(256)(128)(2,1)} %param.5) | copy-start | bytes 772
  2.3 6.3 %copy-start = (bf16[2048,2048]{1,0:T(8,128)(2,1)S(1)}, bf16[2048,2048]{1,0:T(8,128)(2,1)}, u32[]{:S(2)}) copy-start(bf16[2048,2048]{1,0:T(8,128)(2,1)} %states.5) | copy-start | bytes 25165828
  2.3 6.3 %copy-start.1 = (f32[2048]{0:T(1024)S(1)}, f32[2048]{0:T(1024)}, u32[]{:S(2)}) copy-start(f32[2048]{0:T(1024)} %param.7) | copy-start | bytes 24580
  2.5 6.1 %collective-permute-start.2 = (bf16[128,2176]{1,0:T(8,128)(2,1)S(1)}, bf16[128,2176]{1,0:T(8,128)(2,1)S(1)}, u32[]{:S(2)}, u32[]{:S(2)}) collective-permute-start(bf16[128,2176]{1,0:T(8,128)(2,1)S(1)} %shard_map.59.refs_0_), channel_id=1, source_target_pairs={{0,32},{32,0},{64,96},{96,64},{128,160},{160,128},{192,224},{224,1... | collective-permute-start | bytes 1671176 | tf_op jit(solution)/shard_map/ppermute | solution.py:33
  2.6 16.9 %collective-permute-start.1 = (bf16[128,2176]{1,0:T(8,128)(2,1)S(1)}, bf16[128,2176]{1,0:T(8,128)(2,1)S(1)}, u32[]{:S(2)}, u32[]{:S(2)}) collective-permute-start(bf16[128,2176]{1,0:T(8,128)(2,1)S(1)} %shard_map.59.refs_0_), channel_id=1, source_target_pairs={{0,64},{32,240},{64,128},{96,32},{128,192},{160,96},{192,16},{224,... | collective-permute-start | bytes 1671176 | tf_op jit(solution)/shard_map/ppermute | solution.py:33
  4.6 16.4 %collective-permute-start = (bf16[128,2176]{1,0:T(8,128)(2,1)S(1)}, bf16[128,2176]{1,0:T(8,128)(2,1)S(1)}, u32[]{:S(2)}, u32[]{:S(2)}) collective-permute-start(bf16[128,2176]{1,0:T(8,128)(2,1)S(1)} %shard_map.59.refs_0_), channel_id=1, source_target_pairs={{0,208},{32,96},{64,0},{96,160},{128,64},{160,224},{192,128},{224,... | collective-permute-start | bytes 1671176 | tf_op jit(solution)/shard_map/ppermute | solution.py:33
  21.0 4.2 %collective-permute-start.5 = (bf16[128,2176]{1,0:T(8,128)(2,1)S(1)}, bf16[128,2176]{1,0:T(8,128)(2,1)S(1)}, u32[]{:S(2)}, u32[]{:S(2)}) collective-permute-start(bf16[128,2176]{1,0:T(8,128)(2,1)S(1)} %collective-permute-done.1.refs_1_), channel_id=1, source_target_pairs={{0,32},{32,0},{64,96},{96,64},{128,160},{160,128},{192,224},{224,1... | collective-permute-start | bytes 1671176 | tf_op jit(solution)/shard_map/ppermute | solution.py:33
  21.9 3.4 %collective-permute-start.4 = (bf16[128,2176]{1,0:T(8,128)(2,1)S(1)}, bf16[128,2176]{1,0:T(8,128)(2,1)S(1)}, u32[]{:S(2)}, u32[]{:S(2)}) collective-permute-start(bf16[128,2176]{1,0:T(8,128)(2,1)S(1)} %collective-permute-done.refs_0_), channel_id=1, source_target_pairs={{0,32},{32,0},{64,96},{96,64},{128,160},{160,128},{192,224},{224,1... | collective-permute-start | bytes 1671176 | tf_op jit(solution)/shard_map/ppermute | solution.py:33
  21.9 10.4 %collective-permute-start.3 = (bf16[128,2176]{1,0:T(8,128)(2,1)S(1)}, bf16[128,2176]{1,0:T(8,128)(2,1)S(1)}, u32[]{:S(2)}, u32[]{:S(2)}) collective-permute-start(bf16[128,2176]{1,0:T(8,128)(2,1)S(1)} %collective-permute-done.refs_0_), channel_id=1, source_target_pairs={{0,208},{32,96},{64,0},{96,160},{128,64},{160,224},{192,128},{224,... | collective-permute-start | bytes 1671176 | tf_op jit(solution)/shard_map/ppermute | solution.py:33
  30.4 1.2 %collective-permute-start.6 = (f32[1,384]{1,0:T(1,128)S(1)}, f32[1,384]{1,0:T(1,128)S(1)}, u32[]{:S(2)}, u32[]{:S(2)}) collective-permute-start(f32[1,384]{1,0:T(1,128)S(1)} %pad_maximum_fusion), channel_id=1, source_target_pairs={{0,32},{32,0},{64,96},{96,64},{128,160},{160,128},{192,224},{224,1... | collective-permute-start | bytes 4616 | tf_op jit(solution)/shard_map/ppermute | solution.py:33
  32.3 3.8 %collective-permute-start.7 = (bf16[128,2176]{1,0:T(8,128)(2,1)S(1)}, bf16[128,2176]{1,0:T(8,128)(2,1)S(1)}, u32[]{:S(2)}, u32[]{:S(2)}) collective-permute-start(bf16[128,2176]{1,0:T(8,128)(2,1)S(1)} %collective-permute-done.3.refs_0_), channel_id=1, source_target_pairs={{0,32},{32,0},{64,96},{96,64},{128,160},{160,128},{192,224},{224,1... | collective-permute-start | bytes 1671176 | tf_op jit(solution)/shard_map/ppermute | solution.py:33
  32.3 7.5 %collective-permute-start.10 = (f32[1,128]{1,0:T(1,128)S(1)}, f32[1,128]{1,0:T(1,128)S(1)}, u32[]{:S(2)}, u32[]{:S(2)}) collective-permute-start(f32[1,128]{1,0:T(1,128)S(1)} %get-tuple-element.40), channel_id=1, source_target_pairs={{0,64},{32,240},{64,128},{96,32},{128,192},{160,96},{192,16},{224,... | collective-permute-start | bytes 1544 | tf_op jit(solution)/shard_map/ppermute | solution.py:33
  32.3 7.5 %collective-permute-start.11 = (f32[1,128]{1,0:T(1,128)S(1)}, f32[1,128]{1,0:T(1,128)S(1)}, u32[]{:S(2)}, u32[]{:S(2)}) collective-permute-start(f32[1,128]{1,0:T(1,128)S(1)} %get-tuple-element.41), channel_id=1, source_target_pairs={{0,208},{32,96},{64,0},{96,160},{128,64},{160,224},{192,128},{224,... | collective-permute-start | bytes 1544 | tf_op jit(solution)/shard_map/ppermute | solution.py:33
  38.9 4.0 %collective-permute-start.8 = (f32[1,128]{1,0:T(1,128)S(1)}, f32[1,128]{1,0:T(1,128)S(1)}, u32[]{:S(2)}, u32[]{:S(2)}) collective-permute-start(f32[1,128]{1,0:T(1,128)S(1)} %get-tuple-element.32), channel_id=1, source_target_pairs={{0,32},{32,0},{64,96},{96,64},{128,160},{160,128},{192,224},{224,1... | collective-permute-start | bytes 1544 | tf_op jit(solution)/shard_map/ppermute | solution.py:33
  39.2 3.8 %collective-permute-start.9 = (f32[1,2048]{1,0:T(1,128)S(1)}, f32[1,2048]{1,0:T(1,128)S(1)}, u32[]{:S(2)}, u32[]{:S(2)}) collective-permute-start(f32[1,2048]{1,0:T(1,128)S(1)} %get-tuple-element.33), channel_id=1, source_target_pairs={{0,4},{32,36},{64,68},{96,100},{128,132},{160,164},{192,196},{224,... | collective-permute-start | bytes 24584 | tf_op jit(solution)/shard_map/ppermute | solution.py:33
  43.0 3.8 %collective-permute-start.12 = (f32[1,256]{1,0:T(1,128)S(1)}, f32[1,256]{1,0:T(1,128)S(1)}, u32[]{:S(2)}, u32[]{:S(2)}) collective-permute-start(f32[1,256]{1,0:T(1,128)S(1)} %pad_maximum_fusion.1), channel_id=1, source_target_pairs={{0,1},{32,33},{64,65},{96,97},{128,129},{160,161},{192,193},{224,2... | collective-permute-start | bytes 3080 | tf_op jit(solution)/shard_map/ppermute | solution.py:33
  44.6 5.2 %collective-permute-start.13 = (f32[1,2048]{1,0:T(1,128)S(1)}, f32[1,2048]{1,0:T(1,128)S(1)}, u32[]{:S(2)}, u32[]{:S(2)}) collective-permute-start(f32[1,2048]{1,0:T(1,128)S(1)} %max.31), channel_id=1, source_target_pairs={{0,8},{32,40},{64,72},{96,104},{128,136},{160,168},{192,200},{224,... | collective-permute-start | bytes 24584 | tf_op jit(solution)/shard_map/ppermute | solution.py:33
  49.8 5.1 %collective-permute-start.15 = (f32[1,256]{1,0:T(1,128)S(1)}, f32[1,256]{1,0:T(1,128)S(1)}, u32[]{:S(2)}, u32[]{:S(2)}) collective-permute-start(f32[1,256]{1,0:T(1,128)S(1)} %fusion.1), channel_id=1, source_target_pairs={{0,2},{32,34},{64,66},{96,98},{128,130},{160,162},{192,194},{224,2... | collective-permute-start | bytes 3080 | tf_op jit(solution)/shard_map/ppermute | solution.py:33
  54.9 5.7 %collective-permute-start.16 = (f32[1,128]{1,0:T(1,128)S(1)}, f32[1,128]{1,0:T(1,128)S(1)}, u32[]{:S(2)}, u32[]{:S(2)}) collective-permute-start(f32[1,128]{1,0:T(1,128)S(1)} %slice.20), channel_id=1, source_target_pairs={{0,128},{32,176},{64,192},{96,240},{128,16},{160,32},{192,80},{224... | collective-permute-start | bytes 1544 | tf_op jit(solution)/shard_map/ppermute | solution.py:33
  54.9 7.6 %collective-permute-start.14 = (f32[1,2048]{1,0:T(1,128)S(1)}, f32[1,2048]{1,0:T(1,128)S(1)}, u32[]{:S(2)}, u32[]{:S(2)}) collective-permute-start(f32[1,2048]{1,0:T(1,128)S(1)} %max.36), channel_id=1, source_target_pairs={{0,16},{32,48},{64,80},{96,112},{128,144},{160,176},{192,208},{224... | collective-permute-start | bytes 24584 | tf_op jit(solution)/shard_map/ppermute | solution.py:33

commit v13 on v10

--- a/solution.py
+++ b/solution.py
@@ -11,7 +11,7 @@
 NX, NY, NZ, NC = 4, 4, 8, 2
 LANES = 128
 PACK_FLOPS = 10**10
-PACK_VMEM = 55 << 20
+PACK_VMEM = 24 << 20
 
 
 def position(x, y, z, c):

time: 58.9 us -> 58.4 us (level)
  Pallas kernels: 12.9 us -> 11 us
  waiting for transfers between devices: 15.7 us -> 16.5 us
  local copies, waits for them, and re-layouts: 1.08 us -> 1.7 us
    pallas_call x1, Pallas kernels: 2.13 us -> 0.19 us  [pack(): pl.pallas_call(pack_body, in_specs=[there, there], out_specs=pl.BlockSpec...]
    ppermute x19, waiting for transfers between devices: 15.7 us -> 16.5 us  [send(): return lax.ppermute(block, AXES, routes(move))]
    unnamed x6 -> x8, local copies, waits for them, and re-layouts: 1.08 us -> 1.7 us
  transfers between devices with their start and end apart: 19 -> 19, of which waited for: 7 -> 7; matrix products, arithmetic and copies ran while one was open for 1% -> 1% of each run, Pallas kernels for 18% -> 19%
where the time goes in v13:
time: 58.4 us; the launch traced here: 57.8 us
  starting transfers between devices  26.8 us (46%)
  waiting for transfers between devices  16.5 us (28%)
  Pallas kernels  11 us (19%)
  local copies, waits for them, and re-layouts  1.7 us (3%)
  other arithmetic  1.17 us (2%)
  between operations  0.75 us (1%)
    ppermute x19, starting transfers between devices, send(): return lax.ppermute(block, AXES, routes(move))  26.8 us
    ppermute x19, waiting for transfers between devices, send(): return lax.ppermute(block, AXES, routes(move))  16.5 us
    pallas_call x3, Pallas kernels, score(): pl.pallas_call(functools.partial(score_body, tile, tiles, len(blocks)), g...  10.8 us
    unnamed x8, local copies, waits for them, and re-layouts  1.7 us
  transfers between devices with their start and end apart: 19, of which 7 were waited for; matrix products, arithmetic and copies ran while one was open for 1% of the time, Pallas kernels for 19%

profile of v13, /device:TPU:2, one launch (start us, length us, event | category | flops | bytes accessed | tf_op | source)
XLA Modules:
  0.0 57.8 jit_solution(701810066390086791)
XLA Ops:
  0.6 0.0 copy-start.2
  0.6 1.0 %copy-done.2 = bf16[128,2048]{1,0:T(8,128)(2,1)S(1)} copy-done((bf16[128,2048]{1,0:T(8,128)(2,1)S(1)}, bf16[128,2048]{1,0:T(8,128)(2,1)}, u32[]{:S(2)}) %copy-start.2) | copy-done | bytes 524312
  1.7 0.7 %copy-done.3 = bf16[128]{0:T(256)(128)(2,1)S(1)} copy-done((bf16[128]{0:T(256)(128)(2,1)S(1)}, bf16[128]{0:T(256)(128)(2,1)}, u32[]{:S(2)}) %copy-start.3) | copy-done | bytes 280
  2.3 0.2 shard_map.59.refs_0_
  2.5 0.1 collective-permute-start.2
  2.6 2.0 %collective-permute-start.1 = (bf16[128,2176]{1,0:T(8,128)(2,1)S(1)}, bf16[128,2176]{1,0:T(8,128)(2,1)S(1)}, u32[]{:S(2)}, u32[]{:S(2)}) collective-permute-start(bf16[128,2176]{1,0:T(8,128)(2,1)S(1)} %shard_map.59.refs_0_), channel_id=1, source_target_pairs={{0,64},{32,240},{64,128},{96,32},{128,192},{160,96},{192,16},{224,... | collective-permute-start | bytes 1671176 | tf_op jit(solution)/shard_map/ppermute | solution.py:33
  4.6 4.0 %collective-permute-start = (bf16[128,2176]{1,0:T(8,128)(2,1)S(1)}, bf16[128,2176]{1,0:T(8,128)(2,1)S(1)}, u32[]{:S(2)}, u32[]{:S(2)}) collective-permute-start(bf16[128,2176]{1,0:T(8,128)(2,1)S(1)} %shard_map.59.refs_0_), channel_id=1, source_target_pairs={{0,208},{32,96},{64,0},{96,160},{128,64},{160,224},{192,128},{224,... | collective-permute-start | bytes 1671176 | tf_op jit(solution)/shard_map/ppermute | solution.py:33
  8.7 0.0 collective-permute-done.2.refs_1_
  8.7 0.0 copy-done
  8.7 2.8 %shard_map.60 = (f32[1,2048]{1,0:T(1,128)S(1)}, f32[1,128]{1,0:T(1,128)S(1)}, f32[1,128]{1,0:T(1,128)S(1)}) custom-call(f32[1,2048]{1,0:T(1,128)S(1)} %bitcast.5, f32[1,2048]{1,0:T(1,128)S(1)} %bitcast.6, bf16[2048,2048]{1,0:T(8,128)(2,1)S(1)} %copy-done, bf16[128,2176]{1,0:T(8,128)(2,1)S(1)} %shard_map.59.refs_0_, ...), custom_call_target="tpu_custom_call" | custom-call | flops 2147483648 | bytes 9437184 | tf_op jit(solution)/shard_map/pallas_call | solution.py:141
  11.5 8.1 %collective-permute-done.1.refs_1_ = bf16[128,2176]{1,0:T(8,128)(2,1)S(1)} collective-permute-done((bf16[128,2176]{1,0:T(8,128)(2,1)S(1)}, bf16[128,2176]{1,0:T(8,128)(2,1)S(1)}, u32[]{:S(2)}, u32[]{:S(2)}) %collective-permute-start.1) | collective-permute-done | bytes 557088 | tf_op jit(solution)/shard_map/ppermute | solution.py:33
  19.6 1.5 %collective-permute-done.refs_0_ = bf16[128,2176]{1,0:T(8,128)(2,1)S(1)} collective-permute-done((bf16[128,2176]{1,0:T(8,128)(2,1)S(1)}, bf16[128,2176]{1,0:T(8,128)(2,1)S(1)}, u32[]{:S(2)}, u32[]{:S(2)}) %collective-permute-start) | collective-permute-done | bytes 557088 | tf_op jit(solution)/shard_map/ppermute | solution.py:33
  21.0 0.8 %collective-permute-start.5 = (bf16[128,2176]{1,0:T(8,128)(2,1)S(1)}, bf16[128,2176]{1,0:T(8,128)(2,1)S(1)}, u32[]{:S(2)}, u32[]{:S(2)}) collective-permute-start(bf16[128,2176]{1,0:T(8,128)(2,1)S(1)} %collective-permute-done.1.refs_1_), channel_id=1, source_target_pairs={{0,32},{32,0},{64,96},{96,64},{128,160},{160,128},{192,224},{224,1... | collective-permute-start | bytes 1671176 | tf_op jit(solution)/shard_map/ppermute | solution.py:33
  21.9 0.0 collective-permute-start.4
  21.9 3.4 %collective-permute-start.3 = (bf16[128,2176]{1,0:T(8,128)(2,1)S(1)}, bf16[128,2176]{1,0:T(8,128)(2,1)S(1)}, u32[]{:S(2)}, u32[]{:S(2)}) collective-permute-start(bf16[128,2176]{1,0:T(8,128)(2,1)S(1)} %collective-permute-done.refs_0_), channel_id=1, source_target_pairs={{0,208},{32,96},{64,0},{96,160},{128,64},{160,224},{192,128},{224,... | collective-permute-start | bytes 1671176 | tf_op jit(solution)/shard_map/ppermute | solution.py:33
  25.2 0.0 collective-permute-done.5.refs_3_
  25.2 0.0 collective-permute-done.4.refs_2_
  25.2 5.1 %shard_map.61 = (f32[1,2048]{1,0:T(1,128)S(1)}, f32[1,256]{1,0:T(1,128)S(1)}, f32[1,256]{1,0:T(1,128)S(1)}) custom-call(f32[1,2048]{1,0:T(1,128)S(1)} %bitcast.7, f32[1,2048]{1,0:T(1,128)S(1)} %get-tuple-element.23.prev, bf16[2048,2048]{1,0:T(8,128)(2,1)S(1)} %copy-done, bf16[128,2176]{1,0:T(8,128)(2,1)S(1)} %collective-permute-done.refs_0_, ...), custom_call_target="tpu_custom_call" | custom-call | flops 4294967296 | bytes 10485760 | tf_op jit(solution)/shard_map/pallas_call | solution.py:141
  30.4 0.1 collective-permute-start.6
  30.5 1.1 %collective-permute-done.6 = f32[1,384]{1,0:T(1,128)S(1)} collective-permute-done((f32[1,384]{1,0:T(1,128)S(1)}, f32[1,384]{1,0:T(1,128)S(1)}, u32[]{:S(2)}, u32[]{:S(2)}) %collective-permute-start.6) | collective-permute-done | bytes 1568 | tf_op jit(solution)/shard_map/ppermute | solution.py:33
  31.6 0.7 %collective-permute-done.3.refs_0_ = bf16[128,2176]{1,0:T(8,128)(2,1)S(1)} collective-permute-done((bf16[128,2176]{1,0:T(8,128)(2,1)S(1)}, bf16[128,2176]{1,0:T(8,128)(2,1)S(1)}, u32[]{:S(2)}, u32[]{:S(2)}) %collective-permute-start.3) | collective-permute-done | bytes 557088 | tf_op jit(solution)/shard_map/ppermute | solution.py:33
  32.3 0.0 collective-permute-start.7
  32.3 0.0 collective-permute-start.13
  32.3 3.8 %collective-permute-start.14 = (f32[1,128]{1,0:T(1,128)S(1)}, f32[1,128]{1,0:T(1,128)S(1)}, u32[]{:S(2)}, u32[]{:S(2)}) collective-permute-start(f32[1,128]{1,0:T(1,128)S(1)} %get-tuple-element.41), channel_id=1, source_target_pairs={{0,208},{32,96},{64,0},{96,160},{128,64},{160,224},{192,128},{224,... | collective-permute-start | bytes 1544 | tf_op jit(solution)/shard_map/ppermute | solution.py:33
  36.1 0.0 collective-permute-done.7.refs_1_
  36.1 2.8 %shard_map.62 = (f32[1,2048]{1,0:T(1,128)S(1)}, f32[1,128]{1,0:T(1,128)S(1)}, f32[1,128]{1,0:T(1,128)S(1)}) custom-call(f32[1,2048]{1,0:T(1,128)S(1)} %bitcast.8, f32[1,2048]{1,0:T(1,128)S(1)} %get-tuple-element.30.prev, bf16[2048,2048]{1,0:T(8,128)(2,1)S(1)} %copy-done, bf16[128,2176]{1,0:T(8,128)(2,1)S(1)} %collective-permute-done.3.refs_0_, ...), custom_call_target="tpu_custom_call" | custom-call | flops 2147483648 | bytes 9437184 | tf_op jit(solution)/shard_map/pallas_call | solution.py:141
  38.9 0.2 collective-permute-start.8
  39.2 0.7 %collective-permute-start.9 = (f32[1,2048]{1,0:T(1,128)S(1)}, f32[1,2048]{1,0:T(1,128)S(1)}, u32[]{:S(2)}, u32[]{:S(2)}) collective-permute-start(f32[1,2048]{1,0:T(1,128)S(1)} %get-tuple-element.32), channel_id=1, source_target_pairs={{0,4},{32,36},{64,68},{96,100},{128,132},{160,164},{192,196},{224,... | collective-permute-start | bytes 24584 | tf_op jit(solution)/shard_map/ppermute | solution.py:33
  39.8 0.0 collective-permute-done.13
  39.8 0.0 collective-permute-done.14
  39.8 2.2 %collective-permute-start.11 = (f32[1,2048]{1,0:T(1,128)S(1)}, f32[1,2048]{1,0:T(1,128)S(1)}, u32[]{:S(2)}, u32[]{:S(2)}) collective-permute-start(f32[1,2048]{1,0:T(1,128)S(1)} %get-tuple-element.32), channel_id=1, source_target_pairs={{0,12},{32,44},{64,76},{96,108},{128,140},{160,172},{192,204},{224... | collective-permute-start | bytes 24584 | tf_op jit(solution)/shard_map/ppermute | solution.py:33
  42.1 1.4 %collective-permute-start.10 = (f32[1,2048]{1,0:T(1,128)S(1)}, f32[1,2048]{1,0:T(1,128)S(1)}, u32[]{:S(2)}, u32[]{:S(2)}) collective-permute-start(f32[1,2048]{1,0:T(1,128)S(1)} %get-tuple-element.32), channel_id=1, source_target_pairs={{0,8},{32,40},{64,72},{96,104},{128,136},{160,168},{192,200},{224,... | collective-permute-start | bytes 24584 | tf_op jit(solution)/shard_map/ppermute | solution.py:33
  43.5 0.0 collective-permute-done.8
  43.5 0.0 collective-permute-done.9
  43.5 3.3 %collective-permute-start.16 = (f32[1,256]{1,0:T(1,128)S(1)}, f32[1,256]{1,0:T(1,128)S(1)}, u32[]{:S(2)}, u32[]{:S(2)}) collective-permute-start(f32[1,256]{1,0:T(1,128)S(1)} %pad_maximum_fusion.1), channel_id=1, source_target_pairs={{0,2},{32,34},{64,66},{96,98},{128,130},{160,162},{192,194},{224,2... | collective-permute-start | bytes 3080 | tf_op jit(solution)/shard_map/ppermute | solution.py:33
  46.8 1.1 %collective-permute-start.17 = (f32[1,256]{1,0:T(1,128)S(1)}, f32[1,256]{1,0:T(1,128)S(1)}, u32[]{:S(2)}, u32[]{:S(2)}) collective-permute-start(f32[1,256]{1,0:T(1,128)S(1)} %pad_maximum_fusion.1), channel_id=1, source_target_pairs={{0,3},{32,35},{64,67},{96,99},{128,131},{160,163},{192,195},{224,2... | collective-permute-start | bytes 3080 | tf_op jit(solution)/shard_map/ppermute | solution.py:33
  47.8 0.0 collective-permute-start.15
  47.8 0.0 collective-permute-done.11
  47.8 0.0 collective-permute-done.10
  47.9 3.5 %collective-permute-start.12 = (f32[1,2048]{1,0:T(1,128)S(1)}, f32[1,2048]{1,0:T(1,128)S(1)}, u32[]{:S(2)}, u32[]{:S(2)}) collective-permute-start(f32[1,2048]{1,0:T(1,128)S(1)} %maximum_maximum_fusion), channel_id=1, source_target_pairs={{0,16},{32,48},{64,80},{96,112},{128,144},{160,176},{192,208},{224... | collective-permute-start | bytes 24584 | tf_op jit(solution)/shard_map/ppermute | solution.py:33
  51.3 0.0 collective-permute-done.16
  51.3 0.2 collective-permute-done.17
  51.6 0.0 collective-permute-done.15
  51.6 0.2 collective-permute-start.18
  51.8 3.7 %collective-permute-done.12 = f32[1,2048]{1,0:T(1,128)S(1)} collective-permute-done((f32[1,2048]{1,0:T(1,128)S(1)}, f32[1,2048]{1,0:T(1,128)S(1)}, u32[]{:S(2)}, u32[]{:S(2)}) %collective-permute-start.12) | collective-permute-done | bytes 8224 | tf_op jit(solution)/shard_map/ppermute | solution.py:33
  55.5 0.6 %max.40 = f32[1,2048]{1,0:T(1,128)} maximum(f32[1,2048]{1,0:T(1,128)S(1)} %maximum_maximum_fusion, f32[1,2048]{1,0:T(1,128)S(1)} %collective-permute-done.12) | non-fusion elementwise | flops 2048 | bytes 24576 | tf_op jit(solution)/shard_map/max | solution.py:192
  56.1 1.2 %collective-permute-done.18 = f32[1,128]{1,0:T(1,128)S(1)} collective-permute-done((f32[1,128]{1,0:T(1,128)S(1)}, f32[1,128]{1,0:T(1,128)S(1)}, u32[]{:S(2)}, u32[]{:S(2)}) %collective-permute-start.18) | collective-permute-done | bytes 544 | tf_op jit(solution)/shard_map/ppermute | solution.py:33
  57.3 0.5 fusion
  (13 shorter events, 0.1 us)
Async XLA Ops:
  0.6 1.0 %copy-start.2 = (bf16[128,2048]{1,0:T(8,128)(2,1)S(1)}, bf16[128,2048]{1,0:T(8,128)(2,1)}, u32[]{:S(2)}) copy-start(bf16[128,2048]{1,0:T(8,128)(2,1)} %coefficients.1) | copy-start | bytes 1572868
  1.7 0.7 %copy-start.3 = (bf16[128]{0:T(256)(128)(2,1)S(1)}, bf16[128]{0:T(256)(128)(2,1)}, u32[]{:S(2)}) copy-start(bf16[128]{0:T(256)(128)(2,1)} %param.5) | copy-start | bytes 772
  2.3 6.3 %copy-start = (bf16[2048,2048]{1,0:T(8,128)(2,1)S(1)}, bf16[2048,2048]{1,0:T(8,128)(2,1)}, u32[]{:S(2)}) copy-start(bf16[2048,2048]{1,0:T(8,128)(2,1)} %states.5) | copy-start | bytes 25165828
  2.3 6.3 %copy-start.1 = (f32[2048]{0:T(1024)S(1)}, f32[2048]{0:T(1024)}, u32[]{:S(2)}) copy-start(f32[2048]{0:T(1024)} %param.7) | copy-start | bytes 24580
  2.5 6.1 %collective-permute-start.2 = (bf16[128,2176]{1,0:T(8,128)(2,1)S(1)}, bf16[128,2176]{1,0:T(8,128)(2,1)S(1)}, u32[]{:S(2)}, u32[]{:S(2)}) collective-permute-start(bf16[128,2176]{1,0:T(8,128)(2,1)S(1)} %shard_map.59.refs_0_), channel_id=1, source_target_pairs={{0,32},{32,0},{64,96},{96,64},{128,160},{160,128},{192,224},{224,1... | collective-permute-start | bytes 1671176 | tf_op jit(solution)/shard_map/ppermute | solution.py:33
  2.6 16.9 %collective-permute-start.1 = (bf16[128,2176]{1,0:T(8,128)(2,1)S(1)}, bf16[128,2176]{1,0:T(8,128)(2,1)S(1)}, u32[]{:S(2)}, u32[]{:S(2)}) collective-permute-start(bf16[128,2176]{1,0:T(8,128)(2,1)S(1)} %shard_map.59.refs_0_), channel_id=1, source_target_pairs={{0,64},{32,240},{64,128},{96,32},{128,192},{160,96},{192,16},{224,... | collective-permute-start | bytes 1671176 | tf_op jit(solution)/shard_map/ppermute | solution.py:33
  4.6 16.4 %collective-permute-start = (bf16[128,2176]{1,0:T(8,128)(2,1)S(1)}, bf16[128,2176]{1,0:T(8,128)(2,1)S(1)}, u32[]{:S(2)}, u32[]{:S(2)}) collective-permute-start(bf16[128,2176]{1,0:T(8,128)(2,1)S(1)} %shard_map.59.refs_0_), channel_id=1, source_target_pairs={{0,208},{32,96},{64,0},{96,160},{128,64},{160,224},{192,128},{224,... | collective-permute-start | bytes 1671176 | tf_op jit(solution)/shard_map/ppermute | solution.py:33
  21.0 4.2 %collective-permute-start.5 = (bf16[128,2176]{1,0:T(8,128)(2,1)S(1)}, bf16[128,2176]{1,0:T(8,128)(2,1)S(1)}, u32[]{:S(2)}, u32[]{:S(2)}) collective-permute-start(bf16[128,2176]{1,0:T(8,128)(2,1)S(1)} %collective-permute-done.1.refs_1_), channel_id=1, source_target_pairs={{0,32},{32,0},{64,96},{96,64},{128,160},{160,128},{192,224},{224,1... | collective-permute-start | bytes 1671176 | tf_op jit(solution)/shard_map/ppermute | solution.py:33
  21.9 3.4 %collective-permute-start.4 = (bf16[128,2176]{1,0:T(8,128)(2,1)S(1)}, bf16[128,2176]{1,0:T(8,128)(2,1)S(1)}, u32[]{:S(2)}, u32[]{:S(2)}) collective-permute-start(bf16[128,2176]{1,0:T(8,128)(2,1)S(1)} %collective-permute-done.refs_0_), channel_id=1, source_target_pairs={{0,32},{32,0},{64,96},{96,64},{128,160},{160,128},{192,224},{224,1... | collective-permute-start | bytes 1671176 | tf_op jit(solution)/shard_map/ppermute | solution.py:33
  21.9 10.4 %collective-permute-start.3 = (bf16[128,2176]{1,0:T(8,128)(2,1)S(1)}, bf16[128,2176]{1,0:T(8,128)(2,1)S(1)}, u32[]{:S(2)}, u32[]{:S(2)}) collective-permute-start(bf16[128,2176]{1,0:T(8,128)(2,1)S(1)} %collective-permute-done.refs_0_), channel_id=1, source_target_pairs={{0,208},{32,96},{64,0},{96,160},{128,64},{160,224},{192,128},{224,... | collective-permute-start | bytes 1671176 | tf_op jit(solution)/shard_map/ppermute | solution.py:33
  30.4 1.2 %collective-permute-start.6 = (f32[1,384]{1,0:T(1,128)S(1)}, f32[1,384]{1,0:T(1,128)S(1)}, u32[]{:S(2)}, u32[]{:S(2)}) collective-permute-start(f32[1,384]{1,0:T(1,128)S(1)} %pad_maximum_fusion), channel_id=1, source_target_pairs={{0,32},{32,0},{64,96},{96,64},{128,160},{160,128},{192,224},{224,1... | collective-permute-start | bytes 4616 | tf_op jit(solution)/shard_map/ppermute | solution.py:33
  32.3 3.8 %collective-permute-start.7 = (bf16[128,2176]{1,0:T(8,128)(2,1)S(1)}, bf16[128,2176]{1,0:T(8,128)(2,1)S(1)}, u32[]{:S(2)}, u32[]{:S(2)}) collective-permute-start(bf16[128,2176]{1,0:T(8,128)(2,1)S(1)} %collective-permute-done.3.refs_0_), channel_id=1, source_target_pairs={{0,32},{32,0},{64,96},{96,64},{128,160},{160,128},{192,224},{224,1... | collective-permute-start | bytes 1671176 | tf_op jit(solution)/shard_map/ppermute | solution.py:33
  32.3 7.5 %collective-permute-start.13 = (f32[1,128]{1,0:T(1,128)S(1)}, f32[1,128]{1,0:T(1,128)S(1)}, u32[]{:S(2)}, u32[]{:S(2)}) collective-permute-start(f32[1,128]{1,0:T(1,128)S(1)} %get-tuple-element.40), channel_id=1, source_target_pairs={{0,64},{32,240},{64,128},{96,32},{128,192},{160,96},{192,16},{224,... | collective-permute-start | bytes 1544 | tf_op jit(solution)/shard_map/ppermute | solution.py:33
  32.3 7.5 %collective-permute-start.14 = (f32[1,128]{1,0:T(1,128)S(1)}, f32[1,128]{1,0:T(1,128)S(1)}, u32[]{:S(2)}, u32[]{:S(2)}) collective-permute-start(f32[1,128]{1,0:T(1,128)S(1)} %get-tuple-element.41), channel_id=1, source_target_pairs={{0,208},{32,96},{64,0},{96,160},{128,64},{160,224},{192,128},{224,... | collective-permute-start | bytes 1544 | tf_op jit(solution)/shard_map/ppermute | solution.py:33
  38.9 4.6 %collective-permute-start.8 = (f32[1,128]{1,0:T(1,128)S(1)}, f32[1,128]{1,0:T(1,128)S(1)}, u32[]{:S(2)}, u32[]{:S(2)}) collective-permute-start(f32[1,128]{1,0:T(1,128)S(1)} %get-tuple-element.33), channel_id=1, source_target_pairs={{0,32},{32,0},{64,96},{96,64},{128,160},{160,128},{192,224},{224,1... | collective-permute-start | bytes 1544 | tf_op jit(solution)/shard_map/ppermute | solution.py:33
  39.2 4.3 %collective-permute-start.9 = (f32[1,2048]{1,0:T(1,128)S(1)}, f32[1,2048]{1,0:T(1,128)S(1)}, u32[]{:S(2)}, u32[]{:S(2)}) collective-permute-start(f32[1,2048]{1,0:T(1,128)S(1)} %get-tuple-element.32), channel_id=1, source_target_pairs={{0,4},{32,36},{64,68},{96,100},{128,132},{160,164},{192,196},{224,... | collective-permute-start | bytes 24584 | tf_op jit(solution)/shard_map/ppermute | solution.py:33
  39.8 8.0 %collective-permute-start.11 = (f32[1,2048]{1,0:T(1,128)S(1)}, f32[1,2048]{1,0:T(1,128)S(1)}, u32[]{:S(2)}, u32[]{:S(2)}) collective-permute-start(f32[1,2048]{1,0:T(1,128)S(1)} %get-tuple-element.32), channel_id=1, source_target_pairs={{0,12},{32,44},{64,76},{96,108},{128,140},{160,172},{192,204},{224... | collective-permute-start | bytes 24584 | tf_op jit(solution)/shard_map/ppermute | solution.py:33
  42.1 5.8 %collective-permute-start.10 = (f32[1,2048]{1,0:T(1,128)S(1)}, f32[1,2048]{1,0:T(1,128)S(1)}, u32[]{:S(2)}, u32[]{:S(2)}) collective-permute-start(f32[1,2048]{1,0:T(1,128)S(1)} %get-tuple-element.32), channel_id=1, source_target_pairs={{0,8},{32,40},{64,72},{96,104},{128,136},{160,168},{192,200},{224,... | collective-permute-start | bytes 24584 | tf_op jit(solution)/shard_map/ppermute | solution.py:33
  43.5 7.8 %collective-permute-start.16 = (f32[1,256]{1,0:T(1,128)S(1)}, f32[1,256]{1,0:T(1,128)S(1)}, u32[]{:S(2)}, u32[]{:S(2)}) collective-permute-start(f32[1,256]{1,0:T(1,128)S(1)} %pad_maximum_fusion.1), channel_id=1, source_target_pairs={{0,2},{32,34},{64,66},{96,98},{128,130},{160,162},{192,194},{224,2... | collective-permute-start | bytes 3080 | tf_op jit(solution)/shard_map/ppermute | solution.py:33
  46.8 4.8 %collective-permute-start.17 = (f32[1,256]{1,0:T(1,128)S(1)}, f32[1,256]{1,0:T(1,128)S(1)}, u32[]{:S(2)}, u32[]{:S(2)}) collective-permute-start(f32[1,256]{1,0:T(1,128)S(1)} %pad_maximum_fusion.1), channel_id=1, source_target_pairs={{0,3},{32,35},{64,67},{96,99},{128,131},{160,163},{192,195},{224,2... | collective-permute-start | bytes 3080 | tf_op jit(solution)/shard_map/ppermute | solution.py:33
  47.8 3.7 %collective-permute-start.15 = (f32[1,256]{1,0:T(1,128)S(1)}, f32[1,256]{1,0:T(1,128)S(1)}, u32[]{:S(2)}, u32[]{:S(2)}) collective-permute-start(f32[1,256]{1,0:T(1,128)S(1)} %pad_maximum_fusion.1), channel_id=1, source_target_pairs={{0,1},{32,33},{64,65},{96,97},{128,129},{160,161},{192,193},{224,2... | collective-permute-start | bytes 3080 | tf_op jit(solution)/shard_map/ppermute | solution.py:33
  47.9 7.6 %collective-permute-start.12 = (f32[1,2048]{1,0:T(1,128)S(1)}, f32[1,2048]{1,0:T(1,128)S(1)}, u32[]{:S(2)}, u32[]{:S(2)}) collective-permute-start(f32[1,2048]{1,0:T(1,128)S(1)} %maximum_maximum_fusion), channel_id=1, source_target_pairs={{0,16},{32,48},{64,80},{96,112},{128,144},{160,176},{192,208},{224... | collective-permute-start | bytes 24584 | tf_op jit(solution)/shard_map/ppermute | solution.py:33
  51.6 5.7 %collective-permute-start.18 = (f32[1,128]{1,0:T(1,128)S(1)}, f32[1,128]{1,0:T(1,128)S(1)}, u32[]{:S(2)}, u32[]{:S(2)}) collective-permute-start(f32[1,128]{1,0:T(1,128)S(1)} %slice.20), channel_id=1, source_target_pairs={{0,128},{32,176},{64,192},{96,240},{128,16},{160,32},{192,80},{224... | collective-permute-start | bytes 1544 | tf_op jit(solution)/shard_map/ppermute | solution.py:33

commit v14 on v13

--- a/solution.py
+++ b/solution.py
@@ -157,6 +157,10 @@
     )(old, prev, states, *blocks)
 
 
+def exchange(block):
+    return [send(block, over_core)]
+
+
 def body(coefficients, intercepts, states, old_values):
     old = old_values[None, :]
     cuts = coefficients.shape[0]
@@ -164,12 +168,12 @@
 
     own = pack(coefficients, intercepts)
     near = send(own, toward)
-    next_ = send(own, against)
     peer = send(own, over_core)
+    next_ = send(peer, toward)
     top, own_mine, own_other = score([own, peer], old, old, states)
     near, next_, top = fence((near, next_, top))
     two = send(near, toward)
-    blocks = [near, next_, send(near, over_core), send(next_, over_core)]
+    blocks = [near, *exchange(next_), *exchange(near), next_]
     top, side_mine, side_other = score(blocks, old, top, states)
 
     mine = jnp.concatenate([own_mine, side_mine], axis=1)

time: 58.4 us -> 58.5 us (level)
  starting transfers between devices: 26.8 us -> 27.8 us
    ppermute x19, starting transfers between devices: 26.8 us -> 27.8 us  [send(): return lax.ppermute(block, AXES, routes(move))]
  transfers between devices with their start and end apart: 19 -> 19, of which waited for: 7 -> 7; matrix products, arithmetic and copies ran while one was open for 1% -> 1% of each run, Pallas kernels for 19% -> 18%
where the time goes in v14:
time: 58.5 us; the launch traced here: 58.4 us
  starting transfers between devices  27.8 us (48%)
  waiting for transfers between devices  16 us (27%)
  Pallas kernels  10.9 us (19%)
  local copies, waits for them, and re-layouts  1.7 us (3%)
  other arithmetic  1.17 us (2%)
  between operations  0.75 us (1%)
    ppermute x19, starting transfers between devices, send(): return lax.ppermute(block, AXES, routes(move))  27.8 us
    ppermute x19, waiting for transfers between devices, send(): return lax.ppermute(block, AXES, routes(move))  16 us
    pallas_call x3, Pallas kernels, score(): pl.pallas_call(functools.partial(score_body, tile, tiles, len(blocks)), g...  10.7 us
    unnamed x8, local copies, waits for them, and re-layouts  1.7 us
  transfers between devices with their start and end apart: 19, of which 7 were waited for; matrix products, arithmetic and copies ran while one was open for 1% of the time, Pallas kernels for 18%

profile of v14, /device:TPU:2, one launch (start us, length us, event | category | flops | bytes accessed | tf_op | source)
XLA Modules:
  0.0 58.4 jit_solution(9834350755448577105)
XLA Ops:
  0.6 0.0 copy-start.2
  0.6 1.0 %copy-done.2 = bf16[128,2048]{1,0:T(8,128)(2,1)S(1)} copy-done((bf16[128,2048]{1,0:T(8,128)(2,1)S(1)}, bf16[128,2048]{1,0:T(8,128)(2,1)}, u32[]{:S(2)}) %copy-start.2) | copy-done | bytes 524312
  1.7 0.7 %copy-done.3 = bf16[128]{0:T(256)(128)(2,1)S(1)} copy-done((bf16[128]{0:T(256)(128)(2,1)S(1)}, bf16[128]{0:T(256)(128)(2,1)}, u32[]{:S(2)}) %copy-start.3) | copy-done | bytes 280
  2.3 0.2 shard_map.59.refs_0_
  2.5 0.1 collective-permute-start.1
  2.6 5.9 %collective-permute-start = (bf16[128,2176]{1,0:T(8,128)(2,1)S(1)}, bf16[128,2176]{1,0:T(8,128)(2,1)S(1)}, u32[]{:S(2)}, u32[]{:S(2)}) collective-permute-start(bf16[128,2176]{1,0:T(8,128)(2,1)S(1)} %shard_map.59.refs_0_), channel_id=1, source_target_pairs={{0,208},{32,96},{64,0},{96,160},{128,64},{160,224},{192,128},{224,... | collective-permute-start | bytes 1671176 | tf_op jit(solution)/shard_map/ppermute | solution.py:33
  8.6 0.0 collective-permute-done.1.refs_1_
  8.6 1.9 %collective-permute-start.2 = (bf16[128,2176]{1,0:T(8,128)(2,1)S(1)}, bf16[128,2176]{1,0:T(8,128)(2,1)S(1)}, u32[]{:S(2)}, u32[]{:S(2)}) collective-permute-start(bf16[128,2176]{1,0:T(8,128)(2,1)S(1)} %collective-permute-done.1.refs_1_), channel_id=1, source_target_pairs={{0,208},{32,96},{64,0},{96,160},{128,64},{160,224},{192,128},{224,... | collective-permute-start | bytes 1671176 | tf_op jit(solution)/shard_map/ppermute | solution.py:33
  10.4 0.0 copy-done.1
  10.4 2.8 %shard_map.60 = (f32[1,2048]{1,0:T(1,128)S(1)}, f32[1,128]{1,0:T(1,128)S(1)}, f32[1,128]{1,0:T(1,128)S(1)}) custom-call(f32[1,2048]{1,0:T(1,128)S(1)} %bitcast.5, f32[1,2048]{1,0:T(1,128)S(1)} %bitcast.6, bf16[2048,2048]{1,0:T(8,128)(2,1)S(1)} %copy-done, bf16[128,2176]{1,0:T(8,128)(2,1)S(1)} %shard_map.59.refs_0_, ...), custom_call_target="tpu_custom_call" | custom-call | flops 2147483648 | bytes 9437184 | tf_op jit(solution)/shard_map/pallas_call | solution.py:141
  13.3 2.3 %collective-permute-done.refs_0_ = bf16[128,2176]{1,0:T(8,128)(2,1)S(1)} collective-permute-done((bf16[128,2176]{1,0:T(8,128)(2,1)S(1)}, bf16[128,2176]{1,0:T(8,128)(2,1)S(1)}, u32[]{:S(2)}, u32[]{:S(2)}) %collective-permute-start) | collective-permute-done | bytes 557088 | tf_op jit(solution)/shard_map/ppermute | solution.py:33
  15.6 6.0 %collective-permute-done.2.refs_3_ = bf16[128,2176]{1,0:T(8,128)(2,1)S(1)} collective-permute-done((bf16[128,2176]{1,0:T(8,128)(2,1)S(1)}, bf16[128,2176]{1,0:T(8,128)(2,1)S(1)}, u32[]{:S(2)}, u32[]{:S(2)}) %collective-permute-start.2) | collective-permute-done | bytes 557088 | tf_op jit(solution)/shard_map/ppermute | solution.py:33
  21.6 0.0 collective-permute-start.4
  21.6 0.5 collective-permute-start.5
  22.1 3.7 %collective-permute-start.3 = (bf16[128,2176]{1,0:T(8,128)(2,1)S(1)}, bf16[128,2176]{1,0:T(8,128)(2,1)S(1)}, u32[]{:S(2)}, u32[]{:S(2)}) collective-permute-start(bf16[128,2176]{1,0:T(8,128)(2,1)S(1)} %collective-permute-done.refs_0_), channel_id=1, source_target_pairs={{0,208},{32,96},{64,0},{96,160},{128,64},{160,224},{192,128},{224,... | collective-permute-start | bytes 1671176 | tf_op jit(solution)/shard_map/ppermute | solution.py:33
  25.8 0.0 collective-permute-done.4.refs_1_
  25.8 0.0 collective-permute-done.5.refs_2_
  25.8 5.1 %shard_map.61 = (f32[1,2048]{1,0:T(1,128)S(1)}, f32[1,256]{1,0:T(1,128)S(1)}, f32[1,256]{1,0:T(1,128)S(1)}) custom-call(f32[1,2048]{1,0:T(1,128)S(1)} %bitcast.7, f32[1,2048]{1,0:T(1,128)S(1)} %get-tuple-element.23.prev, bf16[2048,2048]{1,0:T(8,128)(2,1)S(1)} %copy-done, bf16[128,2176]{1,0:T(8,128)(2,1)S(1)} %collective-permute-done.refs_0_, ...), custom_call_target="tpu_custom_call" | custom-call | flops 4294967296 | bytes 10485760 | tf_op jit(solution)/shard_map/pallas_call | solution.py:141
  30.9 0.1 collective-permute-start.6
  31.0 1.1 %collective-permute-done.6 = f32[1,384]{1,0:T(1,128)S(1)} collective-permute-done((f32[1,384]{1,0:T(1,128)S(1)}, f32[1,384]{1,0:T(1,128)S(1)}, u32[]{:S(2)}, u32[]{:S(2)}) %collective-permute-start.6) | collective-permute-done | bytes 1568 | tf_op jit(solution)/shard_map/ppermute | solution.py:33
  32.2 0.7 %collective-permute-done.3.refs_0_ = bf16[128,2176]{1,0:T(8,128)(2,1)S(1)} collective-permute-done((bf16[128,2176]{1,0:T(8,128)(2,1)S(1)}, bf16[128,2176]{1,0:T(8,128)(2,1)S(1)}, u32[]{:S(2)}, u32[]{:S(2)}) %collective-permute-start.3) | collective-permute-done | bytes 557088 | tf_op jit(solution)/shard_map/ppermute | solution.py:33
  32.8 0.0 collective-permute-start.7
  32.8 0.0 collective-permute-start.13
  32.9 3.8 %collective-permute-start.14 = (f32[1,128]{1,0:T(1,128)S(1)}, f32[1,128]{1,0:T(1,128)S(1)}, u32[]{:S(2)}, u32[]{:S(2)}) collective-permute-start(f32[1,128]{1,0:T(1,128)S(1)} %get-tuple-element.41), channel_id=1, source_target_pairs={{0,208},{32,96},{64,0},{96,160},{128,64},{160,224},{192,128},{224,... | collective-permute-start | bytes 1544 | tf_op jit(solution)/shard_map/ppermute | solution.py:33
  36.6 0.0 collective-permute-done.7.refs_1_
  36.6 2.8 %shard_map.62 = (f32[1,2048]{1,0:T(1,128)S(1)}, f32[1,128]{1,0:T(1,128)S(1)}, f32[1,128]{1,0:T(1,128)S(1)}) custom-call(f32[1,2048]{1,0:T(1,128)S(1)} %bitcast.8, f32[1,2048]{1,0:T(1,128)S(1)} %get-tuple-element.30.prev, bf16[2048,2048]{1,0:T(8,128)(2,1)S(1)} %copy-done, bf16[128,2176]{1,0:T(8,128)(2,1)S(1)} %collective-permute-done.3.refs_0_, ...), custom_call_target="tpu_custom_call" | custom-call | flops 2147483648 | bytes 9437184 | tf_op jit(solution)/shard_map/pallas_call | solution.py:141
  39.5 0.2 collective-permute-start.8
  39.7 0.7 %collective-permute-start.9 = (f32[1,2048]{1,0:T(1,128)S(1)}, f32[1,2048]{1,0:T(1,128)S(1)}, u32[]{:S(2)}, u32[]{:S(2)}) collective-permute-start(f32[1,2048]{1,0:T(1,128)S(1)} %get-tuple-element.32), channel_id=1, source_target_pairs={{0,4},{32,36},{64,68},{96,100},{128,132},{160,164},{192,196},{224,... | collective-permute-start | bytes 24584 | tf_op jit(solution)/shard_map/ppermute | solution.py:33
  40.4 0.0 collective-permute-done.13
  40.4 0.0 collective-permute-done.14
  40.4 2.2 %collective-permute-start.11 = (f32[1,2048]{1,0:T(1,128)S(1)}, f32[1,2048]{1,0:T(1,128)S(1)}, u32[]{:S(2)}, u32[]{:S(2)}) collective-permute-start(f32[1,2048]{1,0:T(1,128)S(1)} %get-tuple-element.32), channel_id=1, source_target_pairs={{0,12},{32,44},{64,76},{96,108},{128,140},{160,172},{192,204},{224... | collective-permute-start | bytes 24584 | tf_op jit(solution)/shard_map/ppermute | solution.py:33
  42.6 1.4 %collective-permute-start.10 = (f32[1,2048]{1,0:T(1,128)S(1)}, f32[1,2048]{1,0:T(1,128)S(1)}, u32[]{:S(2)}, u32[]{:S(2)}) collective-permute-start(f32[1,2048]{1,0:T(1,128)S(1)} %get-tuple-element.32), channel_id=1, source_target_pairs={{0,8},{32,40},{64,72},{96,104},{128,136},{160,168},{192,200},{224,... | collective-permute-start | bytes 24584 | tf_op jit(solution)/shard_map/ppermute | solution.py:33
  44.0 0.0 collective-permute-done.8
  44.0 0.0 collective-permute-done.9
  44.0 3.3 %collective-permute-start.16 = (f32[1,256]{1,0:T(1,128)S(1)}, f32[1,256]{1,0:T(1,128)S(1)}, u32[]{:S(2)}, u32[]{:S(2)}) collective-permute-start(f32[1,256]{1,0:T(1,128)S(1)} %pad_maximum_fusion.1), channel_id=1, source_target_pairs={{0,2},{32,34},{64,66},{96,98},{128,130},{160,162},{192,194},{224,2... | collective-permute-start | bytes 3080 | tf_op jit(solution)/shard_map/ppermute | solution.py:33
  47.3 1.1 %collective-permute-start.17 = (f32[1,256]{1,0:T(1,128)S(1)}, f32[1,256]{1,0:T(1,128)S(1)}, u32[]{:S(2)}, u32[]{:S(2)}) collective-permute-start(f32[1,256]{1,0:T(1,128)S(1)} %pad_maximum_fusion.1), channel_id=1, source_target_pairs={{0,3},{32,35},{64,67},{96,99},{128,131},{160,163},{192,195},{224,2... | collective-permute-start | bytes 3080 | tf_op jit(solution)/shard_map/ppermute | solution.py:33
  48.4 0.0 collective-permute-start.15
  48.4 0.0 collective-permute-done.11
  48.4 0.0 collective-permute-done.10
  48.4 2.7 %collective-permute-start.12 = (f32[1,2048]{1,0:T(1,128)S(1)}, f32[1,2048]{1,0:T(1,128)S(1)}, u32[]{:S(2)}, u32[]{:S(2)}) collective-permute-start(f32[1,2048]{1,0:T(1,128)S(1)} %maximum_maximum_fusion), channel_id=1, source_target_pairs={{0,16},{32,48},{64,80},{96,112},{128,144},{160,176},{192,208},{224... | collective-permute-start | bytes 24584 | tf_op jit(solution)/shard_map/ppermute | solution.py:33
  51.1 0.0 collective-permute-done.16
  51.1 1.0 %collective-permute-done.17 = f32[1,256]{1,0:T(1,128)S(1)} collective-permute-done((f32[1,256]{1,0:T(1,128)S(1)}, f32[1,256]{1,0:T(1,128)S(1)}, u32[]{:S(2)}, u32[]{:S(2)}) %collective-permute-start.17) | collective-permute-done | bytes 1056 | tf_op jit(solution)/shard_map/ppermute | solution.py:33
  52.1 0.0 collective-permute-done.15
  52.1 0.2 collective-permute-start.18
  52.4 3.7 %collective-permute-done.12 = f32[1,2048]{1,0:T(1,128)S(1)} collective-permute-done((f32[1,2048]{1,0:T(1,128)S(1)}, f32[1,2048]{1,0:T(1,128)S(1)}, u32[]{:S(2)}, u32[]{:S(2)}) %collective-permute-start.12) | collective-permute-done | bytes 8224 | tf_op jit(solution)/shard_map/ppermute | solution.py:33
  56.1 0.6 %max.40 = f32[1,2048]{1,0:T(1,128)} maximum(f32[1,2048]{1,0:T(1,128)S(1)} %maximum_maximum_fusion, f32[1,2048]{1,0:T(1,128)S(1)} %collective-permute-done.12) | non-fusion elementwise | flops 2048 | bytes 24576 | tf_op jit(solution)/shard_map/max | solution.py:196
  56.7 1.2 %collective-permute-done.18 = f32[1,128]{1,0:T(1,128)S(1)} collective-permute-done((f32[1,128]{1,0:T(1,128)S(1)}, f32[1,128]{1,0:T(1,128)S(1)}, u32[]{:S(2)}, u32[]{:S(2)}) %collective-permute-start.18) | collective-permute-done | bytes 544 | tf_op jit(solution)/shard_map/ppermute | solution.py:33
  57.9 0.5 fusion
  (13 shorter events, 0.1 us)
Async XLA Ops:
  0.6 1.0 %copy-start.2 = (bf16[128,2048]{1,0:T(8,128)(2,1)S(1)}, bf16[128,2048]{1,0:T(8,128)(2,1)}, u32[]{:S(2)}) copy-start(bf16[128,2048]{1,0:T(8,128)(2,1)} %coefficients.1) | copy-start | bytes 1572868
  1.7 0.7 %copy-start.3 = (bf16[128]{0:T(256)(128)(2,1)S(1)}, bf16[128]{0:T(256)(128)(2,1)}, u32[]{:S(2)}) copy-start(bf16[128]{0:T(256)(128)(2,1)} %param.5) | copy-start | bytes 772
  2.3 8.1 %copy-start = (bf16[2048,2048]{1,0:T(8,128)(2,1)S(1)}, bf16[2048,2048]{1,0:T(8,128)(2,1)}, u32[]{:S(2)}) copy-start(bf16[2048,2048]{1,0:T(8,128)(2,1)} %states.5) | copy-start | bytes 25165828
  2.3 8.1 %copy-start.1 = (f32[2048]{0:T(1024)S(1)}, f32[2048]{0:T(1024)}, u32[]{:S(2)}) copy-start(f32[2048]{0:T(1024)} %param.7) | copy-start | bytes 24580
  2.5 6.0 %collective-permute-start.1 = (bf16[128,2176]{1,0:T(8,128)(2,1)S(1)}, bf16[128,2176]{1,0:T(8,128)(2,1)S(1)}, u32[]{:S(2)}, u32[]{:S(2)}) collective-permute-start(bf16[128,2176]{1,0:T(8,128)(2,1)S(1)} %shard_map.59.refs_0_), channel_id=1, source_target_pairs={{0,32},{32,0},{64,96},{96,64},{128,160},{160,128},{192,224},{224,1... | collective-permute-start | bytes 1671176 | tf_op jit(solution)/shard_map/ppermute | solution.py:33
  2.6 13.0 %collective-permute-start = (bf16[128,2176]{1,0:T(8,128)(2,1)S(1)}, bf16[128,2176]{1,0:T(8,128)(2,1)S(1)}, u32[]{:S(2)}, u32[]{:S(2)}) collective-permute-start(bf16[128,2176]{1,0:T(8,128)(2,1)S(1)} %shard_map.59.refs_0_), channel_id=1, source_target_pairs={{0,208},{32,96},{64,0},{96,160},{128,64},{160,224},{192,128},{224,... | collective-permute-start | bytes 1671176 | tf_op jit(solution)/shard_map/ppermute | solution.py:33
  8.6 13.0 %collective-permute-start.2 = (bf16[128,2176]{1,0:T(8,128)(2,1)S(1)}, bf16[128,2176]{1,0:T(8,128)(2,1)S(1)}, u32[]{:S(2)}, u32[]{:S(2)}) collective-permute-start(bf16[128,2176]{1,0:T(8,128)(2,1)S(1)} %collective-permute-done.1.refs_1_), channel_id=1, source_target_pairs={{0,208},{32,96},{64,0},{96,160},{128,64},{160,224},{192,128},{224,... | collective-permute-start | bytes 1671176 | tf_op jit(solution)/shard_map/ppermute | solution.py:33
  21.6 4.2 %collective-permute-start.4 = (bf16[128,2176]{1,0:T(8,128)(2,1)S(1)}, bf16[128,2176]{1,0:T(8,128)(2,1)S(1)}, u32[]{:S(2)}, u32[]{:S(2)}) collective-permute-start(bf16[128,2176]{1,0:T(8,128)(2,1)S(1)} %collective-permute-done.2.refs_3_), channel_id=1, source_target_pairs={{0,32},{32,0},{64,96},{96,64},{128,160},{160,128},{192,224},{224,1... | collective-permute-start | bytes 1671176 | tf_op jit(solution)/shard_map/ppermute | solution.py:33
  21.6 4.2 %collective-permute-start.5 = (bf16[128,2176]{1,0:T(8,128)(2,1)S(1)}, bf16[128,2176]{1,0:T(8,128)(2,1)S(1)}, u32[]{:S(2)}, u32[]{:S(2)}) collective-permute-start(bf16[128,2176]{1,0:T(8,128)(2,1)S(1)} %collective-permute-done.refs_0_), channel_id=1, source_target_pairs={{0,32},{32,0},{64,96},{96,64},{128,160},{160,128},{192,224},{224,1... | collective-permute-start | bytes 1671176 | tf_op jit(solution)/shard_map/ppermute | solution.py:33
  22.1 10.7 %collective-permute-start.3 = (bf16[128,2176]{1,0:T(8,128)(2,1)S(1)}, bf16[128,2176]{1,0:T(8,128)(2,1)S(1)}, u32[]{:S(2)}, u32[]{:S(2)}) collective-permute-start(bf16[128,2176]{1,0:T(8,128)(2,1)S(1)} %collective-permute-done.refs_0_), channel_id=1, source_target_pairs={{0,208},{32,96},{64,0},{96,160},{128,64},{160,224},{192,128},{224,... | collective-permute-start | bytes 1671176 | tf_op jit(solution)/shard_map/ppermute | solution.py:33
  30.9 1.2 %collective-permute-start.6 = (f32[1,384]{1,0:T(1,128)S(1)}, f32[1,384]{1,0:T(1,128)S(1)}, u32[]{:S(2)}, u32[]{:S(2)}) collective-permute-start(f32[1,384]{1,0:T(1,128)S(1)} %pad_maximum_fusion), channel_id=1, source_target_pairs={{0,32},{32,0},{64,96},{96,64},{128,160},{160,128},{192,224},{224,1... | collective-permute-start | bytes 4616 | tf_op jit(solution)/shard_map/ppermute | solution.py:33
  32.8 3.8 %collective-permute-start.7 = (bf16[128,2176]{1,0:T(8,128)(2,1)S(1)}, bf16[128,2176]{1,0:T(8,128)(2,1)S(1)}, u32[]{:S(2)}, u32[]{:S(2)}) collective-permute-start(bf16[128,2176]{1,0:T(8,128)(2,1)S(1)} %collective-permute-done.3.refs_0_), channel_id=1, source_target_pairs={{0,32},{32,0},{64,96},{96,64},{128,160},{160,128},{192,224},{224,1... | collective-permute-start | bytes 1671176 | tf_op jit(solution)/shard_map/ppermute | solution.py:33
  32.8 7.5 %collective-permute-start.13 = (f32[1,128]{1,0:T(1,128)S(1)}, f32[1,128]{1,0:T(1,128)S(1)}, u32[]{:S(2)}, u32[]{:S(2)}) collective-permute-start(f32[1,128]{1,0:T(1,128)S(1)} %get-tuple-element.40), channel_id=1, source_target_pairs={{0,64},{32,240},{64,128},{96,32},{128,192},{160,96},{192,16},{224,... | collective-permute-start | bytes 1544 | tf_op jit(solution)/shard_map/ppermute | solution.py:33
  32.9 7.5 %collective-permute-start.14 = (f32[1,128]{1,0:T(1,128)S(1)}, f32[1,128]{1,0:T(1,128)S(1)}, u32[]{:S(2)}, u32[]{:S(2)}) collective-permute-start(f32[1,128]{1,0:T(1,128)S(1)} %get-tuple-element.41), channel_id=1, source_target_pairs={{0,208},{32,96},{64,0},{96,160},{128,64},{160,224},{192,128},{224,... | collective-permute-start | bytes 1544 | tf_op jit(solution)/shard_map/ppermute | solution.py:33
  39.5 4.6 %collective-permute-start.8 = (f32[1,128]{1,0:T(1,128)S(1)}, f32[1,128]{1,0:T(1,128)S(1)}, u32[]{:S(2)}, u32[]{:S(2)}) collective-permute-start(f32[1,128]{1,0:T(1,128)S(1)} %get-tuple-element.33), channel_id=1, source_target_pairs={{0,32},{32,0},{64,96},{96,64},{128,160},{160,128},{192,224},{224,1... | collective-permute-start | bytes 1544 | tf_op jit(solution)/shard_map/ppermute | solution.py:33
  39.7 4.3 %collective-permute-start.9 = (f32[1,2048]{1,0:T(1,128)S(1)}, f32[1,2048]{1,0:T(1,128)S(1)}, u32[]{:S(2)}, u32[]{:S(2)}) collective-permute-start(f32[1,2048]{1,0:T(1,128)S(1)} %get-tuple-element.32), channel_id=1, source_target_pairs={{0,4},{32,36},{64,68},{96,100},{128,132},{160,164},{192,196},{224,... | collective-permute-start | bytes 24584 | tf_op jit(solution)/shard_map/ppermute | solution.py:33
  40.4 8.0 %collective-permute-start.11 = (f32[1,2048]{1,0:T(1,128)S(1)}, f32[1,2048]{1,0:T(1,128)S(1)}, u32[]{:S(2)}, u32[]{:S(2)}) collective-permute-start(f32[1,2048]{1,0:T(1,128)S(1)} %get-tuple-element.32), channel_id=1, source_target_pairs={{0,12},{32,44},{64,76},{96,108},{128,140},{160,172},{192,204},{224... | collective-permute-start | bytes 24584 | tf_op jit(solution)/shard_map/ppermute | solution.py:33
  42.6 5.8 %collective-permute-start.10 = (f32[1,2048]{1,0:T(1,128)S(1)}, f32[1,2048]{1,0:T(1,128)S(1)}, u32[]{:S(2)}, u32[]{:S(2)}) collective-permute-start(f32[1,2048]{1,0:T(1,128)S(1)} %get-tuple-element.32), channel_id=1, source_target_pairs={{0,8},{32,40},{64,72},{96,104},{128,136},{160,168},{192,200},{224,... | collective-permute-start | bytes 24584 | tf_op jit(solution)/shard_map/ppermute | solution.py:33
  44.0 7.1 %collective-permute-start.16 = (f32[1,256]{1,0:T(1,128)S(1)}, f32[1,256]{1,0:T(1,128)S(1)}, u32[]{:S(2)}, u32[]{:S(2)}) collective-permute-start(f32[1,256]{1,0:T(1,128)S(1)} %pad_maximum_fusion.1), channel_id=1, source_target_pairs={{0,2},{32,34},{64,66},{96,98},{128,130},{160,162},{192,194},{224,2... | collective-permute-start | bytes 3080 | tf_op jit(solution)/shard_map/ppermute | solution.py:33
  47.3 4.8 %collective-permute-start.17 = (f32[1,256]{1,0:T(1,128)S(1)}, f32[1,256]{1,0:T(1,128)S(1)}, u32[]{:S(2)}, u32[]{:S(2)}) collective-permute-start(f32[1,256]{1,0:T(1,128)S(1)} %pad_maximum_fusion.1), channel_id=1, source_target_pairs={{0,3},{32,35},{64,67},{96,99},{128,131},{160,163},{192,195},{224,2... | collective-permute-start | bytes 3080 | tf_op jit(solution)/shard_map/ppermute | solution.py:33
  48.4 3.7 %collective-permute-start.15 = (f32[1,256]{1,0:T(1,128)S(1)}, f32[1,256]{1,0:T(1,128)S(1)}, u32[]{:S(2)}, u32[]{:S(2)}) collective-permute-start(f32[1,256]{1,0:T(1,128)S(1)} %pad_maximum_fusion.1), channel_id=1, source_target_pairs={{0,1},{32,33},{64,65},{96,97},{128,129},{160,161},{192,193},{224,2... | collective-permute-start | bytes 3080 | tf_op jit(solution)/shard_map/ppermute | solution.py:33
  48.4 7.6 %collective-permute-start.12 = (f32[1,2048]{1,0:T(1,128)S(1)}, f32[1,2048]{1,0:T(1,128)S(1)}, u32[]{:S(2)}, u32[]{:S(2)}) collective-permute-start(f32[1,2048]{1,0:T(1,128)S(1)} %maximum_maximum_fusion), channel_id=1, source_target_pairs={{0,16},{32,48},{64,80},{96,112},{128,144},{160,176},{192,208},{224... | collective-permute-start | bytes 24584 | tf_op jit(solution)/shard_map/ppermute | solution.py:33
  52.1 5.7 %collective-permute-start.18 = (f32[1,128]{1,0:T(1,128)S(1)}, f32[1,128]{1,0:T(1,128)S(1)}, u32[]{:S(2)}, u32[]{:S(2)}) collective-permute-start(f32[1,128]{1,0:T(1,128)S(1)} %slice.20), channel_id=1, source_target_pairs={{0,128},{32,176},{64,192},{96,240},{128,16},{160,32},{192,80},{224... | collective-permute-start | bytes 1544 | tf_op jit(solution)/shard_map/ppermute | solution.py:33

commit v15 on v7

--- a/solution.py
+++ b/solution.py
@@ -190,7 +190,6 @@
     lifts = functools.reduce(jnp.maximum, for_y, lifts)
     across = send(top, far)
     returned = send(lifts[:, cuts:], two_back)
-    across, returned = fence((across, returned))
     new_values = jnp.maximum(top, across)
     cut_gaps = jnp.maximum(returned, lifts[:, :cuts])
     return new_values[0], cut_gaps[0]

time: 61.8 us -> 60.8 us (0.984); the launches traced: 61.6 us -> 60 us
  waiting for transfers between devices: 20.2 us -> 18.5 us
    ppermute x19, waiting for transfers between devices: 20.2 us -> 18.5 us  [send(): return lax.ppermute(block, AXES, routes(move))]
  transfers between devices with their start and end apart: 19 -> 19, of which waited for: 6 -> 8; matrix products, arithmetic and copies ran while one was open for 0% -> 1% of each run, Pallas kernels for 17% -> 18%
where the time goes in v15:
time: 60.8 us; the launch traced here: 60 us
  starting transfers between devices  26.9 us (44%)
  waiting for transfers between devices  18.5 us (30%)
  Pallas kernels  11 us (18%)
  local copies, waits for them, and re-layouts  1.7 us (3%)
  other arithmetic  1.17 us (2%)
  between operations  0.75 us (1%)
    ppermute x19, starting transfers between devices, send(): return lax.ppermute(block, AXES, routes(move))  26.9 us
    ppermute x19, waiting for transfers between devices, send(): return lax.ppermute(block, AXES, routes(move))  18.5 us
    pallas_call x3, Pallas kernels, score(): pl.pallas_call(functools.partial(score_body, tile, tiles, len(blocks)), g...  10.8 us
    unnamed x8, local copies, waits for them, and re-layouts  1.7 us
  transfers between devices with their start and end apart: 19, of which 8 were waited for; matrix products, arithmetic and copies ran while one was open for 1% of the time, Pallas kernels for 18%

profile of v15, /device:TPU:2, one launch (start us, length us, event | category | flops | bytes accessed | tf_op | source)
XLA Modules:
  0.0 60.0 jit_solution(10404625018451178071)
XLA Ops:
  0.6 0.0 copy-start.2
  0.6 1.0 %copy-done.2 = bf16[128,2048]{1,0:T(8,128)(2,1)S(1)} copy-done((bf16[128,2048]{1,0:T(8,128)(2,1)S(1)}, bf16[128,2048]{1,0:T(8,128)(2,1)}, u32[]{:S(2)}) %copy-start.2) | copy-done | bytes 524312
  1.7 0.7 %copy-done.3 = bf16[128]{0:T(256)(128)(2,1)S(1)} copy-done((bf16[128]{0:T(256)(128)(2,1)S(1)}, bf16[128]{0:T(256)(128)(2,1)}, u32[]{:S(2)}) %copy-start.3) | copy-done | bytes 280
  2.3 0.2 shard_map.59.refs_0_
  2.5 0.1 collective-permute-start.2
  2.6 2.0 %collective-permute-start.1 = (bf16[128,2176]{1,0:T(8,128)(2,1)S(1)}, bf16[128,2176]{1,0:T(8,128)(2,1)S(1)}, u32[]{:S(2)}, u32[]{:S(2)}) collective-permute-start(bf16[128,2176]{1,0:T(8,128)(2,1)S(1)} %shard_map.59.refs_0_), channel_id=1, source_target_pairs={{0,64},{32,240},{64,128},{96,32},{128,192},{160,96},{192,16},{224,... | collective-permute-start | bytes 1671176 | tf_op jit(solution)/shard_map/ppermute | solution.py:33
  4.6 4.0 %collective-permute-start = (bf16[128,2176]{1,0:T(8,128)(2,1)S(1)}, bf16[128,2176]{1,0:T(8,128)(2,1)S(1)}, u32[]{:S(2)}, u32[]{:S(2)}) collective-permute-start(bf16[128,2176]{1,0:T(8,128)(2,1)S(1)} %shard_map.59.refs_0_), channel_id=1, source_target_pairs={{0,208},{32,96},{64,0},{96,160},{128,64},{160,224},{192,128},{224,... | collective-permute-start | bytes 1671176 | tf_op jit(solution)/shard_map/ppermute | solution.py:33
  8.7 0.0 collective-permute-done.2.refs_1_
  8.7 0.0 copy-done.1
  8.7 2.8 %shard_map.60 = (f32[1,2048]{1,0:T(1,128)S(1)}, f32[1,128]{1,0:T(1,128)S(1)}, f32[1,128]{1,0:T(1,128)S(1)}) custom-call(f32[1,2048]{1,0:T(1,128)S(1)} %bitcast.5, f32[1,2048]{1,0:T(1,128)S(1)} %bitcast.6, bf16[2048,2048]{1,0:T(8,128)(2,1)S(1)} %copy-done, bf16[128,2176]{1,0:T(8,128)(2,1)S(1)} %shard_map.59.refs_0_, ...), custom_call_target="tpu_custom_call" | custom-call | flops 2147483648 | bytes 9437184 | tf_op jit(solution)/shard_map/pallas_call | solution.py:141
  11.5 8.1 %collective-permute-done.1.refs_1_ = bf16[128,2176]{1,0:T(8,128)(2,1)S(1)} collective-permute-done((bf16[128,2176]{1,0:T(8,128)(2,1)S(1)}, bf16[128,2176]{1,0:T(8,128)(2,1)S(1)}, u32[]{:S(2)}, u32[]{:S(2)}) %collective-permute-start.1) | collective-permute-done | bytes 557088 | tf_op jit(solution)/shard_map/ppermute | solution.py:33
  19.6 1.5 %collective-permute-done.refs_0_ = bf16[128,2176]{1,0:T(8,128)(2,1)S(1)} collective-permute-done((bf16[128,2176]{1,0:T(8,128)(2,1)S(1)}, bf16[128,2176]{1,0:T(8,128)(2,1)S(1)}, u32[]{:S(2)}, u32[]{:S(2)}) %collective-permute-start) | collective-permute-done | bytes 557088 | tf_op jit(solution)/shard_map/ppermute | solution.py:33
  21.0 0.8 %collective-permute-start.5 = (bf16[128,2176]{1,0:T(8,128)(2,1)S(1)}, bf16[128,2176]{1,0:T(8,128)(2,1)S(1)}, u32[]{:S(2)}, u32[]{:S(2)}) collective-permute-start(bf16[128,2176]{1,0:T(8,128)(2,1)S(1)} %collective-permute-done.1.refs_1_), channel_id=1, source_target_pairs={{0,32},{32,0},{64,96},{96,64},{128,160},{160,128},{192,224},{224,1... | collective-permute-start | bytes 1671176 | tf_op jit(solution)/shard_map/ppermute | solution.py:33
  21.9 0.0 collective-permute-start.4
  21.9 3.4 %collective-permute-start.3 = (bf16[128,2176]{1,0:T(8,128)(2,1)S(1)}, bf16[128,2176]{1,0:T(8,128)(2,1)S(1)}, u32[]{:S(2)}, u32[]{:S(2)}) collective-permute-start(bf16[128,2176]{1,0:T(8,128)(2,1)S(1)} %collective-permute-done.refs_0_), channel_id=1, source_target_pairs={{0,208},{32,96},{64,0},{96,160},{128,64},{160,224},{192,128},{224,... | collective-permute-start | bytes 1671176 | tf_op jit(solution)/shard_map/ppermute | solution.py:33
  25.2 0.0 collective-permute-done.5.refs_3_
  25.2 0.0 collective-permute-done.4.refs_2_
  25.2 5.1 %shard_map.61 = (f32[1,2048]{1,0:T(1,128)S(1)}, f32[1,256]{1,0:T(1,128)S(1)}, f32[1,256]{1,0:T(1,128)S(1)}) custom-call(f32[1,2048]{1,0:T(1,128)S(1)} %bitcast.7, f32[1,2048]{1,0:T(1,128)S(1)} %get-tuple-element.23.prev, bf16[2048,2048]{1,0:T(8,128)(2,1)S(1)} %copy-done, bf16[128,2176]{1,0:T(8,128)(2,1)S(1)} %collective-permute-done.refs_0_, ...), custom_call_target="tpu_custom_call" | custom-call | flops 4294967296 | bytes 10485760 | tf_op jit(solution)/shard_map/pallas_call | solution.py:141
  30.4 0.1 collective-permute-start.6
  30.5 1.1 %collective-permute-done.6 = f32[1,384]{1,0:T(1,128)S(1)} collective-permute-done((f32[1,384]{1,0:T(1,128)S(1)}, f32[1,384]{1,0:T(1,128)S(1)}, u32[]{:S(2)}, u32[]{:S(2)}) %collective-permute-start.6) | collective-permute-done | bytes 1568 | tf_op jit(solution)/shard_map/ppermute | solution.py:33
  31.6 0.7 %collective-permute-done.3.refs_0_ = bf16[128,2176]{1,0:T(8,128)(2,1)S(1)} collective-permute-done((bf16[128,2176]{1,0:T(8,128)(2,1)S(1)}, bf16[128,2176]{1,0:T(8,128)(2,1)S(1)}, u32[]{:S(2)}, u32[]{:S(2)}) %collective-permute-start.3) | collective-permute-done | bytes 557088 | tf_op jit(solution)/shard_map/ppermute | solution.py:33
  32.3 0.0 collective-permute-start.9
  32.3 0.0 collective-permute-start.7
  32.3 3.8 %collective-permute-start.8 = (f32[1,128]{1,0:T(1,128)S(1)}, f32[1,128]{1,0:T(1,128)S(1)}, u32[]{:S(2)}, u32[]{:S(2)}) collective-permute-start(f32[1,128]{1,0:T(1,128)S(1)} %get-tuple-element.41), channel_id=1, source_target_pairs={{0,208},{32,96},{64,0},{96,160},{128,64},{160,224},{192,128},{224,... | collective-permute-start | bytes 1544 | tf_op jit(solution)/shard_map/ppermute | solution.py:33
  36.1 0.0 collective-permute-done.9.refs_1_
  36.1 2.8 %shard_map.62 = (f32[1,2048]{1,0:T(1,128)S(1)}, f32[1,128]{1,0:T(1,128)S(1)}, f32[1,128]{1,0:T(1,128)S(1)}) custom-call(f32[1,2048]{1,0:T(1,128)S(1)} %bitcast.8, f32[1,2048]{1,0:T(1,128)S(1)} %get-tuple-element.31.prev, bf16[2048,2048]{1,0:T(8,128)(2,1)S(1)} %copy-done, bf16[128,2176]{1,0:T(8,128)(2,1)S(1)} %collective-permute-done.3.refs_0_, ...), custom_call_target="tpu_custom_call" | custom-call | flops 2147483648 | bytes 9437184 | tf_op jit(solution)/shard_map/pallas_call | solution.py:141
  38.9 0.2 collective-permute-start.10
  39.2 0.7 %collective-permute-start.11 = (f32[1,2048]{1,0:T(1,128)S(1)}, f32[1,2048]{1,0:T(1,128)S(1)}, u32[]{:S(2)}, u32[]{:S(2)}) collective-permute-start(f32[1,2048]{1,0:T(1,128)S(1)} %get-tuple-element.35), channel_id=1, source_target_pairs={{0,4},{32,36},{64,68},{96,100},{128,132},{160,164},{192,196},{224,... | collective-permute-start | bytes 24584 | tf_op jit(solution)/shard_map/ppermute | solution.py:33
  39.8 0.0 collective-permute-done.7
  39.8 0.0 collective-permute-done.8
  39.8 2.2 %collective-permute-start.14 = (f32[1,2048]{1,0:T(1,128)S(1)}, f32[1,2048]{1,0:T(1,128)S(1)}, u32[]{:S(2)}, u32[]{:S(2)}) collective-permute-start(f32[1,2048]{1,0:T(1,128)S(1)} %get-tuple-element.35), channel_id=1, source_target_pairs={{0,12},{32,44},{64,76},{96,108},{128,140},{160,172},{192,204},{224... | collective-permute-start | bytes 24584 | tf_op jit(solution)/shard_map/ppermute | solution.py:33
  42.1 1.4 %collective-permute-start.13 = (f32[1,2048]{1,0:T(1,128)S(1)}, f32[1,2048]{1,0:T(1,128)S(1)}, u32[]{:S(2)}, u32[]{:S(2)}) collective-permute-start(f32[1,2048]{1,0:T(1,128)S(1)} %get-tuple-element.35), channel_id=1, source_target_pairs={{0,8},{32,40},{64,72},{96,104},{128,136},{160,168},{192,200},{224,... | collective-permute-start | bytes 24584 | tf_op jit(solution)/shard_map/ppermute | solution.py:33
  43.5 0.0 collective-permute-done.10
  43.5 0.0 collective-permute-done.11
  43.5 3.3 %collective-permute-start.16 = (f32[1,256]{1,0:T(1,128)S(1)}, f32[1,256]{1,0:T(1,128)S(1)}, u32[]{:S(2)}, u32[]{:S(2)}) collective-permute-start(f32[1,256]{1,0:T(1,128)S(1)} %pad_maximum_fusion.1), channel_id=1, source_target_pairs={{0,2},{32,34},{64,66},{96,98},{128,130},{160,162},{192,194},{224,2... | collective-permute-start | bytes 3080 | tf_op jit(solution)/shard_map/ppermute | solution.py:33
  46.8 1.1 %collective-permute-start.17 = (f32[1,256]{1,0:T(1,128)S(1)}, f32[1,256]{1,0:T(1,128)S(1)}, u32[]{:S(2)}, u32[]{:S(2)}) collective-permute-start(f32[1,256]{1,0:T(1,128)S(1)} %pad_maximum_fusion.1), channel_id=1, source_target_pairs={{0,3},{32,35},{64,67},{96,99},{128,131},{160,163},{192,195},{224,2... | collective-permute-start | bytes 3080 | tf_op jit(solution)/shard_map/ppermute | solution.py:33
  47.8 0.0 collective-permute-start.12
  47.8 0.0 collective-permute-done.14
  47.8 0.0 collective-permute-done.13
  47.9 3.5 %collective-permute-done.12 = f32[1,256]{1,0:T(1,128)S(1)} collective-permute-done((f32[1,256]{1,0:T(1,128)S(1)}, f32[1,256]{1,0:T(1,128)S(1)}, u32[]{:S(2)}, u32[]{:S(2)}) %collective-permute-start.12) | collective-permute-done | bytes 1056 | tf_op jit(solution)/shard_map/ppermute | solution.py:33
  51.4 0.0 collective-permute-done.16
  51.4 0.2 collective-permute-done.17
  51.6 0.1 collective-permute-start.18
  51.7 3.7 %collective-permute-start.15 = (f32[1,2048]{1,0:T(1,128)S(1)}, f32[1,2048]{1,0:T(1,128)S(1)}, u32[]{:S(2)}, u32[]{:S(2)}) collective-permute-start(f32[1,2048]{1,0:T(1,128)S(1)} %maximum_maximum_fusion), channel_id=1, source_target_pairs={{0,16},{32,48},{64,80},{96,112},{128,144},{160,176},{192,208},{224... | collective-permute-start | bytes 24584 | tf_op jit(solution)/shard_map/ppermute | solution.py:33
  55.4 1.9 %collective-permute-done.18 = f32[1,128]{1,0:T(1,128)S(1)} collective-permute-done((f32[1,128]{1,0:T(1,128)S(1)}, f32[1,128]{1,0:T(1,128)S(1)}, u32[]{:S(2)}, u32[]{:S(2)}) %collective-permute-start.18) | collective-permute-done | bytes 544 | tf_op jit(solution)/shard_map/ppermute | solution.py:33
  57.3 0.5 fusion
  57.8 1.6 %collective-permute-done.15 = f32[1,2048]{1,0:T(1,128)S(1)} collective-permute-done((f32[1,2048]{1,0:T(1,128)S(1)}, f32[1,2048]{1,0:T(1,128)S(1)}, u32[]{:S(2)}, u32[]{:S(2)}) %collective-permute-start.15) | collective-permute-done | bytes 8224 | tf_op jit(solution)/shard_map/ppermute | solution.py:33
  59.4 0.6 %max.43 = f32[1,2048]{1,0:T(1,128)} maximum(f32[1,2048]{1,0:T(1,128)S(1)} %maximum_maximum_fusion, f32[1,2048]{1,0:T(1,128)S(1)} %collective-permute-done.15) | non-fusion elementwise | flops 2048 | bytes 24576 | tf_op jit(solution)/shard_map/max | solution.py:193
  (13 shorter events, 0.1 us)
Async XLA Ops:
  0.6 1.0 %copy-start.2 = (bf16[128,2048]{1,0:T(8,128)(2,1)S(1)}, bf16[128,2048]{1,0:T(8,128)(2,1)}, u32[]{:S(2)}) copy-start(bf16[128,2048]{1,0:T(8,128)(2,1)} %coefficients.1) | copy-start | bytes 1572868
  1.7 0.7 %copy-start.3 = (bf16[128]{0:T(256)(128)(2,1)S(1)}, bf16[128]{0:T(256)(128)(2,1)}, u32[]{:S(2)}) copy-start(bf16[128]{0:T(256)(128)(2,1)} %param.5) | copy-start | bytes 772
  2.3 6.3 %copy-start = (bf16[2048,2048]{1,0:T(8,128)(2,1)S(1)}, bf16[2048,2048]{1,0:T(8,128)(2,1)}, u32[]{:S(2)}) copy-start(bf16[2048,2048]{1,0:T(8,128)(2,1)} %states.5) | copy-start | bytes 25165828
  2.3 6.3 %copy-start.1 = (f32[2048]{0:T(1024)S(1)}, f32[2048]{0:T(1024)}, u32[]{:S(2)}) copy-start(f32[2048]{0:T(1024)} %param.7) | copy-start | bytes 24580
  2.5 6.1 %collective-permute-start.2 = (bf16[128,2176]{1,0:T(8,128)(2,1)S(1)}, bf16[128,2176]{1,0:T(8,128)(2,1)S(1)}, u32[]{:S(2)}, u32[]{:S(2)}) collective-permute-start(bf16[128,2176]{1,0:T(8,128)(2,1)S(1)} %shard_map.59.refs_0_), channel_id=1, source_target_pairs={{0,32},{32,0},{64,96},{96,64},{128,160},{160,128},{192,224},{224,1... | collective-permute-start | bytes 1671176 | tf_op jit(solution)/shard_map/ppermute | solution.py:33
  2.6 16.9 %collective-permute-start.1 = (bf16[128,2176]{1,0:T(8,128)(2,1)S(1)}, bf16[128,2176]{1,0:T(8,128)(2,1)S(1)}, u32[]{:S(2)}, u32[]{:S(2)}) collective-permute-start(bf16[128,2176]{1,0:T(8,128)(2,1)S(1)} %shard_map.59.refs_0_), channel_id=1, source_target_pairs={{0,64},{32,240},{64,128},{96,32},{128,192},{160,96},{192,16},{224,... | collective-permute-start | bytes 1671176 | tf_op jit(solution)/shard_map/ppermute | solution.py:33
  4.6 16.4 %collective-permute-start = (bf16[128,2176]{1,0:T(8,128)(2,1)S(1)}, bf16[128,2176]{1,0:T(8,128)(2,1)S(1)}, u32[]{:S(2)}, u32[]{:S(2)}) collective-permute-start(bf16[128,2176]{1,0:T(8,128)(2,1)S(1)} %shard_map.59.refs_0_), channel_id=1, source_target_pairs={{0,208},{32,96},{64,0},{96,160},{128,64},{160,224},{192,128},{224,... | collective-permute-start | bytes 1671176 | tf_op jit(solution)/shard_map/ppermute | solution.py:33
  21.0 4.2 %collective-permute-start.5 = (bf16[128,2176]{1,0:T(8,128)(2,1)S(1)}, bf16[128,2176]{1,0:T(8,128)(2,1)S(1)}, u32[]{:S(2)}, u32[]{:S(2)}) collective-permute-start(bf16[128,2176]{1,0:T(8,128)(2,1)S(1)} %collective-permute-done.1.refs_1_), channel_id=1, source_target_pairs={{0,32},{32,0},{64,96},{96,64},{128,160},{160,128},{192,224},{224,1... | collective-permute-start | bytes 1671176 | tf_op jit(solution)/shard_map/ppermute | solution.py:33
  21.9 3.4 %collective-permute-start.4 = (bf16[128,2176]{1,0:T(8,128)(2,1)S(1)}, bf16[128,2176]{1,0:T(8,128)(2,1)S(1)}, u32[]{:S(2)}, u32[]{:S(2)}) collective-permute-start(bf16[128,2176]{1,0:T(8,128)(2,1)S(1)} %collective-permute-done.refs_0_), channel_id=1, source_target_pairs={{0,32},{32,0},{64,96},{96,64},{128,160},{160,128},{192,224},{224,1... | collective-permute-start | bytes 1671176 | tf_op jit(solution)/shard_map/ppermute | solution.py:33
  21.9 10.4 %collective-permute-start.3 = (bf16[128,2176]{1,0:T(8,128)(2,1)S(1)}, bf16[128,2176]{1,0:T(8,128)(2,1)S(1)}, u32[]{:S(2)}, u32[]{:S(2)}) collective-permute-start(bf16[128,2176]{1,0:T(8,128)(2,1)S(1)} %collective-permute-done.refs_0_), channel_id=1, source_target_pairs={{0,208},{32,96},{64,0},{96,160},{128,64},{160,224},{192,128},{224,... | collective-permute-start | bytes 1671176 | tf_op jit(solution)/shard_map/ppermute | solution.py:33
  30.4 1.2 %collective-permute-start.6 = (f32[1,384]{1,0:T(1,128)S(1)}, f32[1,384]{1,0:T(1,128)S(1)}, u32[]{:S(2)}, u32[]{:S(2)}) collective-permute-start(f32[1,384]{1,0:T(1,128)S(1)} %pad_maximum_fusion), channel_id=1, source_target_pairs={{0,32},{32,0},{64,96},{96,64},{128,160},{160,128},{192,224},{224,1... | collective-permute-start | bytes 4616 | tf_op jit(solution)/shard_map/ppermute | solution.py:33
  32.3 3.8 %collective-permute-start.9 = (bf16[128,2176]{1,0:T(8,128)(2,1)S(1)}, bf16[128,2176]{1,0:T(8,128)(2,1)S(1)}, u32[]{:S(2)}, u32[]{:S(2)}) collective-permute-start(bf16[128,2176]{1,0:T(8,128)(2,1)S(1)} %collective-permute-done.3.refs_0_), channel_id=1, source_target_pairs={{0,32},{32,0},{64,96},{96,64},{128,160},{160,128},{192,224},{224,1... | collective-permute-start | bytes 1671176 | tf_op jit(solution)/shard_map/ppermute | solution.py:33
  32.3 7.5 %collective-permute-start.7 = (f32[1,128]{1,0:T(1,128)S(1)}, f32[1,128]{1,0:T(1,128)S(1)}, u32[]{:S(2)}, u32[]{:S(2)}) collective-permute-start(f32[1,128]{1,0:T(1,128)S(1)} %get-tuple-element.40), channel_id=1, source_target_pairs={{0,64},{32,240},{64,128},{96,32},{128,192},{160,96},{192,16},{224,... | collective-permute-start | bytes 1544 | tf_op jit(solution)/shard_map/ppermute | solution.py:33
  32.3 7.5 %collective-permute-start.8 = (f32[1,128]{1,0:T(1,128)S(1)}, f32[1,128]{1,0:T(1,128)S(1)}, u32[]{:S(2)}, u32[]{:S(2)}) collective-permute-start(f32[1,128]{1,0:T(1,128)S(1)} %get-tuple-element.41), channel_id=1, source_target_pairs={{0,208},{32,96},{64,0},{96,160},{128,64},{160,224},{192,128},{224,... | collective-permute-start | bytes 1544 | tf_op jit(solution)/shard_map/ppermute | solution.py:33
  38.9 4.6 %collective-permute-start.10 = (f32[1,128]{1,0:T(1,128)S(1)}, f32[1,128]{1,0:T(1,128)S(1)}, u32[]{:S(2)}, u32[]{:S(2)}) collective-permute-start(f32[1,128]{1,0:T(1,128)S(1)} %get-tuple-element.34), channel_id=1, source_target_pairs={{0,32},{32,0},{64,96},{96,64},{128,160},{160,128},{192,224},{224,1... | collective-permute-start | bytes 1544 | tf_op jit(solution)/shard_map/ppermute | solution.py:33
  39.2 4.3 %collective-permute-start.11 = (f32[1,2048]{1,0:T(1,128)S(1)}, f32[1,2048]{1,0:T(1,128)S(1)}, u32[]{:S(2)}, u32[]{:S(2)}) collective-permute-start(f32[1,2048]{1,0:T(1,128)S(1)} %get-tuple-element.35), channel_id=1, source_target_pairs={{0,4},{32,36},{64,68},{96,100},{128,132},{160,164},{192,196},{224,... | collective-permute-start | bytes 24584 | tf_op jit(solution)/shard_map/ppermute | solution.py:33
  39.8 8.0 %collective-permute-start.14 = (f32[1,2048]{1,0:T(1,128)S(1)}, f32[1,2048]{1,0:T(1,128)S(1)}, u32[]{:S(2)}, u32[]{:S(2)}) collective-permute-start(f32[1,2048]{1,0:T(1,128)S(1)} %get-tuple-element.35), channel_id=1, source_target_pairs={{0,12},{32,44},{64,76},{96,108},{128,140},{160,172},{192,204},{224... | collective-permute-start | bytes 24584 | tf_op jit(solution)/shard_map/ppermute | solution.py:33
  42.1 5.8 %collective-permute-start.13 = (f32[1,2048]{1,0:T(1,128)S(1)}, f32[1,2048]{1,0:T(1,128)S(1)}, u32[]{:S(2)}, u32[]{:S(2)}) collective-permute-start(f32[1,2048]{1,0:T(1,128)S(1)} %get-tuple-element.35), channel_id=1, source_target_pairs={{0,8},{32,40},{64,72},{96,104},{128,136},{160,168},{192,200},{224,... | collective-permute-start | bytes 24584 | tf_op jit(solution)/shard_map/ppermute | solution.py:33
  43.5 7.9 %collective-permute-start.16 = (f32[1,256]{1,0:T(1,128)S(1)}, f32[1,256]{1,0:T(1,128)S(1)}, u32[]{:S(2)}, u32[]{:S(2)}) collective-permute-start(f32[1,256]{1,0:T(1,128)S(1)} %pad_maximum_fusion.1), channel_id=1, source_target_pairs={{0,2},{32,34},{64,66},{96,98},{128,130},{160,162},{192,194},{224,2... | collective-permute-start | bytes 3080 | tf_op jit(solution)/shard_map/ppermute | solution.py:33
  46.8 4.8 %collective-permute-start.17 = (f32[1,256]{1,0:T(1,128)S(1)}, f32[1,256]{1,0:T(1,128)S(1)}, u32[]{:S(2)}, u32[]{:S(2)}) collective-permute-start(f32[1,256]{1,0:T(1,128)S(1)} %pad_maximum_fusion.1), channel_id=1, source_target_pairs={{0,3},{32,35},{64,67},{96,99},{128,131},{160,163},{192,195},{224,2... | collective-permute-start | bytes 3080 | tf_op jit(solution)/shard_map/ppermute | solution.py:33
  47.8 3.6 %collective-permute-start.12 = (f32[1,256]{1,0:T(1,128)S(1)}, f32[1,256]{1,0:T(1,128)S(1)}, u32[]{:S(2)}, u32[]{:S(2)}) collective-permute-start(f32[1,256]{1,0:T(1,128)S(1)} %pad_maximum_fusion.1), channel_id=1, source_target_pairs={{0,1},{32,33},{64,65},{96,97},{128,129},{160,161},{192,193},{224,2... | collective-permute-start | bytes 3080 | tf_op jit(solution)/shard_map/ppermute | solution.py:33
  51.6 5.7 %collective-permute-start.18 = (f32[1,128]{1,0:T(1,128)S(1)}, f32[1,128]{1,0:T(1,128)S(1)}, u32[]{:S(2)}, u32[]{:S(2)}) collective-permute-start(f32[1,128]{1,0:T(1,128)S(1)} %slice.20), channel_id=1, source_target_pairs={{0,128},{32,176},{64,192},{96,240},{128,16},{160,32},{192,80},{224... | collective-permute-start | bytes 1544 | tf_op jit(solution)/shard_map/ppermute | solution.py:33
  51.7 7.7 %collective-permute-start.15 = (f32[1,2048]{1,0:T(1,128)S(1)}, f32[1,2048]{1,0:T(1,128)S(1)}, u32[]{:S(2)}, u32[]{:S(2)}) collective-permute-start(f32[1,2048]{1,0:T(1,128)S(1)} %maximum_maximum_fusion), channel_id=1, source_target_pairs={{0,16},{32,48},{64,80},{96,112},{128,144},{160,176},{192,208},{224... | collective-permute-start | bytes 24584 | tf_op jit(solution)/shard_map/ppermute | solution.py:33
